TPU v7x, 128 devices: a whole 4x4x4 slice. The times are simulated.
128 devices in a mesh: gx: 16 (over y, z), gy: 8 (over x, core).
Axes of the slice: x: 4, y: 4, z: 4, core: 2. Of those that a mesh axis runs over, the one named last changes fastest.
Arguments:
- tokens: bfloat16 [1024, 18432], P('gy', 'gx'), may hold values from -125 to 125
- norm_gain: bfloat16 [18432], P('gx'), may hold values from 0.099609375 to 1.8984375
- w_query: bfloat16 [18432, 12288], P('gx', 'gy'), may hold values from -0.046875 to 0.046875
- w_keyvalue: bfloat16 [18432, 512], P('gx', 'gy'), may hold values from -0.109375 to 0.109375
- w_out: bfloat16 [12288, 18432], P('gy', 'gx'), may hold values from -0.21875 to 0.21875
- cache_keys: bfloat16 [512, 2048, 256], P(('gx', 'gy')), may hold values from -250 to 250
- cache_values: bfloat16 [512, 2048, 256], P(('gx', 'gy')), may hold values from -15 to 15
- lengths: int32 [512], P(('gx', 'gy')), may hold values from 1024 to 2048, as said below
Outputs:
- mixed: bfloat16 [1024, 18432], P('gy', 'gx')
Inputs may be any that keep to these rules, and one draw needn't show every extreme that they name: `lengths`: some request has exactly 2048 live slots and some has exactly 1024.
All inputs are finite; a program needn't handle non-finite values.
Results may differ from a plain program's by a relative error of at most 0.035.
Values may be sent and summed in bfloat16 or wider, within the bound.
No kernel may reach another device: no remote copies, remote signals or barrier semaphores. Data moves between devices by JAX's collectives and lax.ppermute only.
A program may use at most 64 MiB of HBM per device.

v0:
```python
import jax
import jax.numpy as jnp
from jax import lax
from jax.sharding import PartitionSpec as P

D = 18432
HD = 256
STEPS = 2


def rotate(values, positions):
    half_dim = values.shape[-1] // 2
    freqs = 10000.0 ** (-jnp.arange(half_dim, dtype=jnp.float32) / half_dim)
    angles = positions.astype(jnp.float32)[..., None] * freqs
    cosine = jnp.cos(angles)
    sine = jnp.sin(angles)
    first = values[..., :half_dim]
    second = values[..., half_dim:]
    return jnp.concatenate(
        [first * cosine - second * sine, second * cosine + first * sine], axis=-1
    )


def normalize(token_rows, sums, squares, norm_gain):
    row_mean = sums / D
    variance = squares / D - row_mean * row_mean
    floated = token_rows.astype(jnp.float32)
    return (
        (floated - row_mean[:, None])
        * lax.rsqrt(variance + 1e-05)[:, None]
        * norm_gain.astype(jnp.float32)
    ).astype(jnp.bfloat16)


def attend(query, new_keys, new_values, cache_keys, cache_values, lengths):
    scale = query.shape[-1] ** (-0.5)
    cached = (
        jnp.einsum("rshd,rld->rshl", query, cache_keys, preferred_element_type=jnp.float32) * scale
    )
    valid = jnp.arange(cache_keys.shape[1], dtype=jnp.int32)[None, :] < lengths[:, None]
    cached = jnp.where(valid[:, None, None, :], cached, -jnp.inf)
    fresh = (
        jnp.einsum("rshd,rtd->rsht", query, new_keys, preferred_element_type=jnp.float32) * scale
    )
    count = query.shape[1]
    causal = jnp.arange(count)[None, :] <= jnp.arange(count)[:, None]
    fresh = jnp.where(causal[None, :, None, :], fresh, -jnp.inf)
    top_score = jnp.maximum(jnp.max(cached, axis=-1), jnp.max(fresh, axis=-1))
    cache_weight = jnp.exp(cached - top_score[..., None])
    fresh_weight = jnp.exp(fresh - top_score[..., None])
    denom = jnp.sum(cache_weight, axis=-1) + jnp.sum(fresh_weight, axis=-1)
    cache_share = (cache_weight / denom[..., None]).astype(jnp.bfloat16)
    fresh_share = (fresh_weight / denom[..., None]).astype(jnp.bfloat16)
    result = jnp.einsum(
        "rshl,rld->rshd", cache_share, cache_values, preferred_element_type=jnp.float32
    )
    result = result + jnp.einsum(
        "rsht,rtd->rshd", fresh_share, new_values, preferred_element_type=jnp.float32
    )
    return result.astype(jnp.bfloat16)


def per_device(tokens, norm_gain, w_query, w_keyvalue, w_out, cache_keys, cache_values, lengths):
    floated = tokens.astype(jnp.float32)
    sums, squares = lax.psum((jnp.sum(floated, axis=1), jnp.sum(floated * floated, axis=1)), "gx")
    gathered = lax.all_gather(normalize(tokens, sums, squares, norm_gain), "gy", axis=0, tiled=True)
    query_part = jnp.dot(gathered, w_query, preferred_element_type=jnp.float32)
    pair_part = jnp.dot(gathered, w_keyvalue, preferred_element_type=jnp.float32)
    query_sum, pair_sum = (
        lax.psum_scatter(
            query_part.astype(jnp.bfloat16), "gx", scatter_dimension=0, tiled=True
        ).astype(jnp.float32),
        lax.psum_scatter(
            pair_part.astype(jnp.bfloat16), "gx", scatter_dimension=0, tiled=True
        ).astype(jnp.float32),
    )
    query, keyvalue = (
        lax.all_to_all(
            query_sum.astype(jnp.bfloat16), "gy", split_axis=0, concat_axis=1, tiled=True
        ),
        lax.all_to_all(
            pair_sum.astype(jnp.bfloat16), "gy", split_axis=0, concat_axis=1, tiled=True
        ),
    )
    local_requests = cache_keys.shape[0]
    head_count = query.shape[1] // HD
    query = query.reshape(local_requests, STEPS, head_count, HD)
    keyvalue = keyvalue.reshape(local_requests, STEPS, 2 * HD)
    positions = lengths[:, None] + jnp.arange(STEPS, dtype=jnp.int32)[None, :]
    rotated_query = rotate(query.astype(jnp.float32), positions[:, :, None]).astype(jnp.bfloat16)
    rotated_key = rotate(keyvalue[..., :HD].astype(jnp.float32), positions).astype(jnp.bfloat16)
    new_value = keyvalue[..., HD:]
    attended = attend(rotated_query, rotated_key, new_value, cache_keys, cache_values, lengths)
    attended = attended.reshape(local_requests * STEPS, head_count * HD)
    returned = lax.all_to_all(attended, "gy", split_axis=1, concat_axis=0, tiled=True)
    partial_out = jnp.dot(
        lax.all_gather(returned, "gx", axis=0, tiled=True),
        w_out,
        preferred_element_type=jnp.float32,
    )
    return lax.psum_scatter(partial_out.astype(jnp.bfloat16), "gy", scatter_dimension=0, tiled=True)


def solution(mesh):
    return jax.shard_map(
        per_device,
        mesh=mesh,
        in_specs=(
            P("gy", "gx"),
            P("gx"),
            P("gx", "gy"),
            P("gx", "gy"),
            P("gy", "gx"),
            P(("gx", "gy"), None, None),
            P(("gx", "gy"), None, None),
            P(("gx", "gy")),
        ),
        out_specs=P("gy", "gx"),
        check_vma=False,
    )
```

profile of v0, /device:TPU:1, one launch (start us, length us, event | category | flops | bytes accessed | tf_op | source)
XLA Modules:
  0.0 357.5 jit_solution(10025993219073232926)
XLA Ops:
  6.5 0.0 copy-start
  6.5 0.0 all-gather.3.cloned.1.call-start
  6.5 1.3 convert_reduce_fusion
  7.8 0.7 convert_element_type.61
  8.5 36.2 %all-reduce = (f32[128]{0:T(128)}, f32[128]{0:T(128)}) all-reduce(f32[128]{0:T(128)S(1)} %get-tuple-element.6, f32[128]{0:T(128)S(1)} %get-tuple-element.5), channel_id=1, replica_groups=mesh['gx'=16,'gy'=8] {'gx'}, use_global_device_ids=true, to_apply=%region_3.0 | all-reduce | flops 256 | bytes 2048 | tf_op jit(solution)/shard_map/psum | solution.py:65
  44.7 0.7 broadcast_multiply_fusion
  45.4 1.9 fusion.13
  47.3 0.0 all-gather.3.cloned.1.call-update
  47.3 0.0 reduce-scatter.6.cloned.1.call-start
  47.3 29.5 %all-gather.3.cloned.1.call-done = bf16[1024,1152]{1,0:T(8,128)(2,1)} async-done(((bf16[128,1152]{1,0:T(8,128)(2,1)}), bf16[1024,1152]{1,0:T(8,128)(2,1)}) %all-gather.3.cloned.1.call-update) | async-done | bytes 2359312 | tf_op jit(solution)/shard_map/all_gather | solution.py:66
  76.9 3.1 convolution_convert_fusion.2
  80.0 0.0 reduce-scatter.6.cloned.1.call-update
  80.0 0.0 reduce-scatter.4.cloned.1.call-start
  80.1 0.0 copy-done
  80.1 7.3 %convolution_convert_fusion.1 = bf16[1024,1536]{1,0:T(8,128)(2,1)} fusion(bf16[1024,1152]{1,0:T(8,128)(2,1)} %all-gather.3.cloned.1.call-done, bf16[1152,1536]{1,0:T(8,128)(2,1)S(1)} %copy-done), kind=kOutput, calls=%fused_computation.5 | convolution fusion | flops 3625451520 | bytes 9043968 | tf_op jit(solution)/shard_map/dot_general | solution.py:67
  87.4 0.0 copy-start.3
  87.4 0.0 reduce-scatter.4.cloned.1.call-update
  87.4 0.6 multiply_power_fusion
  88.0 0.0 copy-done.3
  88.0 0.7 add_convert_fusion.2
  88.7 0.1 iota_compare_fusion
  88.8 61.9 %reduce-scatter.6.cloned.1.call-done = bf16[64,64]{1,0:T(8,128)(2,1)} async-done(((bf16[1024,64]{1,0:T(8,128)(2,1)}), bf16[64,64]{1,0:T(8,128)(2,1)}) %reduce-scatter.6.cloned.1.call-update) | async-done | bytes 8208 | tf_op jit(solution)/shard_map/reduce_scatter | solution.py:73
  150.7 1.4 reshape.135
  152.1 6.6 %all-to-all-start.1 = ((bf16[8,2,256]{2,1,0:T(2,128)(2,1)}), bf16[8,2,256]{2,1,0:T(2,128)(2,1)S(1)}, u32[]{:S(2)}, u32[]{:S(2)}) async-start(bf16[8,2,256]{2,1,0:T(2,128)(2,1)} %reshape.135), calls=%async_computation.3 | async-start | bytes 16384 | tf_op jit(solution)/shard_map/all_to_all | solution.py:81
  158.7 0.6 iota_compare_fusion.1
  159.3 4.0 %all-to-all-done.1 = bf16[8,2,256]{2,1,0:T(2,128)(2,1)S(1)} async-done(((bf16[8,2,256]{2,1,0:T(2,128)(2,1)}), bf16[8,2,256]{2,1,0:T(2,128)(2,1)S(1)}, u32[]{:S(2)}, u32[]{:S(2)}) %all-to-all-start.1) | async-done | bytes 8224 | tf_op jit(solution)/shard_map/all_to_all | solution.py:81
  163.3 0.7 reshape.136
  164.0 1.3 copy.12
  165.3 0.8 reshape.129
  166.2 0.6 slice_convert_fusion
  166.8 62.9 %reduce-scatter.4.cloned.1.call-done = bf16[64,1536]{1,0:T(8,128)(2,1)} async-done(((bf16[1024,1536]{1,0:T(8,128)(2,1)}), bf16[64,1536]{1,0:T(8,128)(2,1)}) %reduce-scatter.4.cloned.1.call-update) | async-done | bytes 196624 | tf_op jit(solution)/shard_map/reduce_scatter | solution.py:70
  229.6 6.6 %all-to-all-start = ((bf16[8,8,1536]{2,1,0:T(8,128)(2,1)}), bf16[8,8,1536]{2,1,0:T(8,128)(2,1)}, u32[]{:S(2)}, u32[]{:S(2)}) async-start(bf16[8,8,1536]{2,1,0:T(8,128)(2,1)} %bitcast.43), calls=%async_computation.1 | async-start | bytes 393216 | tf_op jit(solution)/shard_map/all_to_all | solution.py:78
  236.2 0.0 all-gather.5.cloned.1.call-start
  236.2 1.5 subtract_convert_fusion.1
  237.7 4.5 %all-to-all-done = bf16[8,8,1536]{2,1,0:T(8,128)(2,1)} async-done(((bf16[8,8,1536]{2,1,0:T(8,128)(2,1)}), bf16[8,8,1536]{2,1,0:T(8,128)(2,1)}, u32[]{:S(2)}, u32[]{:S(2)}) %all-to-all-start) | async-done | bytes 196640 | tf_op jit(solution)/shard_map/all_to_all | solution.py:78
  242.2 1.0 convert_bitcast_fusion
  243.2 1.0 copy.11
  244.1 1.8 reshape.130
  246.0 1.1 subtract_convert_fusion
  247.1 0.0 copy-start.1
  247.1 0.0 copy-start.2
  247.1 0.0 copy-start.5
  247.1 0.0 copy-start.4
  247.1 3.8 %fusion.22 = (f32[4,2,48]{2,1,0:T(2,128)S(1)}, f32[4,2,48,2048]{3,2,1,0:T(8,128)S(1)}) fusion(bf16[4,2048,256]{2,1,0:T(8,128)(2,1)} %param.13, bf16[4,2,48,128]{3,2,1,0:T(8,128)(2,1)S(1)} %get-tuple-element.10, bf16[4,2,48,128]{3,2,1,0:T(8,128)(2,1)S(1)} %get-tuple-element.9, pred[4,2048]{1,0:T(4,128)(4,1)S(1)} %iota_compare_fusion), kind=kOutput, calls=%fused_computation.50 | convolution fusion | flops 405405312 | bytes 7546368 | tf_op jit(solution)/shard_map/rshd,rld->rshl/dot_general | solution.py:38
  250.9 0.0 copy-done.1
  250.9 0.0 copy-done.2
  250.9 0.0 copy-done.5
  251.0 0.2 fusion.23
  251.2 0.6 fusion.6
  251.8 0.0 copy-done.4
  251.8 0.9 fusion
  252.8 0.9 fusion.9
  253.7 1.8 all_to_all.41
  255.5 1.0 copy.13
  256.5 9.9 %all_to_all.48 = bf16[8,8,1536]{2,0,1:T(8,128)(2,1)} all-to-all(bf16[8,8,1536]{2,0,1:T(8,128)(2,1)S(1)} %copy.13), channel_id=1, replica_groups=mesh['gx'=16,'gy'=8] {'gy'}, dimensions={1} | all-to-all | bytes 393216 | tf_op jit(solution)/shard_map/all_to_all | solution.py:95
  266.4 0.0 all-gather.5.cloned.1.call-update
  266.4 0.0 reduce-scatter.8.cloned.1.call-start
  266.4 45.5 %all-gather.5.cloned.1.call-done = bf16[1024,1536]{1,0:T(8,128)(2,1)} async-done(((bf16[64,1536]{1,0:T(8,128)(2,1)}), bf16[1024,1536]{1,0:T(8,128)(2,1)}) %all-gather.5.cloned.1.call-update) | async-done | bytes 3145744 | tf_op jit(solution)/shard_map/all_gather | solution.py:97
  312.0 8.6 %convolution_convert_fusion = bf16[1024,1152]{1,0:T(8,128)(2,1)} fusion(bf16[1024,1536]{1,0:T(8,128)(2,1)} %all-gather.5.cloned.1.call-done, bf16[1536,1152]{1,0:T(8,128)(2,1)} %param.12), kind=kOutput, calls=%fused_computation.4 | convolution fusion | flops 3625058304 | bytes 9043968 | tf_op jit(solution)/shard_map/dot_general | solution.py:96
  320.6 0.0 reduce-scatter.8.cloned.1.call-update
  320.6 30.4 %reduce-scatter.8.cloned.1.call-done = bf16[128,1152]{1,0:T(8,128)(2,1)} async-done(((bf16[1024,1152]{1,0:T(8,128)(2,1)}), bf16[128,1152]{1,0:T(8,128)(2,1)}) %reduce-scatter.8.cloned.1.call-update) | async-done | bytes 294928 | tf_op jit(solution)/shard_map/reduce_scatter | solution.py:101
  (3 shorter events, 0.0 us)
Async XLA Ops:
  6.5 73.5 %copy-start = (bf16[1152,1536]{1,0:T(8,128)(2,1)S(1)}, bf16[1152,1536]{1,0:T(8,128)(2,1)}, u32[]{:S(2)}) copy-start(bf16[1152,1536]{1,0:T(8,128)(2,1)} %param.10) | copy-start | bytes 10616836
  6.5 70.3 %all-gather.3.cloned.1.call-start = ((), (), s32[]{:S(2)}) async-start(), calls=%async_computation.6 | async-start | bytes 2654208 | tf_op jit(solution)/shard_map/all_gather | solution.py:66
  47.3 103.4 %reduce-scatter.6.cloned.1.call-start = ((), (), s32[]{:S(2)}) async-start(), calls=%async_computation.8 | async-start | bytes 278528 | tf_op jit(solution)/shard_map/reduce_scatter | solution.py:73
  80.0 149.6 %reduce-scatter.4.cloned.1.call-start = ((), (), s32[]{:S(2)}) async-start(), calls=%async_computation.7 | async-start | bytes 3342336 | tf_op jit(solution)/shard_map/reduce_scatter | solution.py:70
  87.4 0.7 copy-start.3
  152.1 11.2 %all-to-all-start.1 = ((bf16[8,2,256]{2,1,0:T(2,128)(2,1)}), bf16[8,2,256]{2,1,0:T(2,128)(2,1)S(1)}, u32[]{:S(2)}, u32[]{:S(2)}) async-start(bf16[8,2,256]{2,1,0:T(2,128)(2,1)} %reshape.135), calls=%async_computation.3 | async-start | bytes 16384 | tf_op jit(solution)/shard_map/all_to_all | solution.py:81
  229.6 12.6 %all-to-all-start = ((bf16[8,8,1536]{2,1,0:T(8,128)(2,1)}), bf16[8,8,1536]{2,1,0:T(8,128)(2,1)}, u32[]{:S(2)}, u32[]{:S(2)}) async-start(bf16[8,8,1536]{2,1,0:T(8,128)(2,1)} %bitcast.43), calls=%async_computation.1 | async-start | bytes 393216 | tf_op jit(solution)/shard_map/all_to_all | solution.py:78
  236.2 75.8 %all-gather.5.cloned.1.call-start = ((), (), s32[]{:S(2)}) async-start(), calls=%async_computation.9 | async-start | bytes 3342336 | tf_op jit(solution)/shard_map/all_gather | solution.py:97
  247.1 3.9 %copy-start.1 = (bf16[4,2,128]{2,1,0:T(2,128)(2,1)S(1)}, bf16[4,2,128]{2,1,0:T(2,128)(2,1)}, u32[]{:S(2)}) copy-start(bf16[4,2,128]{2,1,0:T(2,128)(2,1)} %get-tuple-element.11) | copy-start | bytes 6148
  247.1 3.9 %copy-start.2 = (bf16[4,2,128]{2,1,0:T(2,128)(2,1)S(1)}, bf16[4,2,128]{2,1,0:T(2,128)(2,1)}, u32[]{:S(2)}) copy-start(bf16[4,2,128]{2,1,0:T(2,128)(2,1)} %get-tuple-element.12) | copy-start | bytes 6148
  247.1 3.9 %copy-start.5 = (pred[2,2]{1,0:T(4,128)(4,1)S(1)}, pred[2,2]{1,0:T(4,128)(4,1)}, u32[]{:S(2)}) copy-start(pred[2,2]{1,0:T(4,128)(4,1)} %iota_compare_fusion.1) | copy-start | bytes 16
  247.1 4.7 %copy-start.4 = (bf16[4,2048,256]{2,1,0:T(8,128)(2,1)S(1)}, bf16[4,2048,256]{2,1,0:T(8,128)(2,1)}, u32[]{:S(2)}) copy-start(bf16[4,2048,256]{2,1,0:T(8,128)(2,1)} %param.14) | copy-start | bytes 12582916
  266.4 84.6 %reduce-scatter.8.cloned.1.call-start = ((), (), s32[]{:S(2)}) async-start(), calls=%async_computation.10 | async-start | bytes 2654208 | tf_op jit(solution)/shard_map/reduce_scatter | solution.py:101
Sparse Core Ops, SparseCore 0:
  47.4 29.3 all-gather.2
  80.1 70.5 reduce-scatter.5
  154.4 75.1 reduce-scatter.3
  266.5 45.3 all-gather.4
  320.7 30.2 reduce-scatter.7
where the time goes:
time: 360 us; the launch traced here: 358 us
  waiting for transfers between devices  239 us (66%)
  blocking collectives  46.1 us (13%)
  matrix products  25 us (7%)
  starting transfers between devices  13.3 us (4%)
  between operations  13.3 us (4%)
  other arithmetic  11.2 us (3%)
  local copies, waits for them, and re-layouts  9.85 us (3%)
    reduce_scatter x1, waiting for transfers between devices, per_device(): lax.psum_scatter(query_part.astype(jnp.bfloat16), 'gx', scatter_dimension...  62.9 us
    reduce_scatter x1, waiting for transfers between devices, per_device(): lax.psum_scatter(pair_part.astype(jnp.bfloat16), 'gx', scatter_dimension=...  61.9 us
    all_gather x1, waiting for transfers between devices, per_device(): lax.all_gather(returned, 'gx', axis=0, tiled=True)  45.5 us
    psum x1, blocking collectives, per_device(): lax.psum((jnp.sum(floated, axis=1), jnp.sum(floated * floated, axis=1)),...  36.2 us
    reduce_scatter x1, waiting for transfers between devices, per_device(): lax.psum_scatter(partial_out.astype(jnp.bfloat16), 'gy', scatter_dimensio...  30.4 us
    all_gather x1, waiting for transfers between devices, per_device(): lax.all_gather(normalize(tokens, sums, squares, norm_gain), 'gy', axis=0,...  29.5 us
    all_to_all x1, blocking collectives, per_device(): lax.all_to_all(attended, 'gy', split_axis=1, concat_axis=0, tiled=True)  9.91 us
    dot_general x1, matrix products, per_device(): jnp.dot(lax.all_gather(returned, 'gx', axis=0, tiled=True), w_out, prefer...  8.63 us
  transfers between devices with their start and end apart: 7, of which 7 were waited for; matrix products, arithmetic and copies ran while one was open for 4% of the time, Pallas kernels for 0%

commit v1 on v0

v1 whole, which is shorter than its diff:
```python
import functools

import jax
import jax.numpy as jnp
from jax import lax
from jax.experimental import pallas as pl
from jax.experimental.pallas import tpu as pltpu
from jax.sharding import PartitionSpec as P

D = 18432
HD = 256
STEPS = 2
VMEM = pl.BlockSpec(memory_space=pltpu.VMEM)
SMEM = pl.BlockSpec(memory_space=pltpu.SMEM)
ANY = pl.BlockSpec(memory_space=pl.ANY)
F32 = jnp.float32
BF16 = jnp.bfloat16


def params():
    return pltpu.CompilerParams(vmem_limit_bytes=50 * 1024 * 1024)


def along_y(value, m):
    return lax.ppermute(value, "gx", [(g, (g // 4 + m) % 4 * 4 + g % 4) for g in range(16)])


def along_z(value, m):
    return lax.ppermute(value, "gx", [(g, g // 4 * 4 + (g + m) % 4) for g in range(16)])


def along_x(value, m):
    return lax.ppermute(value, "gy", [(g, (g // 2 + m) % 4 * 2 + g % 2) for g in range(8)])


def other_core(value):
    return lax.ppermute(value, "gy", [(g, g ^ 1) for g in range(8)])


def project_kernel(place, stats, gain, *refs):
    pieces, (w_query, w_pair), outs = refs[:8], refs[8:10], refs[10:18]
    normed, mean_of, scale_of, weights, sems = refs[18:]
    tiles = w_query.shape[1] // 256
    loads = []
    for t in range(tiles):
        load = pltpu.make_async_copy(
            w_query.at[:, pl.ds(t * 256, 256)], weights.at[t], sems.at[t]
        )
        load.start()
        loads.append(load)
    y, z, x, c = place[0], place[1], place[2], place[3]
    total = stats[0:8, :]
    for g in range(1, 16):
        total = total + stats[g * 8 : g * 8 + 8, :]
    mean = total[:, :128] / D
    variance = total[:, 128:] / D - mean * mean
    mean_columns = mean.T
    scale_columns = lax.rsqrt(variance + 1e-05).T
    for s in range(8):
        mean_of[s] = mean_columns[:, s : s + 1]
        scale_of[s] = scale_columns[:, s : s + 1]
    gains = gain[...].astype(F32)
    for m in range(4):
        source_x = lax.rem(x + 4 - m, 4)
        to_y = lax.rem(source_x + 4 - y, 4)
        for j in range(2):
            source_c = lax.rem(c + j, 2)
            s = source_x * 2 + source_c
            rows = pieces[m * 2 + j][...].astype(F32)
            rows = ((rows - mean_of[s]) * scale_of[s] * gains).astype(BF16)
            for b in range(2):
                to_z = lax.rem(source_c * 2 + b + 4 - z, 4)
                normed[0, to_y, to_z] = rows[b * 64 : b * 64 + 32]
                normed[1, to_z, to_y] = rows[b * 64 + 32 : b * 64 + 64]
    for h in range(2):
        left = normed[h].reshape(512, normed.shape[-1])
        pair = jnp.dot(left, w_pair[...], preferred_element_type=F32).astype(BF16)
        for k in range(4):
            outs[h * 4 + k][:, tiles * 256 :] = pair[k * 128 : k * 128 + 128]
    for t in range(tiles):
        loads[t].wait()
        for h in range(2):
            left = normed[h].reshape(512, normed.shape[-1])
            part = jnp.dot(left, weights[t], preferred_element_type=F32).astype(BF16)
            for k in range(4):
                outs[h * 4 + k][:, t * 256 : t * 256 + 256] = part[k * 128 : k * 128 + 128]


def project(place, stats, gain, pieces, w_query, w_pair):
    depth, width = w_query.shape
    out = jax.ShapeDtypeStruct((128, width + w_pair.shape[1]), BF16)
    return pl.pallas_call(
        project_kernel,
        out_shape=[out] * 8,
        in_specs=[SMEM] + [VMEM] * 10 + [ANY, VMEM],
        out_specs=[VMEM] * 8,
        scratch_shapes=[
            pltpu.VMEM((2, 4, 4, 32, depth), BF16),
            pltpu.VMEM((8, 128, 1), F32),
            pltpu.VMEM((8, 128, 1), F32),
            pltpu.VMEM((width // 256, depth, 256), BF16),
            pltpu.SemaphoreType.DMA((width // 256,)),
        ],
        compiler_params=params(),
        name="project",
    )(place, stats, gain, *pieces, w_query, w_pair)


def add_kernel(pieces, *refs):
    groups = len(refs) // (2 * pieces)
    ins, outs = refs[: groups * pieces], refs[groups * pieces :]
    for g in range(groups):
        total = ins[g * pieces][...].astype(F32)
        for k in range(1, pieces):
            total = total + ins[g * pieces + k][...].astype(F32)
        total = total.astype(BF16)
        rows = total.shape[0] // pieces
        for k in range(pieces):
            outs[g * pieces + k][...] = total[k * rows : k * rows + rows]


def add_and_cut(values, pieces):
    rows, width = values[0].shape
    out = jax.ShapeDtypeStruct((rows // pieces, width), BF16)
    return pl.pallas_call(
        functools.partial(add_kernel, pieces),
        out_shape=[out] * len(values),
        in_specs=[VMEM] * len(values),
        out_specs=[VMEM] * len(values),
        compiler_params=params(),
        name="add_and_cut",
    )(*values)


def attend_kernel(lengths, packed, cosine, sine, keys, values, out, query_rows, new_kv, result):
    request = pl.program_id(0)
    heads = out.shape[1] // HD
    count = 8 * heads

    @pl.when(request == 0)
    def _():
        rows = packed[...].astype(F32)
        cos, sin = cosine[...], sine[...]

        def rotated(first, second):
            return first * cos - second * sin, second * cos + first * sin

        for n in range(count):
            g, h = n // heads, n % heads
            head = rows[g * 8 : g * 8 + 8, h * HD : h * HD + HD]
            for i, half in enumerate(rotated(head[:, :128], head[:, 128:])):
                query_rows[i, pl.ds(n, 8, stride=count), :] = half
        parts = [rows[g * 8 : g * 8 + 8, heads * HD :] for g in range(8)]
        halves = [jnp.concatenate(parts[i : i + 2], axis=-1) for i in range(0, 8, 2)]
        new_kv[0] = jnp.concatenate(rotated(halves[0], halves[1]), axis=-1).astype(BF16)
        new_kv[1] = jnp.concatenate(halves[2:], axis=-1).astype(BF16)

    per = STEPS * count
    start = pl.multiple_of(request * per, per)
    query = jnp.concatenate([query_rows[i, pl.ds(start, per), :] for i in range(2)], axis=-1)
    query = (query.astype(BF16).astype(F32) * HD ** (-0.5)).astype(BF16)
    dims = (((1,), (1,)), ((), ()))
    cached = lax.dot_general(query, keys[0], dims, preferred_element_type=F32)
    slots = lax.broadcasted_iota(jnp.int32, cached.shape, 1)
    cached = jnp.where(slots < lengths[request], cached, -jnp.inf)
    fresh = lax.dot_general(query, new_kv[0], dims, preferred_element_type=F32)
    row_step = lax.broadcasted_iota(jnp.int32, fresh.shape, 0) // count
    key_step = lax.broadcasted_iota(jnp.int32, fresh.shape, 1) - request * STEPS
    fresh = jnp.where((key_step >= 0) & (key_step <= row_step), fresh, -jnp.inf)
    top = jnp.maximum(
        jnp.max(cached, axis=-1, keepdims=True), jnp.max(fresh, axis=-1, keepdims=True)
    )
    cached = jnp.exp(cached - top)
    fresh = jnp.exp(fresh - top)
    denom = jnp.sum(cached, axis=-1, keepdims=True) + jnp.sum(fresh, axis=-1, keepdims=True)
    mixed = jnp.dot(cached.astype(BF16), values[0], preferred_element_type=F32)
    mixed = mixed + jnp.dot(fresh.astype(BF16), new_kv[1], preferred_element_type=F32)
    mixed = mixed / denom
    for i in range(2):
        result[i, pl.ds(start, per), :] = mixed[:, i * 128 : i * 128 + 128]

    @pl.when(request == pl.num_programs(0) - 1)
    def _():
        for g in range(8):
            line = jnp.concatenate(
                [
                    result[i, pl.ds(g * heads + h, 8, stride=count), :]
                    for h in range(heads)
                    for i in range(2)
                ],
                axis=-1,
            )
            out[g * 8 : g * 8 + 8, :] = line


def attend(packed, cosine, sine, cache_keys, cache_values, lengths):
    requests, slots, _ = cache_keys.shape
    width = packed.shape[1] // HD * HD
    count = 8 * (width // HD)
    whole = lambda *shape: pl.BlockSpec(shape, lambda r, *_: (0,) * len(shape))
    cache = pl.BlockSpec((1, slots, HD), lambda r, *_: (r, 0, 0))
    return pl.pallas_call(
        attend_kernel,
        out_shape=jax.ShapeDtypeStruct((64, width), F32),
        grid_spec=pltpu.PrefetchScalarGridSpec(
            num_scalar_prefetch=1,
            grid=(requests,),
            in_specs=[whole(*packed.shape), whole(8, 128), whole(8, 128), cache, cache],
            out_specs=whole(64, width),
            scratch_shapes=[
                pltpu.VMEM((2, 8 * count, 128), F32),
                pltpu.VMEM((2, 8, HD), BF16),
                pltpu.VMEM((2, 8 * count, 128), F32),
            ],
        ),
        compiler_params=params(),
        name="attend",
    )(lengths, packed, cosine, sine, cache_keys, cache_values).astype(BF16)


def mix_kernel(want, place, *refs):
    first, second = refs[:4], refs[4:8]
    w_out, out, rows = refs[8], refs[9], refs[10]
    y, z, x, c = place[0], place[1], place[2], place[3]
    core = lax.rem(c + want, 2)
    for m_z in range(4):
        token_z = lax.rem(z + 4 - m_z, 4)

        @pl.when(token_z // 2 == core)
        def _():
            for m_y in range(4):
                to_x = lax.rem(y + 8 - m_y - x, 4)
                b = lax.rem(token_z, 2)
                rows[to_x, b, 0] = first[m_z][m_y * 32 : m_y * 32 + 32, :]
                rows[to_x, b, 1] = second[m_y][m_z * 32 : m_z * 32 + 32, :]

    left = rows[...].reshape(512, rows.shape[-1])
    width = w_out.shape[1]
    for t in range(0, width, 256):
        n = min(256, width - t)
        part = jnp.dot(left, w_out[:, t : t + n], preferred_element_type=F32)
        out[:, t : t + n] = part.astype(BF16)


def mix(want, place, first, second, w_out):
    depth, width = w_out.shape
    return pl.pallas_call(
        functools.partial(mix_kernel, want),
        out_shape=jax.ShapeDtypeStruct((512, width), BF16),
        in_specs=[SMEM] + [VMEM] * 9,
        out_specs=VMEM,
        scratch_shapes=[pltpu.VMEM((4, 2, 2, 32, depth), BF16)],
        compiler_params=params(),
        name="mix",
    )(place, *first, *second, w_out)


def pair_add_kernel(mine, theirs, *outs):
    for k in range(4):
        rows = slice(k * 128, k * 128 + 128)
        outs[k][...] = (mine[rows, :].astype(F32) + theirs[rows, :].astype(F32)).astype(BF16)


def pair_add(mine, theirs):
    out = jax.ShapeDtypeStruct((128, mine.shape[1]), BF16)
    return pl.pallas_call(
        pair_add_kernel,
        out_shape=[out] * 4,
        in_specs=[VMEM] * 2,
        out_specs=[VMEM] * 4,
        compiler_params=params(),
        name="pair_add",
    )(mine, theirs)


def total(values):
    result = values[0].astype(F32)
    for value in values[1:]:
        result = result + value.astype(F32)
    return result.astype(BF16)


def per_device(tokens, norm_gain, w_query, w_keyvalue, w_out, cache_keys, cache_values, lengths):
    gx, gy = lax.axis_index("gx"), lax.axis_index("gy")
    place = jnp.stack([gx // 4, gx % 4, gy // 2, gy % 2]).astype(jnp.int32)

    arrived = [tokens] + [along_x(tokens, m) for m in range(1, 4)]
    pieces = []
    for piece in arrived:
        pieces += [piece, other_core(piece)]
    floated = tokens.astype(F32)
    sums = jnp.concatenate([jnp.sum(floated, axis=1), jnp.sum(floated * floated, axis=1)])
    stats = lax.all_to_all(
        jnp.broadcast_to(sums[None], (128, 256)), ("gx", "gy"), 0, 0, tiled=True
    )

    parts = project(place, stats, norm_gain[None], pieces, w_query, w_keyvalue)
    by_y = [parts[0]] + [along_y(parts[m], m) for m in range(1, 4)]
    by_z = [parts[4]] + [along_z(parts[4 + m], m) for m in range(1, 4)]
    parts = add_and_cut(by_y + by_z, 4)
    by_z = [parts[0]] + [along_z(parts[m], m) for m in range(1, 4)]
    by_y = [parts[4]] + [along_y(parts[4 + m], m) for m in range(1, 4)]
    query = jnp.concatenate([total(by_z), total(by_y)], axis=0)
    packed = lax.all_to_all(query, "gy", 0, 0, tiled=True)

    half_dim = HD // 2
    freqs = 10000.0 ** (-jnp.arange(half_dim, dtype=F32) / half_dim)
    positions = lengths[:, None] + jnp.arange(STEPS, dtype=jnp.int32)[None, :]
    angles = positions.reshape(-1).astype(F32)[:, None] * freqs
    attended = attend(packed, jnp.cos(angles), jnp.sin(angles), cache_keys, cache_values, lengths)

    returned = lax.all_to_all(attended, "gy", 0, 0, tiled=True)
    halves = [returned[:32], returned[32:]]
    first = jnp.concatenate([halves[0]] + [along_y(halves[0], m) for m in range(1, 4)], axis=0)
    second = jnp.concatenate([halves[1]] + [along_z(halves[1], m) for m in range(1, 4)], axis=0)
    first = [first] + [along_z(first, m) for m in range(1, 4)]
    second = [second] + [along_y(second, m) for m in range(1, 4)]

    theirs = other_core(mix(1, place, first, second, w_out))
    mine = mix(0, place, first, second, w_out)
    parts = pair_add(mine, theirs)
    return total([parts[0]] + [along_x(parts[m], m) for m in range(1, 4)])


def solution(mesh):
    return jax.shard_map(
        per_device,
        mesh=mesh,
        in_specs=(
            P("gy", "gx"),
            P("gx"),
            P("gx", "gy"),
            P("gx", "gy"),
            P("gy", "gx"),
            P(("gx", "gy"), None, None),
            P(("gx", "gy"), None, None),
            P(("gx", "gy")),
        ),
        out_specs=P("gy", "gx"),
        check_vma=False,
    )
```

time: 360 us -> 201 us (0.56)
  waiting for transfers between devices: 239 us -> 80.5 us
  starting transfers between devices: 13.3 us -> 72 us
  blocking collectives: 46.1 us -> 9.26 us
  Pallas kernels: 0 us -> 29.3 us
  matrix products: 25 us -> 0 us
  between operations: 13.3 us -> 0.21 us
  other arithmetic: 11.2 us -> 3.16 us
  local copies, waits for them, and re-layouts: 9.85 us -> 5.91 us
    reduce_scatter x3 -> x0, waiting for transfers between devices: 155 us -> none  [the longest x1 62.9 us: per_device(): lax.psum_scatter(query_part.astype(jnp.bfloat16), 'gx', scatter_dimension...]
    all_gather x2 -> x0, waiting for transfers between devices: 75 us -> none  [the longest x1 45.5 us: per_device(): lax.all_gather(returned, 'gx', axis=0, tiled=True)]
    ppermute x0 -> x35, waiting for transfers between devices: none -> 66.6 us  [the longest x12 26.3 us: along_z(): lax.ppermute(value, 'gx', [(g, g // 4 * 4 + (g + m) % 4) for g in range(1...]
    ppermute x0 -> x35, starting transfers between devices: none -> 54.4 us  [the longest x12 20.2 us: along_y(): lax.ppermute(value, 'gx', [(g, (g // 4 + m) % 4 * 4 + g % 4) for g in ran...]
    psum x1 -> x0, blocking collectives: 36.2 us -> none  [per_device(): lax.psum((jnp.sum(floated, axis=1), jnp.sum(floated * floated, axis=1)),...]
    pallas_call x0 -> x6, Pallas kernels: none -> 29.3 us  [the longest x2 10.8 us: mix(): pl.pallas_call(functools.partial(mix_kernel, want), out_shape=jax.ShapeDt...]
    dot_general x7 -> x0, matrix products: 25 us -> none  [the longest x1 8.63 us: per_device(): jnp.dot(lax.all_gather(returned, 'gx', axis=0, tiled=True), w_out, prefer...]
    all_to_all x2, waiting for transfers between devices: 8.56 us -> 13.9 us  [the longest x1 8 us: per_device(): lax.all_to_all(jnp.broadcast_to(sums[None], (128, 256)), ('gx', 'gy'), 0,...]
  transfers between devices with their start and end apart: 7 -> 37, of which waited for: 7 -> 20; matrix products, arithmetic and copies ran while one was open for 4% -> 2% of each run, Pallas kernels for 0% -> 3%
where the time goes in v1:
time: 201 us; the launch traced here: 200 us
  waiting for transfers between devices  80.5 us (40%)
  starting transfers between devices  72 us (36%)
  Pallas kernels  29.3 us (15%)
  blocking collectives  9.26 us (5%)
  local copies, waits for them, and re-layouts  5.91 us (3%)
  other arithmetic  3.16 us (2%)
    ppermute x12, waiting for transfers between devices, along_z(): lax.ppermute(value, 'gx', [(g, g // 4 * 4 + (g + m) % 4) for g in range(1...  26.3 us
    ppermute x6, waiting for transfers between devices, along_x(): lax.ppermute(value, 'gy', [(g, (g // 2 + m) % 4 * 2 + g % 2) for g in ran...  21.5 us
    ppermute x12, starting transfers between devices, along_y(): lax.ppermute(value, 'gx', [(g, (g // 4 + m) % 4 * 4 + g % 4) for g in ran...  20.2 us
    ppermute x12, waiting for transfers between devices, along_y(): lax.ppermute(value, 'gx', [(g, (g // 4 + m) % 4 * 4 + g % 4) for g in ran...  18.8 us
    ppermute x12, starting transfers between devices, along_z(): lax.ppermute(value, 'gx', [(g, g // 4 * 4 + (g + m) % 4) for g in range(1...  16.4 us
    pallas_call x2, Pallas kernels, mix(): pl.pallas_call(functools.partial(mix_kernel, want), out_shape=jax.ShapeDt...  10.8 us
    all_to_all x1, starting transfers between devices, per_device(): lax.all_to_all(jnp.broadcast_to(sums[None], (128, 256)), ('gx', 'gy'), 0,...  9.74 us
    pallas_call x1, Pallas kernels, project(): pl.pallas_call(project_kernel, out_shape=[out] * 8, in_specs=[SMEM] + [VM...  9.39 us
  transfers between devices with their start and end apart: 37, of which 20 were waited for; matrix products, arithmetic and copies ran while one was open for 2% of the time, Pallas kernels for 3%

profile of v1, /device:TPU:1, one launch (start us, length us, event | category | flops | bytes accessed | tf_op | source)
XLA Modules:
  0.0 200.4 jit_solution(9750648198925250038)
XLA Ops:
  0.0 2.0 %collective-permute-start.1 = (bf16[128,1152]{1,0:T(8,128)(2,1)}, bf16[128,1152]{1,0:T(8,128)(2,1)S(1)}, u32[]{:S(2)}, u32[]{:S(2)}) collective-permute-start(bf16[128,1152]{1,0:T(8,128)(2,1)} %refs_0_.1), channel_id=1, source_target_pairs={{0,2},{1,3},{2,4},{3,5},{4,6},{5,7},{6,0},{7,1},{8,10},{9,11},{10,... | collective-permute-start | bytes 884744 | tf_op jit(solution)/shard_map/ppermute | solution.py:33
  2.0 2.5 %collective-permute-start.3 = (bf16[128,1152]{1,0:T(8,128)(2,1)}, bf16[128,1152]{1,0:T(8,128)(2,1)S(1)}, u32[]{:S(2)}, u32[]{:S(2)}) collective-permute-start(bf16[128,1152]{1,0:T(8,128)(2,1)} %refs_0_.1), channel_id=1, source_target_pairs={{0,4},{1,5},{2,6},{3,7},{4,0},{5,1},{6,2},{7,3},{8,12},{9,13},{10,... | collective-permute-start | bytes 884744 | tf_op jit(solution)/shard_map/ppermute | solution.py:33
  4.5 1.2 collective-permute-start.5
  5.6 1.5 collective-permute-start
  7.2 2.6 %collective-permute-done.1.refs_2_ = bf16[128,1152]{1,0:T(8,128)(2,1)S(1)} collective-permute-done((bf16[128,1152]{1,0:T(8,128)(2,1)}, bf16[128,1152]{1,0:T(8,128)(2,1)S(1)}, u32[]{:S(2)}, u32[]{:S(2)}) %collective-permute-start.1) | collective-permute-done | bytes 294944 | tf_op jit(solution)/shard_map/ppermute | solution.py:33
  9.8 1.7 collective-permute-start.2
  11.5 6.0 %collective-permute-done.3.refs_4_ = bf16[128,1152]{1,0:T(8,128)(2,1)S(1)} collective-permute-done((bf16[128,1152]{1,0:T(8,128)(2,1)}, bf16[128,1152]{1,0:T(8,128)(2,1)S(1)}, u32[]{:S(2)}, u32[]{:S(2)}) %collective-permute-start.3) | collective-permute-done | bytes 294944 | tf_op jit(solution)/shard_map/ppermute | solution.py:33
  17.4 1.5 collective-permute-start.4
  19.0 1.1 convert_reduce_fusion
  20.1 0.7 broadcast_in_dim.4
  20.8 9.7 %all-to-all-start = ((f32[128,1,256]{2,1,0:T(1,128)}), f32[128,1,256]{2,1,0:T(1,128)S(1)}, u32[]{:S(2)}, u32[]{:S(2)}) async-start(f32[128,1,256]{2,1,0:T(1,128)} %broadcast_in_dim.4), calls=%async_computation | async-start | bytes 262144 | tf_op jit(solution)/shard_map/all_to_all | solution.py:293
  30.6 1.1 copy.11.refs_9_
  31.8 0.7 broadcast_in_dim.5.gain
  32.5 8.0 %all-to-all-done = f32[128,1,256]{2,1,0:T(1,128)S(1)} async-done(((f32[128,1,256]{2,1,0:T(1,128)}), f32[128,1,256]{2,1,0:T(1,128)S(1)}, u32[]{:S(2)}, u32[]{:S(2)}) %all-to-all-start) | async-done | bytes 131104 | tf_op jit(solution)/shard_map/all_to_all | solution.py:293
  40.6 1.0 copy-done.1
  41.6 9.4 %project.1 = (bf16[128,1600]{1,0:T(8,128)(2,1)S(1)}, bf16[128,1600]{1,0:T(8,128)(2,1)}, bf16[128,1600]{1,0:T(8,128)(2,1)S(1)}, bf16[128,1600]{1,0:T(8,128)(2,1)}...) custom-call(s32[4]{0:T(128)S(1)} %pad_add_fusion.place, ...), custom_call_target="tpu_custom_call" | custom-call | tf_op jit(solution)/shard_map/project/pallas_call | solution.py:92
  51.0 0.5 collective-permute-start.10
  51.5 1.5 collective-permute-start.11
  53.0 1.5 collective-permute-start.12
  54.8 1.7 collective-permute-start.8
  56.5 7.5 %collective-permute-done.10.refs_5_ = bf16[128,1600]{1,0:T(8,128)(2,1)S(1)} collective-permute-done((bf16[128,1600]{1,0:T(8,128)(2,1)}, bf16[128,1600]{1,0:T(8,128)(2,1)S(1)}, u32[]{:S(2)}, u32[]{:S(2)}) %collective-permute-start.10) | collective-permute-done | bytes 409632 | tf_op jit(solution)/shard_map/ppermute | solution.py:29
  64.0 1.1 collective-permute-start.9
  65.2 6.7 %collective-permute-done.11.refs_6_ = bf16[128,1600]{1,0:T(8,128)(2,1)S(1)} collective-permute-done((bf16[128,1600]{1,0:T(8,128)(2,1)}, bf16[128,1600]{1,0:T(8,128)(2,1)S(1)}, u32[]{:S(2)}, u32[]{:S(2)}) %collective-permute-start.11) | collective-permute-done | bytes 409632 | tf_op jit(solution)/shard_map/ppermute | solution.py:29
  71.9 1.1 collective-permute-done.12.refs_7_
  73.0 1.5 collective-permute-done.8.refs_2_
  74.5 1.0 copy-done.2
  75.5 1.4 add_and_cut.1
  76.9 0.8 collective-permute-start.13
  77.7 2.4 %collective-permute-start.14 = (bf16[32,1600]{1,0:T(8,128)(2,1)S(1)}, bf16[32,1600]{1,0:T(8,128)(2,1)S(1)}, u32[]{:S(2)}, u32[]{:S(2)}) collective-permute-start(bf16[32,1600]{1,0:T(8,128)(2,1)S(1)} %get-tuple-element.35), channel_id=1, source_target_pairs={{0,16},{8,24},{16,0},{24,8},{32,48},{40,56},{48,32},{56,40},{64,80... | collective-permute-start | bytes 307208 | tf_op jit(solution)/shard_map/ppermute | solution.py:29
  80.1 1.7 collective-permute-start.15
  81.8 4.5 %collective-permute-start.16 = (bf16[32,1600]{1,0:T(8,128)(2,1)S(1)}, bf16[32,1600]{1,0:T(8,128)(2,1)S(1)}, u32[]{:S(2)}, u32[]{:S(2)}) collective-permute-start(bf16[32,1600]{1,0:T(8,128)(2,1)S(1)} %get-tuple-element.38), channel_id=1, source_target_pairs={{0,32},{8,40},{16,48},{24,56},{32,64},{40,72},{48,80},{56,88},{64,... | collective-permute-start | bytes 307208 | tf_op jit(solution)/shard_map/ppermute | solution.py:25
  86.3 2.9 %collective-permute-start.17 = (bf16[32,1600]{1,0:T(8,128)(2,1)S(1)}, bf16[32,1600]{1,0:T(8,128)(2,1)S(1)}, u32[]{:S(2)}, u32[]{:S(2)}) collective-permute-start(bf16[32,1600]{1,0:T(8,128)(2,1)S(1)} %get-tuple-element.39), channel_id=1, source_target_pairs={{0,64},{8,72},{16,80},{24,88},{32,96},{40,104},{48,112},{56,120},{... | collective-permute-start | bytes 307208 | tf_op jit(solution)/shard_map/ppermute | solution.py:25
  89.3 2.0 collective-permute-start.18
  91.3 1.1 collective-permute-done.17
  92.4 1.6 collective-permute-done.18
  94.1 0.7 maximum_bitcast_fusion
  94.8 7.9 %all-to-all-start.1 = ((bf16[8,8,1600]{2,1,0:T(8,128)(2,1)}), bf16[8,8,1600]{2,1,0:T(8,128)(2,1)S(1)}, u32[]{:S(2)}, u32[]{:S(2)}) async-start(bf16[8,8,1600]{2,1,0:T(8,128)(2,1)} %maximum_bitcast_fusion), calls=%async_computation.1 | async-start | bytes 425984 | tf_op jit(solution)/shard_map/all_to_all | solution.py:304
  102.8 5.9 %all-to-all-done.1 = bf16[8,8,1600]{2,1,0:T(8,128)(2,1)S(1)} async-done(((bf16[8,8,1600]{2,1,0:T(8,128)(2,1)}), bf16[8,8,1600]{2,1,0:T(8,128)(2,1)S(1)}, u32[]{:S(2)}, u32[]{:S(2)}) %all-to-all-start.1) | async-done | bytes 204832 | tf_op jit(solution)/shard_map/all_to_all | solution.py:304
  108.8 7.4 %attend.1 = f32[64,1536]{1,0:T(8,128)S(1)} custom-call(s32[4]{0:T(128)S(1)} %copy-done.3, bf16[64,1600]{1,0:T(8,128)(2,1)S(1)} %bitcast.16, f32[8,128]{1,0:T(8,128)S(1)} %get-tuple-element.50.cosine, f32[8,128]{1,0:T(8,128)S(1)} %get-tuple-element.49.sine, bf16[4,2048,256]{2,1,0:T(8,128)(2,1)} %keys.1, bf16[4,2048,256]{2,1,0:T(8,128)(2,1)} %values.1), custom_call_target="tpu_custom_call" | custom-call | tf_op jit(solution)/shard_map/attend/pallas_call | solution.py:202
  116.2 9.3 %all_to_all.28 = bf16[8,8,1536]{2,1,0:T(8,128)(2,1)S(1)} all-to-all(bf16[8,8,1536]{2,1,0:T(8,128)(2,1)S(1)} %convert_bitcast_fusion), channel_id=1, replica_groups=mesh['gx'=16,'gy'=8] {'gy'}, dimensions={0} | all-to-all | bytes 393216 | tf_op jit(solution)/shard_map/all_to_all | solution.py:312
  125.4 0.7 collective-permute-start.25
  126.1 2.1 %collective-permute-start.26 = (bf16[32,1536]{1,0:T(8,128)(2,1)S(1)}, bf16[32,1536]{1,0:T(8,128)(2,1)S(1)}, u32[]{:S(2)}, u32[]{:S(2)}) collective-permute-start(bf16[32,1536]{1,0:T(8,128)(2,1)S(1)} %get-tuple-element.47), channel_id=1, source_target_pairs={{0,16},{8,24},{16,0},{24,8},{32,48},{40,56},{48,32},{56,40},{64,80... | collective-permute-start | bytes 294920 | tf_op jit(solution)/shard_map/ppermute | solution.py:29
  128.2 2.0 collective-permute-start.27
  130.2 1.9 collective-permute-done.26
  132.1 0.7 collective-permute-done.27
  133.1 0.9 collective-permute-start.19
  134.0 3.4 %collective-permute-start.20 = (bf16[32,1536]{1,0:T(8,128)(2,1)S(1)}, bf16[32,1536]{1,0:T(8,128)(2,1)S(1)}, u32[]{:S(2)}, u32[]{:S(2)}) collective-permute-start(bf16[32,1536]{1,0:T(8,128)(2,1)S(1)} %get-tuple-element.48), channel_id=1, source_target_pairs={{0,64},{8,72},{16,80},{24,88},{32,96},{40,104},{48,112},{56,120},{... | collective-permute-start | bytes 294920 | tf_op jit(solution)/shard_map/ppermute | solution.py:25
  137.4 2.0 collective-permute-start.21
  139.4 6.5 %collective-permute-done.19 = bf16[32,1536]{1,0:T(8,128)(2,1)S(1)} collective-permute-done((bf16[32,1536]{1,0:T(8,128)(2,1)S(1)}, bf16[32,1536]{1,0:T(8,128)(2,1)S(1)}, u32[]{:S(2)}, u32[]{:S(2)}) %collective-permute-start.19) | collective-permute-done | bytes 98336 | tf_op jit(solution)/shard_map/ppermute | solution.py:25
  145.9 1.2 collective-permute-start.30
  147.1 1.5 collective-permute-done.20
  148.7 3.1 %collective-permute-start.23 = (bf16[128,1536]{1,0:T(8,128)(2,1)S(1)}, bf16[128,1536]{1,0:T(8,128)(2,1)S(1)}, u32[]{:S(2)}, u32[]{:S(2)}) collective-permute-start(bf16[128,1536]{1,0:T(8,128)(2,1)S(1)} %pad_maximum_fusion.refs_0_), channel_id=1, source_target_pairs={{0,16},{8,24},{16,0},{24,8},{32,48},{40,56},{48,32},{56,40},{64,80... | collective-permute-start | bytes 1179656 | tf_op jit(solution)/shard_map/ppermute | solution.py:29
  151.9 5.5 %collective-permute-done.29.refs_6_ = bf16[128,1536]{1,0:T(8,128)(2,1)S(1)} collective-permute-done((bf16[128,1536]{1,0:T(8,128)(2,1)S(1)}, bf16[128,1536]{1,0:T(8,128)(2,1)S(1)}, u32[]{:S(2)}, u32[]{:S(2)}) %collective-permute-start.29) | collective-permute-done | bytes 393248 | tf_op jit(solution)/shard_map/ppermute | solution.py:25
  157.3 1.1 collective-permute-done.30.refs_7_
  158.4 5.0 %collective-permute-done.23.refs_2_ = bf16[128,1536]{1,0:T(8,128)(2,1)S(1)} collective-permute-done((bf16[128,1536]{1,0:T(8,128)(2,1)S(1)}, bf16[128,1536]{1,0:T(8,128)(2,1)S(1)}, u32[]{:S(2)}, u32[]{:S(2)}) %collective-permute-start.23) | collective-permute-done | bytes 393248 | tf_op jit(solution)/shard_map/ppermute | solution.py:29
  163.4 3.4 %collective-permute-done.24.refs_3_ = bf16[128,1536]{1,0:T(8,128)(2,1)S(1)} collective-permute-done((bf16[128,1536]{1,0:T(8,128)(2,1)S(1)}, bf16[128,1536]{1,0:T(8,128)(2,1)S(1)}, u32[]{:S(2)}, u32[]{:S(2)}) %collective-permute-start.24) | collective-permute-done | bytes 393248 | tf_op jit(solution)/shard_map/ppermute | solution.py:29
  166.8 5.4 %mix.3 = bf16[512,1152]{1,0:T(8,128)(2,1)} custom-call(s32[4]{0:T(128)S(1)} %pad_add_fusion.place, bf16[128,1536]{1,0:T(8,128)(2,1)S(1)} %pad_maximum_fusion.refs_0_, bf16[128,1536]{1,0:T(8,128)(2,1)S(1)} %collective-permute-done.22.refs_1_, bf16[128,1536]{1,0:T(8,128)(2,1)S(1)} %collective-permute-done.23.refs_2_, ...), custom_call_target="tpu_custom_call" | custom-call | tf_op jit(solution)/shard_map/mix/pallas_call | solution.py:247
  172.2 3.7 %collective-permute-start.31 = (bf16[512,1152]{1,0:T(8,128)(2,1)}, bf16[512,1152]{1,0:T(8,128)(2,1)S(1)}, u32[]{:S(2)}, u32[]{:S(2)}) collective-permute-start(bf16[512,1152]{1,0:T(8,128)(2,1)} %mix.3), channel_id=1, source_target_pairs={{0,1},{1,0},{2,3},{3,2},{4,5},{5,4},{6,7},{7,6},{8,9},{9,8},{10,11... | collective-permute-start | bytes 3538952 | tf_op jit(solution)/shard_map/ppermute | solution.py:37
  176.0 5.4 %mix.2.mine = bf16[512,1152]{1,0:T(8,128)(2,1)} custom-call(s32[4]{0:T(128)S(1)} %pad_add_fusion.place, bf16[128,1536]{1,0:T(8,128)(2,1)S(1)} %pad_maximum_fusion.refs_0_, bf16[128,1536]{1,0:T(8,128)(2,1)S(1)} %collective-permute-done.22.refs_1_, bf16[128,1536]{1,0:T(8,128)(2,1)S(1)} %collective-permute-done.23.refs_2_, ...), custom_call_target="tpu_custom_call" | custom-call | tf_op jit(solution)/shard_map/mix/pallas_call | solution.py:247
  181.4 1.3 copy-done
  183.3 1.8 collective-permute-start.33
  185.1 1.5 collective-permute-start.34
  186.6 12.6 %collective-permute-done.32 = bf16[128,1152]{1,0:T(8,128)(2,1)S(1)} collective-permute-done((bf16[128,1152]{1,0:T(8,128)(2,1)S(1)}, bf16[128,1152]{1,0:T(8,128)(2,1)S(1)}, u32[]{:S(2)}, u32[]{:S(2)}) %collective-permute-start.32) | collective-permute-done | bytes 294944 | tf_op jit(solution)/shard_map/ppermute | solution.py:33
  199.5 0.9 add_convert_fusion
  (44 shorter events, 2.3 us)
Async XLA Ops:
  0.0 9.8 %collective-permute-start.1 = (bf16[128,1152]{1,0:T(8,128)(2,1)}, bf16[128,1152]{1,0:T(8,128)(2,1)S(1)}, u32[]{:S(2)}, u32[]{:S(2)}) collective-permute-start(bf16[128,1152]{1,0:T(8,128)(2,1)} %refs_0_.1), channel_id=1, source_target_pairs={{0,2},{1,3},{2,4},{3,5},{4,6},{5,7},{6,0},{7,1},{8,10},{9,11},{10,... | collective-permute-start | bytes 884744 | tf_op jit(solution)/shard_map/ppermute | solution.py:33
  2.0 15.4 %collective-permute-start.3 = (bf16[128,1152]{1,0:T(8,128)(2,1)}, bf16[128,1152]{1,0:T(8,128)(2,1)S(1)}, u32[]{:S(2)}, u32[]{:S(2)}) collective-permute-start(bf16[128,1152]{1,0:T(8,128)(2,1)} %refs_0_.1), channel_id=1, source_target_pairs={{0,4},{1,5},{2,6},{3,7},{4,0},{5,1},{6,2},{7,3},{8,12},{9,13},{10,... | collective-permute-start | bytes 884744 | tf_op jit(solution)/shard_map/ppermute | solution.py:33
  4.5 14.5 %collective-permute-start.5 = (bf16[128,1152]{1,0:T(8,128)(2,1)}, bf16[128,1152]{1,0:T(8,128)(2,1)S(1)}, u32[]{:S(2)}, u32[]{:S(2)}) collective-permute-start(bf16[128,1152]{1,0:T(8,128)(2,1)} %refs_0_.1), channel_id=1, source_target_pairs={{0,6},{1,7},{2,0},{3,1},{4,2},{5,3},{6,4},{7,5},{8,14},{9,15},{10,... | collective-permute-start | bytes 884744 | tf_op jit(solution)/shard_map/ppermute | solution.py:33
  5.6 34.9 %collective-permute-start = (bf16[128,1152]{1,0:T(8,128)(2,1)}, bf16[128,1152]{1,0:T(8,128)(2,1)S(1)}, u32[]{:S(2)}, u32[]{:S(2)}) collective-permute-start(bf16[128,1152]{1,0:T(8,128)(2,1)} %refs_0_.1), channel_id=1, source_target_pairs={{0,1},{1,0},{2,3},{3,2},{4,5},{5,4},{6,7},{7,6},{8,9},{9,8},{10,11... | collective-permute-start | bytes 884744 | tf_op jit(solution)/shard_map/ppermute | solution.py:37
  9.8 30.8 %collective-permute-start.2 = (bf16[128,1152]{1,0:T(8,128)(2,1)S(1)}, bf16[128,1152]{1,0:T(8,128)(2,1)S(1)}, u32[]{:S(2)}, u32[]{:S(2)}) collective-permute-start(bf16[128,1152]{1,0:T(8,128)(2,1)S(1)} %collective-permute-done.1.refs_2_), channel_id=1, source_target_pairs={{0,1},{1,0},{2,3},{3,2},{4,5},{5,4},{6,7},{7,6},{8,9},{9,8},{10,11... | collective-permute-start | bytes 884744 | tf_op jit(solution)/shard_map/ppermute | solution.py:37
  17.4 23.2 %collective-permute-start.4 = (bf16[128,1152]{1,0:T(8,128)(2,1)S(1)}, bf16[128,1152]{1,0:T(8,128)(2,1)S(1)}, u32[]{:S(2)}, u32[]{:S(2)}) collective-permute-start(bf16[128,1152]{1,0:T(8,128)(2,1)S(1)} %collective-permute-done.3.refs_4_), channel_id=1, source_target_pairs={{0,1},{1,0},{2,3},{3,2},{4,5},{5,4},{6,7},{7,6},{8,9},{9,8},{10,11... | collective-permute-start | bytes 884744 | tf_op jit(solution)/shard_map/ppermute | solution.py:37
  19.0 21.6 %collective-permute-start.6 = (bf16[128,1152]{1,0:T(8,128)(2,1)S(1)}, bf16[128,1152]{1,0:T(8,128)(2,1)S(1)}, u32[]{:S(2)}, u32[]{:S(2)}) collective-permute-start(bf16[128,1152]{1,0:T(8,128)(2,1)S(1)} %collective-permute-done.5.refs_6_), channel_id=1, source_target_pairs={{0,1},{1,0},{2,3},{3,2},{4,5},{5,4},{6,7},{7,6},{8,9},{9,8},{10,11... | collective-permute-start | bytes 884744 | tf_op jit(solution)/shard_map/ppermute | solution.py:37
  20.8 19.7 %all-to-all-start = ((f32[128,1,256]{2,1,0:T(1,128)}), f32[128,1,256]{2,1,0:T(1,128)S(1)}, u32[]{:S(2)}, u32[]{:S(2)}) async-start(f32[128,1,256]{2,1,0:T(1,128)} %broadcast_in_dim.4), calls=%async_computation | async-start | bytes 262144 | tf_op jit(solution)/shard_map/all_to_all | solution.py:293
  30.6 34.4 %copy-start.3 = (s32[4]{0:T(128)S(1)}, s32[4]{0:T(128)}, u32[]{:S(2)}) copy-start(s32[4]{0:T(128)} %lengths.1) | copy-start | bytes 52
  40.6 1.0 copy-start.1
  51.0 13.0 %collective-permute-start.10 = (bf16[128,1600]{1,0:T(8,128)(2,1)}, bf16[128,1600]{1,0:T(8,128)(2,1)S(1)}, u32[]{:S(2)}, u32[]{:S(2)}) collective-permute-start(bf16[128,1600]{1,0:T(8,128)(2,1)} %get-tuple-element.30), channel_id=1, source_target_pairs={{0,8},{8,16},{16,24},{24,0},{32,40},{40,48},{48,56},{56,32},{64,72... | collective-permute-start | bytes 1228808 | tf_op jit(solution)/shard_map/ppermute | solution.py:29
  51.5 20.4 %collective-permute-start.11 = (bf16[128,1600]{1,0:T(8,128)(2,1)}, bf16[128,1600]{1,0:T(8,128)(2,1)S(1)}, u32[]{:S(2)}, u32[]{:S(2)}) collective-permute-start(bf16[128,1600]{1,0:T(8,128)(2,1)} %get-tuple-element.31), channel_id=1, source_target_pairs={{0,16},{8,24},{16,0},{24,8},{32,48},{40,56},{48,32},{56,40},{64,80... | collective-permute-start | bytes 1228808 | tf_op jit(solution)/shard_map/ppermute | solution.py:29
  53.0 20.0 %collective-permute-start.12 = (bf16[128,1600]{1,0:T(8,128)(2,1)}, bf16[128,1600]{1,0:T(8,128)(2,1)}, u32[]{:S(2)}, u32[]{:S(2)}) collective-permute-start(bf16[128,1600]{1,0:T(8,128)(2,1)} %get-tuple-element.32), channel_id=1, source_target_pairs={{0,24},{8,0},{16,8},{24,16},{32,56},{40,32},{48,40},{56,48},{64,88... | collective-permute-start | bytes 1228808 | tf_op jit(solution)/shard_map/ppermute | solution.py:29
  54.5 18.5 %collective-permute-start.7 = (bf16[128,1600]{1,0:T(8,128)(2,1)}, bf16[128,1600]{1,0:T(8,128)(2,1)S(1)}, u32[]{:S(2)}, u32[]{:S(2)}) collective-permute-start(bf16[128,1600]{1,0:T(8,128)(2,1)} %get-tuple-element.26), channel_id=1, source_target_pairs={{0,32},{8,40},{16,48},{24,56},{32,64},{40,72},{48,80},{56,88},{64,... | collective-permute-start | bytes 1228808 | tf_op jit(solution)/shard_map/ppermute | solution.py:25
  54.8 19.6 %collective-permute-start.8 = (bf16[128,1600]{1,0:T(8,128)(2,1)S(1)}, bf16[128,1600]{1,0:T(8,128)(2,1)S(1)}, u32[]{:S(2)}, u32[]{:S(2)}) collective-permute-start(bf16[128,1600]{1,0:T(8,128)(2,1)S(1)} %get-tuple-element.27), channel_id=1, source_target_pairs={{0,64},{8,72},{16,80},{24,88},{32,96},{40,104},{48,112},{56,120},{... | collective-permute-start | bytes 1228808 | tf_op jit(solution)/shard_map/ppermute | solution.py:25
  64.0 10.5 %collective-permute-start.9 = (bf16[128,1600]{1,0:T(8,128)(2,1)}, bf16[128,1600]{1,0:T(8,128)(2,1)S(1)}, u32[]{:S(2)}, u32[]{:S(2)}) collective-permute-start(bf16[128,1600]{1,0:T(8,128)(2,1)} %get-tuple-element.28), channel_id=1, source_target_pairs={{0,96},{8,104},{16,112},{24,120},{32,0},{40,8},{48,16},{56,24},{64... | collective-permute-start | bytes 1228808 | tf_op jit(solution)/shard_map/ppermute | solution.py:25
  74.5 1.0 copy-start.2
  76.9 12.3 %collective-permute-start.13 = (bf16[32,1600]{1,0:T(8,128)(2,1)S(1)}, bf16[32,1600]{1,0:T(8,128)(2,1)S(1)}, u32[]{:S(2)}, u32[]{:S(2)}) collective-permute-start(bf16[32,1600]{1,0:T(8,128)(2,1)S(1)} %get-tuple-element.34), channel_id=1, source_target_pairs={{0,8},{8,16},{16,24},{24,0},{32,40},{40,48},{48,56},{56,32},{64,72... | collective-permute-start | bytes 307208 | tf_op jit(solution)/shard_map/ppermute | solution.py:29
  77.7 13.5 %collective-permute-start.14 = (bf16[32,1600]{1,0:T(8,128)(2,1)S(1)}, bf16[32,1600]{1,0:T(8,128)(2,1)S(1)}, u32[]{:S(2)}, u32[]{:S(2)}) collective-permute-start(bf16[32,1600]{1,0:T(8,128)(2,1)S(1)} %get-tuple-element.35), channel_id=1, source_target_pairs={{0,16},{8,24},{16,0},{24,8},{32,48},{40,56},{48,32},{56,40},{64,80... | collective-permute-start | bytes 307208 | tf_op jit(solution)/shard_map/ppermute | solution.py:29
  80.1 11.1 %collective-permute-start.15 = (bf16[32,1600]{1,0:T(8,128)(2,1)S(1)}, bf16[32,1600]{1,0:T(8,128)(2,1)S(1)}, u32[]{:S(2)}, u32[]{:S(2)}) collective-permute-start(bf16[32,1600]{1,0:T(8,128)(2,1)S(1)} %get-tuple-element.36), channel_id=1, source_target_pairs={{0,24},{8,0},{16,8},{24,16},{32,56},{40,32},{48,40},{56,48},{64,88... | collective-permute-start | bytes 307208 | tf_op jit(solution)/shard_map/ppermute | solution.py:29
  81.8 9.5 %collective-permute-start.16 = (bf16[32,1600]{1,0:T(8,128)(2,1)S(1)}, bf16[32,1600]{1,0:T(8,128)(2,1)S(1)}, u32[]{:S(2)}, u32[]{:S(2)}) collective-permute-start(bf16[32,1600]{1,0:T(8,128)(2,1)S(1)} %get-tuple-element.38), channel_id=1, source_target_pairs={{0,32},{8,40},{16,48},{24,56},{32,64},{40,72},{48,80},{56,88},{64,... | collective-permute-start | bytes 307208 | tf_op jit(solution)/shard_map/ppermute | solution.py:25
  86.3 6.1 %collective-permute-start.17 = (bf16[32,1600]{1,0:T(8,128)(2,1)S(1)}, bf16[32,1600]{1,0:T(8,128)(2,1)S(1)}, u32[]{:S(2)}, u32[]{:S(2)}) collective-permute-start(bf16[32,1600]{1,0:T(8,128)(2,1)S(1)} %get-tuple-element.39), channel_id=1, source_target_pairs={{0,64},{8,72},{16,80},{24,88},{32,96},{40,104},{48,112},{56,120},{... | collective-permute-start | bytes 307208 | tf_op jit(solution)/shard_map/ppermute | solution.py:25
  89.3 4.8 %collective-permute-start.18 = (bf16[32,1600]{1,0:T(8,128)(2,1)S(1)}, bf16[32,1600]{1,0:T(8,128)(2,1)S(1)}, u32[]{:S(2)}, u32[]{:S(2)}) collective-permute-start(bf16[32,1600]{1,0:T(8,128)(2,1)S(1)} %get-tuple-element.40), channel_id=1, source_target_pairs={{0,96},{8,104},{16,112},{24,120},{32,0},{40,8},{48,16},{56,24},{64... | collective-permute-start | bytes 307208 | tf_op jit(solution)/shard_map/ppermute | solution.py:25
  94.8 13.9 %all-to-all-start.1 = ((bf16[8,8,1600]{2,1,0:T(8,128)(2,1)}), bf16[8,8,1600]{2,1,0:T(8,128)(2,1)S(1)}, u32[]{:S(2)}, u32[]{:S(2)}) async-start(bf16[8,8,1600]{2,1,0:T(8,128)(2,1)} %maximum_bitcast_fusion), calls=%async_computation.1 | async-start | bytes 425984 | tf_op jit(solution)/shard_map/all_to_all | solution.py:304
  125.4 4.8 %collective-permute-start.25 = (bf16[32,1536]{1,0:T(8,128)(2,1)S(1)}, bf16[32,1536]{1,0:T(8,128)(2,1)S(1)}, u32[]{:S(2)}, u32[]{:S(2)}) collective-permute-start(bf16[32,1536]{1,0:T(8,128)(2,1)S(1)} %get-tuple-element.47), channel_id=1, source_target_pairs={{0,8},{8,16},{16,24},{24,0},{32,40},{40,48},{48,56},{56,32},{64,72... | collective-permute-start | bytes 294920 | tf_op jit(solution)/shard_map/ppermute | solution.py:29
  126.1 6.0 %collective-permute-start.26 = (bf16[32,1536]{1,0:T(8,128)(2,1)S(1)}, bf16[32,1536]{1,0:T(8,128)(2,1)S(1)}, u32[]{:S(2)}, u32[]{:S(2)}) collective-permute-start(bf16[32,1536]{1,0:T(8,128)(2,1)S(1)} %get-tuple-element.47), channel_id=1, source_target_pairs={{0,16},{8,24},{16,0},{24,8},{32,48},{40,56},{48,32},{56,40},{64,80... | collective-permute-start | bytes 294920 | tf_op jit(solution)/shard_map/ppermute | solution.py:29
  128.2 4.6 %collective-permute-start.27 = (bf16[32,1536]{1,0:T(8,128)(2,1)S(1)}, bf16[32,1536]{1,0:T(8,128)(2,1)S(1)}, u32[]{:S(2)}, u32[]{:S(2)}) collective-permute-start(bf16[32,1536]{1,0:T(8,128)(2,1)S(1)} %get-tuple-element.47), channel_id=1, source_target_pairs={{0,24},{8,0},{16,8},{24,16},{32,56},{40,32},{48,40},{56,48},{64,88... | collective-permute-start | bytes 294920 | tf_op jit(solution)/shard_map/ppermute | solution.py:29
  132.8 19.1 %collective-permute-start.28 = (bf16[128,1536]{1,0:T(8,128)(2,1)S(1)}, bf16[128,1536]{1,0:T(8,128)(2,1)S(1)}, u32[]{:S(2)}, u32[]{:S(2)}) collective-permute-start(bf16[128,1536]{1,0:T(8,128)(2,1)S(1)} %pad_maximum_fusion.1.refs_4_), channel_id=1, source_target_pairs={{0,32},{8,40},{16,48},{24,56},{32,64},{40,72},{48,80},{56,88},{64,... | collective-permute-start | bytes 1179656 | tf_op jit(solution)/shard_map/ppermute | solution.py:25
  133.1 12.8 %collective-permute-start.19 = (bf16[32,1536]{1,0:T(8,128)(2,1)S(1)}, bf16[32,1536]{1,0:T(8,128)(2,1)S(1)}, u32[]{:S(2)}, u32[]{:S(2)}) collective-permute-start(bf16[32,1536]{1,0:T(8,128)(2,1)S(1)} %get-tuple-element.48), channel_id=1, source_target_pairs={{0,32},{8,40},{16,48},{24,56},{32,64},{40,72},{48,80},{56,88},{64,... | collective-permute-start | bytes 294920 | tf_op jit(solution)/shard_map/ppermute | solution.py:25
  134.0 14.6 %collective-permute-start.20 = (bf16[32,1536]{1,0:T(8,128)(2,1)S(1)}, bf16[32,1536]{1,0:T(8,128)(2,1)S(1)}, u32[]{:S(2)}, u32[]{:S(2)}) collective-permute-start(bf16[32,1536]{1,0:T(8,128)(2,1)S(1)} %get-tuple-element.48), channel_id=1, source_target_pairs={{0,64},{8,72},{16,80},{24,88},{32,96},{40,104},{48,112},{56,120},{... | collective-permute-start | bytes 294920 | tf_op jit(solution)/shard_map/ppermute | solution.py:25
  137.4 11.2 %collective-permute-start.21 = (bf16[32,1536]{1,0:T(8,128)(2,1)S(1)}, bf16[32,1536]{1,0:T(8,128)(2,1)S(1)}, u32[]{:S(2)}, u32[]{:S(2)}) collective-permute-start(bf16[32,1536]{1,0:T(8,128)(2,1)S(1)} %get-tuple-element.48), channel_id=1, source_target_pairs={{0,96},{8,104},{16,112},{24,120},{32,0},{40,8},{48,16},{56,24},{64... | collective-permute-start | bytes 294920 | tf_op jit(solution)/shard_map/ppermute | solution.py:25
  139.4 17.9 %collective-permute-start.29 = (bf16[128,1536]{1,0:T(8,128)(2,1)S(1)}, bf16[128,1536]{1,0:T(8,128)(2,1)S(1)}, u32[]{:S(2)}, u32[]{:S(2)}) collective-permute-start(bf16[128,1536]{1,0:T(8,128)(2,1)S(1)} %pad_maximum_fusion.1.refs_4_), channel_id=1, source_target_pairs={{0,64},{8,72},{16,80},{24,88},{32,96},{40,104},{48,112},{56,120},{... | collective-permute-start | bytes 1179656 | tf_op jit(solution)/shard_map/ppermute | solution.py:25
  145.9 12.5 %collective-permute-start.30 = (bf16[128,1536]{1,0:T(8,128)(2,1)S(1)}, bf16[128,1536]{1,0:T(8,128)(2,1)S(1)}, u32[]{:S(2)}, u32[]{:S(2)}) collective-permute-start(bf16[128,1536]{1,0:T(8,128)(2,1)S(1)} %pad_maximum_fusion.1.refs_4_), channel_id=1, source_target_pairs={{0,96},{8,104},{16,112},{24,120},{32,0},{40,8},{48,16},{56,24},{64... | collective-permute-start | bytes 1179656 | tf_op jit(solution)/shard_map/ppermute | solution.py:25
  148.7 9.8 %collective-permute-start.22 = (bf16[128,1536]{1,0:T(8,128)(2,1)S(1)}, bf16[128,1536]{1,0:T(8,128)(2,1)S(1)}, u32[]{:S(2)}, u32[]{:S(2)}) collective-permute-start(bf16[128,1536]{1,0:T(8,128)(2,1)S(1)} %pad_maximum_fusion.refs_0_), channel_id=1, source_target_pairs={{0,8},{8,16},{16,24},{24,0},{32,40},{40,48},{48,56},{56,32},{64,72... | collective-permute-start | bytes 1179656 | tf_op jit(solution)/shard_map/ppermute | solution.py:29
  148.7 14.7 %collective-permute-start.23 = (bf16[128,1536]{1,0:T(8,128)(2,1)S(1)}, bf16[128,1536]{1,0:T(8,128)(2,1)S(1)}, u32[]{:S(2)}, u32[]{:S(2)}) collective-permute-start(bf16[128,1536]{1,0:T(8,128)(2,1)S(1)} %pad_maximum_fusion.refs_0_), channel_id=1, source_target_pairs={{0,16},{8,24},{16,0},{24,8},{32,48},{40,56},{48,32},{56,40},{64,80... | collective-permute-start | bytes 1179656 | tf_op jit(solution)/shard_map/ppermute | solution.py:29
  151.9 15.0 %collective-permute-start.24 = (bf16[128,1536]{1,0:T(8,128)(2,1)S(1)}, bf16[128,1536]{1,0:T(8,128)(2,1)S(1)}, u32[]{:S(2)}, u32[]{:S(2)}) collective-permute-start(bf16[128,1536]{1,0:T(8,128)(2,1)S(1)} %pad_maximum_fusion.refs_0_), channel_id=1, source_target_pairs={{0,24},{8,0},{16,8},{24,16},{32,56},{40,32},{48,40},{56,48},{64,88... | collective-permute-start | bytes 1179656 | tf_op jit(solution)/shard_map/ppermute | solution.py:29
  172.2 9.1 %collective-permute-start.31 = (bf16[512,1152]{1,0:T(8,128)(2,1)}, bf16[512,1152]{1,0:T(8,128)(2,1)S(1)}, u32[]{:S(2)}, u32[]{:S(2)}) collective-permute-start(bf16[512,1152]{1,0:T(8,128)(2,1)} %mix.3), channel_id=1, source_target_pairs={{0,1},{1,0},{2,3},{3,2},{4,5},{5,4},{6,7},{7,6},{8,9},{9,8},{10,11... | collective-permute-start | bytes 3538952 | tf_op jit(solution)/shard_map/ppermute | solution.py:37
  181.4 1.3 copy-start
  183.0 16.2 %collective-permute-start.32 = (bf16[128,1152]{1,0:T(8,128)(2,1)S(1)}, bf16[128,1152]{1,0:T(8,128)(2,1)S(1)}, u32[]{:S(2)}, u32[]{:S(2)}) collective-permute-start(bf16[128,1152]{1,0:T(8,128)(2,1)S(1)} %get-tuple-element.42), channel_id=1, source_target_pairs={{0,2},{1,3},{2,4},{3,5},{4,6},{5,7},{6,0},{7,1},{8,10},{9,11},{10,... | collective-permute-start | bytes 884744 | tf_op jit(solution)/shard_map/ppermute | solution.py:33
  183.3 15.9 %collective-permute-start.33 = (bf16[128,1152]{1,0:T(8,128)(2,1)S(1)}, bf16[128,1152]{1,0:T(8,128)(2,1)S(1)}, u32[]{:S(2)}, u32[]{:S(2)}) collective-permute-start(bf16[128,1152]{1,0:T(8,128)(2,1)S(1)} %get-tuple-element.43), channel_id=1, source_target_pairs={{0,4},{1,5},{2,6},{3,7},{4,0},{5,1},{6,2},{7,3},{8,12},{9,13},{10,... | collective-permute-start | bytes 884744 | tf_op jit(solution)/shard_map/ppermute | solution.py:33
  185.1 14.4 %collective-permute-start.34 = (bf16[128,1152]{1,0:T(8,128)(2,1)S(1)}, bf16[128,1152]{1,0:T(8,128)(2,1)S(1)}, u32[]{:S(2)}, u32[]{:S(2)}) collective-permute-start(bf16[128,1152]{1,0:T(8,128)(2,1)S(1)} %get-tuple-element.44), channel_id=1, source_target_pairs={{0,6},{1,7},{2,0},{3,1},{4,2},{5,3},{6,4},{7,5},{8,14},{9,15},{10,... | collective-permute-start | bytes 884744 | tf_op jit(solution)/shard_map/ppermute | solution.py:33

commit v2 on v1

v2 whole, which is shorter than its diff:
```python
import functools

import jax
import jax.numpy as jnp
from jax import lax
from jax.experimental import pallas as pl
from jax.experimental.pallas import tpu as pltpu
from jax.sharding import PartitionSpec as P

D = 18432
HD = 256
STEPS = 2
VMEM = pl.BlockSpec(memory_space=pltpu.VMEM)
SMEM = pl.BlockSpec(memory_space=pltpu.SMEM)
ANY = pl.BlockSpec(memory_space=pl.ANY)
F32 = jnp.float32
BF16 = jnp.bfloat16


def params(mib):
    return pltpu.CompilerParams(vmem_limit_bytes=mib * 1024 * 1024)


def along_y(value, m):
    return lax.ppermute(value, "gx", [(g, g ^ (4 * m)) for g in range(16)])


def along_z(value, m):
    return lax.ppermute(value, "gx", [(g, g ^ m) for g in range(16)])


def along_x(value, m):
    return lax.ppermute(value, "gy", [(g, g ^ (2 * m)) for g in range(8)])


def other_core(value):
    return lax.ppermute(value, "gy", [(g, g ^ 1) for g in range(8)])


def load_tiles(source, tiles, sems):
    loads = []
    wide = tiles.shape[2]
    for t in range(tiles.shape[0]):
        load = pltpu.make_async_copy(source.at[:, pl.ds(t * wide, wide)], tiles.at[t], sems.at[t])
        load.start()
        loads.append(load)
    return loads


def multiply(left, w_pair, tiles, loads, outs):
    width = tiles.shape[0] * 256

    def put(part, at, size):
        for k, out in enumerate(outs):
            out[:, at : at + size] = part[k * 128 : k * 128 + 128]

    pair = jnp.dot(left, w_pair[...], preferred_element_type=F32).astype(BF16)
    put(pair, width, w_pair.shape[1])
    for t in range(tiles.shape[0]):
        loads[t].wait()
        put(jnp.dot(left, tiles[t], preferred_element_type=F32).astype(BF16), t * 256, 256)


def project_kernel(place, stats, gain, *refs):
    pieces, (w_query, w_pair), outs, rest = refs[:8], refs[8:10], refs[10:14], refs[14]
    normed, mean_of, scale_of, tiles, sems = refs[15:]
    loads = load_tiles(w_query, tiles, sems)
    y, z, x, c = place[0], place[1], place[2], place[3]
    total = stats[0:8, :]
    for g in range(1, 16):
        total = total + stats[g * 8 : g * 8 + 8, :]
    mean = total[:, :128] / D
    variance = total[:, 128:] / D - mean * mean
    mean_columns = mean.T
    scale_columns = lax.rsqrt(variance + 1e-05).T
    for s in range(8):
        mean_of[s] = mean_columns[:, s : s + 1]
        scale_of[s] = scale_columns[:, s : s + 1]
    gains = gain[...].astype(F32)
    for m in range(4):
        for j in range(2):
            source_c = c ^ j
            s = (x ^ m) * 2 + source_c
            rows = pieces[m * 2 + j][...].astype(F32)
            rows = ((rows - mean_of[s]) * scale_of[s] * gains).astype(BF16)
            to_y = x ^ m ^ y
            for b in range(2):
                to_z = (source_c * 2 + b) ^ z
                normed[0, to_y, to_z] = rows[b * 64 : b * 64 + 32]
                normed[1, to_z, to_y] = rows[b * 64 + 32 : b * 64 + 64]
    depth = normed.shape[-1]
    for h in range(2):
        for i, k in enumerate((0, 3)):
            at = (h * 2 + i) * 128
            rest[at : at + 128, :] = normed[h, k].reshape(128, depth)
    left = normed[:, 1:3].reshape(512, depth)
    multiply(left, w_pair, tiles, loads, outs)


def project(place, stats, gain, pieces, w_query, w_pair):
    depth, width = w_query.shape
    out = jax.ShapeDtypeStruct((128, width + w_pair.shape[1]), BF16)
    return pl.pallas_call(
        project_kernel,
        out_shape=[out] * 4 + [jax.ShapeDtypeStruct((512, depth), BF16)],
        in_specs=[SMEM] + [VMEM] * 10 + [ANY, VMEM],
        out_specs=[VMEM] * 5,
        scratch_shapes=[
            pltpu.VMEM((2, 4, 4, 32, depth), BF16),
            pltpu.VMEM((8, 128, 1), F32),
            pltpu.VMEM((8, 128, 1), F32),
            pltpu.VMEM((width // 256, depth, 256), BF16),
            pltpu.SemaphoreType.DMA((width // 256,)),
        ],
        compiler_params=params(28),
        name="project",
    )(place, stats, gain, *pieces, w_query, w_pair)


def project_rest_kernel(left, w_query, w_pair, *refs):
    outs, tiles, sems = refs[:4], refs[4], refs[5]
    multiply(left[...], w_pair, tiles, load_tiles(w_query, tiles, sems), outs)


def project_rest(left, w_query, w_pair):
    depth, width = w_query.shape
    out = jax.ShapeDtypeStruct((128, width + w_pair.shape[1]), BF16)
    return pl.pallas_call(
        project_rest_kernel,
        out_shape=[out] * 4,
        in_specs=[VMEM, ANY, VMEM],
        out_specs=[VMEM] * 4,
        scratch_shapes=[
            pltpu.VMEM((width // 256, depth, 256), BF16),
            pltpu.SemaphoreType.DMA((width // 256,)),
        ],
        compiler_params=params(20),
        name="project_rest",
    )(left, w_query, w_pair)


def add_kernel(pieces, *refs):
    groups = len(refs) // (2 * pieces)
    ins, outs = refs[: groups * pieces], refs[groups * pieces :]
    for g in range(groups):
        total = ins[g * pieces][...].astype(F32)
        for k in range(1, pieces):
            total = total + ins[g * pieces + k][...].astype(F32)
        total = total.astype(BF16)
        rows = total.shape[0] // pieces
        for k in range(pieces):
            outs[g * pieces + k][...] = total[k * rows : k * rows + rows]


def add_and_cut(values, pieces):
    rows, width = values[0].shape
    out = jax.ShapeDtypeStruct((rows // pieces, width), BF16)
    return pl.pallas_call(
        functools.partial(add_kernel, pieces),
        out_shape=[out] * len(values),
        in_specs=[VMEM] * len(values),
        out_specs=[VMEM] * len(values),
        compiler_params=params(16),
        name="add_and_cut",
    )(*values)


def finish_kernel(place, *refs):
    ins, (mine, theirs), blocks = refs[:8], refs[8:10], refs[10]
    x, c = place[2], place[3]
    for h in range(2):
        total = ins[h * 4][...].astype(F32)
        for k in range(1, 4):
            total = total + ins[h * 4 + k][...].astype(F32)
        for i in range(4):
            blocks[c ^ (i % 2), x ^ (h * 2 + i // 2)] = total[i * 8 : i * 8 + 8]
    width = blocks.shape[-1]
    mine[...] = blocks[0].reshape(32, width).astype(BF16)
    theirs[...] = blocks[1].reshape(32, width).astype(BF16)


def finish(place, values):
    shape = values[0].shape
    return pl.pallas_call(
        finish_kernel,
        out_shape=[jax.ShapeDtypeStruct(shape, BF16)] * 2,
        in_specs=[SMEM] + [VMEM] * 8,
        out_specs=[VMEM] * 2,
        scratch_shapes=[pltpu.VMEM((2, 4, 8, shape[1]), F32)],
        compiler_params=params(8),
        name="finish",
    )(place, *values)


def pair_kernel(by_core, place, mine, theirs, *outs):
    first, second = mine[...].astype(F32), theirs[...].astype(F32)
    if by_core:
        swap = place[3] == 1
        first, second = jnp.where(swap, second, first), jnp.where(swap, first, second)
    for m, out in enumerate(outs):
        rows = slice(m * 8, m * 8 + 8)
        out[...] = jnp.concatenate([first[rows], second[rows]], axis=0).astype(BF16)


def pair(by_core, place, mine, theirs):
    out = jax.ShapeDtypeStruct((16, mine.shape[1]), BF16)
    return pl.pallas_call(
        functools.partial(pair_kernel, by_core),
        out_shape=[out] * 4,
        in_specs=[SMEM] + [VMEM] * 2,
        out_specs=[VMEM] * 4,
        compiler_params=params(8),
        name="pair",
    )(place, mine, theirs)


def attend_kernel(lengths, place, *refs):
    packed, (cosine, sine, keys, values, mine, theirs) = refs[:4], refs[4:10]
    query_rows, new_pieces, new_kv, result = refs[10:]
    request = pl.program_id(0)
    heads = mine.shape[1] // HD
    count = 8 * heads

    @pl.when(request == 0)
    def _():
        x, c = place[2], place[3]
        cos, sin = cosine[...], sine[...]

        def rotated(first, second):
            return first * cos - second * sin, second * cos + first * sin

        for m in range(4):
            rows = packed[m][...].astype(F32)
            for j in range(2):
                block = rows[j * 8 : j * 8 + 8]
                for h in range(heads):
                    head = block[:, h * HD : h * HD + HD]
                    at = (m * 2 + j) * heads + h
                    for i, half in enumerate(rotated(head[:, :128], head[:, 128:])):
                        query_rows[i, pl.ds(at, 8, stride=count), :] = half
                new_pieces[(x ^ m) * 2 + (c ^ j)] = block[:, heads * HD :]
        halves = [
            jnp.concatenate([new_pieces[i], new_pieces[i + 1]], axis=-1) for i in range(0, 8, 2)
        ]
        new_kv[0] = jnp.concatenate(rotated(halves[0], halves[1]), axis=-1).astype(BF16)
        new_kv[1] = jnp.concatenate(halves[2:], axis=-1).astype(BF16)

    per = STEPS * count
    start = pl.multiple_of(request * per, per)
    query = jnp.concatenate([query_rows[i, pl.ds(start, per), :] for i in range(2)], axis=-1)
    query = (query.astype(BF16).astype(F32) * HD ** (-0.5)).astype(BF16)
    dims = (((1,), (1,)), ((), ()))
    cached = lax.dot_general(query, keys[0], dims, preferred_element_type=F32)
    slots = lax.broadcasted_iota(jnp.int32, cached.shape, 1)
    cached = jnp.where(slots < lengths[request], cached, -jnp.inf)
    fresh = lax.dot_general(query, new_kv[0], dims, preferred_element_type=F32)
    row_step = lax.broadcasted_iota(jnp.int32, fresh.shape, 0) // count
    key_step = lax.broadcasted_iota(jnp.int32, fresh.shape, 1) - request * STEPS
    fresh = jnp.where((key_step >= 0) & (key_step <= row_step), fresh, -jnp.inf)
    top = jnp.maximum(
        jnp.max(cached, axis=-1, keepdims=True), jnp.max(fresh, axis=-1, keepdims=True)
    )
    cached = jnp.exp(cached - top)
    fresh = jnp.exp(fresh - top)
    denom = jnp.sum(cached, axis=-1, keepdims=True) + jnp.sum(fresh, axis=-1, keepdims=True)
    mixed = jnp.dot(cached.astype(BF16), values[0], preferred_element_type=F32)
    mixed = mixed + jnp.dot(fresh.astype(BF16), new_kv[1], preferred_element_type=F32)
    mixed = mixed / denom
    for i in range(2):
        result[i, pl.ds(start, per), :] = mixed[:, i * 128 : i * 128 + 128]

    @pl.when(request == pl.num_programs(0) - 1)
    def _():
        for j, out in enumerate((mine, theirs)):
            lines = []
            for m in range(4):
                at = (m * 2 + j) * heads
                halves = [
                    result[i, pl.ds(at + h, 8, stride=count), :]
                    for h in range(heads)
                    for i in range(2)
                ]
                lines.append(jnp.concatenate(halves, axis=-1))
            out[...] = jnp.concatenate(lines, axis=0).astype(BF16)


def attend(place, packed, cosine, sine, cache_keys, cache_values, lengths):
    requests, slots, _ = cache_keys.shape
    total = packed[0].shape[1]
    width = total // HD * HD
    count = 8 * (width // HD)
    whole = lambda *shape: pl.BlockSpec(shape, lambda r, *_: (0,) * len(shape))
    cache = pl.BlockSpec((1, slots, HD), lambda r, *_: (r, 0, 0))
    return pl.pallas_call(
        attend_kernel,
        out_shape=[jax.ShapeDtypeStruct((32, width), BF16)] * 2,
        grid_spec=pltpu.PrefetchScalarGridSpec(
            num_scalar_prefetch=2,
            grid=(requests,),
            in_specs=[whole(16, total)] * 4 + [whole(8, 128)] * 2 + [cache] * 2,
            out_specs=[whole(32, width)] * 2,
            scratch_shapes=[
                pltpu.VMEM((2, 8 * count, 128), F32),
                pltpu.VMEM((8, 8, total - width), F32),
                pltpu.VMEM((2, 8, HD), BF16),
                pltpu.VMEM((2, 8 * count, 128), F32),
            ],
        ),
        compiler_params=params(20),
        name="attend",
    )(lengths, place, *packed, cosine, sine, cache_keys, cache_values)


def mix_kernel(place, *refs):
    first, second, (w_out, mine, theirs) = refs[:2], refs[2:6], refs[6:9]
    rows, tiles, sems = refs[9:]
    loads = load_tiles(w_out, tiles, sems)
    y, z, x, c = place[0], place[1], place[2], place[3]
    for i in range(2):
        core = z // 2 ^ i ^ c
        for m_y in range(4):
            to_x = y ^ m_y ^ x
            for k in range(2):
                at = m_y * 32 + k * 16
                rows[core, to_x, x ^ k] = first[i][at : at + 16, :]
                at = i * 32 + k * 16
                rows[core, to_x, x ^ (k + 2)] = second[m_y][at : at + 16, :]
    left = rows[...].reshape(512, rows.shape[-1])
    for t, load in enumerate(loads):
        load.wait()
        part = jnp.dot(left, tiles[t], preferred_element_type=F32).astype(BF16)
        wide = tiles.shape[2]
        mine[:, t * wide : t * wide + wide] = part[:256]
        theirs[:, t * wide : t * wide + wide] = part[256:]


def mix(place, first, second, w_out):
    depth, width = w_out.shape
    return pl.pallas_call(
        mix_kernel,
        out_shape=[jax.ShapeDtypeStruct((256, width), BF16)] * 2,
        in_specs=[SMEM] + [VMEM] * 6 + [ANY],
        out_specs=[VMEM] * 2,
        scratch_shapes=[
            pltpu.VMEM((2, 4, 4, 16, depth), BF16),
            pltpu.VMEM((3, depth, width // 3), BF16),
            pltpu.SemaphoreType.DMA((3,)),
        ],
        compiler_params=params(20),
        name="mix",
    )(place, *first, *second, w_out)


def pair_add_kernel(mine, theirs, *outs):
    for k in range(4):
        rows = slice(k * 64, k * 64 + 64)
        outs[k][...] = (mine[rows, :].astype(F32) + theirs[rows, :].astype(F32)).astype(BF16)


def pair_add(mine, theirs):
    out = jax.ShapeDtypeStruct((64, mine.shape[1]), BF16)
    return pl.pallas_call(
        pair_add_kernel,
        out_shape=[out] * 4,
        in_specs=[VMEM] * 2,
        out_specs=[VMEM] * 4,
        compiler_params=params(8),
        name="pair_add",
    )(mine, theirs)


def sum_of(values):
    result = values[0].astype(F32)
    for value in values[1:]:
        result = result + value.astype(F32)
    return result.astype(BF16)


def exchanged(along, parts):
    return [parts[0]] + [along(parts[m], m) for m in range(1, 4)]


def per_device(tokens, norm_gain, w_query, w_keyvalue, w_out, cache_keys, cache_values, lengths):
    gx, gy = lax.axis_index("gx"), lax.axis_index("gy")
    place = jnp.stack([gx // 4, gx % 4, gy // 2, gy % 2]).astype(jnp.int32)

    floated = tokens.astype(F32)
    sums = jnp.concatenate([jnp.sum(floated, axis=1), jnp.sum(floated * floated, axis=1)])
    stats = jnp.broadcast_to(sums[None], (128, 256))
    tokens, stats = lax.optimization_barrier((tokens, stats))
    arrived = exchanged(along_x, [tokens] * 4)
    stats = lax.all_to_all(stats, ("gx", "gy"), 0, 0, tiled=True)
    arrived[1:], stats = lax.optimization_barrier((arrived[1:], stats))
    pieces = []
    for piece in arrived:
        pieces += [piece, other_core(piece)]

    *sent, rest = project(place, stats, norm_gain[None], pieces, w_query, w_keyvalue)
    kept = project_rest(rest, w_query, w_keyvalue)
    by_y = exchanged(along_y, [kept[0], sent[0], sent[1], kept[1]])
    by_z = exchanged(along_z, [kept[2], sent[2], sent[3], kept[3]])
    parts = add_and_cut(by_y + by_z, 4)
    parts = exchanged(along_z, parts[:4]) + exchanged(along_y, parts[4:])
    mine, theirs = finish(place, parts)
    packed = exchanged(along_x, pair(False, place, mine, other_core(theirs)))

    half_dim = HD // 2
    freqs = 10000.0 ** (-jnp.arange(half_dim, dtype=F32) / half_dim)
    positions = lengths[:, None] + jnp.arange(STEPS, dtype=jnp.int32)[None, :]
    angles = positions.reshape(-1).astype(F32)[:, None] * freqs
    mine, theirs = attend(
        place, packed, jnp.cos(angles), jnp.sin(angles), cache_keys, cache_values, lengths
    )

    returned = exchanged(along_x, pair(True, place, mine, other_core(theirs)))
    first = jnp.concatenate(returned[:2], axis=0)
    second = jnp.concatenate(returned[2:], axis=0)
    first = jnp.concatenate(exchanged(along_y, [first] * 4), axis=0)
    second = exchanged(along_z, [second] * 4)

    halves = []
    for k in range(2):
        left = [first if k == 0 else along_z(first, 1), along_z(first, 2 + k)]
        right = jnp.concatenate([second[k], second[k + 2]], axis=0)
        mine, theirs = mix(place, left, exchanged(along_y, [right] * 4), w_out)
        halves.append(sum_of(exchanged(along_x, pair_add(mine, other_core(theirs)))))
    odd = place[1] % 2 == 1
    return jnp.concatenate(
        [jnp.where(odd, halves[1], halves[0]), jnp.where(odd, halves[0], halves[1])], axis=0
    )


def solution(mesh):
    return jax.shard_map(
        per_device,
        mesh=mesh,
        in_specs=(
            P("gy", "gx"),
            P("gx"),
            P("gx", "gy"),
            P("gx", "gy"),
            P("gy", "gx"),
            P(("gx", "gy"), None, None),
            P(("gx", "gy"), None, None),
            P(("gx", "gy")),
        ),
        out_specs=P("gy", "gx"),
        check_vma=False,
    )
```

time: 201 us -> 178 us (0.89)
  waiting for transfers between devices: 80.5 us -> 56.5 us
  blocking collectives: 9.26 us -> 0 us
  starting transfers between devices: 72 us -> 79.2 us
  local copies, waits for them, and re-layouts: 5.91 us -> 10.1 us
    ppermute x30 -> x42, waiting for transfers between devices: 66.6 us -> 43.9 us  [the longest x12 19 us: along_z(): return lax.ppermute(value, 'gx', [(g, g ^ m) for g in range(16)])]
    all_to_all x1 -> x0, blocking collectives: 9.26 us -> none  [per_device(): returned = lax.all_to_all(attended, 'gy', 0, 0, tiled=True)]
    ppermute x5 -> x8, starting transfers between devices: 8.47 us -> 17.1 us  [other_core(): return lax.ppermute(value, 'gy', [(g, g ^ 1) for g in range(8)])]
    all_to_all x2 -> x1, starting transfers between devices: 17.6 us -> 11.4 us  [per_device(): stats = lax.all_to_all(stats, ('gx', 'gy'), 0, 0, tiled=True)]
    ppermute x30 -> x42, starting transfers between devices: 45.9 us -> 50.8 us  [the longest x15 19.6 us: along_x(): return lax.ppermute(value, 'gy', [(g, g ^ 2 * m) for g in range(8)])]
    unnamed x10 -> x20, local copies, waits for them, and re-layouts: 4.38 us -> 8.52 us
    all_to_all x2 -> x1, waiting for transfers between devices: 13.9 us -> 10.7 us  [per_device(): stats = lax.all_to_all(stats, ('gx', 'gy'), 0, 0, tiled=True)]
    pallas_call x4 -> x8, Pallas kernels: 27.6 us -> 28.8 us  [the longest x2 8.15 us: mix(): pl.pallas_call(mix_kernel, out_shape=[jax.ShapeDtypeStruct((256, width),...]
  transfers between devices with their start and end apart: 37 -> 51, of which waited for: 20 -> 21; matrix products, arithmetic and copies ran while one was open for 2% -> 1% of each run, Pallas kernels for 3% -> 5%
where the time goes in v2:
time: 178 us
  starting transfers between devices  79.2 us (44%)
  waiting for transfers between devices  56.5 us (32%)
  Pallas kernels  29.5 us (17%)
  local copies, waits for them, and re-layouts  10.1 us (6%)
  other arithmetic  2.32 us (1%)
    ppermute x15, starting transfers between devices, along_x(): return lax.ppermute(value, 'gy', [(g, g ^ 2 * m) for g in range(8)])  19.6 us
    ppermute x12, waiting for transfers between devices, along_z(): return lax.ppermute(value, 'gx', [(g, g ^ m) for g in range(16)])  19 us
    ppermute x8, starting transfers between devices, other_core(): return lax.ppermute(value, 'gy', [(g, g ^ 1) for g in range(8)])  17.1 us
    ppermute x15, starting transfers between devices, along_y(): return lax.ppermute(value, 'gx', [(g, g ^ 4 * m) for g in range(16)])  16.8 us
    ppermute x15, waiting for transfers between devices, along_x(): return lax.ppermute(value, 'gy', [(g, g ^ 2 * m) for g in range(8)])  16.4 us
    ppermute x12, starting transfers between devices, along_z(): return lax.ppermute(value, 'gx', [(g, g ^ m) for g in range(16)])  14.3 us
    all_to_all x1, starting transfers between devices, per_device(): stats = lax.all_to_all(stats, ('gx', 'gy'), 0, 0, tiled=True)  11.4 us
    all_to_all x1, waiting for transfers between devices, per_device(): stats = lax.all_to_all(stats, ('gx', 'gy'), 0, 0, tiled=True)  10.7 us
  transfers between devices with their start and end apart: 51, of which 21 were waited for; matrix products, arithmetic and copies ran while one was open for 1% of the time, Pallas kernels for 5%

profile of v2, /device:TPU:1, one launch (start us, length us, event | category | flops | bytes accessed | tf_op | source)
XLA Modules:
  0.0 178.0 jit_solution(17065928293157642741)
XLA Ops:
  0.0 1.1 convert_reduce_fusion
  1.1 2.1 %collective-permute-start = (bf16[128,1152]{1,0:T(8,128)(2,1)}, bf16[128,1152]{1,0:T(8,128)(2,1)S(1)}, u32[]{:S(2)}, u32[]{:S(2)}) collective-permute-start(bf16[128,1152]{1,0:T(8,128)(2,1)} %refs_0_), channel_id=1, source_target_pairs={{0,2},{1,3},{2,0},{3,1},{4,6},{5,7},{6,4},{7,5},{8,10},{9,11},{10,... | collective-permute-start | bytes 884744 | tf_op jit(solution)/shard_map/ppermute | solution.py:33
  3.3 2.5 %collective-permute-start.1 = (bf16[128,1152]{1,0:T(8,128)(2,1)}, bf16[128,1152]{1,0:T(8,128)(2,1)S(1)}, u32[]{:S(2)}, u32[]{:S(2)}) collective-permute-start(bf16[128,1152]{1,0:T(8,128)(2,1)} %refs_0_), channel_id=1, source_target_pairs={{0,4},{1,5},{2,6},{3,7},{4,0},{5,1},{6,2},{7,3},{8,12},{9,13},{10,... | collective-permute-start | bytes 884744 | tf_op jit(solution)/shard_map/ppermute | solution.py:33
  5.8 0.7 all_to_all.8
  6.5 11.4 %all-to-all-start = ((f32[128,1,256]{2,1,0:T(1,128)}), f32[128,1,256]{2,1,0:T(1,128)S(1)}, u32[]{:S(2)}, u32[]{:S(2)}) async-start(f32[128,1,256]{2,1,0:T(1,128)} %all_to_all.8), calls=%async_computation | async-start | bytes 262144 | tf_op jit(solution)/shard_map/all_to_all | solution.py:392
  17.9 1.1 collective-permute-start.3
  19.1 10.7 %all-to-all-done = f32[128,1,256]{2,1,0:T(1,128)S(1)} async-done(((f32[128,1,256]{2,1,0:T(1,128)}), f32[128,1,256]{2,1,0:T(1,128)S(1)}, u32[]{:S(2)}, u32[]{:S(2)}) %all-to-all-start) | async-done | bytes 131104 | tf_op jit(solution)/shard_map/all_to_all | solution.py:392
  30.9 1.1 copy.13.refs_9_.w_pair
  32.0 0.7 broadcast_in_dim.5.gain
  32.8 2.0 %copy-done = bf16[1152,1536]{1,0:T(8,128)(2,1)S(1)} copy-done((bf16[1152,1536]{1,0:T(8,128)(2,1)S(1)}, bf16[1152,1536]{1,0:T(8,128)(2,1)}, u32[]{:S(2)}) %copy-start) | copy-done | bytes 3538968
  34.8 1.0 copy-done.4
  35.8 7.7 %project.1 = (bf16[128,1600]{1,0:T(8,128)(2,1)S(1)}, bf16[128,1600]{1,0:T(8,128)(2,1)S(1)}, bf16[128,1600]{1,0:T(8,128)(2,1)S(1)}, bf16[128,1600]{1,0:T(8,128)(2,1)S(1)}, bf16[512,1152]{1,0:T(8,128)(2,1)S(1)}) custom-call(s32[4]{0:T(128)S(1)} %pad_add_fusion.place, f32[128,256]{1,0:T(8,128)S(1)} %bitcast.7, bf16[1,1152]{1,0:T(2,128)(2,1)S(1)} %broadcast_in_dim.5.gain, ...), custom_call_target="tpu_custom_call" | custom-call | tf_op jit(solution)/shard_map/project/pallas_call | solution.py:103
  43.5 5.8 %project_rest.1 = (bf16[128,1600]{1,0:T(8,128)(2,1)S(1)}, bf16[128,1600]{1,0:T(8,128)(2,1)S(1)}, bf16[128,1600]{1,0:T(8,128)(2,1)S(1)}, bf16[128,1600]{1,0:T(8,128)(2,1)S(1)}) custom-call(bf16[512,1152]{1,0:T(8,128)(2,1)S(1)} %get-tuple-element.58.left, bf16[1152,1536]{1,0:T(8,128)(2,1)S(1)} %copy-done, bf16[1152,64]{1,0:T(8,128)(2,1)S(1)} %copy.13.refs_9_.w_pair), custom_call_target="tpu_custom_call" | custom-call | tf_op jit(solution)/shard_map/project_rest/pallas_call | solution.py:128
  49.6 0.8 collective-permute-start.9
  50.4 0.7 collective-permute-start.10
  51.1 2.9 %collective-permute-start.11 = (bf16[128,1600]{1,0:T(8,128)(2,1)S(1)}, bf16[128,1600]{1,0:T(8,128)(2,1)S(1)}, u32[]{:S(2)}, u32[]{:S(2)}) collective-permute-start(bf16[128,1600]{1,0:T(8,128)(2,1)S(1)} %get-tuple-element.65), channel_id=1, source_target_pairs={{0,16},{8,24},{16,0},{24,8},{32,48},{40,56},{48,32},{56,40},{64,80... | collective-permute-start | bytes 1228808 | tf_op jit(solution)/shard_map/ppermute | solution.py:29
  54.0 7.9 %collective-permute-done.12.refs_7_ = bf16[128,1600]{1,0:T(8,128)(2,1)S(1)} collective-permute-done((bf16[128,1600]{1,0:T(8,128)(2,1)S(1)}, bf16[128,1600]{1,0:T(8,128)(2,1)S(1)}, u32[]{:S(2)}, u32[]{:S(2)}) %collective-permute-start.12) | collective-permute-done | bytes 409632 | tf_op jit(solution)/shard_map/ppermute | solution.py:29
  61.9 1.0 collective-permute-start.8
  63.0 9.4 %collective-permute-done.11.refs_6_ = bf16[128,1600]{1,0:T(8,128)(2,1)S(1)} collective-permute-done((bf16[128,1600]{1,0:T(8,128)(2,1)S(1)}, bf16[128,1600]{1,0:T(8,128)(2,1)S(1)}, u32[]{:S(2)}, u32[]{:S(2)}) %collective-permute-start.11) | collective-permute-done | bytes 409632 | tf_op jit(solution)/shard_map/ppermute | solution.py:29
  72.4 2.9 %collective-permute-done.8.refs_2_ = bf16[128,1600]{1,0:T(8,128)(2,1)S(1)} collective-permute-done((bf16[128,1600]{1,0:T(8,128)(2,1)S(1)}, bf16[128,1600]{1,0:T(8,128)(2,1)S(1)}, u32[]{:S(2)}, u32[]{:S(2)}) %collective-permute-start.8) | collective-permute-done | bytes 409632 | tf_op jit(solution)/shard_map/ppermute | solution.py:25
  75.9 1.3 collective-permute-start.14
  77.2 2.5 %collective-permute-start.15 = (bf16[32,1600]{1,0:T(8,128)(2,1)S(1)}, bf16[32,1600]{1,0:T(8,128)(2,1)S(1)}, u32[]{:S(2)}, u32[]{:S(2)}) collective-permute-start(bf16[32,1600]{1,0:T(8,128)(2,1)S(1)} %get-tuple-element.70), channel_id=1, source_target_pairs={{0,24},{8,16},{16,8},{24,0},{32,56},{40,48},{48,40},{56,32},{64,88... | collective-permute-start | bytes 307208 | tf_op jit(solution)/shard_map/ppermute | solution.py:29
  79.7 2.0 %collective-permute-start.17 = (bf16[32,1600]{1,0:T(8,128)(2,1)S(1)}, bf16[32,1600]{1,0:T(8,128)(2,1)S(1)}, u32[]{:S(2)}, u32[]{:S(2)}) collective-permute-start(bf16[32,1600]{1,0:T(8,128)(2,1)S(1)} %get-tuple-element.73), channel_id=1, source_target_pairs={{0,64},{8,72},{16,80},{24,88},{32,96},{40,104},{48,112},{56,120},{... | collective-permute-start | bytes 307208 | tf_op jit(solution)/shard_map/ppermute | solution.py:25
  81.7 1.9 %collective-permute-start.18 = (bf16[32,1600]{1,0:T(8,128)(2,1)S(1)}, bf16[32,1600]{1,0:T(8,128)(2,1)S(1)}, u32[]{:S(2)}, u32[]{:S(2)}) collective-permute-start(bf16[32,1600]{1,0:T(8,128)(2,1)S(1)} %get-tuple-element.74), channel_id=1, source_target_pairs={{0,96},{8,104},{16,112},{24,120},{32,64},{40,72},{48,80},{56,88},{... | collective-permute-start | bytes 307208 | tf_op jit(solution)/shard_map/ppermute | solution.py:25
  83.8 1.1 collective-permute-done.17.refs_6_
  84.9 1.5 collective-permute-done.18.refs_7_
  86.5 0.7 finish.1
  87.1 4.3 %collective-permute-start.19 = (bf16[32,1600]{1,0:T(8,128)(2,1)S(1)}, bf16[32,1600]{1,0:T(8,128)(2,1)S(1)}, u32[]{:S(2)}, u32[]{:S(2)}) collective-permute-start(bf16[32,1600]{1,0:T(8,128)(2,1)S(1)} %get-tuple-element.76), channel_id=1, source_target_pairs={{0,1},{1,0},{2,3},{3,2},{4,5},{5,4},{6,7},{7,6},{8,9},{9,8},{10,11... | collective-permute-start | bytes 307208 | tf_op jit(solution)/shard_map/ppermute | solution.py:37
  91.4 0.9 collective-permute-done.19.theirs
  93.0 1.4 collective-permute-start.21
  94.4 2.5 %collective-permute-start.22 = (bf16[16,1600]{1,0:T(8,128)(2,1)S(1)}, bf16[16,1600]{1,0:T(8,128)(2,1)S(1)}, u32[]{:S(2)}, u32[]{:S(2)}) collective-permute-start(bf16[16,1600]{1,0:T(8,128)(2,1)S(1)} %get-tuple-element.80), channel_id=1, source_target_pairs={{0,6},{1,7},{2,4},{3,5},{4,2},{5,3},{6,0},{7,1},{8,14},{9,15},{10,... | collective-permute-start | bytes 153608 | tf_op jit(solution)/shard_map/ppermute | solution.py:33
  97.6 1.4 collective-permute-done.22.refs_3_
  99.0 2.2 %copy-done.2 = bf16[4,2048,256]{2,1,0:T(8,128)(2,1)S(1)} copy-done((bf16[4,2048,256]{2,1,0:T(8,128)(2,1)S(1)}, bf16[4,2048,256]{2,1,0:T(8,128)(2,1)}, u32[]{:S(2)}) %copy-start.2) | copy-done | bytes 4194328
  101.2 2.2 %copy-done.3 = bf16[4,2048,256]{2,1,0:T(8,128)(2,1)S(1)} copy-done((bf16[4,2048,256]{2,1,0:T(8,128)(2,1)S(1)}, bf16[4,2048,256]{2,1,0:T(8,128)(2,1)}, u32[]{:S(2)}) %copy-start.3) | copy-done | bytes 4194328
  103.4 5.3 %attend.1 = (bf16[32,1536]{1,0:T(8,128)(2,1)S(1)}, bf16[32,1536]{1,0:T(8,128)(2,1)S(1)}) custom-call(s32[4]{0:T(128)S(1)} %copy-done.5, s32[4]{0:T(128)S(1)} %pad_add_fusion.place, bf16[16,1600]{1,0:T(8,128)(2,1)S(1)} %get-tuple-element.77.refs_0_, bf16[16,1600]{1,0:T(8,128)(2,1)S(1)} %collective-permute-done.20.refs_1_, ...), custom_call_target="tpu_custom_call" | custom-call | tf_op jit(solution)/shard_map/attend/pallas_call | solution.py:294
  108.7 1.7 collective-permute-start.23
  110.4 0.9 collective-permute-done.23.theirs
  111.9 0.7 collective-permute-start.30
  112.7 2.0 %collective-permute-start.31 = (bf16[16,1536]{1,0:T(8,128)(2,1)S(1)}, bf16[16,1536]{1,0:T(8,128)(2,1)S(1)}, u32[]{:S(2)}, u32[]{:S(2)}) collective-permute-start(bf16[16,1536]{1,0:T(8,128)(2,1)S(1)} %get-tuple-element.86), channel_id=1, source_target_pairs={{0,6},{1,7},{2,4},{3,5},{4,2},{5,3},{6,0},{7,1},{8,14},{9,15},{10,... | collective-permute-start | bytes 147464 | tf_op jit(solution)/shard_map/ppermute | solution.py:33
  115.2 1.3 collective-permute-done.30
  116.5 1.5 collective-permute-done.31
  118.3 3.1 %collective-permute-start.26 = (bf16[32,1536]{1,0:T(8,128)(2,1)S(1)}, bf16[32,1536]{1,0:T(8,128)(2,1)S(1)}, u32[]{:S(2)}, u32[]{:S(2)}) collective-permute-start(bf16[32,1536]{1,0:T(8,128)(2,1)S(1)} %get-tuple-element.108), channel_id=1, source_target_pairs={{0,64},{8,72},{16,80},{24,88},{32,96},{40,104},{48,112},{56,120},{... | collective-permute-start | bytes 294920 | tf_op jit(solution)/shard_map/ppermute | solution.py:25
  121.4 0.8 collective-permute-start.27
  122.2 0.7 collective-permute-start.32
  123.0 2.2 %collective-permute-start.33 = (bf16[32,1536]{1,0:T(8,128)(2,1)S(1)}, bf16[32,1536]{1,0:T(8,128)(2,1)S(1)}, u32[]{:S(2)}, u32[]{:S(2)}) collective-permute-start(bf16[32,1536]{1,0:T(8,128)(2,1)S(1)} %get-tuple-element.105), channel_id=1, source_target_pairs={{0,24},{8,16},{16,8},{24,0},{32,56},{40,48},{48,40},{56,32},{64,88... | collective-permute-start | bytes 294920 | tf_op jit(solution)/shard_map/ppermute | solution.py:29
  125.4 3.1 %collective-permute-start.44 = (bf16[64,1536]{1,0:T(8,128)(2,1)S(1)}, bf16[64,1536]{1,0:T(8,128)(2,1)S(1)}, u32[]{:S(2)}, u32[]{:S(2)}) collective-permute-start(bf16[64,1536]{1,0:T(8,128)(2,1)S(1)} %constant_dynamic-update-slice_fusion.11.refs_2_), channel_id=1, source_target_pairs={{0,64},{8,72},{16,80},{24,88},{32,96},{40,104},{48,112},{56,120},{... | collective-permute-start | bytes 589832 | tf_op jit(solution)/shard_map/ppermute | solution.py:25
  128.5 0.9 collective-permute-start.45
  129.4 1.8 %collective-permute-start.41 = (bf16[128,1536]{1,0:T(8,128)(2,1)S(1)}, bf16[128,1536]{1,0:T(8,128)(2,1)S(1)}, u32[]{:S(2)}, u32[]{:S(2)}) collective-permute-start(bf16[128,1536]{1,0:T(8,128)(2,1)S(1)} %constant_dynamic-update-slice_fusion.2.refs_0_), channel_id=1, source_target_pairs={{0,16},{8,24},{16,0},{24,8},{32,48},{40,56},{48,32},{56,40},{64,80... | collective-permute-start | bytes 1179656 | tf_op jit(solution)/shard_map/ppermute | solution.py:29
  131.4 1.5 collective-permute-start.29
  132.9 2.0 %collective-permute-done.44.refs_4_ = bf16[64,1536]{1,0:T(8,128)(2,1)S(1)} collective-permute-done((bf16[64,1536]{1,0:T(8,128)(2,1)S(1)}, bf16[64,1536]{1,0:T(8,128)(2,1)S(1)}, u32[]{:S(2)}, u32[]{:S(2)}) %collective-permute-start.44) | collective-permute-done | bytes 196640 | tf_op jit(solution)/shard_map/ppermute | solution.py:25
  134.8 0.9 collective-permute-done.45.refs_5_
  135.7 1.2 collective-permute-start.35
  136.9 1.5 collective-permute-done.41.refs_1_
  138.4 1.9 %collective-permute-start.36 = (bf16[64,1536]{1,0:T(8,128)(2,1)S(1)}, bf16[64,1536]{1,0:T(8,128)(2,1)S(1)}, u32[]{:S(2)}, u32[]{:S(2)}) collective-permute-start(bf16[64,1536]{1,0:T(8,128)(2,1)S(1)} %constant_dynamic-update-slice_fusion.9.refs_2_), channel_id=1, source_target_pairs={{0,96},{8,104},{16,112},{24,120},{32,64},{40,72},{48,80},{56,88},{... | collective-permute-start | bytes 589832 | tf_op jit(solution)/shard_map/ppermute | solution.py:25
  140.3 4.1 %mix.3 = (bf16[256,1152]{1,0:T(8,128)(2,1)S(1)}, bf16[256,1152]{1,0:T(8,128)(2,1)S(1)}) custom-call(s32[4]{0:T(128)S(1)} %pad_add_fusion.place, bf16[128,1536]{1,0:T(8,128)(2,1)S(1)} %constant_dynamic-update-slice_fusion.2.refs_0_, bf16[128,1536]{1,0:T(8,128)(2,1)S(1)} %collective-permute-done.41.refs_1_, ...), custom_call_target="tpu_custom_call" | custom-call | tf_op jit(solution)/shard_map/mix/pallas_call | solution.py:339
  144.4 8.3 %collective-permute-start.46 = (bf16[256,1152]{1,0:T(8,128)(2,1)S(1)}, bf16[256,1152]{1,0:T(8,128)(2,1)S(1)}, u32[]{:S(2)}, u32[]{:S(2)}) collective-permute-start(bf16[256,1152]{1,0:T(8,128)(2,1)S(1)} %get-tuple-element.94), channel_id=1, source_target_pairs={{0,1},{1,0},{2,3},{3,2},{4,5},{5,4},{6,7},{7,6},{8,9},{9,8},{10,11... | collective-permute-start | bytes 1769480 | tf_op jit(solution)/shard_map/ppermute | solution.py:37
  152.7 4.1 %mix.2 = (bf16[256,1152]{1,0:T(8,128)(2,1)S(1)}, bf16[256,1152]{1,0:T(8,128)(2,1)S(1)}) custom-call(s32[4]{0:T(128)S(1)} %pad_add_fusion.place, bf16[128,1536]{1,0:T(8,128)(2,1)S(1)} %collective-permute-done.28.refs_0_, bf16[128,1536]{1,0:T(8,128)(2,1)S(1)} %collective-permute-done.29.refs_1_, ...), custom_call_target="tpu_custom_call" | custom-call | tf_op jit(solution)/shard_map/mix/pallas_call | solution.py:339
  158.2 2.9 %collective-permute-start.48 = (bf16[64,1152]{1,0:T(8,128)(2,1)S(1)}, bf16[64,1152]{1,0:T(8,128)(2,1)S(1)}, u32[]{:S(2)}, u32[]{:S(2)}) collective-permute-start(bf16[64,1152]{1,0:T(8,128)(2,1)S(1)} %get-tuple-element.97), channel_id=1, source_target_pairs={{0,4},{1,5},{2,6},{3,7},{4,0},{5,1},{6,2},{7,3},{8,12},{9,13},{10,... | collective-permute-start | bytes 442376 | tf_op jit(solution)/shard_map/ppermute | solution.py:33
  161.7 3.5 %collective-permute-start.39 = (bf16[64,1152]{1,0:T(8,128)(2,1)S(1)}, bf16[64,1152]{1,0:T(8,128)(2,1)S(1)}, u32[]{:S(2)}, u32[]{:S(2)}) collective-permute-start(bf16[64,1152]{1,0:T(8,128)(2,1)S(1)} %get-tuple-element.91), channel_id=1, source_target_pairs={{0,4},{1,5},{2,6},{3,7},{4,0},{5,1},{6,2},{7,3},{8,12},{9,13},{10,... | collective-permute-start | bytes 442376 | tf_op jit(solution)/shard_map/ppermute | solution.py:33
  165.6 2.7 %collective-permute-done.48 = bf16[64,1152]{1,0:T(8,128)(2,1)S(1)} collective-permute-done((bf16[64,1152]{1,0:T(8,128)(2,1)S(1)}, bf16[64,1152]{1,0:T(8,128)(2,1)S(1)}, u32[]{:S(2)}, u32[]{:S(2)}) %collective-permute-start.48) | collective-permute-done | bytes 147488 | tf_op jit(solution)/shard_map/ppermute | solution.py:33
  168.3 2.5 %collective-permute-done.49 = bf16[64,1152]{1,0:T(8,128)(2,1)S(1)} collective-permute-done((bf16[64,1152]{1,0:T(8,128)(2,1)S(1)}, bf16[64,1152]{1,0:T(8,128)(2,1)S(1)}, u32[]{:S(2)}, u32[]{:S(2)}) %collective-permute-start.49) | collective-permute-done | bytes 147488 | tf_op jit(solution)/shard_map/ppermute | solution.py:33
  170.8 3.9 %collective-permute-done.39 = bf16[64,1152]{1,0:T(8,128)(2,1)S(1)} collective-permute-done((bf16[64,1152]{1,0:T(8,128)(2,1)S(1)}, bf16[64,1152]{1,0:T(8,128)(2,1)S(1)}, u32[]{:S(2)}, u32[]{:S(2)}) %collective-permute-start.39) | collective-permute-done | bytes 147488 | tf_op jit(solution)/shard_map/ppermute | solution.py:33
  174.7 2.4 %collective-permute-done.40 = bf16[64,1152]{1,0:T(8,128)(2,1)S(1)} collective-permute-done((bf16[64,1152]{1,0:T(8,128)(2,1)S(1)}, bf16[64,1152]{1,0:T(8,128)(2,1)S(1)}, u32[]{:S(2)}, u32[]{:S(2)}) %collective-permute-start.40) | collective-permute-done | bytes 147488 | tf_op jit(solution)/shard_map/ppermute | solution.py:33
  177.3 0.7 pad_maximum_fusion
  (86 shorter events, 8.1 us)
Async XLA Ops:
  1.1 28.7 %collective-permute-start = (bf16[128,1152]{1,0:T(8,128)(2,1)}, bf16[128,1152]{1,0:T(8,128)(2,1)S(1)}, u32[]{:S(2)}, u32[]{:S(2)}) collective-permute-start(bf16[128,1152]{1,0:T(8,128)(2,1)} %refs_0_), channel_id=1, source_target_pairs={{0,2},{1,3},{2,0},{3,1},{4,6},{5,7},{6,4},{7,5},{8,10},{9,11},{10,... | collective-permute-start | bytes 884744 | tf_op jit(solution)/shard_map/ppermute | solution.py:33
  3.3 26.6 %collective-permute-start.1 = (bf16[128,1152]{1,0:T(8,128)(2,1)}, bf16[128,1152]{1,0:T(8,128)(2,1)S(1)}, u32[]{:S(2)}, u32[]{:S(2)}) collective-permute-start(bf16[128,1152]{1,0:T(8,128)(2,1)} %refs_0_), channel_id=1, source_target_pairs={{0,4},{1,5},{2,6},{3,7},{4,0},{5,1},{6,2},{7,3},{8,12},{9,13},{10,... | collective-permute-start | bytes 884744 | tf_op jit(solution)/shard_map/ppermute | solution.py:33
  5.7 24.1 %collective-permute-start.2 = (bf16[128,1152]{1,0:T(8,128)(2,1)}, bf16[128,1152]{1,0:T(8,128)(2,1)S(1)}, u32[]{:S(2)}, u32[]{:S(2)}) collective-permute-start(bf16[128,1152]{1,0:T(8,128)(2,1)} %refs_0_), channel_id=1, source_target_pairs={{0,6},{1,7},{2,4},{3,5},{4,2},{5,3},{6,0},{7,1},{8,14},{9,15},{10,... | collective-permute-start | bytes 884744 | tf_op jit(solution)/shard_map/ppermute | solution.py:33
  6.5 23.3 %all-to-all-start = ((f32[128,1,256]{2,1,0:T(1,128)}), f32[128,1,256]{2,1,0:T(1,128)S(1)}, u32[]{:S(2)}, u32[]{:S(2)}) async-start(f32[128,1,256]{2,1,0:T(1,128)} %all_to_all.8), calls=%async_computation | async-start | bytes 262144 | tf_op jit(solution)/shard_map/all_to_all | solution.py:392
  17.9 14.9 %collective-permute-start.3 = (bf16[128,1152]{1,0:T(8,128)(2,1)}, bf16[128,1152]{1,0:T(8,128)(2,1)S(1)}, u32[]{:S(2)}, u32[]{:S(2)}) collective-permute-start(bf16[128,1152]{1,0:T(8,128)(2,1)} %refs_0_), channel_id=1, source_target_pairs={{0,1},{1,0},{2,3},{3,2},{4,5},{5,4},{6,7},{7,6},{8,9},{9,8},{10,11... | collective-permute-start | bytes 884744 | tf_op jit(solution)/shard_map/ppermute | solution.py:37
  29.8 2.9 %collective-permute-start.4 = (bf16[128,1152]{1,0:T(8,128)(2,1)S(1)}, bf16[128,1152]{1,0:T(8,128)(2,1)S(1)}, u32[]{:S(2)}, u32[]{:S(2)}) collective-permute-start(bf16[128,1152]{1,0:T(8,128)(2,1)S(1)} %collective-permute-done.refs_2_), channel_id=1, source_target_pairs={{0,1},{1,0},{2,3},{3,2},{4,5},{5,4},{6,7},{7,6},{8,9},{9,8},{10,11... | collective-permute-start | bytes 884744 | tf_op jit(solution)/shard_map/ppermute | solution.py:37
  30.4 2.4 %collective-permute-start.5 = (bf16[128,1152]{1,0:T(8,128)(2,1)S(1)}, bf16[128,1152]{1,0:T(8,128)(2,1)S(1)}, u32[]{:S(2)}, u32[]{:S(2)}) collective-permute-start(bf16[128,1152]{1,0:T(8,128)(2,1)S(1)} %collective-permute-done.1.refs_4_), channel_id=1, source_target_pairs={{0,1},{1,0},{2,3},{3,2},{4,5},{5,4},{6,7},{7,6},{8,9},{9,8},{10,11... | collective-permute-start | bytes 884744 | tf_op jit(solution)/shard_map/ppermute | solution.py:37
  30.4 2.3 %collective-permute-start.6 = (bf16[128,1152]{1,0:T(8,128)(2,1)S(1)}, bf16[128,1152]{1,0:T(8,128)(2,1)S(1)}, u32[]{:S(2)}, u32[]{:S(2)}) collective-permute-start(bf16[128,1152]{1,0:T(8,128)(2,1)S(1)} %collective-permute-done.2.refs_6_), channel_id=1, source_target_pairs={{0,1},{1,0},{2,3},{3,2},{4,5},{5,4},{6,7},{7,6},{8,9},{9,8},{10,11... | collective-permute-start | bytes 884744 | tf_op jit(solution)/shard_map/ppermute | solution.py:37
  32.8 2.0 %copy-start = (bf16[1152,1536]{1,0:T(8,128)(2,1)S(1)}, bf16[1152,1536]{1,0:T(8,128)(2,1)}, u32[]{:S(2)}) copy-start(bf16[1152,1536]{1,0:T(8,128)(2,1)} %w_query.1) | copy-start | bytes 10616836
  34.8 1.0 copy-start.4
  43.4 40.1 %copy-start.5 = (s32[4]{0:T(128)S(1)}, s32[4]{0:T(128)}, u32[]{:S(2)}) copy-start(s32[4]{0:T(128)} %lengths.1) | copy-start | bytes 52
  49.3 12.7 %collective-permute-start.12 = (bf16[128,1600]{1,0:T(8,128)(2,1)S(1)}, bf16[128,1600]{1,0:T(8,128)(2,1)S(1)}, u32[]{:S(2)}, u32[]{:S(2)}) collective-permute-start(bf16[128,1600]{1,0:T(8,128)(2,1)S(1)} %get-tuple-element.66), channel_id=1, source_target_pairs={{0,24},{8,16},{16,8},{24,0},{32,56},{40,48},{48,40},{56,32},{64,88... | collective-permute-start | bytes 1228808 | tf_op jit(solution)/shard_map/ppermute | solution.py:29
  49.6 13.4 %collective-permute-start.9 = (bf16[128,1600]{1,0:T(8,128)(2,1)S(1)}, bf16[128,1600]{1,0:T(8,128)(2,1)S(1)}, u32[]{:S(2)}, u32[]{:S(2)}) collective-permute-start(bf16[128,1600]{1,0:T(8,128)(2,1)S(1)} %get-tuple-element.62), channel_id=1, source_target_pairs={{0,96},{8,104},{16,112},{24,120},{32,64},{40,72},{48,80},{56,88},{... | collective-permute-start | bytes 1228808 | tf_op jit(solution)/shard_map/ppermute | solution.py:25
  50.4 12.6 %collective-permute-start.10 = (bf16[128,1600]{1,0:T(8,128)(2,1)S(1)}, bf16[128,1600]{1,0:T(8,128)(2,1)S(1)}, u32[]{:S(2)}, u32[]{:S(2)}) collective-permute-start(bf16[128,1600]{1,0:T(8,128)(2,1)S(1)} %get-tuple-element.64), channel_id=1, source_target_pairs={{0,8},{8,0},{16,24},{24,16},{32,40},{40,32},{48,56},{56,48},{64,72... | collective-permute-start | bytes 1228808 | tf_op jit(solution)/shard_map/ppermute | solution.py:29
  51.1 21.3 %collective-permute-start.11 = (bf16[128,1600]{1,0:T(8,128)(2,1)S(1)}, bf16[128,1600]{1,0:T(8,128)(2,1)S(1)}, u32[]{:S(2)}, u32[]{:S(2)}) collective-permute-start(bf16[128,1600]{1,0:T(8,128)(2,1)S(1)} %get-tuple-element.65), channel_id=1, source_target_pairs={{0,16},{8,24},{16,0},{24,8},{32,48},{40,56},{48,32},{56,40},{64,80... | collective-permute-start | bytes 1228808 | tf_op jit(solution)/shard_map/ppermute | solution.py:29
  54.0 18.4 %collective-permute-start.7 = (bf16[128,1600]{1,0:T(8,128)(2,1)S(1)}, bf16[128,1600]{1,0:T(8,128)(2,1)S(1)}, u32[]{:S(2)}, u32[]{:S(2)}) collective-permute-start(bf16[128,1600]{1,0:T(8,128)(2,1)S(1)} %get-tuple-element.60), channel_id=1, source_target_pairs={{0,32},{8,40},{16,48},{24,56},{32,0},{40,8},{48,16},{56,24},{64,96... | collective-permute-start | bytes 1228808 | tf_op jit(solution)/shard_map/ppermute | solution.py:25
  61.9 13.4 %collective-permute-start.8 = (bf16[128,1600]{1,0:T(8,128)(2,1)S(1)}, bf16[128,1600]{1,0:T(8,128)(2,1)S(1)}, u32[]{:S(2)}, u32[]{:S(2)}) collective-permute-start(bf16[128,1600]{1,0:T(8,128)(2,1)S(1)} %get-tuple-element.61), channel_id=1, source_target_pairs={{0,64},{8,72},{16,80},{24,88},{32,96},{40,104},{48,112},{56,120},{... | collective-permute-start | bytes 1228808 | tf_op jit(solution)/shard_map/ppermute | solution.py:25
  75.8 5.9 %collective-permute-start.13 = (bf16[32,1600]{1,0:T(8,128)(2,1)S(1)}, bf16[32,1600]{1,0:T(8,128)(2,1)S(1)}, u32[]{:S(2)}, u32[]{:S(2)}) collective-permute-start(bf16[32,1600]{1,0:T(8,128)(2,1)S(1)} %get-tuple-element.68), channel_id=1, source_target_pairs={{0,8},{8,0},{16,24},{24,16},{32,40},{40,32},{48,56},{56,48},{64,72... | collective-permute-start | bytes 307208 | tf_op jit(solution)/shard_map/ppermute | solution.py:29
  75.9 7.9 %collective-permute-start.14 = (bf16[32,1600]{1,0:T(8,128)(2,1)S(1)}, bf16[32,1600]{1,0:T(8,128)(2,1)S(1)}, u32[]{:S(2)}, u32[]{:S(2)}) collective-permute-start(bf16[32,1600]{1,0:T(8,128)(2,1)S(1)} %get-tuple-element.69), channel_id=1, source_target_pairs={{0,16},{8,24},{16,0},{24,8},{32,48},{40,56},{48,32},{56,40},{64,80... | collective-permute-start | bytes 307208 | tf_op jit(solution)/shard_map/ppermute | solution.py:29
  77.2 6.5 %collective-permute-start.15 = (bf16[32,1600]{1,0:T(8,128)(2,1)S(1)}, bf16[32,1600]{1,0:T(8,128)(2,1)S(1)}, u32[]{:S(2)}, u32[]{:S(2)}) collective-permute-start(bf16[32,1600]{1,0:T(8,128)(2,1)S(1)} %get-tuple-element.70), channel_id=1, source_target_pairs={{0,24},{8,16},{16,8},{24,0},{32,56},{40,48},{48,40},{56,32},{64,88... | collective-permute-start | bytes 307208 | tf_op jit(solution)/shard_map/ppermute | solution.py:29
  79.7 4.0 %collective-permute-start.16 = (bf16[32,1600]{1,0:T(8,128)(2,1)S(1)}, bf16[32,1600]{1,0:T(8,128)(2,1)S(1)}, u32[]{:S(2)}, u32[]{:S(2)}) collective-permute-start(bf16[32,1600]{1,0:T(8,128)(2,1)S(1)} %get-tuple-element.72), channel_id=1, source_target_pairs={{0,32},{8,40},{16,48},{24,56},{32,0},{40,8},{48,16},{56,24},{64,96... | collective-permute-start | bytes 307208 | tf_op jit(solution)/shard_map/ppermute | solution.py:25
  79.7 5.2 %collective-permute-start.17 = (bf16[32,1600]{1,0:T(8,128)(2,1)S(1)}, bf16[32,1600]{1,0:T(8,128)(2,1)S(1)}, u32[]{:S(2)}, u32[]{:S(2)}) collective-permute-start(bf16[32,1600]{1,0:T(8,128)(2,1)S(1)} %get-tuple-element.73), channel_id=1, source_target_pairs={{0,64},{8,72},{16,80},{24,88},{32,96},{40,104},{48,112},{56,120},{... | collective-permute-start | bytes 307208 | tf_op jit(solution)/shard_map/ppermute | solution.py:25
  81.7 4.8 %collective-permute-start.18 = (bf16[32,1600]{1,0:T(8,128)(2,1)S(1)}, bf16[32,1600]{1,0:T(8,128)(2,1)S(1)}, u32[]{:S(2)}, u32[]{:S(2)}) collective-permute-start(bf16[32,1600]{1,0:T(8,128)(2,1)S(1)} %get-tuple-element.74), channel_id=1, source_target_pairs={{0,96},{8,104},{16,112},{24,120},{32,64},{40,72},{48,80},{56,88},{... | collective-permute-start | bytes 307208 | tf_op jit(solution)/shard_map/ppermute | solution.py:25
  87.1 5.2 %collective-permute-start.19 = (bf16[32,1600]{1,0:T(8,128)(2,1)S(1)}, bf16[32,1600]{1,0:T(8,128)(2,1)S(1)}, u32[]{:S(2)}, u32[]{:S(2)}) collective-permute-start(bf16[32,1600]{1,0:T(8,128)(2,1)S(1)} %get-tuple-element.76), channel_id=1, source_target_pairs={{0,1},{1,0},{2,3},{3,2},{4,5},{5,4},{6,7},{7,6},{8,9},{9,8},{10,11... | collective-permute-start | bytes 307208 | tf_op jit(solution)/shard_map/ppermute | solution.py:37
  92.9 4.1 %collective-permute-start.20 = (bf16[16,1600]{1,0:T(8,128)(2,1)S(1)}, bf16[16,1600]{1,0:T(8,128)(2,1)S(1)}, u32[]{:S(2)}, u32[]{:S(2)}) collective-permute-start(bf16[16,1600]{1,0:T(8,128)(2,1)S(1)} %get-tuple-element.78), channel_id=1, source_target_pairs={{0,2},{1,3},{2,0},{3,1},{4,6},{5,7},{6,4},{7,5},{8,10},{9,11},{10,... | collective-permute-start | bytes 153608 | tf_op jit(solution)/shard_map/ppermute | solution.py:33
  93.0 4.6 %collective-permute-start.21 = (bf16[16,1600]{1,0:T(8,128)(2,1)S(1)}, bf16[16,1600]{1,0:T(8,128)(2,1)S(1)}, u32[]{:S(2)}, u32[]{:S(2)}) collective-permute-start(bf16[16,1600]{1,0:T(8,128)(2,1)S(1)} %get-tuple-element.79), channel_id=1, source_target_pairs={{0,4},{1,5},{2,6},{3,7},{4,0},{5,1},{6,2},{7,3},{8,12},{9,13},{10,... | collective-permute-start | bytes 153608 | tf_op jit(solution)/shard_map/ppermute | solution.py:33
  94.4 4.6 %collective-permute-start.22 = (bf16[16,1600]{1,0:T(8,128)(2,1)S(1)}, bf16[16,1600]{1,0:T(8,128)(2,1)S(1)}, u32[]{:S(2)}, u32[]{:S(2)}) collective-permute-start(bf16[16,1600]{1,0:T(8,128)(2,1)S(1)} %get-tuple-element.80), channel_id=1, source_target_pairs={{0,6},{1,7},{2,4},{3,5},{4,2},{5,3},{6,0},{7,1},{8,14},{9,15},{10,... | collective-permute-start | bytes 153608 | tf_op jit(solution)/shard_map/ppermute | solution.py:33
  99.0 2.2 %copy-start.2 = (bf16[4,2048,256]{2,1,0:T(8,128)(2,1)S(1)}, bf16[4,2048,256]{2,1,0:T(8,128)(2,1)}, u32[]{:S(2)}) copy-start(bf16[4,2048,256]{2,1,0:T(8,128)(2,1)} %refs_6_.3) | copy-start | bytes 12582916
  101.2 2.2 %copy-start.3 = (bf16[4,2048,256]{2,1,0:T(8,128)(2,1)S(1)}, bf16[4,2048,256]{2,1,0:T(8,128)(2,1)}, u32[]{:S(2)}) copy-start(bf16[4,2048,256]{2,1,0:T(8,128)(2,1)} %refs_7_.1) | copy-start | bytes 12582916
  103.4 36.9 %copy-start.1 = (bf16[1536,1152]{1,0:T(8,128)(2,1)S(1)}, bf16[1536,1152]{1,0:T(8,128)(2,1)}, u32[]{:S(2)}) copy-start(bf16[1536,1152]{1,0:T(8,128)(2,1)} %refs_6_.5) | copy-start | bytes 10616836
  108.7 2.7 %collective-permute-start.23 = (bf16[32,1536]{1,0:T(8,128)(2,1)S(1)}, bf16[32,1536]{1,0:T(8,128)(2,1)S(1)}, u32[]{:S(2)}, u32[]{:S(2)}) collective-permute-start(bf16[32,1536]{1,0:T(8,128)(2,1)S(1)} %get-tuple-element.82), channel_id=1, source_target_pairs={{0,1},{1,0},{2,3},{3,2},{4,5},{5,4},{6,7},{7,6},{8,9},{9,8},{10,11... | collective-permute-start | bytes 294920 | tf_op jit(solution)/shard_map/ppermute | solution.py:37
  111.9 4.5 %collective-permute-start.30 = (bf16[16,1536]{1,0:T(8,128)(2,1)S(1)}, bf16[16,1536]{1,0:T(8,128)(2,1)S(1)}, u32[]{:S(2)}, u32[]{:S(2)}) collective-permute-start(bf16[16,1536]{1,0:T(8,128)(2,1)S(1)} %get-tuple-element.85), channel_id=1, source_target_pairs={{0,4},{1,5},{2,6},{3,7},{4,0},{5,1},{6,2},{7,3},{8,12},{9,13},{10,... | collective-permute-start | bytes 147464 | tf_op jit(solution)/shard_map/ppermute | solution.py:33
  112.7 5.3 %collective-permute-start.31 = (bf16[16,1536]{1,0:T(8,128)(2,1)S(1)}, bf16[16,1536]{1,0:T(8,128)(2,1)S(1)}, u32[]{:S(2)}, u32[]{:S(2)}) collective-permute-start(bf16[16,1536]{1,0:T(8,128)(2,1)S(1)} %get-tuple-element.86), channel_id=1, source_target_pairs={{0,6},{1,7},{2,4},{3,5},{4,2},{5,3},{6,0},{7,1},{8,14},{9,15},{10,... | collective-permute-start | bytes 147464 | tf_op jit(solution)/shard_map/ppermute | solution.py:33
  114.6 3.6 %collective-permute-start.24 = (bf16[16,1536]{1,0:T(8,128)(2,1)S(1)}, bf16[16,1536]{1,0:T(8,128)(2,1)S(1)}, u32[]{:S(2)}, u32[]{:S(2)}) collective-permute-start(bf16[16,1536]{1,0:T(8,128)(2,1)S(1)} %get-tuple-element.84), channel_id=1, source_target_pairs={{0,2},{1,3},{2,0},{3,1},{4,6},{5,7},{6,4},{7,5},{8,10},{9,11},{10,... | collective-permute-start | bytes 147464 | tf_op jit(solution)/shard_map/ppermute | solution.py:33
  118.0 5.1 %collective-permute-start.42 = (bf16[32,1536]{1,0:T(8,128)(2,1)S(1)}, bf16[32,1536]{1,0:T(8,128)(2,1)S(1)}, u32[]{:S(2)}, u32[]{:S(2)}) collective-permute-start(bf16[32,1536]{1,0:T(8,128)(2,1)S(1)} %get-tuple-element.105), channel_id=1, source_target_pairs={{0,16},{8,24},{16,0},{24,8},{32,48},{40,56},{48,32},{56,40},{64,80... | collective-permute-start | bytes 294920 | tf_op jit(solution)/shard_map/ppermute | solution.py:29
  118.2 7.1 %collective-permute-start.25 = (bf16[32,1536]{1,0:T(8,128)(2,1)S(1)}, bf16[32,1536]{1,0:T(8,128)(2,1)S(1)}, u32[]{:S(2)}, u32[]{:S(2)}) collective-permute-start(bf16[32,1536]{1,0:T(8,128)(2,1)S(1)} %get-tuple-element.108), channel_id=1, source_target_pairs={{0,32},{8,40},{16,48},{24,56},{32,0},{40,8},{48,16},{56,24},{64,96... | collective-permute-start | bytes 294920 | tf_op jit(solution)/shard_map/ppermute | solution.py:25
  118.3 7.1 %collective-permute-start.26 = (bf16[32,1536]{1,0:T(8,128)(2,1)S(1)}, bf16[32,1536]{1,0:T(8,128)(2,1)S(1)}, u32[]{:S(2)}, u32[]{:S(2)}) collective-permute-start(bf16[32,1536]{1,0:T(8,128)(2,1)S(1)} %get-tuple-element.108), channel_id=1, source_target_pairs={{0,64},{8,72},{16,80},{24,88},{32,96},{40,104},{48,112},{56,120},{... | collective-permute-start | bytes 294920 | tf_op jit(solution)/shard_map/ppermute | solution.py:25
  121.4 7.2 %collective-permute-start.27 = (bf16[32,1536]{1,0:T(8,128)(2,1)S(1)}, bf16[32,1536]{1,0:T(8,128)(2,1)S(1)}, u32[]{:S(2)}, u32[]{:S(2)}) collective-permute-start(bf16[32,1536]{1,0:T(8,128)(2,1)S(1)} %get-tuple-element.108), channel_id=1, source_target_pairs={{0,96},{8,104},{16,112},{24,120},{32,64},{40,72},{48,80},{56,88},{... | collective-permute-start | bytes 294920 | tf_op jit(solution)/shard_map/ppermute | solution.py:25
  122.2 7.3 %collective-permute-start.32 = (bf16[32,1536]{1,0:T(8,128)(2,1)S(1)}, bf16[32,1536]{1,0:T(8,128)(2,1)S(1)}, u32[]{:S(2)}, u32[]{:S(2)}) collective-permute-start(bf16[32,1536]{1,0:T(8,128)(2,1)S(1)} %get-tuple-element.105), channel_id=1, source_target_pairs={{0,8},{8,0},{16,24},{24,16},{32,40},{40,32},{48,56},{56,48},{64,72... | collective-permute-start | bytes 294920 | tf_op jit(solution)/shard_map/ppermute | solution.py:29
  123.0 8.2 %collective-permute-start.33 = (bf16[32,1536]{1,0:T(8,128)(2,1)S(1)}, bf16[32,1536]{1,0:T(8,128)(2,1)S(1)}, u32[]{:S(2)}, u32[]{:S(2)}) collective-permute-start(bf16[32,1536]{1,0:T(8,128)(2,1)S(1)} %get-tuple-element.105), channel_id=1, source_target_pairs={{0,24},{8,16},{16,8},{24,0},{32,56},{40,48},{48,40},{56,32},{64,88... | collective-permute-start | bytes 294920 | tf_op jit(solution)/shard_map/ppermute | solution.py:29
  125.3 6.1 %collective-permute-start.43 = (bf16[64,1536]{1,0:T(8,128)(2,1)S(1)}, bf16[64,1536]{1,0:T(8,128)(2,1)S(1)}, u32[]{:S(2)}, u32[]{:S(2)}) collective-permute-start(bf16[64,1536]{1,0:T(8,128)(2,1)S(1)} %constant_dynamic-update-slice_fusion.11.refs_2_), channel_id=1, source_target_pairs={{0,32},{8,40},{16,48},{24,56},{32,0},{40,8},{48,16},{56,24},{64,96... | collective-permute-start | bytes 589832 | tf_op jit(solution)/shard_map/ppermute | solution.py:25
  125.4 9.4 %collective-permute-start.44 = (bf16[64,1536]{1,0:T(8,128)(2,1)S(1)}, bf16[64,1536]{1,0:T(8,128)(2,1)S(1)}, u32[]{:S(2)}, u32[]{:S(2)}) collective-permute-start(bf16[64,1536]{1,0:T(8,128)(2,1)S(1)} %constant_dynamic-update-slice_fusion.11.refs_2_), channel_id=1, source_target_pairs={{0,64},{8,72},{16,80},{24,88},{32,96},{40,104},{48,112},{56,120},{... | collective-permute-start | bytes 589832 | tf_op jit(solution)/shard_map/ppermute | solution.py:25
  128.5 7.2 %collective-permute-start.45 = (bf16[64,1536]{1,0:T(8,128)(2,1)S(1)}, bf16[64,1536]{1,0:T(8,128)(2,1)S(1)}, u32[]{:S(2)}, u32[]{:S(2)}) collective-permute-start(bf16[64,1536]{1,0:T(8,128)(2,1)S(1)} %constant_dynamic-update-slice_fusion.11.refs_2_), channel_id=1, source_target_pairs={{0,96},{8,104},{16,112},{24,120},{32,64},{40,72},{48,80},{56,88},{... | collective-permute-start | bytes 589832 | tf_op jit(solution)/shard_map/ppermute | solution.py:25
  129.4 9.0 %collective-permute-start.41 = (bf16[128,1536]{1,0:T(8,128)(2,1)S(1)}, bf16[128,1536]{1,0:T(8,128)(2,1)S(1)}, u32[]{:S(2)}, u32[]{:S(2)}) collective-permute-start(bf16[128,1536]{1,0:T(8,128)(2,1)S(1)} %constant_dynamic-update-slice_fusion.2.refs_0_), channel_id=1, source_target_pairs={{0,16},{8,24},{16,0},{24,8},{32,48},{40,56},{48,32},{56,40},{64,80... | collective-permute-start | bytes 1179656 | tf_op jit(solution)/shard_map/ppermute | solution.py:29
  131.3 21.5 %collective-permute-start.28 = (bf16[128,1536]{1,0:T(8,128)(2,1)S(1)}, bf16[128,1536]{1,0:T(8,128)(2,1)S(1)}, u32[]{:S(2)}, u32[]{:S(2)}) collective-permute-start(bf16[128,1536]{1,0:T(8,128)(2,1)S(1)} %constant_dynamic-update-slice_fusion.2.refs_0_), channel_id=1, source_target_pairs={{0,8},{8,0},{16,24},{24,16},{32,40},{40,32},{48,56},{56,48},{64,72... | collective-permute-start | bytes 1179656 | tf_op jit(solution)/shard_map/ppermute | solution.py:29
  131.4 21.4 %collective-permute-start.29 = (bf16[128,1536]{1,0:T(8,128)(2,1)S(1)}, bf16[128,1536]{1,0:T(8,128)(2,1)S(1)}, u32[]{:S(2)}, u32[]{:S(2)}) collective-permute-start(bf16[128,1536]{1,0:T(8,128)(2,1)S(1)} %constant_dynamic-update-slice_fusion.2.refs_0_), channel_id=1, source_target_pairs={{0,24},{8,16},{16,8},{24,0},{32,56},{40,48},{48,40},{56,32},{64,88... | collective-permute-start | bytes 1179656 | tf_op jit(solution)/shard_map/ppermute | solution.py:29
  134.8 9.6 %collective-permute-start.34 = (bf16[64,1536]{1,0:T(8,128)(2,1)S(1)}, bf16[64,1536]{1,0:T(8,128)(2,1)S(1)}, u32[]{:S(2)}, u32[]{:S(2)}) collective-permute-start(bf16[64,1536]{1,0:T(8,128)(2,1)S(1)} %constant_dynamic-update-slice_fusion.9.refs_2_), channel_id=1, source_target_pairs={{0,32},{8,40},{16,48},{24,56},{32,0},{40,8},{48,16},{56,24},{64,96... | collective-permute-start | bytes 589832 | tf_op jit(solution)/shard_map/ppermute | solution.py:25
  135.7 17.0 %collective-permute-start.35 = (bf16[64,1536]{1,0:T(8,128)(2,1)S(1)}, bf16[64,1536]{1,0:T(8,128)(2,1)S(1)}, u32[]{:S(2)}, u32[]{:S(2)}) collective-permute-start(bf16[64,1536]{1,0:T(8,128)(2,1)S(1)} %constant_dynamic-update-slice_fusion.9.refs_2_), channel_id=1, source_target_pairs={{0,64},{8,72},{16,80},{24,88},{32,96},{40,104},{48,112},{56,120},{... | collective-permute-start | bytes 589832 | tf_op jit(solution)/shard_map/ppermute | solution.py:25
  138.4 14.3 %collective-permute-start.36 = (bf16[64,1536]{1,0:T(8,128)(2,1)S(1)}, bf16[64,1536]{1,0:T(8,128)(2,1)S(1)}, u32[]{:S(2)}, u32[]{:S(2)}) collective-permute-start(bf16[64,1536]{1,0:T(8,128)(2,1)S(1)} %constant_dynamic-update-slice_fusion.9.refs_2_), channel_id=1, source_target_pairs={{0,96},{8,104},{16,112},{24,120},{32,64},{40,72},{48,80},{56,88},{... | collective-permute-start | bytes 589832 | tf_op jit(solution)/shard_map/ppermute | solution.py:25
  144.4 13.0 %collective-permute-start.46 = (bf16[256,1152]{1,0:T(8,128)(2,1)S(1)}, bf16[256,1152]{1,0:T(8,128)(2,1)S(1)}, u32[]{:S(2)}, u32[]{:S(2)}) collective-permute-start(bf16[256,1152]{1,0:T(8,128)(2,1)S(1)} %get-tuple-element.94), channel_id=1, source_target_pairs={{0,1},{1,0},{2,3},{3,2},{4,5},{5,4},{6,7},{7,6},{8,9},{9,8},{10,11... | collective-permute-start | bytes 1769480 | tf_op jit(solution)/shard_map/ppermute | solution.py:37
  156.8 4.7 %collective-permute-start.37 = (bf16[256,1152]{1,0:T(8,128)(2,1)S(1)}, bf16[256,1152]{1,0:T(8,128)(2,1)S(1)}, u32[]{:S(2)}, u32[]{:S(2)}) collective-permute-start(bf16[256,1152]{1,0:T(8,128)(2,1)S(1)} %get-tuple-element.88), channel_id=1, source_target_pairs={{0,1},{1,0},{2,3},{3,2},{4,5},{5,4},{6,7},{7,6},{8,9},{9,8},{10,11... | collective-permute-start | bytes 1769480 | tf_op jit(solution)/shard_map/ppermute | solution.py:37
  157.5 7.6 %collective-permute-start.47 = (bf16[64,1152]{1,0:T(8,128)(2,1)S(1)}, bf16[64,1152]{1,0:T(8,128)(2,1)S(1)}, u32[]{:S(2)}, u32[]{:S(2)}) collective-permute-start(bf16[64,1152]{1,0:T(8,128)(2,1)S(1)} %get-tuple-element.96), channel_id=1, source_target_pairs={{0,2},{1,3},{2,0},{3,1},{4,6},{5,7},{6,4},{7,5},{8,10},{9,11},{10,... | collective-permute-start | bytes 442376 | tf_op jit(solution)/shard_map/ppermute | solution.py:33
  158.2 10.1 %collective-permute-start.48 = (bf16[64,1152]{1,0:T(8,128)(2,1)S(1)}, bf16[64,1152]{1,0:T(8,128)(2,1)S(1)}, u32[]{:S(2)}, u32[]{:S(2)}) collective-permute-start(bf16[64,1152]{1,0:T(8,128)(2,1)S(1)} %get-tuple-element.97), channel_id=1, source_target_pairs={{0,4},{1,5},{2,6},{3,7},{4,0},{5,1},{6,2},{7,3},{8,12},{9,13},{10,... | collective-permute-start | bytes 442376 | tf_op jit(solution)/shard_map/ppermute | solution.py:33
  161.1 9.7 %collective-permute-start.49 = (bf16[64,1152]{1,0:T(8,128)(2,1)S(1)}, bf16[64,1152]{1,0:T(8,128)(2,1)S(1)}, u32[]{:S(2)}, u32[]{:S(2)}) collective-permute-start(bf16[64,1152]{1,0:T(8,128)(2,1)S(1)} %get-tuple-element.98), channel_id=1, source_target_pairs={{0,6},{1,7},{2,4},{3,5},{4,2},{5,3},{6,0},{7,1},{8,14},{9,15},{10,... | collective-permute-start | bytes 442376 | tf_op jit(solution)/shard_map/ppermute | solution.py:33
  161.6 9.1 %collective-permute-start.38 = (bf16[64,1152]{1,0:T(8,128)(2,1)S(1)}, bf16[64,1152]{1,0:T(8,128)(2,1)S(1)}, u32[]{:S(2)}, u32[]{:S(2)}) collective-permute-start(bf16[64,1152]{1,0:T(8,128)(2,1)S(1)} %get-tuple-element.90), channel_id=1, source_target_pairs={{0,2},{1,3},{2,0},{3,1},{4,6},{5,7},{6,4},{7,5},{8,10},{9,11},{10,... | collective-permute-start | bytes 442376 | tf_op jit(solution)/shard_map/ppermute | solution.py:33
  161.7 12.9 %collective-permute-start.39 = (bf16[64,1152]{1,0:T(8,128)(2,1)S(1)}, bf16[64,1152]{1,0:T(8,128)(2,1)S(1)}, u32[]{:S(2)}, u32[]{:S(2)}) collective-permute-start(bf16[64,1152]{1,0:T(8,128)(2,1)S(1)} %get-tuple-element.91), channel_id=1, source_target_pairs={{0,4},{1,5},{2,6},{3,7},{4,0},{5,1},{6,2},{7,3},{8,12},{9,13},{10,... | collective-permute-start | bytes 442376 | tf_op jit(solution)/shard_map/ppermute | solution.py:33
  165.2 11.9 %collective-permute-start.40 = (bf16[64,1152]{1,0:T(8,128)(2,1)S(1)}, bf16[64,1152]{1,0:T(8,128)(2,1)S(1)}, u32[]{:S(2)}, u32[]{:S(2)}) collective-permute-start(bf16[64,1152]{1,0:T(8,128)(2,1)S(1)} %get-tuple-element.92), channel_id=1, source_target_pairs={{0,6},{1,7},{2,4},{3,5},{4,2},{5,3},{6,0},{7,1},{8,14},{9,15},{10,... | collective-permute-start | bytes 442376 | tf_op jit(solution)/shard_map/ppermute | solution.py:33

commit v3 on v2

--- a/solution.py
+++ b/solution.py
@@ -12,13 +12,17 @@
 STEPS = 2
 VMEM = pl.BlockSpec(memory_space=pltpu.VMEM)
 SMEM = pl.BlockSpec(memory_space=pltpu.SMEM)
-ANY = pl.BlockSpec(memory_space=pl.ANY)
+HBM = pl.BlockSpec(memory_space=pltpu.HBM)
 F32 = jnp.float32
 BF16 = jnp.bfloat16
 
 
 def params(mib):
     return pltpu.CompilerParams(vmem_limit_bytes=mib * 1024 * 1024)
+
+
+def cost(flops, size):
+    return pl.CostEstimate(flops=int(flops), bytes_accessed=int(size), transcendentals=0)
 
 
 def along_y(value, m):
@@ -48,22 +52,27 @@
 
 
 def multiply(left, w_pair, tiles, loads, outs):
-    width = tiles.shape[0] * 256
+    wide = tiles.shape[2]
+    width = tiles.shape[0] * wide
 
     def put(part, at, size):
         for k, out in enumerate(outs):
             out[:, at : at + size] = part[k * 128 : k * 128 + 128]
 
-    pair = jnp.dot(left, w_pair[...], preferred_element_type=F32).astype(BF16)
-    put(pair, width, w_pair.shape[1])
+    dims = (((1,), (1,)), ((), ()))
+    pair = lax.dot_general(left, w_pair[...], dims, preferred_element_type=F32).astype(BF16)
+    put(pair, width, w_pair.shape[0])
     for t in range(tiles.shape[0]):
         loads[t].wait()
-        put(jnp.dot(left, tiles[t], preferred_element_type=F32).astype(BF16), t * 256, 256)
+        put(jnp.dot(left, tiles[t], preferred_element_type=F32).astype(BF16), t * wide, wide)
 
 
 def project_kernel(place, stats, gain, *refs):
-    pieces, (w_query, w_pair), outs, rest = refs[:8], refs[8:10], refs[10:14], refs[14]
-    normed, mean_of, scale_of, tiles, sems = refs[15:]
+    pieces, (w_query, w_pair), outs, rest = list(refs[:8]), refs[8:10], refs[10:14], refs[14]
+    normed, own, mean_of, scale_of, tiles, sems, own_sem = refs[15:]
+    own_load = pltpu.make_async_copy(pieces[0], own, own_sem)
+    own_load.start()
+    pieces[0] = own
     loads = load_tiles(w_query, tiles, sems)
     y, z, x, c = place[0], place[1], place[2], place[3]
     total = stats[0:8, :]
@@ -77,6 +86,7 @@
         mean_of[s] = mean_columns[:, s : s + 1]
         scale_of[s] = scale_columns[:, s : s + 1]
     gains = gain[...].astype(F32)
+    own_load.wait()
     for m in range(4):
         for j in range(2):
             source_c = c ^ j
@@ -99,20 +109,23 @@
 
 def project(place, stats, gain, pieces, w_query, w_pair):
     depth, width = w_query.shape
-    out = jax.ShapeDtypeStruct((128, width + w_pair.shape[1]), BF16)
+    out = jax.ShapeDtypeStruct((128, width + w_pair.shape[0]), BF16)
     return pl.pallas_call(
         project_kernel,
         out_shape=[out] * 4 + [jax.ShapeDtypeStruct((512, depth), BF16)],
-        in_specs=[SMEM] + [VMEM] * 10 + [ANY, VMEM],
+        in_specs=[SMEM] + [VMEM] * 2 + [HBM] + [VMEM] * 7 + [HBM, VMEM],
         out_specs=[VMEM] * 5,
         scratch_shapes=[
             pltpu.VMEM((2, 4, 4, 32, depth), BF16),
+            pltpu.VMEM((128, depth), BF16),
             pltpu.VMEM((8, 128, 1), F32),
             pltpu.VMEM((8, 128, 1), F32),
-            pltpu.VMEM((width // 256, depth, 256), BF16),
-            pltpu.SemaphoreType.DMA((width // 256,)),
+            pltpu.VMEM((width // 512, depth, 512), BF16),
+            pltpu.SemaphoreType.DMA((width // 512,)),
+            pltpu.SemaphoreType.DMA,
         ],
-        compiler_params=params(28),
+        compiler_params=params(50),
+        cost_estimate=cost(6e9, 1.2e7),
         name="project",
     )(place, stats, gain, *pieces, w_query, w_pair)
 
@@ -124,43 +137,60 @@
 
 def project_rest(left, w_query, w_pair):
     depth, width = w_query.shape
-    out = jax.ShapeDtypeStruct((128, width + w_pair.shape[1]), BF16)
+    out = jax.ShapeDtypeStruct((128, width + w_pair.shape[0]), BF16)
     return pl.pallas_call(
         project_rest_kernel,
         out_shape=[out] * 4,
-        in_specs=[VMEM, ANY, VMEM],
+        in_specs=[VMEM, HBM, VMEM],
         out_specs=[VMEM] * 4,
         scratch_shapes=[
-            pltpu.VMEM((width // 256, depth, 256), BF16),
-            pltpu.SemaphoreType.DMA((width // 256,)),
+            pltpu.VMEM((width // 512, depth, 512), BF16),
+            pltpu.SemaphoreType.DMA((width // 512,)),
         ],
-        compiler_params=params(20),
+        compiler_params=params(50),
+        cost_estimate=cost(6e9, 9e6),
         name="project_rest",
     )(left, w_query, w_pair)
 
 
-def add_kernel(pieces, *refs):
-    groups = len(refs) // (2 * pieces)
-    ins, outs = refs[: groups * pieces], refs[groups * pieces :]
-    for g in range(groups):
-        total = ins[g * pieces][...].astype(F32)
-        for k in range(1, pieces):
-            total = total + ins[g * pieces + k][...].astype(F32)
-        total = total.astype(BF16)
-        rows = total.shape[0] // pieces
-        for k in range(pieces):
-            outs[g * pieces + k][...] = total[k * rows : k * rows + rows]
-
-
-def add_and_cut(values, pieces):
+def add_kernel(*refs):
+    for g in range(2):
+        first, second, third = refs[g * 3 : g * 3 + 3]
+        total = first[...].astype(F32) + second[...].astype(F32)
+        refs[6 + g][...] = total + third[...].astype(F32)
+
+
+def add_three(values):
+    out = jax.ShapeDtypeStruct(values[0].shape, F32)
+    return pl.pallas_call(
+        add_kernel,
+        out_shape=[out] * 2,
+        in_specs=[VMEM] * 6,
+        out_specs=[VMEM] * 2,
+        compiler_params=params(16),
+        cost_estimate=cost(1e9, 4e6),
+        name="add_three",
+    )(*values)
+
+
+def add_and_cut_kernel(*refs):
+    for g in range(2):
+        total = (refs[g][...] + refs[2 + g][...].astype(F32)).astype(BF16)
+        rows = total.shape[0] // 4
+        for k in range(4):
+            refs[4 + g * 4 + k][...] = total[k * rows : k * rows + rows]
+
+
+def add_and_cut(values):
     rows, width = values[0].shape
-    out = jax.ShapeDtypeStruct((rows // pieces, width), BF16)
-    return pl.pallas_call(
-        functools.partial(add_kernel, pieces),
-        out_shape=[out] * len(values),
-        in_specs=[VMEM] * len(values),
-        out_specs=[VMEM] * len(values),
+    out = jax.ShapeDtypeStruct((rows // 4, width), BF16)
+    return pl.pallas_call(
+        add_and_cut_kernel,
+        out_shape=[out] * 8,
+        in_specs=[VMEM] * 4,
+        out_specs=[VMEM] * 8,
         compiler_params=params(16),
+        cost_estimate=cost(1e8, 3e6),
         name="add_and_cut",
     )(*values)
 
@@ -188,6 +218,7 @@
         out_specs=[VMEM] * 2,
         scratch_shapes=[pltpu.VMEM((2, 4, 8, shape[1]), F32)],
         compiler_params=params(8),
+        cost_estimate=cost(1e8, 1e6),
         name="finish",
     )(place, *values)
 
@@ -210,6 +241,7 @@
         in_specs=[SMEM] + [VMEM] * 2,
         out_specs=[VMEM] * 4,
         compiler_params=params(8),
+        cost_estimate=cost(1e8, 4e5),
         name="pair",
     )(place, mine, theirs)
 
@@ -306,7 +338,8 @@
                 pltpu.VMEM((2, 8 * count, 128), F32),
             ],
         ),
-        compiler_params=params(20),
+        compiler_params=params(52),
+        cost_estimate=cost(6e9, 1.8e7),
         name="attend",
     )(lengths, place, *packed, cosine, sine, cache_keys, cache_values)
 
@@ -339,7 +372,7 @@
     return pl.pallas_call(
         mix_kernel,
         out_shape=[jax.ShapeDtypeStruct((256, width), BF16)] * 2,
-        in_specs=[SMEM] + [VMEM] * 6 + [ANY],
+        in_specs=[SMEM] + [VMEM] * 6 + [HBM],
         out_specs=[VMEM] * 2,
         scratch_shapes=[
             pltpu.VMEM((2, 4, 4, 16, depth), BF16),
@@ -347,6 +380,7 @@
             pltpu.SemaphoreType.DMA((3,)),
         ],
         compiler_params=params(20),
+        cost_estimate=cost(4e9, 8e6),
         name="mix",
     )(place, *first, *second, w_out)
 
@@ -365,6 +399,7 @@
         in_specs=[VMEM] * 2,
         out_specs=[VMEM] * 4,
         compiler_params=params(8),
+        cost_estimate=cost(1e8, 1e6),
         name="pair_add",
     )(mine, theirs)
 
@@ -395,11 +430,12 @@
     for piece in arrived:
         pieces += [piece, other_core(piece)]
 
-    *sent, rest = project(place, stats, norm_gain[None], pieces, w_query, w_keyvalue)
-    kept = project_rest(rest, w_query, w_keyvalue)
+    w_pair = w_keyvalue.T
+    *sent, rest = project(place, stats, norm_gain[None], pieces, w_query, w_pair)
+    kept = project_rest(rest, w_query, w_pair)
     by_y = exchanged(along_y, [kept[0], sent[0], sent[1], kept[1]])
     by_z = exchanged(along_z, [kept[2], sent[2], sent[3], kept[3]])
-    parts = add_and_cut(by_y + by_z, 4)
+    parts = add_and_cut([*add_three(by_y[:3] + by_z[:3]), by_y[3], by_z[3]])
     parts = exchanged(along_z, parts[:4]) + exchanged(along_y, parts[4:])
     mine, theirs = finish(place, parts)
     packed = exchanged(along_x, pair(False, place, mine, other_core(theirs)))
@@ -415,15 +451,26 @@
     returned = exchanged(along_x, pair(True, place, mine, other_core(theirs)))
     first = jnp.concatenate(returned[:2], axis=0)
     second = jnp.concatenate(returned[2:], axis=0)
-    first = jnp.concatenate(exchanged(along_y, [first] * 4), axis=0)
-    second = exchanged(along_z, [second] * 4)
-
-    halves = []
-    for k in range(2):
-        left = [first if k == 0 else along_z(first, 1), along_z(first, 2 + k)]
-        right = jnp.concatenate([second[k], second[k + 2]], axis=0)
-        mine, theirs = mix(place, left, exchanged(along_y, [right] * 4), w_out)
-        halves.append(sum_of(exchanged(along_x, pair_add(mine, other_core(theirs)))))
+    first, second = exchanged(along_y, [first] * 4), exchanged(along_z, [second] * 4)
+    first, second = lax.optimization_barrier((first, second))
+    first = jnp.concatenate(first, axis=0)
+
+    lefts = [first, along_z(first, 2)], [along_z(first, 1), along_z(first, 3)]
+    rights = [
+        exchanged(along_y, [jnp.concatenate([second[k], second[k + 2]], axis=0)] * 4)
+        for k in range(2)
+    ]
+    lefts[0][1], lefts[1][0] = lax.optimization_barrier((lefts[0][1], lefts[1][0]))
+    mine, theirs = mix(place, lefts[0], rights[0], w_out)
+    theirs = other_core(theirs)
+    mine, rights[1][1:], lefts[1][1] = lax.optimization_barrier(
+        (mine, rights[1][1:], lefts[1][1])
+    )
+    half = sum_of(exchanged(along_x, pair_add(mine, theirs)))
+    mine, theirs = mix(place, lefts[1], rights[1], w_out)
+    theirs = other_core(theirs)
+    mine, half = lax.optimization_barrier((mine, half))
+    halves = [half, sum_of(exchanged(along_x, pair_add(mine, theirs)))]
     odd = place[1] % 2 == 1
     return jnp.concatenate(
         [jnp.where(odd, halves[1], halves[0]), jnp.where(odd, halves[0], halves[1])], axis=0

time: 178 us -> 189 us (1.062)
  waiting for transfers between devices: 56.5 us -> 75.1 us
  local copies, waits for them, and re-layouts: 10.1 us -> 4.77 us
    ppermute x15, waiting for transfers between devices: 8.51 us -> 32 us  [along_y(): return lax.ppermute(value, 'gx', [(g, g ^ 4 * m) for g in range(16)])]
    unnamed x20 -> x18, local copies, waits for them, and re-layouts: 8.52 us -> 3.21 us
    ppermute x12, waiting for transfers between devices: 19 us -> 14.5 us  [along_z(): return lax.ppermute(value, 'gx', [(g, g ^ m) for g in range(16)])]
    ppermute x8, starting transfers between devices: 17.1 us -> 13 us  [other_core(): return lax.ppermute(value, 'gy', [(g, g ^ 1) for g in range(8)])]
    ppermute x15, starting transfers between devices: 16.8 us -> 19.6 us  [along_y(): return lax.ppermute(value, 'gx', [(g, g ^ 4 * m) for g in range(16)])]
    pallas_call x1, Pallas kernels: 5.3 us -> 7.65 us  [attend(): pl.pallas_call(attend_kernel, out_shape=[jax.ShapeDtypeStruct((32, width)...]
    pallas_call x1, Pallas kernels: 7.68 us -> 5.71 us  [project(): pl.pallas_call(project_kernel, out_shape=[out] * 4 + [jax.ShapeDtypeStruc...]
  transfers between devices with their start and end apart: 51 -> 51, of which waited for: 21 -> 27; matrix products, arithmetic and copies ran while one was open for 1% -> 1% of each run, Pallas kernels for 5% -> 7%
where the time goes in v3:
time: 189 us; the launch traced here: 188 us
  starting transfers between devices  77.6 us (41%)
  waiting for transfers between devices  75.1 us (40%)
  Pallas kernels  28.2 us (15%)
  local copies, waits for them, and re-layouts  4.77 us (3%)
  other arithmetic  2.33 us (1%)
    ppermute x15, waiting for transfers between devices, along_y(): return lax.ppermute(value, 'gx', [(g, g ^ 4 * m) for g in range(16)])  32 us
    ppermute x15, starting transfers between devices, along_x(): return lax.ppermute(value, 'gy', [(g, g ^ 2 * m) for g in range(8)])  19.6 us
    ppermute x15, starting transfers between devices, along_y(): return lax.ppermute(value, 'gx', [(g, g ^ 4 * m) for g in range(16)])  19.6 us
    ppermute x15, waiting for transfers between devices, along_x(): return lax.ppermute(value, 'gy', [(g, g ^ 2 * m) for g in range(8)])  14.6 us
    ppermute x12, waiting for transfers between devices, along_z(): return lax.ppermute(value, 'gx', [(g, g ^ m) for g in range(16)])  14.5 us
    ppermute x12, starting transfers between devices, along_z(): return lax.ppermute(value, 'gx', [(g, g ^ m) for g in range(16)])  14 us
    ppermute x8, starting transfers between devices, other_core(): return lax.ppermute(value, 'gy', [(g, g ^ 1) for g in range(8)])  13 us
    all_to_all x1, starting transfers between devices, per_device(): stats = lax.all_to_all(stats, ('gx', 'gy'), 0, 0, tiled=True)  11.4 us
  transfers between devices with their start and end apart: 51, of which 27 were waited for; matrix products, arithmetic and copies ran while one was open for 1% of the time, Pallas kernels for 7%

profile of v3, /device:TPU:1, one launch (start us, length us, event | category | flops | bytes accessed | tf_op | source)
XLA Modules:
  0.0 188.3 jit_solution(6442165206912867725)
XLA Ops:
  0.0 1.1 convert_reduce_fusion
  1.1 2.1 %collective-permute-start = (bf16[128,1152]{1,0:T(8,128)(2,1)}, bf16[128,1152]{1,0:T(8,128)(2,1)S(1)}, u32[]{:S(2)}, u32[]{:S(2)}) collective-permute-start(bf16[128,1152]{1,0:T(8,128)(2,1)} %refs_0_), channel_id=1, source_target_pairs={{0,2},{1,3},{2,0},{3,1},{4,6},{5,7},{6,4},{7,5},{8,10},{9,11},{10,... | collective-permute-start | bytes 884744 | tf_op jit(solution)/shard_map/ppermute | solution.py:37
  3.3 2.5 %collective-permute-start.1 = (bf16[128,1152]{1,0:T(8,128)(2,1)}, bf16[128,1152]{1,0:T(8,128)(2,1)S(1)}, u32[]{:S(2)}, u32[]{:S(2)}) collective-permute-start(bf16[128,1152]{1,0:T(8,128)(2,1)} %refs_0_), channel_id=1, source_target_pairs={{0,4},{1,5},{2,6},{3,7},{4,0},{5,1},{6,2},{7,3},{8,12},{9,13},{10,... | collective-permute-start | bytes 884744 | tf_op jit(solution)/shard_map/ppermute | solution.py:37
  5.8 0.7 all_to_all.8
  6.5 11.4 %all-to-all-start = ((f32[128,1,256]{2,1,0:T(1,128)}), f32[128,1,256]{2,1,0:T(1,128)S(1)}, u32[]{:S(2)}, u32[]{:S(2)}) async-start(f32[128,1,256]{2,1,0:T(1,128)} %all_to_all.8), calls=%async_computation | async-start | bytes 262144 | tf_op jit(solution)/shard_map/all_to_all | solution.py:427
  17.9 1.1 collective-permute-start.3
  19.1 10.7 %all-to-all-done = f32[128,1,256]{2,1,0:T(1,128)S(1)} async-done(((f32[128,1,256]{2,1,0:T(1,128)}), f32[128,1,256]{2,1,0:T(1,128)S(1)}, u32[]{:S(2)}, u32[]{:S(2)}) %all-to-all-start) | async-done | bytes 131104 | tf_op jit(solution)/shard_map/all_to_all | solution.py:427
  32.4 1.0 copy-done
  33.4 0.9 copy-done.3
  34.3 5.7 %project.1 = (bf16[128,1600]{1,0:T(8,128)(2,1)S(1)}, bf16[128,1600]{1,0:T(8,128)(2,1)S(1)}, bf16[128,1600]{1,0:T(8,128)(2,1)S(1)}, bf16[128,1600]{1,0:T(8,128)(2,1)}, bf16[512,1152]{1,0:T(8,128)(2,1)}) custom-call(s32[4]{0:T(128)S(1)} %pad_add_fusion.place, f32[128,256]{1,0:T(8,128)S(1)} %bitcast.8, bf16[1,1152]{1,0:T(2,128)(2,1)S(1)} %broadcast_in_dim.5.gain, ...), custom_call_target="tpu_custom_call" | custom-call | flops 6000000000 | bytes 12000000 | tf_op jit(solution)/shard_map/project/pallas_call | solution.py:113
  40.0 1.3 collective-permute-start.10
  41.7 1.6 collective-permute-start.8
  43.2 1.3 copy-done.4
  44.5 4.2 %project_rest.1 = (bf16[128,1600]{1,0:T(8,128)(2,1)S(1)}, bf16[128,1600]{1,0:T(8,128)(2,1)S(1)}, bf16[128,1600]{1,0:T(8,128)(2,1)S(1)}, bf16[128,1600]{1,0:T(8,128)(2,1)S(1)}) custom-call(bf16[512,1152]{1,0:T(8,128)(2,1)S(1)} %copy-done.4, bf16[1152,1536]{1,0:T(8,128)(2,1)} %w_query.1, bf16[64,1152]{1,0:T(8,128)(2,1)S(1)} %bitcast.10), custom_call_target="tpu_custom_call" | custom-call | flops 6000000000 | bytes 9000000 | tf_op jit(solution)/shard_map/project_rest/pallas_call | solution.py:141
  48.7 2.0 %collective-permute-start.11 = (bf16[128,1600]{1,0:T(8,128)(2,1)S(1)}, bf16[128,1600]{1,0:T(8,128)(2,1)S(1)}, u32[]{:S(2)}, u32[]{:S(2)}) collective-permute-start(bf16[128,1600]{1,0:T(8,128)(2,1)S(1)} %get-tuple-element.86), channel_id=1, source_target_pairs={{0,96},{8,104},{16,112},{24,120},{32,64},{40,72},{48,80},{56,88},{... | collective-permute-start | bytes 1228808 | tf_op jit(solution)/shard_map/ppermute | solution.py:29
  50.7 2.1 %collective-permute-done.10.refs_5_ = bf16[128,1600]{1,0:T(8,128)(2,1)S(1)} collective-permute-done((bf16[128,1600]{1,0:T(8,128)(2,1)}, bf16[128,1600]{1,0:T(8,128)(2,1)S(1)}, u32[]{:S(2)}, u32[]{:S(2)}) %collective-permute-start.10) | collective-permute-done | bytes 409632 | tf_op jit(solution)/shard_map/ppermute | solution.py:33
  53.1 8.6 %collective-permute-done.8.refs_2_ = bf16[128,1600]{1,0:T(8,128)(2,1)S(1)} collective-permute-done((bf16[128,1600]{1,0:T(8,128)(2,1)S(1)}, bf16[128,1600]{1,0:T(8,128)(2,1)S(1)}, u32[]{:S(2)}, u32[]{:S(2)}) %collective-permute-start.8) | collective-permute-done | bytes 409632 | tf_op jit(solution)/shard_map/ppermute | solution.py:29
  61.9 8.0 %collective-permute-done.11.refs_2_ = bf16[128,1600]{1,0:T(8,128)(2,1)S(1)} collective-permute-done((bf16[128,1600]{1,0:T(8,128)(2,1)S(1)}, bf16[128,1600]{1,0:T(8,128)(2,1)S(1)}, u32[]{:S(2)}, u32[]{:S(2)}) %collective-permute-start.11) | collective-permute-done | bytes 409632 | tf_op jit(solution)/shard_map/ppermute | solution.py:29
  70.1 1.3 collective-permute-start.13
  71.4 1.8 collective-permute-start.14
  73.2 0.8 collective-permute-start.15
  74.0 3.1 %collective-permute-start.17 = (bf16[32,1600]{1,0:T(8,128)(2,1)S(1)}, bf16[32,1600]{1,0:T(8,128)(2,1)S(1)}, u32[]{:S(2)}, u32[]{:S(2)}) collective-permute-start(bf16[32,1600]{1,0:T(8,128)(2,1)S(1)} %get-tuple-element.94), channel_id=1, source_target_pairs={{0,64},{8,72},{16,80},{24,88},{32,96},{40,104},{48,112},{56,120},{... | collective-permute-start | bytes 307208 | tf_op jit(solution)/shard_map/ppermute | solution.py:29
  77.1 0.8 collective-permute-start.18
  78.1 1.1 collective-permute-done.15.refs_3_
  79.2 1.2 collective-permute-done.17.refs_6_
  80.3 1.8 collective-permute-done.18.refs_7_
  82.9 3.6 %collective-permute-start.19 = (bf16[32,1600]{1,0:T(8,128)(2,1)S(1)}, bf16[32,1600]{1,0:T(8,128)(2,1)S(1)}, u32[]{:S(2)}, u32[]{:S(2)}) collective-permute-start(bf16[32,1600]{1,0:T(8,128)(2,1)S(1)} %get-tuple-element.97), channel_id=1, source_target_pairs={{0,1},{1,0},{2,3},{3,2},{4,5},{5,4},{6,7},{7,6},{8,9},{9,8},{10,11... | collective-permute-start | bytes 307208 | tf_op jit(solution)/shard_map/ppermute | solution.py:41
  86.5 0.9 collective-permute-done.19.theirs
  88.1 1.4 collective-permute-start.21
  89.5 2.5 %collective-permute-start.22 = (bf16[16,1600]{1,0:T(8,128)(2,1)S(1)}, bf16[16,1600]{1,0:T(8,128)(2,1)S(1)}, u32[]{:S(2)}, u32[]{:S(2)}) collective-permute-start(bf16[16,1600]{1,0:T(8,128)(2,1)S(1)} %get-tuple-element.101), channel_id=1, source_target_pairs={{0,6},{1,7},{2,4},{3,5},{4,2},{5,3},{6,0},{7,1},{8,14},{9,15},{10,... | collective-permute-start | bytes 153608 | tf_op jit(solution)/shard_map/ppermute | solution.py:37
  92.1 0.8 collective-permute-done.21.refs_2_
  92.9 1.4 collective-permute-done.22.refs_3_
  94.2 7.7 %attend.1 = (bf16[32,1536]{1,0:T(8,128)(2,1)S(1)}, bf16[32,1536]{1,0:T(8,128)(2,1)S(1)}) custom-call(s32[4]{0:T(128)S(1)} %copy-done.1, s32[4]{0:T(128)S(1)} %pad_add_fusion.place, bf16[16,1600]{1,0:T(8,128)(2,1)S(1)} %get-tuple-element.98.refs_0_, bf16[16,1600]{1,0:T(8,128)(2,1)S(1)} %collective-permute-done.20.refs_1_, ...), custom_call_target="tpu_custom_call" | custom-call | flops 6000000000 | bytes 18000000 | tf_op jit(solution)/shard_map/attend/pallas_call | solution.py:326
  101.9 1.6 collective-permute-start.23
  103.5 0.9 collective-permute-done.23.theirs
  105.7 2.0 %collective-permute-start.29 = (bf16[16,1536]{1,0:T(8,128)(2,1)S(1)}, bf16[16,1536]{1,0:T(8,128)(2,1)S(1)}, u32[]{:S(2)}, u32[]{:S(2)}) collective-permute-start(bf16[16,1536]{1,0:T(8,128)(2,1)S(1)} %get-tuple-element.107), channel_id=1, source_target_pairs={{0,6},{1,7},{2,4},{3,5},{4,2},{5,3},{6,0},{7,1},{8,14},{9,15},{10,... | collective-permute-start | bytes 147464 | tf_op jit(solution)/shard_map/ppermute | solution.py:37
  108.2 1.3 collective-permute-done.28
  109.6 1.5 collective-permute-done.29
  111.0 3.2 %collective-permute-start.31 = (bf16[32,1536]{1,0:T(8,128)(2,1)S(1)}, bf16[32,1536]{1,0:T(8,128)(2,1)S(1)}, u32[]{:S(2)}, u32[]{:S(2)}) collective-permute-start(bf16[32,1536]{1,0:T(8,128)(2,1)S(1)} %constant_dynamic-update-slice_fusion.2), channel_id=1, source_target_pairs={{0,16},{8,24},{16,0},{24,8},{32,48},{40,56},{48,32},{56,40},{64,80... | collective-permute-start | bytes 294920 | tf_op jit(solution)/shard_map/ppermute | solution.py:33
  115.0 1.9 %collective-permute-start.26 = (bf16[32,1536]{1,0:T(8,128)(2,1)S(1)}, bf16[32,1536]{1,0:T(8,128)(2,1)S(1)}, u32[]{:S(2)}, u32[]{:S(2)}) collective-permute-start(bf16[32,1536]{1,0:T(8,128)(2,1)S(1)} %constant_dynamic-update-slice_fusion), channel_id=1, source_target_pairs={{0,64},{8,72},{16,80},{24,88},{32,96},{40,104},{48,112},{56,120},{... | collective-permute-start | bytes 294920 | tf_op jit(solution)/shard_map/ppermute | solution.py:29
  116.9 1.9 %collective-permute-start.27 = (bf16[32,1536]{1,0:T(8,128)(2,1)S(1)}, bf16[32,1536]{1,0:T(8,128)(2,1)S(1)}, u32[]{:S(2)}, u32[]{:S(2)}) collective-permute-start(bf16[32,1536]{1,0:T(8,128)(2,1)S(1)} %constant_dynamic-update-slice_fusion), channel_id=1, source_target_pairs={{0,96},{8,104},{16,112},{24,120},{32,64},{40,72},{48,80},{56,88},{... | collective-permute-start | bytes 294920 | tf_op jit(solution)/shard_map/ppermute | solution.py:29
  118.8 1.9 collective-permute-done.32
  120.7 1.9 %collective-permute-done.27 = bf16[32,1536]{1,0:T(8,128)(2,1)S(1)} collective-permute-done((bf16[32,1536]{1,0:T(8,128)(2,1)S(1)}, bf16[32,1536]{1,0:T(8,128)(2,1)S(1)}, u32[]{:S(2)}, u32[]{:S(2)}) %collective-permute-start.27) | collective-permute-done | bytes 98336 | tf_op jit(solution)/shard_map/ppermute | solution.py:29
  123.4 2.0 %collective-permute-start.34 = (bf16[128,1536]{1,0:T(8,128)(2,1)S(1)}, bf16[128,1536]{1,0:T(8,128)(2,1)S(1)}, u32[]{:S(2)}, u32[]{:S(2)}) collective-permute-start(bf16[128,1536]{1,0:T(8,128)(2,1)S(1)} %constant_dynamic-update-slice_fusion.4.refs_0_), channel_id=1, source_target_pairs={{0,8},{8,0},{16,24},{24,16},{32,40},{40,32},{48,56},{56,48},{64,72... | collective-permute-start | bytes 1179656 | tf_op jit(solution)/shard_map/ppermute | solution.py:33
  125.5 3.1 %collective-permute-start.36 = (bf16[64,1536]{1,0:T(8,128)(2,1)S(1)}, bf16[64,1536]{1,0:T(8,128)(2,1)S(1)}, u32[]{:S(2)}, u32[]{:S(2)}) collective-permute-start(bf16[64,1536]{1,0:T(8,128)(2,1)S(1)} %constant_dynamic-update-slice_fusion.8.refs_2_), channel_id=1, source_target_pairs={{0,64},{8,72},{16,80},{24,88},{32,96},{40,104},{48,112},{56,120},{... | collective-permute-start | bytes 589832 | tf_op jit(solution)/shard_map/ppermute | solution.py:29
  128.5 0.8 collective-permute-start.37
  129.3 3.3 %collective-permute-done.33.refs_1_ = bf16[128,1536]{1,0:T(8,128)(2,1)S(1)} collective-permute-done((bf16[128,1536]{1,0:T(8,128)(2,1)S(1)}, bf16[128,1536]{1,0:T(8,128)(2,1)S(1)}, u32[]{:S(2)}, u32[]{:S(2)}) %collective-permute-start.33) | collective-permute-done | bytes 393248 | tf_op jit(solution)/shard_map/ppermute | solution.py:33
  132.6 2.0 %collective-permute-start.41 = (bf16[128,1536]{1,0:T(8,128)(2,1)S(1)}, bf16[128,1536]{1,0:T(8,128)(2,1)S(1)}, u32[]{:S(2)}, u32[]{:S(2)}) collective-permute-start(bf16[128,1536]{1,0:T(8,128)(2,1)S(1)} %constant_dynamic-update-slice_fusion.4.refs_0_), channel_id=1, source_target_pairs={{0,24},{8,16},{16,8},{24,0},{32,56},{40,48},{48,40},{56,32},{64,88... | collective-permute-start | bytes 1179656 | tf_op jit(solution)/shard_map/ppermute | solution.py:33
  134.6 6.0 %collective-permute-done.34.refs_0_ = bf16[128,1536]{1,0:T(8,128)(2,1)S(1)} collective-permute-done((bf16[128,1536]{1,0:T(8,128)(2,1)S(1)}, bf16[128,1536]{1,0:T(8,128)(2,1)S(1)}, u32[]{:S(2)}, u32[]{:S(2)}) %collective-permute-start.34) | collective-permute-done | bytes 393248 | tf_op jit(solution)/shard_map/ppermute | solution.py:33
  140.7 4.1 %mix.2 = (bf16[256,1152]{1,0:T(8,128)(2,1)S(1)}, bf16[256,1152]{1,0:T(8,128)(2,1)S(1)}) custom-call(s32[4]{0:T(128)S(1)} %pad_add_fusion.place, bf16[128,1536]{1,0:T(8,128)(2,1)S(1)} %constant_dynamic-update-slice_fusion.4.refs_0_, bf16[128,1536]{1,0:T(8,128)(2,1)S(1)} %collective-permute-done.33.refs_1_, ...), custom_call_target="tpu_custom_call" | custom-call | flops 4000000000 | bytes 8000000 | tf_op jit(solution)/shard_map/mix/pallas_call | solution.py:372
  144.8 3.3 %collective-permute-start.42 = (bf16[256,1152]{1,0:T(8,128)(2,1)S(1)}, bf16[256,1152]{1,0:T(8,128)(2,1)S(1)}, u32[]{:S(2)}, u32[]{:S(2)}) collective-permute-start(bf16[256,1152]{1,0:T(8,128)(2,1)S(1)} %get-tuple-element.125), channel_id=1, source_target_pairs={{0,1},{1,0},{2,3},{3,2},{4,5},{5,4},{6,7},{7,6},{8,9},{9,8},{10,11... | collective-permute-start | bytes 1769480 | tf_op jit(solution)/shard_map/ppermute | solution.py:41
  148.2 3.1 %collective-permute-start.39 = (bf16[64,1536]{1,0:T(8,128)(2,1)S(1)}, bf16[64,1536]{1,0:T(8,128)(2,1)S(1)}, u32[]{:S(2)}, u32[]{:S(2)}) collective-permute-start(bf16[64,1536]{1,0:T(8,128)(2,1)S(1)} %constant_dynamic-update-slice_fusion.10.refs_2_), channel_id=1, source_target_pairs={{0,64},{8,72},{16,80},{24,88},{32,96},{40,104},{48,112},{56,120},{... | collective-permute-start | bytes 589832 | tf_op jit(solution)/shard_map/ppermute | solution.py:29
  151.2 0.8 collective-permute-start.40
  152.0 2.7 %collective-permute-done.38.refs_3_ = bf16[64,1536]{1,0:T(8,128)(2,1)S(1)} collective-permute-done((bf16[64,1536]{1,0:T(8,128)(2,1)S(1)}, bf16[64,1536]{1,0:T(8,128)(2,1)S(1)}, u32[]{:S(2)}, u32[]{:S(2)}) %collective-permute-start.38) | collective-permute-done | bytes 196640 | tf_op jit(solution)/shard_map/ppermute | solution.py:29
  154.6 5.9 %collective-permute-done.39.refs_4_ = bf16[64,1536]{1,0:T(8,128)(2,1)S(1)} collective-permute-done((bf16[64,1536]{1,0:T(8,128)(2,1)S(1)}, bf16[64,1536]{1,0:T(8,128)(2,1)S(1)}, u32[]{:S(2)}, u32[]{:S(2)}) %collective-permute-start.39) | collective-permute-done | bytes 196640 | tf_op jit(solution)/shard_map/ppermute | solution.py:29
  160.5 2.0 %collective-permute-done.40.refs_5_ = bf16[64,1536]{1,0:T(8,128)(2,1)S(1)} collective-permute-done((bf16[64,1536]{1,0:T(8,128)(2,1)S(1)}, bf16[64,1536]{1,0:T(8,128)(2,1)S(1)}, u32[]{:S(2)}, u32[]{:S(2)}) %collective-permute-start.40) | collective-permute-done | bytes 196640 | tf_op jit(solution)/shard_map/ppermute | solution.py:29
  162.8 3.2 %collective-permute-start.44 = (bf16[64,1152]{1,0:T(8,128)(2,1)S(1)}, bf16[64,1152]{1,0:T(8,128)(2,1)S(1)}, u32[]{:S(2)}, u32[]{:S(2)}) collective-permute-start(bf16[64,1152]{1,0:T(8,128)(2,1)S(1)} %get-tuple-element.128), channel_id=1, source_target_pairs={{0,4},{1,5},{2,6},{3,7},{4,0},{5,1},{6,2},{7,3},{8,12},{9,13},{10,... | collective-permute-start | bytes 442376 | tf_op jit(solution)/shard_map/ppermute | solution.py:37
  166.6 4.1 %mix.3 = (bf16[256,1152]{1,0:T(8,128)(2,1)S(1)}, bf16[256,1152]{1,0:T(8,128)(2,1)S(1)}) custom-call(s32[4]{0:T(128)S(1)} %pad_add_fusion.place, bf16[128,1536]{1,0:T(8,128)(2,1)S(1)} %collective-permute-done.34.refs_0_, bf16[128,1536]{1,0:T(8,128)(2,1)S(1)} %collective-permute-done.41.refs_1_, ...), custom_call_target="tpu_custom_call" | custom-call | flops 4000000000 | bytes 8000000 | tf_op jit(solution)/shard_map/mix/pallas_call | solution.py:372
  170.7 2.4 %collective-permute-start.46 = (bf16[256,1152]{1,0:T(8,128)(2,1)S(1)}, bf16[256,1152]{1,0:T(8,128)(2,1)S(1)}, u32[]{:S(2)}, u32[]{:S(2)}) collective-permute-start(bf16[256,1152]{1,0:T(8,128)(2,1)S(1)} %get-tuple-element.131), channel_id=1, source_target_pairs={{0,1},{1,0},{2,3},{3,2},{4,5},{5,4},{6,7},{7,6},{8,9},{9,8},{10,11... | collective-permute-start | bytes 1769480 | tf_op jit(solution)/shard_map/ppermute | solution.py:41
  173.1 1.0 collective-permute-done.45
  174.9 3.2 %collective-permute-start.48 = (bf16[64,1152]{1,0:T(8,128)(2,1)S(1)}, bf16[64,1152]{1,0:T(8,128)(2,1)S(1)}, u32[]{:S(2)}, u32[]{:S(2)}) collective-permute-start(bf16[64,1152]{1,0:T(8,128)(2,1)S(1)} %get-tuple-element.134), channel_id=1, source_target_pairs={{0,4},{1,5},{2,6},{3,7},{4,0},{5,1},{6,2},{7,3},{8,12},{9,13},{10,... | collective-permute-start | bytes 442376 | tf_op jit(solution)/shard_map/ppermute | solution.py:37
  178.9 6.0 %collective-permute-done.48 = bf16[64,1152]{1,0:T(8,128)(2,1)S(1)} collective-permute-done((bf16[64,1152]{1,0:T(8,128)(2,1)S(1)}, bf16[64,1152]{1,0:T(8,128)(2,1)S(1)}, u32[]{:S(2)}, u32[]{:S(2)}) %collective-permute-start.48) | collective-permute-done | bytes 147488 | tf_op jit(solution)/shard_map/ppermute | solution.py:37
  184.9 2.5 %collective-permute-done.49 = bf16[64,1152]{1,0:T(8,128)(2,1)S(1)} collective-permute-done((bf16[64,1152]{1,0:T(8,128)(2,1)S(1)}, bf16[64,1152]{1,0:T(8,128)(2,1)S(1)}, u32[]{:S(2)}, u32[]{:S(2)}) %collective-permute-start.49) | collective-permute-done | bytes 147488 | tf_op jit(solution)/shard_map/ppermute | solution.py:37
  187.5 0.7 pad_maximum_fusion
  (87 shorter events, 11.5 us)
Async XLA Ops:
  1.1 28.7 %collective-permute-start = (bf16[128,1152]{1,0:T(8,128)(2,1)}, bf16[128,1152]{1,0:T(8,128)(2,1)S(1)}, u32[]{:S(2)}, u32[]{:S(2)}) collective-permute-start(bf16[128,1152]{1,0:T(8,128)(2,1)} %refs_0_), channel_id=1, source_target_pairs={{0,2},{1,3},{2,0},{3,1},{4,6},{5,7},{6,4},{7,5},{8,10},{9,11},{10,... | collective-permute-start | bytes 884744 | tf_op jit(solution)/shard_map/ppermute | solution.py:37
  3.3 26.6 %collective-permute-start.1 = (bf16[128,1152]{1,0:T(8,128)(2,1)}, bf16[128,1152]{1,0:T(8,128)(2,1)S(1)}, u32[]{:S(2)}, u32[]{:S(2)}) collective-permute-start(bf16[128,1152]{1,0:T(8,128)(2,1)} %refs_0_), channel_id=1, source_target_pairs={{0,4},{1,5},{2,6},{3,7},{4,0},{5,1},{6,2},{7,3},{8,12},{9,13},{10,... | collective-permute-start | bytes 884744 | tf_op jit(solution)/shard_map/ppermute | solution.py:37
  5.7 24.1 %collective-permute-start.2 = (bf16[128,1152]{1,0:T(8,128)(2,1)}, bf16[128,1152]{1,0:T(8,128)(2,1)S(1)}, u32[]{:S(2)}, u32[]{:S(2)}) collective-permute-start(bf16[128,1152]{1,0:T(8,128)(2,1)} %refs_0_), channel_id=1, source_target_pairs={{0,6},{1,7},{2,4},{3,5},{4,2},{5,3},{6,0},{7,1},{8,14},{9,15},{10,... | collective-permute-start | bytes 884744 | tf_op jit(solution)/shard_map/ppermute | solution.py:37
  6.5 23.3 %all-to-all-start = ((f32[128,1,256]{2,1,0:T(1,128)}), f32[128,1,256]{2,1,0:T(1,128)S(1)}, u32[]{:S(2)}, u32[]{:S(2)}) async-start(f32[128,1,256]{2,1,0:T(1,128)} %all_to_all.8), calls=%async_computation | async-start | bytes 262144 | tf_op jit(solution)/shard_map/all_to_all | solution.py:427
  17.9 13.7 %collective-permute-start.3 = (bf16[128,1152]{1,0:T(8,128)(2,1)}, bf16[128,1152]{1,0:T(8,128)(2,1)S(1)}, u32[]{:S(2)}, u32[]{:S(2)}) collective-permute-start(bf16[128,1152]{1,0:T(8,128)(2,1)} %refs_0_), channel_id=1, source_target_pairs={{0,1},{1,0},{2,3},{3,2},{4,5},{5,4},{6,7},{7,6},{8,9},{9,8},{10,11... | collective-permute-start | bytes 884744 | tf_op jit(solution)/shard_map/ppermute | solution.py:41
  29.8 1.8 collective-permute-start.4
  30.4 1.6 collective-permute-start.5
  30.4 2.0 %collective-permute-start.6 = (bf16[128,1152]{1,0:T(8,128)(2,1)S(1)}, bf16[128,1152]{1,0:T(8,128)(2,1)S(1)}, u32[]{:S(2)}, u32[]{:S(2)}) collective-permute-start(bf16[128,1152]{1,0:T(8,128)(2,1)S(1)} %collective-permute-done.2.refs_6_), channel_id=1, source_target_pairs={{0,1},{1,0},{2,3},{3,2},{4,5},{5,4},{6,7},{7,6},{8,9},{9,8},{10,11... | collective-permute-start | bytes 884744 | tf_op jit(solution)/shard_map/ppermute | solution.py:41
  32.4 1.0 copy-start
  33.4 0.9 copy-start.3
  40.0 12.8 %collective-permute-start.10 = (bf16[128,1600]{1,0:T(8,128)(2,1)}, bf16[128,1600]{1,0:T(8,128)(2,1)S(1)}, u32[]{:S(2)}, u32[]{:S(2)}) collective-permute-start(bf16[128,1600]{1,0:T(8,128)(2,1)} %get-tuple-element.83), channel_id=1, source_target_pairs={{0,16},{8,24},{16,0},{24,8},{32,48},{40,56},{48,32},{56,40},{64,80... | collective-permute-start | bytes 1228808 | tf_op jit(solution)/shard_map/ppermute | solution.py:33
  41.3 11.8 %collective-permute-start.7 = (bf16[128,1600]{1,0:T(8,128)(2,1)S(1)}, bf16[128,1600]{1,0:T(8,128)(2,1)S(1)}, u32[]{:S(2)}, u32[]{:S(2)}) collective-permute-start(bf16[128,1600]{1,0:T(8,128)(2,1)S(1)} %get-tuple-element.79), channel_id=1, source_target_pairs={{0,32},{8,40},{16,48},{24,56},{32,0},{40,8},{48,16},{56,24},{64,96... | collective-permute-start | bytes 1228808 | tf_op jit(solution)/shard_map/ppermute | solution.py:29
  41.7 20.0 %collective-permute-start.8 = (bf16[128,1600]{1,0:T(8,128)(2,1)S(1)}, bf16[128,1600]{1,0:T(8,128)(2,1)S(1)}, u32[]{:S(2)}, u32[]{:S(2)}) collective-permute-start(bf16[128,1600]{1,0:T(8,128)(2,1)S(1)} %get-tuple-element.80), channel_id=1, source_target_pairs={{0,64},{8,72},{16,80},{24,88},{32,96},{40,104},{48,112},{56,120},{... | collective-permute-start | bytes 1228808 | tf_op jit(solution)/shard_map/ppermute | solution.py:29
  43.2 18.4 %collective-permute-start.9 = (bf16[128,1600]{1,0:T(8,128)(2,1)S(1)}, bf16[128,1600]{1,0:T(8,128)(2,1)S(1)}, u32[]{:S(2)}, u32[]{:S(2)}) collective-permute-start(bf16[128,1600]{1,0:T(8,128)(2,1)S(1)} %get-tuple-element.82), channel_id=1, source_target_pairs={{0,8},{8,0},{16,24},{24,16},{32,40},{40,32},{48,56},{56,48},{64,72... | collective-permute-start | bytes 1228808 | tf_op jit(solution)/shard_map/ppermute | solution.py:33
  43.2 1.3 copy-start.4
  48.7 29.2 %copy-start.1 = (s32[4]{0:T(128)S(1)}, s32[4]{0:T(128)}, u32[]{:S(2)}) copy-start(s32[4]{0:T(128)} %lengths.1) | copy-start | bytes 52
  48.7 21.2 %collective-permute-start.11 = (bf16[128,1600]{1,0:T(8,128)(2,1)S(1)}, bf16[128,1600]{1,0:T(8,128)(2,1)S(1)}, u32[]{:S(2)}, u32[]{:S(2)}) collective-permute-start(bf16[128,1600]{1,0:T(8,128)(2,1)S(1)} %get-tuple-element.86), channel_id=1, source_target_pairs={{0,96},{8,104},{16,112},{24,120},{32,64},{40,72},{48,80},{56,88},{... | collective-permute-start | bytes 1228808 | tf_op jit(solution)/shard_map/ppermute | solution.py:29
  52.8 17.1 %collective-permute-start.12 = (bf16[128,1600]{1,0:T(8,128)(2,1)S(1)}, bf16[128,1600]{1,0:T(8,128)(2,1)S(1)}, u32[]{:S(2)}, u32[]{:S(2)}) collective-permute-start(bf16[128,1600]{1,0:T(8,128)(2,1)S(1)} %get-tuple-element.87), channel_id=1, source_target_pairs={{0,24},{8,16},{16,8},{24,0},{32,56},{40,48},{48,40},{56,32},{64,88... | collective-permute-start | bytes 1228808 | tf_op jit(solution)/shard_map/ppermute | solution.py:33
  70.1 7.0 %collective-permute-start.13 = (bf16[32,1600]{1,0:T(8,128)(2,1)S(1)}, bf16[32,1600]{1,0:T(8,128)(2,1)S(1)}, u32[]{:S(2)}, u32[]{:S(2)}) collective-permute-start(bf16[32,1600]{1,0:T(8,128)(2,1)S(1)} %get-tuple-element.89), channel_id=1, source_target_pairs={{0,8},{8,0},{16,24},{24,16},{32,40},{40,32},{48,56},{56,48},{64,72... | collective-permute-start | bytes 307208 | tf_op jit(solution)/shard_map/ppermute | solution.py:33
  71.4 6.6 %collective-permute-start.14 = (bf16[32,1600]{1,0:T(8,128)(2,1)S(1)}, bf16[32,1600]{1,0:T(8,128)(2,1)S(1)}, u32[]{:S(2)}, u32[]{:S(2)}) collective-permute-start(bf16[32,1600]{1,0:T(8,128)(2,1)S(1)} %get-tuple-element.90), channel_id=1, source_target_pairs={{0,16},{8,24},{16,0},{24,8},{32,48},{40,56},{48,32},{56,40},{64,80... | collective-permute-start | bytes 307208 | tf_op jit(solution)/shard_map/ppermute | solution.py:33
  73.2 6.0 %collective-permute-start.15 = (bf16[32,1600]{1,0:T(8,128)(2,1)S(1)}, bf16[32,1600]{1,0:T(8,128)(2,1)S(1)}, u32[]{:S(2)}, u32[]{:S(2)}) collective-permute-start(bf16[32,1600]{1,0:T(8,128)(2,1)S(1)} %get-tuple-element.91), channel_id=1, source_target_pairs={{0,24},{8,16},{16,8},{24,0},{32,56},{40,48},{48,40},{56,32},{64,88... | collective-permute-start | bytes 307208 | tf_op jit(solution)/shard_map/ppermute | solution.py:33
  74.0 5.1 %collective-permute-start.16 = (bf16[32,1600]{1,0:T(8,128)(2,1)S(1)}, bf16[32,1600]{1,0:T(8,128)(2,1)S(1)}, u32[]{:S(2)}, u32[]{:S(2)}) collective-permute-start(bf16[32,1600]{1,0:T(8,128)(2,1)S(1)} %get-tuple-element.93), channel_id=1, source_target_pairs={{0,32},{8,40},{16,48},{24,56},{32,0},{40,8},{48,16},{56,24},{64,96... | collective-permute-start | bytes 307208 | tf_op jit(solution)/shard_map/ppermute | solution.py:29
  74.0 6.3 %collective-permute-start.17 = (bf16[32,1600]{1,0:T(8,128)(2,1)S(1)}, bf16[32,1600]{1,0:T(8,128)(2,1)S(1)}, u32[]{:S(2)}, u32[]{:S(2)}) collective-permute-start(bf16[32,1600]{1,0:T(8,128)(2,1)S(1)} %get-tuple-element.94), channel_id=1, source_target_pairs={{0,64},{8,72},{16,80},{24,88},{32,96},{40,104},{48,112},{56,120},{... | collective-permute-start | bytes 307208 | tf_op jit(solution)/shard_map/ppermute | solution.py:29
  77.1 5.1 %collective-permute-start.18 = (bf16[32,1600]{1,0:T(8,128)(2,1)S(1)}, bf16[32,1600]{1,0:T(8,128)(2,1)S(1)}, u32[]{:S(2)}, u32[]{:S(2)}) collective-permute-start(bf16[32,1600]{1,0:T(8,128)(2,1)S(1)} %get-tuple-element.95), channel_id=1, source_target_pairs={{0,96},{8,104},{16,112},{24,120},{32,64},{40,72},{48,80},{56,88},{... | collective-permute-start | bytes 307208 | tf_op jit(solution)/shard_map/ppermute | solution.py:29
  82.9 4.6 %collective-permute-start.19 = (bf16[32,1600]{1,0:T(8,128)(2,1)S(1)}, bf16[32,1600]{1,0:T(8,128)(2,1)S(1)}, u32[]{:S(2)}, u32[]{:S(2)}) collective-permute-start(bf16[32,1600]{1,0:T(8,128)(2,1)S(1)} %get-tuple-element.97), channel_id=1, source_target_pairs={{0,1},{1,0},{2,3},{3,2},{4,5},{5,4},{6,7},{7,6},{8,9},{9,8},{10,11... | collective-permute-start | bytes 307208 | tf_op jit(solution)/shard_map/ppermute | solution.py:41
  88.0 4.1 %collective-permute-start.20 = (bf16[16,1600]{1,0:T(8,128)(2,1)S(1)}, bf16[16,1600]{1,0:T(8,128)(2,1)S(1)}, u32[]{:S(2)}, u32[]{:S(2)}) collective-permute-start(bf16[16,1600]{1,0:T(8,128)(2,1)S(1)} %get-tuple-element.99), channel_id=1, source_target_pairs={{0,2},{1,3},{2,0},{3,1},{4,6},{5,7},{6,4},{7,5},{8,10},{9,11},{10,... | collective-permute-start | bytes 153608 | tf_op jit(solution)/shard_map/ppermute | solution.py:37
  88.1 4.7 %collective-permute-start.21 = (bf16[16,1600]{1,0:T(8,128)(2,1)S(1)}, bf16[16,1600]{1,0:T(8,128)(2,1)S(1)}, u32[]{:S(2)}, u32[]{:S(2)}) collective-permute-start(bf16[16,1600]{1,0:T(8,128)(2,1)S(1)} %get-tuple-element.100), channel_id=1, source_target_pairs={{0,4},{1,5},{2,6},{3,7},{4,0},{5,1},{6,2},{7,3},{8,12},{9,13},{10,... | collective-permute-start | bytes 153608 | tf_op jit(solution)/shard_map/ppermute | solution.py:37
  89.5 4.8 %collective-permute-start.22 = (bf16[16,1600]{1,0:T(8,128)(2,1)S(1)}, bf16[16,1600]{1,0:T(8,128)(2,1)S(1)}, u32[]{:S(2)}, u32[]{:S(2)}) collective-permute-start(bf16[16,1600]{1,0:T(8,128)(2,1)S(1)} %get-tuple-element.101), channel_id=1, source_target_pairs={{0,6},{1,7},{2,4},{3,5},{4,2},{5,3},{6,0},{7,1},{8,14},{9,15},{10,... | collective-permute-start | bytes 153608 | tf_op jit(solution)/shard_map/ppermute | solution.py:37
  94.2 46.4 %copy-start.2 = (bf16[1536,1152]{1,0:T(8,128)(2,1)S(1)}, bf16[1536,1152]{1,0:T(8,128)(2,1)}, u32[]{:S(2)}) copy-start(bf16[1536,1152]{1,0:T(8,128)(2,1)} %refs_6_.5) | copy-start | bytes 10616836
  101.9 2.5 %collective-permute-start.23 = (bf16[32,1536]{1,0:T(8,128)(2,1)S(1)}, bf16[32,1536]{1,0:T(8,128)(2,1)S(1)}, u32[]{:S(2)}, u32[]{:S(2)}) collective-permute-start(bf16[32,1536]{1,0:T(8,128)(2,1)S(1)} %get-tuple-element.103), channel_id=1, source_target_pairs={{0,1},{1,0},{2,3},{3,2},{4,5},{5,4},{6,7},{7,6},{8,9},{9,8},{10,11... | collective-permute-start | bytes 294920 | tf_op jit(solution)/shard_map/ppermute | solution.py:41
  105.0 4.5 %collective-permute-start.28 = (bf16[16,1536]{1,0:T(8,128)(2,1)S(1)}, bf16[16,1536]{1,0:T(8,128)(2,1)S(1)}, u32[]{:S(2)}, u32[]{:S(2)}) collective-permute-start(bf16[16,1536]{1,0:T(8,128)(2,1)S(1)} %get-tuple-element.106), channel_id=1, source_target_pairs={{0,4},{1,5},{2,6},{3,7},{4,0},{5,1},{6,2},{7,3},{8,12},{9,13},{10,... | collective-permute-start | bytes 147464 | tf_op jit(solution)/shard_map/ppermute | solution.py:37
  105.7 5.3 %collective-permute-start.29 = (bf16[16,1536]{1,0:T(8,128)(2,1)S(1)}, bf16[16,1536]{1,0:T(8,128)(2,1)S(1)}, u32[]{:S(2)}, u32[]{:S(2)}) collective-permute-start(bf16[16,1536]{1,0:T(8,128)(2,1)S(1)} %get-tuple-element.107), channel_id=1, source_target_pairs={{0,6},{1,7},{2,4},{3,5},{4,2},{5,3},{6,0},{7,1},{8,14},{9,15},{10,... | collective-permute-start | bytes 147464 | tf_op jit(solution)/shard_map/ppermute | solution.py:37
  107.7 7.2 %collective-permute-start.24 = (bf16[16,1536]{1,0:T(8,128)(2,1)S(1)}, bf16[16,1536]{1,0:T(8,128)(2,1)S(1)}, u32[]{:S(2)}, u32[]{:S(2)}) collective-permute-start(bf16[16,1536]{1,0:T(8,128)(2,1)S(1)} %get-tuple-element.105), channel_id=1, source_target_pairs={{0,2},{1,3},{2,0},{3,1},{4,6},{5,7},{6,4},{7,5},{8,10},{9,11},{10,... | collective-permute-start | bytes 147464 | tf_op jit(solution)/shard_map/ppermute | solution.py:37
  111.0 5.9 %collective-permute-start.30 = (bf16[32,1536]{1,0:T(8,128)(2,1)S(1)}, bf16[32,1536]{1,0:T(8,128)(2,1)S(1)}, u32[]{:S(2)}, u32[]{:S(2)}) collective-permute-start(bf16[32,1536]{1,0:T(8,128)(2,1)S(1)} %constant_dynamic-update-slice_fusion.2), channel_id=1, source_target_pairs={{0,8},{8,0},{16,24},{24,16},{32,40},{40,32},{48,56},{56,48},{64,72... | collective-permute-start | bytes 294920 | tf_op jit(solution)/shard_map/ppermute | solution.py:33
  111.0 7.8 %collective-permute-start.31 = (bf16[32,1536]{1,0:T(8,128)(2,1)S(1)}, bf16[32,1536]{1,0:T(8,128)(2,1)S(1)}, u32[]{:S(2)}, u32[]{:S(2)}) collective-permute-start(bf16[32,1536]{1,0:T(8,128)(2,1)S(1)} %constant_dynamic-update-slice_fusion.2), channel_id=1, source_target_pairs={{0,16},{8,24},{16,0},{24,8},{32,48},{40,56},{48,32},{56,40},{64,80... | collective-permute-start | bytes 294920 | tf_op jit(solution)/shard_map/ppermute | solution.py:33
  114.2 6.5 %collective-permute-start.32 = (bf16[32,1536]{1,0:T(8,128)(2,1)S(1)}, bf16[32,1536]{1,0:T(8,128)(2,1)S(1)}, u32[]{:S(2)}, u32[]{:S(2)}) collective-permute-start(bf16[32,1536]{1,0:T(8,128)(2,1)S(1)} %constant_dynamic-update-slice_fusion.2), channel_id=1, source_target_pairs={{0,24},{8,16},{16,8},{24,0},{32,56},{40,48},{48,40},{56,32},{64,88... | collective-permute-start | bytes 294920 | tf_op jit(solution)/shard_map/ppermute | solution.py:33
  114.9 5.8 %collective-permute-start.25 = (bf16[32,1536]{1,0:T(8,128)(2,1)S(1)}, bf16[32,1536]{1,0:T(8,128)(2,1)S(1)}, u32[]{:S(2)}, u32[]{:S(2)}) collective-permute-start(bf16[32,1536]{1,0:T(8,128)(2,1)S(1)} %constant_dynamic-update-slice_fusion), channel_id=1, source_target_pairs={{0,32},{8,40},{16,48},{24,56},{32,0},{40,8},{48,16},{56,24},{64,96... | collective-permute-start | bytes 294920 | tf_op jit(solution)/shard_map/ppermute | solution.py:29
  115.0 5.7 %collective-permute-start.26 = (bf16[32,1536]{1,0:T(8,128)(2,1)S(1)}, bf16[32,1536]{1,0:T(8,128)(2,1)S(1)}, u32[]{:S(2)}, u32[]{:S(2)}) collective-permute-start(bf16[32,1536]{1,0:T(8,128)(2,1)S(1)} %constant_dynamic-update-slice_fusion), channel_id=1, source_target_pairs={{0,64},{8,72},{16,80},{24,88},{32,96},{40,104},{48,112},{56,120},{... | collective-permute-start | bytes 294920 | tf_op jit(solution)/shard_map/ppermute | solution.py:29
  116.9 5.7 %collective-permute-start.27 = (bf16[32,1536]{1,0:T(8,128)(2,1)S(1)}, bf16[32,1536]{1,0:T(8,128)(2,1)S(1)}, u32[]{:S(2)}, u32[]{:S(2)}) collective-permute-start(bf16[32,1536]{1,0:T(8,128)(2,1)S(1)} %constant_dynamic-update-slice_fusion), channel_id=1, source_target_pairs={{0,96},{8,104},{16,112},{24,120},{32,64},{40,72},{48,80},{56,88},{... | collective-permute-start | bytes 294920 | tf_op jit(solution)/shard_map/ppermute | solution.py:29
  122.7 9.9 %collective-permute-start.33 = (bf16[128,1536]{1,0:T(8,128)(2,1)S(1)}, bf16[128,1536]{1,0:T(8,128)(2,1)S(1)}, u32[]{:S(2)}, u32[]{:S(2)}) collective-permute-start(bf16[128,1536]{1,0:T(8,128)(2,1)S(1)} %constant_dynamic-update-slice_fusion.4.refs_0_), channel_id=1, source_target_pairs={{0,16},{8,24},{16,0},{24,8},{32,48},{40,56},{48,32},{56,40},{64,80... | collective-permute-start | bytes 1179656 | tf_op jit(solution)/shard_map/ppermute | solution.py:33
  123.4 17.3 %collective-permute-start.34 = (bf16[128,1536]{1,0:T(8,128)(2,1)S(1)}, bf16[128,1536]{1,0:T(8,128)(2,1)S(1)}, u32[]{:S(2)}, u32[]{:S(2)}) collective-permute-start(bf16[128,1536]{1,0:T(8,128)(2,1)S(1)} %constant_dynamic-update-slice_fusion.4.refs_0_), channel_id=1, source_target_pairs={{0,8},{8,0},{16,24},{24,16},{32,40},{40,32},{48,56},{56,48},{64,72... | collective-permute-start | bytes 1179656 | tf_op jit(solution)/shard_map/ppermute | solution.py:33
  125.4 15.3 %collective-permute-start.35 = (bf16[64,1536]{1,0:T(8,128)(2,1)S(1)}, bf16[64,1536]{1,0:T(8,128)(2,1)S(1)}, u32[]{:S(2)}, u32[]{:S(2)}) collective-permute-start(bf16[64,1536]{1,0:T(8,128)(2,1)S(1)} %constant_dynamic-update-slice_fusion.8.refs_2_), channel_id=1, source_target_pairs={{0,32},{8,40},{16,48},{24,56},{32,0},{40,8},{48,16},{56,24},{64,96... | collective-permute-start | bytes 589832 | tf_op jit(solution)/shard_map/ppermute | solution.py:29
  125.5 15.2 %collective-permute-start.36 = (bf16[64,1536]{1,0:T(8,128)(2,1)S(1)}, bf16[64,1536]{1,0:T(8,128)(2,1)S(1)}, u32[]{:S(2)}, u32[]{:S(2)}) collective-permute-start(bf16[64,1536]{1,0:T(8,128)(2,1)S(1)} %constant_dynamic-update-slice_fusion.8.refs_2_), channel_id=1, source_target_pairs={{0,64},{8,72},{16,80},{24,88},{32,96},{40,104},{48,112},{56,120},{... | collective-permute-start | bytes 589832 | tf_op jit(solution)/shard_map/ppermute | solution.py:29
  128.5 12.1 %collective-permute-start.37 = (bf16[64,1536]{1,0:T(8,128)(2,1)S(1)}, bf16[64,1536]{1,0:T(8,128)(2,1)S(1)}, u32[]{:S(2)}, u32[]{:S(2)}) collective-permute-start(bf16[64,1536]{1,0:T(8,128)(2,1)S(1)} %constant_dynamic-update-slice_fusion.8.refs_2_), channel_id=1, source_target_pairs={{0,96},{8,104},{16,112},{24,120},{32,64},{40,72},{48,80},{56,88},{... | collective-permute-start | bytes 589832 | tf_op jit(solution)/shard_map/ppermute | solution.py:29
  132.6 29.9 %collective-permute-start.41 = (bf16[128,1536]{1,0:T(8,128)(2,1)S(1)}, bf16[128,1536]{1,0:T(8,128)(2,1)S(1)}, u32[]{:S(2)}, u32[]{:S(2)}) collective-permute-start(bf16[128,1536]{1,0:T(8,128)(2,1)S(1)} %constant_dynamic-update-slice_fusion.4.refs_0_), channel_id=1, source_target_pairs={{0,24},{8,16},{16,8},{24,0},{32,56},{40,48},{48,40},{56,32},{64,88... | collective-permute-start | bytes 1179656 | tf_op jit(solution)/shard_map/ppermute | solution.py:33
  144.8 17.8 %collective-permute-start.42 = (bf16[256,1152]{1,0:T(8,128)(2,1)S(1)}, bf16[256,1152]{1,0:T(8,128)(2,1)S(1)}, u32[]{:S(2)}, u32[]{:S(2)}) collective-permute-start(bf16[256,1152]{1,0:T(8,128)(2,1)S(1)} %get-tuple-element.125), channel_id=1, source_target_pairs={{0,1},{1,0},{2,3},{3,2},{4,5},{5,4},{6,7},{7,6},{8,9},{9,8},{10,11... | collective-permute-start | bytes 1769480 | tf_op jit(solution)/shard_map/ppermute | solution.py:41
  148.1 6.6 %collective-permute-start.38 = (bf16[64,1536]{1,0:T(8,128)(2,1)S(1)}, bf16[64,1536]{1,0:T(8,128)(2,1)S(1)}, u32[]{:S(2)}, u32[]{:S(2)}) collective-permute-start(bf16[64,1536]{1,0:T(8,128)(2,1)S(1)} %constant_dynamic-update-slice_fusion.10.refs_2_), channel_id=1, source_target_pairs={{0,32},{8,40},{16,48},{24,56},{32,0},{40,8},{48,16},{56,24},{64,96... | collective-permute-start | bytes 589832 | tf_op jit(solution)/shard_map/ppermute | solution.py:29
  148.2 12.4 %collective-permute-start.39 = (bf16[64,1536]{1,0:T(8,128)(2,1)S(1)}, bf16[64,1536]{1,0:T(8,128)(2,1)S(1)}, u32[]{:S(2)}, u32[]{:S(2)}) collective-permute-start(bf16[64,1536]{1,0:T(8,128)(2,1)S(1)} %constant_dynamic-update-slice_fusion.10.refs_2_), channel_id=1, source_target_pairs={{0,64},{8,72},{16,80},{24,88},{32,96},{40,104},{48,112},{56,120},{... | collective-permute-start | bytes 589832 | tf_op jit(solution)/shard_map/ppermute | solution.py:29
  151.2 11.3 %collective-permute-start.40 = (bf16[64,1536]{1,0:T(8,128)(2,1)S(1)}, bf16[64,1536]{1,0:T(8,128)(2,1)S(1)}, u32[]{:S(2)}, u32[]{:S(2)}) collective-permute-start(bf16[64,1536]{1,0:T(8,128)(2,1)S(1)} %constant_dynamic-update-slice_fusion.10.refs_2_), channel_id=1, source_target_pairs={{0,96},{8,104},{16,112},{24,120},{32,64},{40,72},{48,80},{56,88},{... | collective-permute-start | bytes 589832 | tf_op jit(solution)/shard_map/ppermute | solution.py:29
  162.7 10.4 %collective-permute-start.43 = (bf16[64,1152]{1,0:T(8,128)(2,1)S(1)}, bf16[64,1152]{1,0:T(8,128)(2,1)S(1)}, u32[]{:S(2)}, u32[]{:S(2)}) collective-permute-start(bf16[64,1152]{1,0:T(8,128)(2,1)S(1)} %get-tuple-element.127), channel_id=1, source_target_pairs={{0,2},{1,3},{2,0},{3,1},{4,6},{5,7},{6,4},{7,5},{8,10},{9,11},{10,... | collective-permute-start | bytes 442376 | tf_op jit(solution)/shard_map/ppermute | solution.py:37
  162.8 10.3 %collective-permute-start.44 = (bf16[64,1152]{1,0:T(8,128)(2,1)S(1)}, bf16[64,1152]{1,0:T(8,128)(2,1)S(1)}, u32[]{:S(2)}, u32[]{:S(2)}) collective-permute-start(bf16[64,1152]{1,0:T(8,128)(2,1)S(1)} %get-tuple-element.128), channel_id=1, source_target_pairs={{0,4},{1,5},{2,6},{3,7},{4,0},{5,1},{6,2},{7,3},{8,12},{9,13},{10,... | collective-permute-start | bytes 442376 | tf_op jit(solution)/shard_map/ppermute | solution.py:37
  166.0 8.1 %collective-permute-start.45 = (bf16[64,1152]{1,0:T(8,128)(2,1)S(1)}, bf16[64,1152]{1,0:T(8,128)(2,1)S(1)}, u32[]{:S(2)}, u32[]{:S(2)}) collective-permute-start(bf16[64,1152]{1,0:T(8,128)(2,1)S(1)} %get-tuple-element.129), channel_id=1, source_target_pairs={{0,6},{1,7},{2,4},{3,5},{4,2},{5,3},{6,0},{7,1},{8,14},{9,15},{10,... | collective-permute-start | bytes 442376 | tf_op jit(solution)/shard_map/ppermute | solution.py:37
  170.7 4.0 %collective-permute-start.46 = (bf16[256,1152]{1,0:T(8,128)(2,1)S(1)}, bf16[256,1152]{1,0:T(8,128)(2,1)S(1)}, u32[]{:S(2)}, u32[]{:S(2)}) collective-permute-start(bf16[256,1152]{1,0:T(8,128)(2,1)S(1)} %get-tuple-element.131), channel_id=1, source_target_pairs={{0,1},{1,0},{2,3},{3,2},{4,5},{5,4},{6,7},{7,6},{8,9},{9,8},{10,11... | collective-permute-start | bytes 1769480 | tf_op jit(solution)/shard_map/ppermute | solution.py:41
  174.8 4.1 %collective-permute-start.47 = (bf16[64,1152]{1,0:T(8,128)(2,1)S(1)}, bf16[64,1152]{1,0:T(8,128)(2,1)S(1)}, u32[]{:S(2)}, u32[]{:S(2)}) collective-permute-start(bf16[64,1152]{1,0:T(8,128)(2,1)S(1)} %get-tuple-element.133), channel_id=1, source_target_pairs={{0,2},{1,3},{2,0},{3,1},{4,6},{5,7},{6,4},{7,5},{8,10},{9,11},{10,... | collective-permute-start | bytes 442376 | tf_op jit(solution)/shard_map/ppermute | solution.py:37
  174.9 10.0 %collective-permute-start.48 = (bf16[64,1152]{1,0:T(8,128)(2,1)S(1)}, bf16[64,1152]{1,0:T(8,128)(2,1)S(1)}, u32[]{:S(2)}, u32[]{:S(2)}) collective-permute-start(bf16[64,1152]{1,0:T(8,128)(2,1)S(1)} %get-tuple-element.134), channel_id=1, source_target_pairs={{0,4},{1,5},{2,6},{3,7},{4,0},{5,1},{6,2},{7,3},{8,12},{9,13},{10,... | collective-permute-start | bytes 442376 | tf_op jit(solution)/shard_map/ppermute | solution.py:37
  178.1 9.3 %collective-permute-start.49 = (bf16[64,1152]{1,0:T(8,128)(2,1)S(1)}, bf16[64,1152]{1,0:T(8,128)(2,1)S(1)}, u32[]{:S(2)}, u32[]{:S(2)}) collective-permute-start(bf16[64,1152]{1,0:T(8,128)(2,1)S(1)} %get-tuple-element.135), channel_id=1, source_target_pairs={{0,6},{1,7},{2,4},{3,5},{4,2},{5,3},{6,0},{7,1},{8,14},{9,15},{10,... | collective-permute-start | bytes 442376 | tf_op jit(solution)/shard_map/ppermute | solution.py:37

commit v4 on v1

v4 whole, which is shorter than its diff:
```python
import jax
import jax.numpy as jnp
from jax import lax
from jax.experimental import pallas as pl
from jax.experimental.pallas import tpu as pltpu
from jax.sharding import PartitionSpec as P

D = 18432
HD = 256
STEPS = 2
VMEM = pl.BlockSpec(memory_space=pltpu.VMEM)
SMEM = pl.BlockSpec(memory_space=pltpu.SMEM)
ANY = pl.BlockSpec(memory_space=pl.ANY)
F32 = jnp.float32
BF16 = jnp.bfloat16


def params(mib):
    return pltpu.CompilerParams(vmem_limit_bytes=mib * 1024 * 1024)


def cost(flops, size):
    return pl.CostEstimate(flops=int(flops), bytes_accessed=int(size), transcendentals=0)


def exchange_pairs(core_along_y, m):
    pairs = []
    for d in range(128):
        far = 32 * m if d % 2 == core_along_y else 8 * m
        pairs.append((d, d ^ far))
    return pairs


def along_first(value, m):
    return lax.ppermute(value, ("gx", "gy"), exchange_pairs(0, m))


def along_second(value, m):
    return lax.ppermute(value, ("gx", "gy"), exchange_pairs(1, m))


def along_x(value, m):
    return lax.ppermute(value, "gy", [(g, g ^ (2 * m)) for g in range(8)])


def other_core(value):
    return lax.ppermute(value, "gy", [(g, g ^ 1) for g in range(8)])


def exchanged(along, parts):
    return [parts[0]] + [along(parts[m], m) for m in range(1, 4)]


def groups_of(rows, first, count):
    return jnp.concatenate([rows[16 * i + first : 16 * i + first + 8] for i in range(count)], axis=0)


def prepare_kernel(place, tokens, stats, mine, theirs):
    rows = tokens[...].astype(F32)
    by_core = [groups_of(rows, 0, 8), groups_of(rows, 8, 8)]
    swap = place[3] == 1
    mine[...] = jnp.where(swap, by_core[1], by_core[0]).astype(BF16)
    theirs[...] = jnp.where(swap, by_core[0], by_core[1]).astype(BF16)
    lines = []
    for power in range(2):
        sums = [
            jnp.sum(part if power == 0 else part * part, axis=1, keepdims=True) for part in by_core
        ]
        column = jnp.broadcast_to(jnp.concatenate(sums, axis=0), (128, 128))
        lines.append(column.T[0:1])
    line = jnp.concatenate(lines, axis=1)
    stats[...] = jnp.broadcast_to(line[:, None, :], stats.shape)


def prepare(place, tokens):
    half = jax.ShapeDtypeStruct((64, tokens.shape[1]), BF16)
    return pl.pallas_call(
        prepare_kernel,
        out_shape=[jax.ShapeDtypeStruct((128, 1, 256), F32), half, half],
        in_specs=[SMEM, VMEM],
        out_specs=[VMEM] * 3,
        compiler_params=params(8),
        cost_estimate=cost(1e8, 1e6),
        name="prepare",
    )(place, tokens)


def load_tiles(source, tiles, sems, at):
    loads = []
    wide = tiles.shape[2]
    for t in range(source.shape[1] // wide):
        load = pltpu.make_async_copy(
            source.at[:, pl.ds(t * wide, wide)], tiles.at[at + t], sems.at[at + t]
        )
        load.start()
        loads.append(load)
    return loads


def project_kernel(place, stats, gain, *refs):
    pieces, weights, pairs, outs = refs[:4], refs[4:6], refs[6:8], refs[8:12]
    normed, mean_of, scale_of, tiles, sems = refs[12:]
    count = tiles.shape[0] // 2
    loads = load_tiles(weights[0], tiles, sems, 0) + load_tiles(weights[1], tiles, sems, count)
    y, z, x, c = place[0], place[1], place[2], place[3]
    total = stats[0:8, :]
    for g in range(1, 16):
        total = total + stats[g * 8 : g * 8 + 8, :]
    mean = total[:, :128] / D
    variance = total[:, 128:] / D - mean * mean
    mean_columns = mean.T
    scale_columns = lax.rsqrt(variance + 1e-05).T
    for s in range(8):
        mean_of[s] = mean_columns[:, s : s + 1]
        scale_of[s] = scale_columns[:, s : s + 1]
    gains = gain[...].astype(F32)
    along_y = c == 0
    for m in range(4):
        to_y = x ^ m ^ y
        for j in range(2):
            source_c = c ^ j
            s = (x ^ m) * 2 + source_c
            rows = pieces[m][j * 64 : j * 64 + 64, :].astype(F32)
            of_core = pl.ds(pl.multiple_of(c * 64, 64), 64)
            rows = ((rows - mean_of[s, of_core]) * scale_of[s, of_core] * gains).astype(BF16)
            for b in range(2):
                to_z = (source_c * 2 + b) ^ z
                first = jnp.where(along_y, to_y, to_z)
                second = jnp.where(along_y, to_z, to_y)
                normed[first, second] = rows[b * 32 : b * 32 + 32]
    left = normed[...].reshape(512, normed.shape[-1])

    def put(part, at, size):
        for k, out in enumerate(outs):
            out[:, at : at + size] = part[k * 128 : k * 128 + 128]

    dims = (((1,), (1,)), ((), ()))
    wide = tiles.shape[2]
    width = tiles.shape[0] * wide
    pair = jnp.concatenate([pairs[0][...], pairs[1][...]], axis=0)
    pair = lax.dot_general(left, pair, dims, preferred_element_type=F32).astype(BF16)
    put(pair, width, pair.shape[1])
    for t, load in enumerate(loads):
        load.wait()
        put(jnp.dot(left, tiles[t], preferred_element_type=F32).astype(BF16), t * wide, wide)


def project(place, stats, gain, pieces, weights, pairs):
    depth, width = weights[0].shape
    out = jax.ShapeDtypeStruct((128, 2 * (width + pairs[0].shape[0])), BF16)
    count = 2 * width // 512
    return pl.pallas_call(
        project_kernel,
        out_shape=[out] * 4,
        in_specs=[SMEM] + [VMEM] * 6 + [ANY] * 2 + [VMEM] * 2,
        out_specs=[VMEM] * 4,
        scratch_shapes=[
            pltpu.VMEM((4, 4, 32, depth), BF16),
            pltpu.VMEM((8, 128, 1), F32),
            pltpu.VMEM((8, 128, 1), F32),
            pltpu.VMEM((count, depth, 512), BF16),
            pltpu.SemaphoreType.DMA((count,)),
        ],
        compiler_params=params(32),
        cost_estimate=cost(8e9, 1.2e7),
        name="project",
    )(place, stats, gain, *pieces, *weights, *pairs)


def sum_of(refs):
    total = refs[0][...].astype(F32)
    for ref in refs[1:]:
        total = total + ref[...].astype(F32)
    return total


def add_and_cut_kernel(*refs):
    total = sum_of(refs[:4]).astype(BF16)
    rows = total.shape[0] // 4
    for k in range(4):
        refs[4 + k][...] = total[k * rows : k * rows + rows]


def add_and_cut(values):
    rows, width = values[0].shape
    out = jax.ShapeDtypeStruct((rows // 4, width), BF16)
    return pl.pallas_call(
        add_and_cut_kernel,
        out_shape=[out] * 4,
        in_specs=[VMEM] * 4,
        out_specs=[VMEM] * 4,
        compiler_params=params(12),
        cost_estimate=cost(1e8, 1e6),
        name="add_and_cut",
    )(*values)


def finish_kernel(place, *refs):
    ins, outs, blocks = refs[:4], refs[4:8], refs[8]
    total = sum_of(ins)
    for i in range(4):
        blocks[place[2] ^ i] = total[i * 8 : i * 8 + 8]
    for m in range(4):
        outs[m][...] = blocks[m].astype(BF16)


def finish(place, values):
    rows, width = values[0].shape
    out = jax.ShapeDtypeStruct((rows // 4, width), BF16)
    return pl.pallas_call(
        finish_kernel,
        out_shape=[out] * 4,
        in_specs=[SMEM] + [VMEM] * 4,
        out_specs=[VMEM] * 4,
        scratch_shapes=[pltpu.VMEM((4, rows // 4, width), F32)],
        compiler_params=params(8),
        cost_estimate=cost(1e8, 1e6),
        name="finish",
    )(place, *values)


def line_up_kernel(place, *refs):
    ins, out, blocks = refs[:4], refs[4], refs[5]
    for m in range(4):
        blocks[place[2] ^ m] = ins[m][...].astype(F32)
    out[...] = blocks[...].reshape(out.shape).astype(BF16)


def line_up(place, values):
    rows, width = values[0].shape
    return pl.pallas_call(
        line_up_kernel,
        out_shape=jax.ShapeDtypeStruct((4 * rows, width), BF16),
        in_specs=[SMEM] + [VMEM] * 4,
        out_specs=VMEM,
        scratch_shapes=[pltpu.VMEM((4, rows, width), F32)],
        compiler_params=params(8),
        cost_estimate=cost(1e8, 1e6),
        name="line_up",
    )(place, *values)


def attend_kernel(lengths, place, *refs):
    packed, (cosine, sine, keys, values), outs = refs[:4], refs[4:8], refs[8:12]
    query_rows, new_pieces, new_kv, result = refs[12:]
    request = pl.program_id(0)
    width = outs[0].shape[1]
    heads = width // HD
    count = 4 * heads

    @pl.when(request == 0)
    def _():
        x, c = place[2], place[3]
        cos, sin = cosine[...], sine[...]

        def rotated(first, second):
            return first * cos - second * sin, second * cos + first * sin

        for m in range(4):
            rows = packed[m][...].astype(F32)
            for h in range(heads):
                head = rows[:, h * HD : h * HD + HD]
                for i, half in enumerate(rotated(head[:, :128], head[:, 128:])):
                    query_rows[i, pl.ds(m * heads + h, 8, stride=count), :] = half
            size = (rows.shape[1] - width) // 2
            for j in range(2):
                at = width + j * size
                new_pieces[(x ^ m) * 2 + (c ^ j)] = rows[:, at : at + size]
        halves = [
            jnp.concatenate([new_pieces[i], new_pieces[i + 1]], axis=-1) for i in range(0, 8, 2)
        ]
        new_kv[0] = jnp.concatenate(rotated(halves[0], halves[1]), axis=-1).astype(BF16)
        new_kv[1] = jnp.concatenate(halves[2:], axis=-1).astype(BF16)

    per = STEPS * count
    start = pl.multiple_of(request * per, per)
    query = jnp.concatenate([query_rows[i, pl.ds(start, per), :] for i in range(2)], axis=-1)
    query = (query.astype(BF16).astype(F32) * HD ** (-0.5)).astype(BF16)
    dims = (((1,), (1,)), ((), ()))
    cached = lax.dot_general(query, keys[0], dims, preferred_element_type=F32)
    slots = lax.broadcasted_iota(jnp.int32, cached.shape, 1)
    cached = jnp.where(slots < lengths[request], cached, -jnp.inf)
    fresh = lax.dot_general(query, new_kv[0], dims, preferred_element_type=F32)
    row_step = lax.broadcasted_iota(jnp.int32, fresh.shape, 0) // count
    key_step = lax.broadcasted_iota(jnp.int32, fresh.shape, 1) - request * STEPS
    fresh = jnp.where((key_step >= 0) & (key_step <= row_step), fresh, -jnp.inf)
    top = jnp.maximum(
        jnp.max(cached, axis=-1, keepdims=True), jnp.max(fresh, axis=-1, keepdims=True)
    )
    cached = jnp.exp(cached - top)
    fresh = jnp.exp(fresh - top)
    denom = jnp.sum(cached, axis=-1, keepdims=True) + jnp.sum(fresh, axis=-1, keepdims=True)
    mixed = jnp.dot(cached.astype(BF16), values[0], preferred_element_type=F32)
    mixed = mixed + jnp.dot(fresh.astype(BF16), new_kv[1], preferred_element_type=F32)
    mixed = mixed / denom
    for i in range(2):
        result[i, pl.ds(start, per), :] = mixed[:, i * 128 : i * 128 + 128]

    @pl.when(request == pl.num_programs(0) - 1)
    def _():
        for m, out in enumerate(outs):
            halves = [
                result[i, pl.ds(m * heads + h, 8, stride=count), :]
                for h in range(heads)
                for i in range(2)
            ]
            out[...] = jnp.concatenate(halves, axis=-1).astype(BF16)


def attend(place, packed, cosine, sine, cache_keys, cache_values, lengths, width):
    requests, slots, _ = cache_keys.shape
    total = packed[0].shape[1]
    count = 4 * (width // HD)
    whole = lambda *shape: pl.BlockSpec(shape, lambda r, *_: (0,) * len(shape))
    cache = pl.BlockSpec((1, slots, HD), lambda r, *_: (r, 0, 0))
    return pl.pallas_call(
        attend_kernel,
        out_shape=[jax.ShapeDtypeStruct((8, width), BF16)] * 4,
        grid_spec=pltpu.PrefetchScalarGridSpec(
            num_scalar_prefetch=2,
            grid=(requests,),
            in_specs=[whole(8, total)] * 4 + [whole(8, 128)] * 2 + [cache] * 2,
            out_specs=[whole(8, width)] * 4,
            scratch_shapes=[
                pltpu.VMEM((2, 8 * count, 128), F32),
                pltpu.VMEM((8, 8, (total - width) // 2), F32),
                pltpu.VMEM((2, 8, HD), BF16),
                pltpu.VMEM((2, 8 * count, 128), F32),
            ],
        ),
        compiler_params=params(52),
        cost_estimate=cost(6e9, 1.8e7),
        name="attend",
    )(lengths, place, *packed, cosine, sine, cache_keys, cache_values)


def mix_kernel(place, *refs):
    lefts, weights, outs = refs[:4], refs[4:6], refs[6:10]
    rows, tiles, sems = refs[10:]
    count = tiles.shape[0] // 2
    loads = load_tiles(weights[0], tiles, sems, 0) + load_tiles(weights[1], tiles, sems, count)
    y, z, x, c = place[0], place[1], place[2], place[3]
    along_y = c == 0
    for second in range(4):
        for first in range(4):
            to_x = y ^ x ^ jnp.where(along_y, first, second)
            token_z = z ^ jnp.where(along_y, second, first)
            slot = (token_z // 2 ^ c) * 2 + token_z % 2
            rows[to_x, slot] = lefts[second][first * 32 : first * 32 + 32, :]
    left = rows[...].reshape(512, rows.shape[-1])
    depth = left.shape[1] // 2
    wide = tiles.shape[2]
    for t in range(count):
        loads[t].wait()
        part = jnp.dot(left[:, :depth], tiles[t], preferred_element_type=F32)
        loads[count + t].wait()
        part = part + jnp.dot(left[:, depth:], tiles[count + t], preferred_element_type=F32)
        part = part.astype(BF16)
        for k, out in enumerate(outs):
            out[:, t * wide : t * wide + wide] = part[k * 128 : k * 128 + 128]


def mix(place, lefts, weights):
    depth, width = weights[0].shape
    return pl.pallas_call(
        mix_kernel,
        out_shape=[jax.ShapeDtypeStruct((128, width), BF16)] * 4,
        in_specs=[SMEM] + [VMEM] * 4 + [ANY] * 2,
        out_specs=[VMEM] * 4,
        scratch_shapes=[
            pltpu.VMEM((4, 4, 32, 2 * depth), BF16),
            pltpu.VMEM((6, depth, width // 3), BF16),
            pltpu.SemaphoreType.DMA((6,)),
        ],
        compiler_params=params(32),
        cost_estimate=cost(8e9, 1.2e7),
        name="mix",
    )(place, *lefts, *weights)


def last_sum_kernel(*refs):
    total = sum_of(refs[:4]).astype(BF16)
    refs[4][...] = total[:64]
    refs[5][...] = total[64:]


def last_sum(values):
    half = jax.ShapeDtypeStruct((64, values[0].shape[1]), BF16)
    return pl.pallas_call(
        last_sum_kernel,
        out_shape=[half] * 2,
        in_specs=[VMEM] * 4,
        out_specs=[VMEM] * 2,
        compiler_params=params(8),
        cost_estimate=cost(1e8, 1e6),
        name="last_sum",
    )(*values)


def interleave_kernel(place, mine, theirs, out):
    first, second = mine[...].astype(F32), theirs[...].astype(F32)
    swap = place[3] == 1
    first, second = jnp.where(swap, second, first), jnp.where(swap, first, second)
    groups = []
    for i in range(8):
        groups += [first[i * 8 : i * 8 + 8], second[i * 8 : i * 8 + 8]]
    out[...] = jnp.concatenate(groups, axis=0).astype(BF16)


def interleave(place, mine, theirs):
    rows, width = mine.shape
    return pl.pallas_call(
        interleave_kernel,
        out_shape=jax.ShapeDtypeStruct((2 * rows, width), BF16),
        in_specs=[SMEM] + [VMEM] * 2,
        out_specs=VMEM,
        compiler_params=params(8),
        cost_estimate=cost(1e8, 1e6),
        name="interleave",
    )(place, mine, theirs)


def per_device(tokens, norm_gain, w_query, w_keyvalue, w_out, cache_keys, cache_values, lengths):
    gx, gy = lax.axis_index("gx"), lax.axis_index("gy")
    place = jnp.stack([gx // 4, gx % 4, gy // 2, gy % 2]).astype(jnp.int32)

    stats, mine, theirs = prepare(place, tokens)
    piece = jnp.concatenate([mine, other_core(theirs)], axis=0)
    piece, stats = lax.optimization_barrier((piece, stats))
    pieces = exchanged(along_x, [piece] * 4)
    stats = lax.all_to_all(stats, ("gx", "gy"), 0, 0, tiled=True).reshape(128, 256)
    w_pair = w_keyvalue.T
    weights = [w_query, other_core(w_query)]
    parts = project(
        place, stats, norm_gain[None], pieces, weights, [w_pair, other_core(w_pair)]
    )

    parts = add_and_cut(exchanged(along_first, parts))
    parts = finish(place, exchanged(along_second, parts))
    packed = exchanged(along_x, parts)

    half_dim = HD // 2
    freqs = 10000.0 ** (-jnp.arange(half_dim, dtype=F32) / half_dim)
    positions = lengths[:, None] + jnp.arange(STEPS, dtype=jnp.int32)[None, :]
    angles = positions.reshape(-1).astype(F32)[:, None] * freqs
    attended = attend(
        place,
        packed,
        jnp.cos(angles),
        jnp.sin(angles),
        cache_keys,
        cache_values,
        lengths,
        2 * w_query.shape[1],
    )

    rows = line_up(place, exchanged(along_x, attended))
    rows = jnp.concatenate(exchanged(along_first, [rows] * 4), axis=0)
    parts = mix(place, exchanged(along_second, [rows] * 4), [w_out, other_core(w_out)])
    mine, theirs = last_sum(exchanged(along_x, parts))
    return interleave(place, mine, other_core(theirs))


def solution(mesh):
    return jax.shard_map(
        per_device,
        mesh=mesh,
        in_specs=(
            P("gy", "gx"),
            P("gx"),
            P("gx", "gy"),
            P("gx", "gy"),
            P("gy", "gx"),
            P(("gx", "gy"), None, None),
            P(("gx", "gy"), None, None),
            P(("gx", "gy")),
        ),
        out_specs=P("gy", "gx"),
        check_vma=False,
    )
```

time: 201 us -> 168 us (0.84)
  starting transfers between devices: 72 us -> 54.9 us
  blocking collectives: 9.26 us -> 0 us
  other arithmetic: 3.16 us -> 0.34 us
    ppermute x30 -> x24, starting transfers between devices: 45.9 us -> 30.3 us  [the longest x12 15.7 us: along_x(): return lax.ppermute(value, 'gy', [(g, g ^ 2 * m) for g in range(8)])]
    all_to_all x1 -> x0, blocking collectives: 9.26 us -> none  [per_device(): returned = lax.all_to_all(attended, 'gy', 0, 0, tiled=True)]
    all_to_all x2 -> x1, starting transfers between devices: 17.6 us -> 9.92 us  [per_device(): lax.all_to_all(stats, ('gx', 'gy'), 0, 0, tiled=True).reshape(128, 256)]
    ppermute x5, starting transfers between devices: 8.47 us -> 14.7 us  [other_core(): return lax.ppermute(value, 'gy', [(g, g ^ 1) for g in range(8)])]
    ppermute x5, waiting for transfers between devices: 0.01 us -> 4.47 us  [other_core(): return lax.ppermute(value, 'gy', [(g, g ^ 1) for g in range(8)])]
    ppermute x30 -> x24, waiting for transfers between devices: 66.6 us -> 64.2 us  [the longest x6 26.3 us: along_first(): return lax.ppermute(value, ('gx', 'gy'), exchange_pairs(0, m))]
    all_to_all x2 -> x1, waiting for transfers between devices: 13.9 us -> 11.9 us  [per_device(): lax.all_to_all(stats, ('gx', 'gy'), 0, 0, tiled=True).reshape(128, 256)]
    pallas_call x6 -> x9, Pallas kernels: 29.3 us -> 27.5 us  [the longest x1 7.8 us: mix(): pl.pallas_call(mix_kernel, out_shape=[jax.ShapeDtypeStruct((128, width),...]
  transfers between devices with their start and end apart: 37 -> 30, of which waited for: 20 -> 21; matrix products, arithmetic and copies ran while one was open for 2% -> 1% of each run, Pallas kernels for 3% -> 11%
where the time goes in v4:
time: 168 us
  waiting for transfers between devices  80.6 us (48%)
  starting transfers between devices  54.9 us (33%)
  Pallas kernels  27.5 us (16%)
  local copies, waits for them, and re-layouts  4.66 us (3%)
    ppermute x6, waiting for transfers between devices, along_first(): return lax.ppermute(value, ('gx', 'gy'), exchange_pairs(0, m))  26.3 us
    ppermute x6, waiting for transfers between devices, along_second(): return lax.ppermute(value, ('gx', 'gy'), exchange_pairs(1, m))  25 us
    ppermute x12, starting transfers between devices, along_x(): return lax.ppermute(value, 'gy', [(g, g ^ 2 * m) for g in range(8)])  15.7 us
    ppermute x5, starting transfers between devices, other_core(): return lax.ppermute(value, 'gy', [(g, g ^ 1) for g in range(8)])  14.7 us
    ppermute x12, waiting for transfers between devices, along_x(): return lax.ppermute(value, 'gy', [(g, g ^ 2 * m) for g in range(8)])  13 us
    all_to_all x1, waiting for transfers between devices, per_device(): lax.all_to_all(stats, ('gx', 'gy'), 0, 0, tiled=True).reshape(128, 256)  11.9 us
    all_to_all x1, starting transfers between devices, per_device(): lax.all_to_all(stats, ('gx', 'gy'), 0, 0, tiled=True).reshape(128, 256)  9.92 us
    ppermute x6, starting transfers between devices, along_first(): return lax.ppermute(value, ('gx', 'gy'), exchange_pairs(0, m))  7.87 us
  transfers between devices with their start and end apart: 30, of which 21 were waited for; matrix products, arithmetic and copies ran while one was open for 1% of the time, Pallas kernels for 11%

profile of v4, /device:TPU:1, one launch (start us, length us, event | category | flops | bytes accessed | tf_op | source)
XLA Modules:
  0.0 168.1 jit_solution(10132617056328696527)
XLA Ops:
  0.0 1.4 collective-permute-start.4
  1.5 1.0 copy-done.3
  2.5 1.6 prepare.1
  4.0 3.5 %collective-permute-done = bf16[64,1152]{1,0:T(8,128)(2,1)S(1)} collective-permute-done((bf16[64,1152]{1,0:T(8,128)(2,1)S(1)}, bf16[64,1152]{1,0:T(8,128)(2,1)S(1)}, u32[]{:S(2)}, u32[]{:S(2)}) %collective-permute-start) | collective-permute-done | bytes 147488 | tf_op jit(solution)/shard_map/ppermute | solution.py:47
  7.5 1.4 collective-permute-start.1
  8.9 2.5 %collective-permute-start.2 = (bf16[128,1152]{1,0:T(8,128)(2,1)S(1)}, bf16[128,1152]{1,0:T(8,128)(2,1)S(1)}, u32[]{:S(2)}, u32[]{:S(2)}) collective-permute-start(bf16[128,1152]{1,0:T(8,128)(2,1)S(1)} %pad_maximum_fusion.1.refs_0_), channel_id=1, source_target_pairs={{0,4},{1,5},{2,6},{3,7},{4,0},{5,1},{6,2},{7,3},{8,12},{9,13},{10,... | collective-permute-start | bytes 884744 | tf_op jit(solution)/shard_map/ppermute | solution.py:43
  11.3 0.1 collective-permute-start.3
  11.4 1.2 collective-permute-start.5
  12.7 9.9 %all-to-all-start = ((f32[128,1,256]{2,1,0:T(1,128)}), f32[128,1,256]{2,1,0:T(1,128)S(1)}, u32[]{:S(2)}, u32[]{:S(2)}) async-start(f32[128,1,256]{2,1,0:T(1,128)} %get-tuple-element.35), calls=%async_computation | async-start | bytes 262144 | tf_op jit(solution)/shard_map/all_to_all | solution.py:431
  22.6 0.7 broadcast_in_dim.2.gain
  23.3 11.9 %all-to-all-done = f32[128,1,256]{2,1,0:T(1,128)S(1)} async-done(((f32[128,1,256]{2,1,0:T(1,128)}), f32[128,1,256]{2,1,0:T(1,128)S(1)}, u32[]{:S(2)}, u32[]{:S(2)}) %all-to-all-start) | async-done | bytes 131104 | tf_op jit(solution)/shard_map/all_to_all | solution.py:431
  35.2 0.5 collective-permute-start.24
  35.8 2.0 %copy-done.1 = bf16[1152,1536]{1,0:T(8,128)(2,1)S(1)} copy-done((bf16[1152,1536]{1,0:T(8,128)(2,1)S(1)}, bf16[1152,1536]{1,0:T(8,128)(2,1)}, u32[]{:S(2)}) %copy-start.1) | copy-done | bytes 3538968
  37.8 0.9 copy-done.4
  38.7 7.2 %project.1 = (bf16[128,3200]{1,0:T(8,128)(2,1)S(1)}, bf16[128,3200]{1,0:T(8,128)(2,1)S(1)}, bf16[128,3200]{1,0:T(8,128)(2,1)S(1)}, bf16[128,3200]{1,0:T(8,128)(2,1)S(1)}) custom-call(s32[4]{0:T(128)S(1)} %pad_add_fusion.place, f32[128,256]{1,0:T(8,128)S(1)} %bitcast.8, bf16[1,1152]{1,0:T(2,128)(2,1)S(1)} %broadcast_in_dim.2.gain, ...), custom_call_target="tpu_custom_call" | custom-call | flops 8000000000 | bytes 12000000 | tf_op jit(solution)/shard_map/project/pallas_call | solution.py:152
  45.9 0.8 collective-permute-start.6
  46.7 0.7 collective-permute-start.7
  47.4 2.4 %collective-permute-start.8 = (bf16[128,3200]{1,0:T(8,128)(2,1)S(1)}, bf16[128,3200]{1,0:T(8,128)(2,1)S(1)}, u32[]{:S(2)}, u32[]{:S(2)}) collective-permute-start(bf16[128,3200]{1,0:T(8,128)(2,1)S(1)} %get-tuple-element.40), channel_id=1, source_target_pairs={{0,96},{1,25},{2,98},{3,27},{4,100},{5,29},{6,102},{7,31},{8,104},... | collective-permute-start | bytes 2457608 | tf_op jit(solution)/shard_map/ppermute | solution.py:35
  49.9 7.6 %collective-permute-done.6.refs_1_ = bf16[128,3200]{1,0:T(8,128)(2,1)S(1)} collective-permute-done((bf16[128,3200]{1,0:T(8,128)(2,1)S(1)}, bf16[128,3200]{1,0:T(8,128)(2,1)S(1)}, u32[]{:S(2)}, u32[]{:S(2)}) %collective-permute-start.6) | collective-permute-done | bytes 819232 | tf_op jit(solution)/shard_map/ppermute | solution.py:35
  57.5 8.8 %collective-permute-done.7.refs_2_ = bf16[128,3200]{1,0:T(8,128)(2,1)S(1)} collective-permute-done((bf16[128,3200]{1,0:T(8,128)(2,1)S(1)}, bf16[128,3200]{1,0:T(8,128)(2,1)S(1)}, u32[]{:S(2)}, u32[]{:S(2)}) %collective-permute-start.7) | collective-permute-done | bytes 819232 | tf_op jit(solution)/shard_map/ppermute | solution.py:35
  66.3 2.6 %collective-permute-done.8.refs_3_ = bf16[128,3200]{1,0:T(8,128)(2,1)S(1)} collective-permute-done((bf16[128,3200]{1,0:T(8,128)(2,1)S(1)}, bf16[128,3200]{1,0:T(8,128)(2,1)S(1)}, u32[]{:S(2)}, u32[]{:S(2)}) %collective-permute-start.8) | collective-permute-done | bytes 819232 | tf_op jit(solution)/shard_map/ppermute | solution.py:35
  68.9 0.4 add_and_cut.1
  69.3 0.9 collective-permute-start.10
  70.2 1.7 %collective-permute-start.11 = (bf16[32,3200]{1,0:T(8,128)(2,1)S(1)}, bf16[32,3200]{1,0:T(8,128)(2,1)S(1)}, u32[]{:S(2)}, u32[]{:S(2)}) collective-permute-start(bf16[32,3200]{1,0:T(8,128)(2,1)S(1)} %get-tuple-element.44), channel_id=1, source_target_pairs={{0,24},{1,97},{2,26},{3,99},{4,28},{5,101},{6,30},{7,103},{8,16},{... | collective-permute-start | bytes 614408 | tf_op jit(solution)/shard_map/ppermute | solution.py:39
  71.9 0.2 collective-permute-start.9
  72.1 0.1 convert_element_type.11
  72.2 3.4 %collective-permute-done.10.refs_2_ = bf16[32,3200]{1,0:T(8,128)(2,1)S(1)} collective-permute-done((bf16[32,3200]{1,0:T(8,128)(2,1)S(1)}, bf16[32,3200]{1,0:T(8,128)(2,1)S(1)}, u32[]{:S(2)}, u32[]{:S(2)}) %collective-permute-start.10) | collective-permute-done | bytes 204832 | tf_op jit(solution)/shard_map/ppermute | solution.py:39
  75.6 2.4 %collective-permute-done.11.refs_3_ = bf16[32,3200]{1,0:T(8,128)(2,1)S(1)} collective-permute-done((bf16[32,3200]{1,0:T(8,128)(2,1)S(1)}, bf16[32,3200]{1,0:T(8,128)(2,1)S(1)}, u32[]{:S(2)}, u32[]{:S(2)}) %collective-permute-start.11) | collective-permute-done | bytes 204832 | tf_op jit(solution)/shard_map/ppermute | solution.py:39
  78.0 0.7 finish.1
  78.7 0.1 collective-permute-start.12
  78.8 1.4 collective-permute-start.13
  80.2 2.5 %collective-permute-start.14 = (bf16[8,3200]{1,0:T(8,128)(2,1)S(1)}, bf16[8,3200]{1,0:T(8,128)(2,1)S(1)}, u32[]{:S(2)}, u32[]{:S(2)}) collective-permute-start(bf16[8,3200]{1,0:T(8,128)(2,1)S(1)} %get-tuple-element.48), channel_id=1, source_target_pairs={{0,6},{1,7},{2,4},{3,5},{4,2},{5,3},{6,0},{7,1},{8,14},{9,15},{10,... | collective-permute-start | bytes 153608 | tf_op jit(solution)/shard_map/ppermute | solution.py:43
  82.7 0.1 multiply_sine_fusion
  82.8 0.6 collective-permute-done.13.refs_2_
  83.4 1.0 collective-permute-done.14.refs_3_
  84.3 7.7 %attend.1 = (bf16[8,3072]{1,0:T(8,128)(2,1)S(1)}, bf16[8,3072]{1,0:T(8,128)(2,1)S(1)}, bf16[8,3072]{1,0:T(8,128)(2,1)S(1)}, bf16[8,3072]{1,0:T(8,128)(2,1)S(1)}) custom-call(s32[4]{0:T(128)S(1)} %copy-done, s32[4]{0:T(128)S(1)} %pad_add_fusion.place, bf16[8,3200]{1,0:T(8,128)(2,1)S(1)} %get-tuple-element.45.refs_0_, ...), custom_call_target="tpu_custom_call" | custom-call | flops 6000000000 | bytes 18000000 | tf_op jit(solution)/shard_map/attend/pallas_call | solution.py:316
  92.1 0.5 collective-permute-start.15
  92.6 3.3 %collective-permute-start.16 = (bf16[8,3072]{1,0:T(8,128)(2,1)S(1)}, bf16[8,3072]{1,0:T(8,128)(2,1)S(1)}, u32[]{:S(2)}, u32[]{:S(2)}) collective-permute-start(bf16[8,3072]{1,0:T(8,128)(2,1)S(1)} %get-tuple-element.51), channel_id=1, source_target_pairs={{0,4},{1,5},{2,6},{3,7},{4,0},{5,1},{6,2},{7,3},{8,12},{9,13},{10,... | collective-permute-start | bytes 147464 | tf_op jit(solution)/shard_map/ppermute | solution.py:43
  95.8 0.2 collective-permute-start.17
  96.0 1.8 %collective-permute-done.16.refs_2_ = bf16[8,3072]{1,0:T(8,128)(2,1)S(1)} collective-permute-done((bf16[8,3072]{1,0:T(8,128)(2,1)S(1)}, bf16[8,3072]{1,0:T(8,128)(2,1)S(1)}, u32[]{:S(2)}, u32[]{:S(2)}) %collective-permute-start.16) | collective-permute-done | bytes 49184 | tf_op jit(solution)/shard_map/ppermute | solution.py:43
  97.8 2.1 %collective-permute-done.17.refs_3_ = bf16[8,3072]{1,0:T(8,128)(2,1)S(1)} collective-permute-done((bf16[8,3072]{1,0:T(8,128)(2,1)S(1)}, bf16[8,3072]{1,0:T(8,128)(2,1)S(1)}, u32[]{:S(2)}, u32[]{:S(2)}) %collective-permute-start.17) | collective-permute-done | bytes 49184 | tf_op jit(solution)/shard_map/ppermute | solution.py:43
  100.0 0.6 line_up.1
  100.6 0.1 collective-permute-start.18
  100.7 3.8 %collective-permute-start.19 = (bf16[32,3072]{1,0:T(8,128)(2,1)S(1)}, bf16[32,3072]{1,0:T(8,128)(2,1)S(1)}, u32[]{:S(2)}, u32[]{:S(2)}) collective-permute-start(bf16[32,3072]{1,0:T(8,128)(2,1)S(1)} %line_up.1), channel_id=1, source_target_pairs={{0,64},{1,17},{2,66},{3,19},{4,68},{5,21},{6,70},{7,23},{8,72},{9,... | collective-permute-start | bytes 589832 | tf_op jit(solution)/shard_map/ppermute | solution.py:35
  104.5 1.0 collective-permute-done.18
  105.5 4.2 %collective-permute-done.19 = bf16[32,3072]{1,0:T(8,128)(2,1)S(1)} collective-permute-done((bf16[32,3072]{1,0:T(8,128)(2,1)S(1)}, bf16[32,3072]{1,0:T(8,128)(2,1)S(1)}, u32[]{:S(2)}, u32[]{:S(2)}) %collective-permute-start.19) | collective-permute-done | bytes 196640 | tf_op jit(solution)/shard_map/ppermute | solution.py:35
  109.7 2.0 %collective-permute-done.20 = bf16[32,3072]{1,0:T(8,128)(2,1)S(1)} collective-permute-done((bf16[32,3072]{1,0:T(8,128)(2,1)S(1)}, bf16[32,3072]{1,0:T(8,128)(2,1)S(1)}, u32[]{:S(2)}, u32[]{:S(2)}) %collective-permute-start.20) | collective-permute-done | bytes 196640 | tf_op jit(solution)/shard_map/ppermute | solution.py:35
  111.8 0.1 collective-permute-start.21
  111.9 1.7 %collective-permute-start.22 = (bf16[128,3072]{1,0:T(8,128)(2,1)S(1)}, bf16[128,3072]{1,0:T(8,128)(2,1)S(1)}, u32[]{:S(2)}, u32[]{:S(2)}) collective-permute-start(bf16[128,3072]{1,0:T(8,128)(2,1)S(1)} %pad_maximum_fusion.refs_0_), channel_id=1, source_target_pairs={{0,16},{1,65},{2,18},{3,67},{4,20},{5,69},{6,22},{7,71},{8,24},{9,... | collective-permute-start | bytes 2359304 | tf_op jit(solution)/shard_map/ppermute | solution.py:39
  113.6 2.1 %collective-permute-start.23 = (bf16[128,3072]{1,0:T(8,128)(2,1)S(1)}, bf16[128,3072]{1,0:T(8,128)(2,1)S(1)}, u32[]{:S(2)}, u32[]{:S(2)}) collective-permute-start(bf16[128,3072]{1,0:T(8,128)(2,1)S(1)} %pad_maximum_fusion.refs_0_), channel_id=1, source_target_pairs={{0,24},{1,97},{2,26},{3,99},{4,28},{5,101},{6,30},{7,103},{8,16},{... | collective-permute-start | bytes 2359304 | tf_op jit(solution)/shard_map/ppermute | solution.py:39
  115.7 7.3 %collective-permute-done.21.refs_1_ = bf16[128,3072]{1,0:T(8,128)(2,1)S(1)} collective-permute-done((bf16[128,3072]{1,0:T(8,128)(2,1)S(1)}, bf16[128,3072]{1,0:T(8,128)(2,1)S(1)}, u32[]{:S(2)}, u32[]{:S(2)}) %collective-permute-start.21) | collective-permute-done | bytes 786464 | tf_op jit(solution)/shard_map/ppermute | solution.py:39
  123.0 9.8 %collective-permute-done.22.refs_2_ = bf16[128,3072]{1,0:T(8,128)(2,1)S(1)} collective-permute-done((bf16[128,3072]{1,0:T(8,128)(2,1)S(1)}, bf16[128,3072]{1,0:T(8,128)(2,1)S(1)}, u32[]{:S(2)}, u32[]{:S(2)}) %collective-permute-start.22) | collective-permute-done | bytes 786464 | tf_op jit(solution)/shard_map/ppermute | solution.py:39
  132.8 2.1 %collective-permute-done.23.refs_3_ = bf16[128,3072]{1,0:T(8,128)(2,1)S(1)} collective-permute-done((bf16[128,3072]{1,0:T(8,128)(2,1)S(1)}, bf16[128,3072]{1,0:T(8,128)(2,1)S(1)}, u32[]{:S(2)}, u32[]{:S(2)}) %collective-permute-start.23) | collective-permute-done | bytes 786464 | tf_op jit(solution)/shard_map/ppermute | solution.py:39
  134.9 7.8 %mix.1 = (bf16[128,1152]{1,0:T(8,128)(2,1)S(1)}, bf16[128,1152]{1,0:T(8,128)(2,1)S(1)}, bf16[128,1152]{1,0:T(8,128)(2,1)S(1)}, bf16[128,1152]{1,0:T(8,128)(2,1)S(1)}) custom-call(s32[4]{0:T(128)S(1)} %pad_add_fusion.place, bf16[128,3072]{1,0:T(8,128)(2,1)S(1)} %pad_maximum_fusion.refs_0_, bf16[128,3072]{1,0:T(8,128)(2,1)S(1)} %collective-permute-done.21.refs_1_, ...), custom_call_target="tpu_custom_call" | custom-call | flops 8000000000 | bytes 12000000 | tf_op jit(solution)/shard_map/mix/pallas_call | solution.py:365
  142.7 0.1 collective-permute-start.25
  142.8 1.4 collective-permute-start.26
  144.2 2.5 %collective-permute-start.27 = (bf16[128,1152]{1,0:T(8,128)(2,1)S(1)}, bf16[128,1152]{1,0:T(8,128)(2,1)S(1)}, u32[]{:S(2)}, u32[]{:S(2)}) collective-permute-start(bf16[128,1152]{1,0:T(8,128)(2,1)S(1)} %get-tuple-element.56), channel_id=1, source_target_pairs={{0,6},{1,7},{2,4},{3,5},{4,2},{5,3},{6,0},{7,1},{8,14},{9,15},{10,... | collective-permute-start | bytes 884744 | tf_op jit(solution)/shard_map/ppermute | solution.py:43
  146.7 1.7 %collective-permute-done.25.refs_1_ = bf16[128,1152]{1,0:T(8,128)(2,1)S(1)} collective-permute-done((bf16[128,1152]{1,0:T(8,128)(2,1)S(1)}, bf16[128,1152]{1,0:T(8,128)(2,1)S(1)}, u32[]{:S(2)}, u32[]{:S(2)}) %collective-permute-start.25) | collective-permute-done | bytes 294944 | tf_op jit(solution)/shard_map/ppermute | solution.py:43
  148.4 3.2 %collective-permute-done.26.refs_2_ = bf16[128,1152]{1,0:T(8,128)(2,1)S(1)} collective-permute-done((bf16[128,1152]{1,0:T(8,128)(2,1)S(1)}, bf16[128,1152]{1,0:T(8,128)(2,1)S(1)}, u32[]{:S(2)}, u32[]{:S(2)}) %collective-permute-start.26) | collective-permute-done | bytes 294944 | tf_op jit(solution)/shard_map/ppermute | solution.py:43
  151.6 2.6 %collective-permute-done.27.refs_3_ = bf16[128,1152]{1,0:T(8,128)(2,1)S(1)} collective-permute-done((bf16[128,1152]{1,0:T(8,128)(2,1)S(1)}, bf16[128,1152]{1,0:T(8,128)(2,1)S(1)}, u32[]{:S(2)}, u32[]{:S(2)}) %collective-permute-start.27) | collective-permute-done | bytes 294944 | tf_op jit(solution)/shard_map/ppermute | solution.py:43
  154.1 0.1 last_sum.1
  154.3 11.5 %collective-permute-start.28 = (bf16[64,1152]{1,0:T(8,128)(2,1)S(1)}, bf16[64,1152]{1,0:T(8,128)(2,1)S(1)}, u32[]{:S(2)}, u32[]{:S(2)}) collective-permute-start(bf16[64,1152]{1,0:T(8,128)(2,1)S(1)} %get-tuple-element.58), channel_id=1, source_target_pairs={{0,1},{1,0},{2,3},{3,2},{4,5},{5,4},{6,7},{7,6},{8,9},{9,8},{10,11... | collective-permute-start | bytes 442376 | tf_op jit(solution)/shard_map/ppermute | solution.py:47
  165.8 1.0 collective-permute-done.28.theirs
  166.8 1.3 interleave.1
  (24 shorter events, 0.3 us)
Async XLA Ops:
  0.0 35.7 %collective-permute-start.4 = (bf16[1152,1536]{1,0:T(8,128)(2,1)}, bf16[1152,1536]{1,0:T(8,128)(2,1)}, u32[]{:S(2)}, u32[]{:S(2)}) collective-permute-start(bf16[1152,1536]{1,0:T(8,128)(2,1)} %refs_4_.2), channel_id=1, source_target_pairs={{0,1},{1,0},{2,3},{3,2},{4,5},{5,4},{6,7},{7,6},{8,9},{9,8},{10,11... | collective-permute-start | bytes 10616840 | tf_op jit(solution)/shard_map/ppermute | solution.py:47
  1.5 1.0 copy-start.3
  4.0 3.5 %collective-permute-start = (bf16[64,1152]{1,0:T(8,128)(2,1)S(1)}, bf16[64,1152]{1,0:T(8,128)(2,1)S(1)}, u32[]{:S(2)}, u32[]{:S(2)}) collective-permute-start(bf16[64,1152]{1,0:T(8,128)(2,1)S(1)} %get-tuple-element.33), channel_id=1, source_target_pairs={{0,1},{1,0},{2,3},{3,2},{4,5},{5,4},{6,7},{7,6},{8,9},{9,8},{10,11... | collective-permute-start | bytes 442376 | tf_op jit(solution)/shard_map/ppermute | solution.py:47
  7.5 28.2 %collective-permute-start.1 = (bf16[128,1152]{1,0:T(8,128)(2,1)S(1)}, bf16[128,1152]{1,0:T(8,128)(2,1)S(1)}, u32[]{:S(2)}, u32[]{:S(2)}) collective-permute-start(bf16[128,1152]{1,0:T(8,128)(2,1)S(1)} %pad_maximum_fusion.1.refs_0_), channel_id=1, source_target_pairs={{0,2},{1,3},{2,0},{3,1},{4,6},{5,7},{6,4},{7,5},{8,10},{9,11},{10,... | collective-permute-start | bytes 884744 | tf_op jit(solution)/shard_map/ppermute | solution.py:43
  8.9 26.9 %collective-permute-start.2 = (bf16[128,1152]{1,0:T(8,128)(2,1)S(1)}, bf16[128,1152]{1,0:T(8,128)(2,1)S(1)}, u32[]{:S(2)}, u32[]{:S(2)}) collective-permute-start(bf16[128,1152]{1,0:T(8,128)(2,1)S(1)} %pad_maximum_fusion.1.refs_0_), channel_id=1, source_target_pairs={{0,4},{1,5},{2,6},{3,7},{4,0},{5,1},{6,2},{7,3},{8,12},{9,13},{10,... | collective-permute-start | bytes 884744 | tf_op jit(solution)/shard_map/ppermute | solution.py:43
  11.3 24.4 %collective-permute-start.3 = (bf16[128,1152]{1,0:T(8,128)(2,1)S(1)}, bf16[128,1152]{1,0:T(8,128)(2,1)S(1)}, u32[]{:S(2)}, u32[]{:S(2)}) collective-permute-start(bf16[128,1152]{1,0:T(8,128)(2,1)S(1)} %pad_maximum_fusion.1.refs_0_), channel_id=1, source_target_pairs={{0,6},{1,7},{2,4},{3,5},{4,2},{5,3},{6,0},{7,1},{8,14},{9,15},{10,... | collective-permute-start | bytes 884744 | tf_op jit(solution)/shard_map/ppermute | solution.py:43
  11.4 23.8 %collective-permute-start.5 = (bf16[64,1152]{1,0:T(8,128)(2,1)}, bf16[64,1152]{1,0:T(8,128)(2,1)S(1)}, u32[]{:S(2)}, u32[]{:S(2)}) collective-permute-start(bf16[64,1152]{1,0:T(8,128)(2,1)} %bitcast.9), channel_id=1, source_target_pairs={{0,1},{1,0},{2,3},{3,2},{4,5},{5,4},{6,7},{7,6},{8,9},{9,8},{10,11... | collective-permute-start | bytes 442376 | tf_op jit(solution)/shard_map/ppermute | solution.py:47
  12.7 22.5 %all-to-all-start = ((f32[128,1,256]{2,1,0:T(1,128)}), f32[128,1,256]{2,1,0:T(1,128)S(1)}, u32[]{:S(2)}, u32[]{:S(2)}) async-start(f32[128,1,256]{2,1,0:T(1,128)} %get-tuple-element.35), calls=%async_computation | async-start | bytes 262144 | tf_op jit(solution)/shard_map/all_to_all | solution.py:431
  35.2 80.5 %collective-permute-start.24 = (bf16[1536,1152]{1,0:T(8,128)(2,1)}, bf16[1536,1152]{1,0:T(8,128)(2,1)}, u32[]{:S(2)}, u32[]{:S(2)}) collective-permute-start(bf16[1536,1152]{1,0:T(8,128)(2,1)} %refs_4_.3), channel_id=1, source_target_pairs={{0,1},{1,0},{2,3},{3,2},{4,5},{5,4},{6,7},{7,6},{8,9},{9,8},{10,11... | collective-permute-start | bytes 10616840 | tf_op jit(solution)/shard_map/ppermute | solution.py:47
  35.8 2.0 %copy-start.1 = (bf16[1152,1536]{1,0:T(8,128)(2,1)S(1)}, bf16[1152,1536]{1,0:T(8,128)(2,1)}, u32[]{:S(2)}) copy-start(bf16[1152,1536]{1,0:T(8,128)(2,1)} %refs_4_.2) | copy-start | bytes 10616836
  37.8 0.9 copy-start.4
  45.9 11.6 %collective-permute-start.6 = (bf16[128,3200]{1,0:T(8,128)(2,1)S(1)}, bf16[128,3200]{1,0:T(8,128)(2,1)S(1)}, u32[]{:S(2)}, u32[]{:S(2)}) collective-permute-start(bf16[128,3200]{1,0:T(8,128)(2,1)S(1)} %get-tuple-element.38), channel_id=1, source_target_pairs={{0,32},{1,9},{2,34},{3,11},{4,36},{5,13},{6,38},{7,15},{8,40},{9,1... | collective-permute-start | bytes 2457608 | tf_op jit(solution)/shard_map/ppermute | solution.py:35
  46.7 19.6 %collective-permute-start.7 = (bf16[128,3200]{1,0:T(8,128)(2,1)S(1)}, bf16[128,3200]{1,0:T(8,128)(2,1)S(1)}, u32[]{:S(2)}, u32[]{:S(2)}) collective-permute-start(bf16[128,3200]{1,0:T(8,128)(2,1)S(1)} %get-tuple-element.39), channel_id=1, source_target_pairs={{0,64},{1,17},{2,66},{3,19},{4,68},{5,21},{6,70},{7,23},{8,72},{9,... | collective-permute-start | bytes 2457608 | tf_op jit(solution)/shard_map/ppermute | solution.py:35
  47.4 21.5 %collective-permute-start.8 = (bf16[128,3200]{1,0:T(8,128)(2,1)S(1)}, bf16[128,3200]{1,0:T(8,128)(2,1)S(1)}, u32[]{:S(2)}, u32[]{:S(2)}) collective-permute-start(bf16[128,3200]{1,0:T(8,128)(2,1)S(1)} %get-tuple-element.40), channel_id=1, source_target_pairs={{0,96},{1,25},{2,98},{3,27},{4,100},{5,29},{6,102},{7,31},{8,104},... | collective-permute-start | bytes 2457608 | tf_op jit(solution)/shard_map/ppermute | solution.py:35
  68.9 3.1 %copy-start = (s32[4]{0:T(128)S(1)}, s32[4]{0:T(128)}, u32[]{:S(2)}) copy-start(s32[4]{0:T(128)} %lengths.1) | copy-start | bytes 52
  69.3 6.3 %collective-permute-start.10 = (bf16[32,3200]{1,0:T(8,128)(2,1)S(1)}, bf16[32,3200]{1,0:T(8,128)(2,1)S(1)}, u32[]{:S(2)}, u32[]{:S(2)}) collective-permute-start(bf16[32,3200]{1,0:T(8,128)(2,1)S(1)} %get-tuple-element.43), channel_id=1, source_target_pairs={{0,16},{1,65},{2,18},{3,67},{4,20},{5,69},{6,22},{7,71},{8,24},{9,... | collective-permute-start | bytes 614408 | tf_op jit(solution)/shard_map/ppermute | solution.py:39
  70.2 7.8 %collective-permute-start.11 = (bf16[32,3200]{1,0:T(8,128)(2,1)S(1)}, bf16[32,3200]{1,0:T(8,128)(2,1)S(1)}, u32[]{:S(2)}, u32[]{:S(2)}) collective-permute-start(bf16[32,3200]{1,0:T(8,128)(2,1)S(1)} %get-tuple-element.44), channel_id=1, source_target_pairs={{0,24},{1,97},{2,26},{3,99},{4,28},{5,101},{6,30},{7,103},{8,16},{... | collective-permute-start | bytes 614408 | tf_op jit(solution)/shard_map/ppermute | solution.py:39
  71.9 6.1 %collective-permute-start.9 = (bf16[32,3200]{1,0:T(8,128)(2,1)S(1)}, bf16[32,3200]{1,0:T(8,128)(2,1)S(1)}, u32[]{:S(2)}, u32[]{:S(2)}) collective-permute-start(bf16[32,3200]{1,0:T(8,128)(2,1)S(1)} %get-tuple-element.42), channel_id=1, source_target_pairs={{0,8},{1,33},{2,10},{3,35},{4,12},{5,37},{6,14},{7,39},{8,0},{9,41... | collective-permute-start | bytes 614408 | tf_op jit(solution)/shard_map/ppermute | solution.py:39
  78.7 4.1 %collective-permute-start.12 = (bf16[8,3200]{1,0:T(8,128)(2,1)S(1)}, bf16[8,3200]{1,0:T(8,128)(2,1)S(1)}, u32[]{:S(2)}, u32[]{:S(2)}) collective-permute-start(bf16[8,3200]{1,0:T(8,128)(2,1)S(1)} %get-tuple-element.46), channel_id=1, source_target_pairs={{0,2},{1,3},{2,0},{3,1},{4,6},{5,7},{6,4},{7,5},{8,10},{9,11},{10,... | collective-permute-start | bytes 153608 | tf_op jit(solution)/shard_map/ppermute | solution.py:43
  78.8 4.5 %collective-permute-start.13 = (bf16[8,3200]{1,0:T(8,128)(2,1)S(1)}, bf16[8,3200]{1,0:T(8,128)(2,1)S(1)}, u32[]{:S(2)}, u32[]{:S(2)}) collective-permute-start(bf16[8,3200]{1,0:T(8,128)(2,1)S(1)} %get-tuple-element.47), channel_id=1, source_target_pairs={{0,4},{1,5},{2,6},{3,7},{4,0},{5,1},{6,2},{7,3},{8,12},{9,13},{10,... | collective-permute-start | bytes 153608 | tf_op jit(solution)/shard_map/ppermute | solution.py:43
  80.2 4.2 %collective-permute-start.14 = (bf16[8,3200]{1,0:T(8,128)(2,1)S(1)}, bf16[8,3200]{1,0:T(8,128)(2,1)S(1)}, u32[]{:S(2)}, u32[]{:S(2)}) collective-permute-start(bf16[8,3200]{1,0:T(8,128)(2,1)S(1)} %get-tuple-element.48), channel_id=1, source_target_pairs={{0,6},{1,7},{2,4},{3,5},{4,2},{5,3},{6,0},{7,1},{8,14},{9,15},{10,... | collective-permute-start | bytes 153608 | tf_op jit(solution)/shard_map/ppermute | solution.py:43
  84.3 50.6 %copy-start.2 = (bf16[1536,1152]{1,0:T(8,128)(2,1)S(1)}, bf16[1536,1152]{1,0:T(8,128)(2,1)}, u32[]{:S(2)}) copy-start(bf16[1536,1152]{1,0:T(8,128)(2,1)} %refs_4_.3) | copy-start | bytes 10616836
  92.1 3.9 %collective-permute-start.15 = (bf16[8,3072]{1,0:T(8,128)(2,1)S(1)}, bf16[8,3072]{1,0:T(8,128)(2,1)S(1)}, u32[]{:S(2)}, u32[]{:S(2)}) collective-permute-start(bf16[8,3072]{1,0:T(8,128)(2,1)S(1)} %get-tuple-element.50), channel_id=1, source_target_pairs={{0,2},{1,3},{2,0},{3,1},{4,6},{5,7},{6,4},{7,5},{8,10},{9,11},{10,... | collective-permute-start | bytes 147464 | tf_op jit(solution)/shard_map/ppermute | solution.py:43
  92.6 5.3 %collective-permute-start.16 = (bf16[8,3072]{1,0:T(8,128)(2,1)S(1)}, bf16[8,3072]{1,0:T(8,128)(2,1)S(1)}, u32[]{:S(2)}, u32[]{:S(2)}) collective-permute-start(bf16[8,3072]{1,0:T(8,128)(2,1)S(1)} %get-tuple-element.51), channel_id=1, source_target_pairs={{0,4},{1,5},{2,6},{3,7},{4,0},{5,1},{6,2},{7,3},{8,12},{9,13},{10,... | collective-permute-start | bytes 147464 | tf_op jit(solution)/shard_map/ppermute | solution.py:43
  95.8 4.2 %collective-permute-start.17 = (bf16[8,3072]{1,0:T(8,128)(2,1)S(1)}, bf16[8,3072]{1,0:T(8,128)(2,1)S(1)}, u32[]{:S(2)}, u32[]{:S(2)}) collective-permute-start(bf16[8,3072]{1,0:T(8,128)(2,1)S(1)} %get-tuple-element.52), channel_id=1, source_target_pairs={{0,6},{1,7},{2,4},{3,5},{4,2},{5,3},{6,0},{7,1},{8,14},{9,15},{10,... | collective-permute-start | bytes 147464 | tf_op jit(solution)/shard_map/ppermute | solution.py:43
  100.6 4.9 %collective-permute-start.18 = (bf16[32,3072]{1,0:T(8,128)(2,1)S(1)}, bf16[32,3072]{1,0:T(8,128)(2,1)S(1)}, u32[]{:S(2)}, u32[]{:S(2)}) collective-permute-start(bf16[32,3072]{1,0:T(8,128)(2,1)S(1)} %line_up.1), channel_id=1, source_target_pairs={{0,32},{1,9},{2,34},{3,11},{4,36},{5,13},{6,38},{7,15},{8,40},{9,1... | collective-permute-start | bytes 589832 | tf_op jit(solution)/shard_map/ppermute | solution.py:35
  100.7 9.1 %collective-permute-start.19 = (bf16[32,3072]{1,0:T(8,128)(2,1)S(1)}, bf16[32,3072]{1,0:T(8,128)(2,1)S(1)}, u32[]{:S(2)}, u32[]{:S(2)}) collective-permute-start(bf16[32,3072]{1,0:T(8,128)(2,1)S(1)} %line_up.1), channel_id=1, source_target_pairs={{0,64},{1,17},{2,66},{3,19},{4,68},{5,21},{6,70},{7,23},{8,72},{9,... | collective-permute-start | bytes 589832 | tf_op jit(solution)/shard_map/ppermute | solution.py:35
  104.5 7.3 %collective-permute-start.20 = (bf16[32,3072]{1,0:T(8,128)(2,1)S(1)}, bf16[32,3072]{1,0:T(8,128)(2,1)S(1)}, u32[]{:S(2)}, u32[]{:S(2)}) collective-permute-start(bf16[32,3072]{1,0:T(8,128)(2,1)S(1)} %line_up.1), channel_id=1, source_target_pairs={{0,96},{1,25},{2,98},{3,27},{4,100},{5,29},{6,102},{7,31},{8,104},... | collective-permute-start | bytes 589832 | tf_op jit(solution)/shard_map/ppermute | solution.py:35
  111.8 11.2 %collective-permute-start.21 = (bf16[128,3072]{1,0:T(8,128)(2,1)S(1)}, bf16[128,3072]{1,0:T(8,128)(2,1)S(1)}, u32[]{:S(2)}, u32[]{:S(2)}) collective-permute-start(bf16[128,3072]{1,0:T(8,128)(2,1)S(1)} %pad_maximum_fusion.refs_0_), channel_id=1, source_target_pairs={{0,8},{1,33},{2,10},{3,35},{4,12},{5,37},{6,14},{7,39},{8,0},{9,41... | collective-permute-start | bytes 2359304 | tf_op jit(solution)/shard_map/ppermute | solution.py:39
  111.9 20.9 %collective-permute-start.22 = (bf16[128,3072]{1,0:T(8,128)(2,1)S(1)}, bf16[128,3072]{1,0:T(8,128)(2,1)S(1)}, u32[]{:S(2)}, u32[]{:S(2)}) collective-permute-start(bf16[128,3072]{1,0:T(8,128)(2,1)S(1)} %pad_maximum_fusion.refs_0_), channel_id=1, source_target_pairs={{0,16},{1,65},{2,18},{3,67},{4,20},{5,69},{6,22},{7,71},{8,24},{9,... | collective-permute-start | bytes 2359304 | tf_op jit(solution)/shard_map/ppermute | solution.py:39
  113.6 21.3 %collective-permute-start.23 = (bf16[128,3072]{1,0:T(8,128)(2,1)S(1)}, bf16[128,3072]{1,0:T(8,128)(2,1)S(1)}, u32[]{:S(2)}, u32[]{:S(2)}) collective-permute-start(bf16[128,3072]{1,0:T(8,128)(2,1)S(1)} %pad_maximum_fusion.refs_0_), channel_id=1, source_target_pairs={{0,24},{1,97},{2,26},{3,99},{4,28},{5,101},{6,30},{7,103},{8,16},{... | collective-permute-start | bytes 2359304 | tf_op jit(solution)/shard_map/ppermute | solution.py:39
  142.7 5.7 %collective-permute-start.25 = (bf16[128,1152]{1,0:T(8,128)(2,1)S(1)}, bf16[128,1152]{1,0:T(8,128)(2,1)S(1)}, u32[]{:S(2)}, u32[]{:S(2)}) collective-permute-start(bf16[128,1152]{1,0:T(8,128)(2,1)S(1)} %get-tuple-element.54), channel_id=1, source_target_pairs={{0,2},{1,3},{2,0},{3,1},{4,6},{5,7},{6,4},{7,5},{8,10},{9,11},{10,... | collective-permute-start | bytes 884744 | tf_op jit(solution)/shard_map/ppermute | solution.py:43
  142.8 8.7 %collective-permute-start.26 = (bf16[128,1152]{1,0:T(8,128)(2,1)S(1)}, bf16[128,1152]{1,0:T(8,128)(2,1)S(1)}, u32[]{:S(2)}, u32[]{:S(2)}) collective-permute-start(bf16[128,1152]{1,0:T(8,128)(2,1)S(1)} %get-tuple-element.55), channel_id=1, source_target_pairs={{0,4},{1,5},{2,6},{3,7},{4,0},{5,1},{6,2},{7,3},{8,12},{9,13},{10,... | collective-permute-start | bytes 884744 | tf_op jit(solution)/shard_map/ppermute | solution.py:43
  144.2 9.9 %collective-permute-start.27 = (bf16[128,1152]{1,0:T(8,128)(2,1)S(1)}, bf16[128,1152]{1,0:T(8,128)(2,1)S(1)}, u32[]{:S(2)}, u32[]{:S(2)}) collective-permute-start(bf16[128,1152]{1,0:T(8,128)(2,1)S(1)} %get-tuple-element.56), channel_id=1, source_target_pairs={{0,6},{1,7},{2,4},{3,5},{4,2},{5,3},{6,0},{7,1},{8,14},{9,15},{10,... | collective-permute-start | bytes 884744 | tf_op jit(solution)/shard_map/ppermute | solution.py:43
  154.3 12.5 %collective-permute-start.28 = (bf16[64,1152]{1,0:T(8,128)(2,1)S(1)}, bf16[64,1152]{1,0:T(8,128)(2,1)S(1)}, u32[]{:S(2)}, u32[]{:S(2)}) collective-permute-start(bf16[64,1152]{1,0:T(8,128)(2,1)S(1)} %get-tuple-element.58), channel_id=1, source_target_pairs={{0,1},{1,0},{2,3},{3,2},{4,5},{5,4},{6,7},{7,6},{8,9},{9,8},{10,11... | collective-permute-start | bytes 442376 | tf_op jit(solution)/shard_map/ppermute | solution.py:47

commit v5 on v4

--- a/solution.py
+++ b/solution.py
@@ -1,3 +1,5 @@
+import functools
+
 import jax
 import jax.numpy as jnp
 from jax import lax
@@ -51,16 +53,17 @@
     return [parts[0]] + [along(parts[m], m) for m in range(1, 4)]
 
 
-def groups_of(rows, first, count):
-    return jnp.concatenate([rows[16 * i + first : 16 * i + first + 8] for i in range(count)], axis=0)
-
-
-def prepare_kernel(place, tokens, stats, mine, theirs):
-    rows = tokens[...].astype(F32)
-    by_core = [groups_of(rows, 0, 8), groups_of(rows, 8, 8)]
+def groups_of(rows, first):
+    groups = [rows[at + first : at + first + 8] for at in range(0, rows.shape[0], 16)]
+    return jnp.concatenate(groups, axis=0)
+
+
+def prepare_kernel(place, tokens, theirs, stats, piece):
+    rows, others = tokens[...].astype(F32), theirs[...].astype(F32)
+    by_core = [groups_of(rows, 0), groups_of(rows, 8)]
     swap = place[3] == 1
-    mine[...] = jnp.where(swap, by_core[1], by_core[0]).astype(BF16)
-    theirs[...] = jnp.where(swap, by_core[0], by_core[1]).astype(BF16)
+    piece[:64] = jnp.where(swap, by_core[1], by_core[0]).astype(BF16)
+    piece[64:] = jnp.where(swap, groups_of(others, 8), groups_of(others, 0)).astype(BF16)
     lines = []
     for power in range(2):
         sums = [
@@ -72,17 +75,19 @@
     stats[...] = jnp.broadcast_to(line[:, None, :], stats.shape)
 
 
-def prepare(place, tokens):
-    half = jax.ShapeDtypeStruct((64, tokens.shape[1]), BF16)
+def prepare(place, tokens, theirs):
     return pl.pallas_call(
         prepare_kernel,
-        out_shape=[jax.ShapeDtypeStruct((128, 1, 256), F32), half, half],
-        in_specs=[SMEM, VMEM],
-        out_specs=[VMEM] * 3,
+        out_shape=[
+            jax.ShapeDtypeStruct((128, 1, 256), F32),
+            jax.ShapeDtypeStruct(tokens.shape, BF16),
+        ],
+        in_specs=[SMEM, VMEM, VMEM],
+        out_specs=[VMEM] * 2,
         compiler_params=params(8),
         cost_estimate=cost(1e8, 1e6),
         name="prepare",
-    )(place, tokens)
+    )(place, tokens, theirs)
 
 
 def load_tiles(source, tiles, sems, at):
@@ -97,74 +102,167 @@
     return loads
 
 
-def project_kernel(place, stats, gain, *refs):
-    pieces, weights, pairs, outs = refs[:4], refs[4:6], refs[6:8], refs[8:12]
-    normed, mean_of, scale_of, tiles, sems = refs[12:]
+def fill_left(blocks, place, gain, pieces, left):
+    y, z, x, c = place[0], place[1], place[2], place[3]
+    gains = gain[...].astype(F32)
+    along_y = c == 0
+    for m in range(4):
+        to_y = x ^ m ^ y
+        for j in range(2):
+            for b in range(2):
+                to_z = ((c ^ j) * 2 + b) ^ z
+                first = jnp.where(along_y, to_y, to_z)
+                second = jnp.where(along_y, to_z, to_y)
+
+                @pl.when((first == blocks[0]) | (first == blocks[1]))
+                def _():
+                    at = j * 64 + b * 32
+                    rows = pieces[m][at : at + 32, :].astype(F32)
+                    rows = rows - jnp.sum(rows, axis=1, keepdims=True) / rows.shape[1]
+                    slot = jnp.where(first == blocks[0], 0, 4) + second
+                    left[pl.ds(pl.multiple_of(slot * 32, 32), 32)] = (rows * gains).astype(BF16)
+
+
+def multiply(left, tiles, loads, pairs, put):
+    wide = tiles.shape[2]
+    width = tiles.shape[0] * wide
+    pair = jnp.concatenate([pairs[0][...], pairs[1][...]], axis=0)
+    dims = (((1,), (1,)), ((), ()))
+    put(lax.dot_general(left[...], pair, dims, preferred_element_type=F32), width, pair.shape[0])
+    for t, load in enumerate(loads):
+        load.wait()
+        put(jnp.dot(left[...], tiles[t], preferred_element_type=F32), t * wide, wide)
+
+
+def load_both(weights, tiles, sems):
     count = tiles.shape[0] // 2
-    loads = load_tiles(weights[0], tiles, sems, 0) + load_tiles(weights[1], tiles, sems, count)
-    y, z, x, c = place[0], place[1], place[2], place[3]
+    return load_tiles(weights[0], tiles, sems, 0) + load_tiles(weights[1], tiles, sems, count)
+
+
+def project_kernel(blocks, place, gain, *refs):
+    pieces, weights, pairs = refs[:4], refs[4:6], refs[6:8]
+    out, gain_row, left, tiles, sems = refs[8:]
+    loads = load_both(weights, tiles, sems)
+    left[256:] = jnp.broadcast_to(gain[...], (16, gain.shape[1]))
+    fill_left(blocks, place, gain, pieces, left)
+
+    def put(part, at, size):
+        out[:, at : at + size] = part[:256].astype(BF16)
+        gain_row[:, at : at + size] = part[256:264]
+
+    multiply(left, tiles, loads, pairs, put)
+
+
+def project_scratch(rows, weights):
+    depth, width = weights[0].shape
+    count = 2 * width // 512
+    return [
+        pltpu.VMEM((rows, depth), BF16),
+        pltpu.VMEM((count, depth, 512), BF16),
+        pltpu.SemaphoreType.DMA((count,)),
+    ]
+
+
+def project(blocks, place, gain, pieces, weights, pairs):
+    total = 2 * (weights[0].shape[1] + pairs[0].shape[0])
+    return pl.pallas_call(
+        functools.partial(project_kernel, blocks),
+        out_shape=[
+            jax.ShapeDtypeStruct((256, total), BF16),
+            jax.ShapeDtypeStruct((8, total), F32),
+        ],
+        in_specs=[SMEM] + [VMEM] * 5 + [ANY] * 2 + [VMEM] * 2,
+        out_specs=[VMEM] * 2,
+        scratch_shapes=project_scratch(272, weights),
+        compiler_params=params(48),
+        cost_estimate=cost(4e9, 1e7),
+        name="project",
+    )(place, gain, *pieces, *weights, *pairs)
+
+
+def fill_columns(place, stats, shift_of, scale_of):
+    y, z = place[0], place[1]
     total = stats[0:8, :]
     for g in range(1, 16):
         total = total + stats[g * 8 : g * 8 + 8, :]
     mean = total[:, :128] / D
     variance = total[:, 128:] / D - mean * mean
-    mean_columns = mean.T
+    here = stats[pl.ds(pl.multiple_of((y * 4 + z) * 8, 8), 8), :]
+    shift_columns = (here[:, :128] / (D // 16) - mean).T
     scale_columns = lax.rsqrt(variance + 1e-05).T
     for s in range(8):
-        mean_of[s] = mean_columns[:, s : s + 1]
+        shift_of[s] = shift_columns[:, s : s + 1]
         scale_of[s] = scale_columns[:, s : s + 1]
-    gains = gain[...].astype(F32)
-    along_y = c == 0
-    for m in range(4):
-        to_y = x ^ m ^ y
-        for j in range(2):
-            source_c = c ^ j
-            s = (x ^ m) * 2 + source_c
-            rows = pieces[m][j * 64 : j * 64 + 64, :].astype(F32)
-            of_core = pl.ds(pl.multiple_of(c * 64, 64), 64)
-            rows = ((rows - mean_of[s, of_core]) * scale_of[s, of_core] * gains).astype(BF16)
-            for b in range(2):
-                to_z = (source_c * 2 + b) ^ z
-                first = jnp.where(along_y, to_y, to_z)
-                second = jnp.where(along_y, to_z, to_y)
-                normed[first, second] = rows[b * 32 : b * 32 + 32]
-    left = normed[...].reshape(512, normed.shape[-1])
+
+
+def columns_of(place, block, second):
+    y, z, c = place[0], place[1], place[3]
+    token_y = y ^ jnp.where(c == 0, block, second)
+    token_z = z ^ jnp.where(c == 0, second, block)
+    rows = pl.ds(pl.multiple_of(c * 64 + token_z % 2 * 32, 32), 32)
+    return token_y * 2 + token_z // 2, rows
+
+
+def scale_kernel(blocks, place, stats, gain_row, parts, *refs):
+    outs, shift_of, scale_of = refs[:2], refs[2], refs[3]
+    fill_columns(place, stats, shift_of, scale_of)
+    line = gain_row[0:1, :]
+    for i, out in enumerate(outs):
+        for second in range(4):
+            s, at = columns_of(place, blocks[i], second)
+            rows = parts[i * 128 + second * 32 : i * 128 + second * 32 + 32, :]
+            rows = (rows.astype(F32) + shift_of[s, at] * line) * scale_of[s, at]
+            out[second * 32 : second * 32 + 32, :] = rows.astype(BF16)
+
+
+def scale(blocks, place, stats, gain_row, parts):
+    out = jax.ShapeDtypeStruct((128, parts.shape[1]), BF16)
+    return pl.pallas_call(
+        functools.partial(scale_kernel, blocks),
+        out_shape=[out] * 2,
+        in_specs=[SMEM] + [VMEM] * 3,
+        out_specs=[VMEM] * 2,
+        scratch_shapes=[pltpu.VMEM((8, 128, 1), F32)] * 2,
+        compiler_params=params(12),
+        cost_estimate=cost(1e9, 2e6),
+        name="scale",
+    )(place, stats, gain_row, parts)
+
+
+def project_rest_kernel(blocks, place, stats, gain_row, gain, *refs):
+    pieces, weights, pairs = refs[:4], refs[4:6], refs[6:8]
+    outs, (left, tiles, sems, shift_of, scale_of, shift, factor) = refs[8:10], refs[10:]
+    loads = load_both(weights, tiles, sems)
+    fill_columns(place, stats, shift_of, scale_of)
+    for k in range(8):
+        s, at = columns_of(place, blocks[k // 4], k % 4)
+        shift[k * 32 : k * 32 + 32] = shift_of[s, at]
+        factor[k * 32 : k * 32 + 32] = scale_of[s, at]
+    fill_left(blocks, place, gain, pieces, left)
 
     def put(part, at, size):
-        for k, out in enumerate(outs):
-            out[:, at : at + size] = part[k * 128 : k * 128 + 128]
-
-    dims = (((1,), (1,)), ((), ()))
-    wide = tiles.shape[2]
-    width = tiles.shape[0] * wide
-    pair = jnp.concatenate([pairs[0][...], pairs[1][...]], axis=0)
-    pair = lax.dot_general(left, pair, dims, preferred_element_type=F32).astype(BF16)
-    put(pair, width, pair.shape[1])
-    for t, load in enumerate(loads):
-        load.wait()
-        put(jnp.dot(left, tiles[t], preferred_element_type=F32).astype(BF16), t * wide, wide)
-
-
-def project(place, stats, gain, pieces, weights, pairs):
-    depth, width = weights[0].shape
-    out = jax.ShapeDtypeStruct((128, 2 * (width + pairs[0].shape[0])), BF16)
-    count = 2 * width // 512
-    return pl.pallas_call(
-        project_kernel,
-        out_shape=[out] * 4,
-        in_specs=[SMEM] + [VMEM] * 6 + [ANY] * 2 + [VMEM] * 2,
-        out_specs=[VMEM] * 4,
-        scratch_shapes=[
-            pltpu.VMEM((4, 4, 32, depth), BF16),
-            pltpu.VMEM((8, 128, 1), F32),
-            pltpu.VMEM((8, 128, 1), F32),
-            pltpu.VMEM((count, depth, 512), BF16),
-            pltpu.SemaphoreType.DMA((count,)),
-        ],
-        compiler_params=params(32),
-        cost_estimate=cost(8e9, 1.2e7),
-        name="project",
-    )(place, stats, gain, *pieces, *weights, *pairs)
+        line = gain_row[0:1, at : at + size]
+        part = ((part + shift[...] * line) * factor[...]).astype(BF16)
+        for i, out in enumerate(outs):
+            out[:, at : at + size] = part[i * 128 : i * 128 + 128]
+
+    multiply(left, tiles, loads, pairs, put)
+
+
+def project_rest(blocks, place, stats, gain_row, gain, pieces, weights, pairs):
+    out = jax.ShapeDtypeStruct((128, gain_row.shape[1]), BF16)
+    return pl.pallas_call(
+        functools.partial(project_rest_kernel, blocks),
+        out_shape=[out] * 2,
+        in_specs=[SMEM] + [VMEM] * 7 + [ANY] * 2 + [VMEM] * 2,
+        out_specs=[VMEM] * 2,
+        scratch_shapes=project_scratch(256, weights)
+        + [pltpu.VMEM((8, 128, 1), F32)] * 2
+        + [pltpu.VMEM((256, 1), F32)] * 2,
+        compiler_params=params(48),
+        cost_estimate=cost(5e9, 1e7),
+        name="project_rest",
+    )(place, stats, gain_row, gain, *pieces, *weights, *pairs)
 
 
 def sum_of(refs):
@@ -334,48 +432,84 @@
     )(lengths, place, *packed, cosine, sine, cache_keys, cache_values)
 
 
-def mix_kernel(place, *refs):
-    lefts, weights, outs = refs[:4], refs[4:6], refs[6:10]
-    rows, tiles, sems = refs[10:]
+def multiply_rows(lefts, tiles, loads, put):
+    left = jnp.concatenate([ref[...] for ref in lefts], axis=0)
+    depth = left.shape[1] // 2
     count = tiles.shape[0] // 2
-    loads = load_tiles(weights[0], tiles, sems, 0) + load_tiles(weights[1], tiles, sems, count)
-    y, z, x, c = place[0], place[1], place[2], place[3]
-    along_y = c == 0
-    for second in range(4):
-        for first in range(4):
-            to_x = y ^ x ^ jnp.where(along_y, first, second)
-            token_z = z ^ jnp.where(along_y, second, first)
-            slot = (token_z // 2 ^ c) * 2 + token_z % 2
-            rows[to_x, slot] = lefts[second][first * 32 : first * 32 + 32, :]
-    left = rows[...].reshape(512, rows.shape[-1])
-    depth = left.shape[1] // 2
     wide = tiles.shape[2]
     for t in range(count):
         loads[t].wait()
         part = jnp.dot(left[:, :depth], tiles[t], preferred_element_type=F32)
         loads[count + t].wait()
         part = part + jnp.dot(left[:, depth:], tiles[count + t], preferred_element_type=F32)
-        part = part.astype(BF16)
-        for k, out in enumerate(outs):
-            out[:, t * wide : t * wide + wide] = part[k * 128 : k * 128 + 128]
-
-
-def mix(place, lefts, weights):
+        put(part.astype(BF16), t * wide, wide)
+
+
+def mix_kernel(*refs):
+    lefts, weights, out, tiles, sems = refs[:3], refs[3:5], refs[5], refs[6], refs[7]
+    loads = load_tiles(weights[0], tiles, sems, 0) + load_tiles(weights[1], tiles, sems, 3)
+
+    def put(part, at, size):
+        out[:, at : at + size] = part
+
+    multiply_rows(lefts, tiles, loads, put)
+
+
+def mix_rest_kernel(place, done, last, *refs):
+    weights, outs = refs[:2], refs[2:6]
+    result, tiles, sems = refs[6:]
+    loads = load_tiles(weights[0], tiles, sems, 0) + load_tiles(weights[1], tiles, sems, 3)
+    y, z, x, c = place[0], place[1], place[2], place[3]
+    along_y = c == 0
+
+    def slots(second, first):
+        to_x = y ^ x ^ jnp.where(along_y, first, second)
+        token_z = z ^ jnp.where(along_y, second, first)
+        return to_x, (token_z // 2 ^ c) * 2 + token_z % 2
+
+    for k in range(12):
+        result[slots((0, 1, 3)[k // 4], k % 4)] = done[k * 32 : k * 32 + 32, :]
+
+    def put(part, at, size):
+        for k in range(4):
+            to_x, slot = slots(2, k)
+            result[to_x, slot, :, at : at + size] = part[k * 32 : k * 32 + 32]
+
+    multiply_rows([last], tiles, loads, put)
+    for k, out in enumerate(outs):
+        out[...] = result[k].reshape(out.shape)
+
+
+def mix_scratch(depth, width):
+    return [pltpu.VMEM((6, depth, width // 3), BF16), pltpu.SemaphoreType.DMA((6,))]
+
+
+def mix(lefts, weights):
     depth, width = weights[0].shape
     return pl.pallas_call(
         mix_kernel,
+        out_shape=jax.ShapeDtypeStruct((384, width), BF16),
+        in_specs=[VMEM] * 3 + [ANY] * 2,
+        out_specs=VMEM,
+        scratch_shapes=mix_scratch(depth, width),
+        compiler_params=params(24),
+        cost_estimate=cost(4e9, 8e6),
+        name="mix",
+    )(*lefts, *weights)
+
+
+def mix_rest(place, done, last, weights):
+    depth, width = weights[0].shape
+    return pl.pallas_call(
+        mix_rest_kernel,
         out_shape=[jax.ShapeDtypeStruct((128, width), BF16)] * 4,
-        in_specs=[SMEM] + [VMEM] * 4 + [ANY] * 2,
+        in_specs=[SMEM] + [VMEM] * 2 + [ANY] * 2,
         out_specs=[VMEM] * 4,
-        scratch_shapes=[
-            pltpu.VMEM((4, 4, 32, 2 * depth), BF16),
-            pltpu.VMEM((6, depth, width // 3), BF16),
-            pltpu.SemaphoreType.DMA((6,)),
-        ],
-        compiler_params=params(32),
-        cost_estimate=cost(8e9, 1.2e7),
-        name="mix",
-    )(place, *lefts, *weights)
+        scratch_shapes=[pltpu.VMEM((4, 4, 32, width), BF16)] + mix_scratch(depth, width),
+        compiler_params=params(24),
+        cost_estimate=cost(4e9, 8e6),
+        name="mix_rest",
+    )(place, done, last, *weights)
 
 
 def last_sum_kernel(*refs):
@@ -424,16 +558,19 @@
     gx, gy = lax.axis_index("gx"), lax.axis_index("gy")
     place = jnp.stack([gx // 4, gx % 4, gy // 2, gy % 2]).astype(jnp.int32)
 
-    stats, mine, theirs = prepare(place, tokens)
-    piece = jnp.concatenate([mine, other_core(theirs)], axis=0)
-    piece, stats = lax.optimization_barrier((piece, stats))
+    stats, piece = prepare(place, tokens, other_core(tokens))
     pieces = exchanged(along_x, [piece] * 4)
-    stats = lax.all_to_all(stats, ("gx", "gy"), 0, 0, tiled=True).reshape(128, 256)
+    stats = lax.all_to_all(stats, ("gx", "gy"), 0, 0, tiled=True)
     w_pair = w_keyvalue.T
-    weights = [w_query, other_core(w_query)]
-    parts = project(
-        place, stats, norm_gain[None], pieces, weights, [w_pair, other_core(w_pair)]
-    )
+    w_query, w_pair, piece = lax.optimization_barrier((w_query, w_pair, piece))
+    weights, pairs = [w_query, other_core(w_query)], [w_pair, other_core(w_pair)]
+    gain = norm_gain[None]
+    parts, gain_row = project((1, 3), place, gain, pieces, weights, pairs)
+    parts, stats = lax.optimization_barrier((parts, stats))
+    stats = stats.reshape(128, 256)
+    sent = scale((1, 3), place, stats, gain_row, parts)
+    kept = project_rest((2, 0), place, stats, gain_row, gain, pieces, weights, pairs)
+    parts = [kept[1], sent[0], kept[0], sent[1]]
 
     parts = add_and_cut(exchanged(along_first, parts))
     parts = finish(place, exchanged(along_second, parts))
@@ -456,7 +593,12 @@
 
     rows = line_up(place, exchanged(along_x, attended))
     rows = jnp.concatenate(exchanged(along_first, [rows] * 4), axis=0)
-    parts = mix(place, exchanged(along_second, [rows] * 4), [w_out, other_core(w_out)])
+    near = [along_second(rows, 1), along_second(rows, 3)]
+    late, *near = lax.optimization_barrier((rows, *near))
+    blocks = [rows, near[0], along_second(late, 2), near[1]]
+    weights = [w_out, other_core(w_out)]
+    done = mix([blocks[0], blocks[1], blocks[3]], weights)
+    parts = mix_rest(place, done, blocks[2], weights)
     mine, theirs = last_sum(exchanged(along_x, parts))
     return interleave(place, mine, other_core(theirs))
 

time: 168 us -> 160 us (0.952)
  waiting for transfers between devices: 80.6 us -> 64.5 us
  Pallas kernels: 27.5 us -> 36.1 us
  local copies, waits for them, and re-layouts: 4.66 us -> 2.66 us
    all_to_all x1, waiting for transfers between devices: 11.9 us -> 2.44 us  [per_device(): stats = lax.all_to_all(stats, ('gx', 'gy'), 0, 0, tiled=True)]
    pallas_call x2 -> x5, Pallas kernels: 15 us -> 23.9 us  [the longest x1 6.78 us: mix(): pl.pallas_call(mix_kernel, out_shape=jax.ShapeDtypeStruct((384, width), B...]
    ppermute x6, waiting for transfers between devices: 26.3 us -> 18.2 us  [along_first(): return lax.ppermute(value, ('gx', 'gy'), exchange_pairs(0, m))]
    ppermute x12, waiting for transfers between devices: 13 us -> 16.7 us  [along_x(): return lax.ppermute(value, 'gy', [(g, g ^ 2 * m) for g in range(8)])]
    ppermute x5, starting transfers between devices: 14.7 us -> 16.9 us  [other_core(): return lax.ppermute(value, 'gy', [(g, g ^ 1) for g in range(8)])]
    ppermute x5, waiting for transfers between devices: 4.47 us -> 2.36 us  [other_core(): return lax.ppermute(value, 'gy', [(g, g ^ 1) for g in range(8)])]
    unnamed x11 -> x7, local copies, waits for them, and re-layouts: 3.89 us -> 1.89 us
  transfers between devices with their start and end apart: 30 -> 30, of which waited for: 21 -> 23; matrix products, arithmetic and copies ran while one was open for 1% -> 1% of each run, Pallas kernels for 11% -> 17%
where the time goes in v5:
time: 160 us
  waiting for transfers between devices  64.5 us (40%)
  starting transfers between devices  55.8 us (35%)
  Pallas kernels  36.1 us (23%)
  local copies, waits for them, and re-layouts  2.66 us (2%)
    ppermute x6, waiting for transfers between devices, along_second(): return lax.ppermute(value, ('gx', 'gy'), exchange_pairs(1, m))  24.7 us
    ppermute x6, waiting for transfers between devices, along_first(): return lax.ppermute(value, ('gx', 'gy'), exchange_pairs(0, m))  18.2 us
    ppermute x5, starting transfers between devices, other_core(): return lax.ppermute(value, 'gy', [(g, g ^ 1) for g in range(8)])  16.9 us
    ppermute x12, waiting for transfers between devices, along_x(): return lax.ppermute(value, 'gy', [(g, g ^ 2 * m) for g in range(8)])  16.7 us
    ppermute x12, starting transfers between devices, along_x(): return lax.ppermute(value, 'gy', [(g, g ^ 2 * m) for g in range(8)])  15.7 us
    all_to_all x1, starting transfers between devices, per_device(): stats = lax.all_to_all(stats, ('gx', 'gy'), 0, 0, tiled=True)  9.92 us
    pallas_call x1, Pallas kernels, attend(): pl.pallas_call(attend_kernel, out_shape=[jax.ShapeDtypeStruct((8, width),...  7.48 us
    ppermute x6, starting transfers between devices, along_first(): return lax.ppermute(value, ('gx', 'gy'), exchange_pairs(0, m))  7.34 us
  transfers between devices with their start and end apart: 30, of which 23 were waited for; matrix products, arithmetic and copies ran while one was open for 1% of the time, Pallas kernels for 17%

profile of v5, /device:TPU:1, one launch (start us, length us, event | category | flops | bytes accessed | tf_op | source)
XLA Modules:
  0.0 159.6 jit_solution(2017749154555829022)
XLA Ops:
  0.0 1.4 collective-permute-start
  1.5 1.3 collective-permute-done.theirs
  2.8 1.0 copy-done
  3.8 1.6 prepare.1
  5.4 0.4 collective-permute-start.4
  5.7 1.3 collective-permute-start.1
  7.0 2.5 %collective-permute-start.2 = (bf16[128,1152]{1,0:T(8,128)(2,1)S(1)}, bf16[128,1152]{1,0:T(8,128)(2,1)S(1)}, u32[]{:S(2)}, u32[]{:S(2)}) collective-permute-start(bf16[128,1152]{1,0:T(8,128)(2,1)S(1)} %get-tuple-element.38.refs_0_), channel_id=1, source_target_pairs={{0,4},{1,5},{2,6},{3,7},{4,0},{5,1},{6,2},{7,3},{8,12},{9,13},{10,... | collective-permute-start | bytes 884744 | tf_op jit(solution)/shard_map/ppermute | solution.py:45
  9.5 0.1 collective-permute-start.3
  9.6 1.0 collective-permute-start.5
  10.6 0.7 broadcast_in_dim.2.gain
  11.3 9.9 %all-to-all-start = ((f32[128,1,256]{2,1,0:T(1,128)}), f32[128,1,256]{2,1,0:T(1,128)S(1)}, u32[]{:S(2)}, u32[]{:S(2)}) async-start(f32[128,1,256]{2,1,0:T(1,128)} %get-tuple-element.42), calls=%async_computation | async-start | bytes 262144 | tf_op jit(solution)/shard_map/all_to_all | solution.py:563
  21.2 1.6 %collective-permute-done.2.refs_2_ = bf16[128,1152]{1,0:T(8,128)(2,1)S(1)} collective-permute-done((bf16[128,1152]{1,0:T(8,128)(2,1)S(1)}, bf16[128,1152]{1,0:T(8,128)(2,1)S(1)}, u32[]{:S(2)}, u32[]{:S(2)}) %collective-permute-start.2) | collective-permute-done | bytes 294944 | tf_op jit(solution)/shard_map/ppermute | solution.py:45
  22.9 2.1 %collective-permute-done.3.refs_3_ = bf16[128,1152]{1,0:T(8,128)(2,1)S(1)} collective-permute-done((bf16[128,1152]{1,0:T(8,128)(2,1)S(1)}, bf16[128,1152]{1,0:T(8,128)(2,1)S(1)}, u32[]{:S(2)}, u32[]{:S(2)}) %collective-permute-start.3) | collective-permute-done | bytes 294944 | tf_op jit(solution)/shard_map/ppermute | solution.py:45
  25.0 0.9 copy-done.2
  25.9 5.0 %project.1 = (bf16[256,3200]{1,0:T(8,128)(2,1)S(1)}, f32[8,3200]{1,0:T(8,128)S(1)}) custom-call(s32[4]{0:T(128)S(1)} %pad_add_fusion.place, bf16[1,1152]{1,0:T(2,128)(2,1)S(1)} %broadcast_in_dim.2.gain, bf16[128,1152]{1,0:T(8,128)(2,1)S(1)} %get-tuple-element.38.refs_0_, bf16[128,1152]{1,0:T(8,128)(2,1)S(1)} %collective-permute-done.1.refs_1_, ...), custom_call_target="tpu_custom_call" | custom-call | flops 4000000000 | bytes 10000000 | tf_op jit(solution)/shard_map/project/pallas_call | solution.py:168
  30.9 2.4 %all-to-all-done = f32[128,1,256]{2,1,0:T(1,128)S(1)} async-done(((f32[128,1,256]{2,1,0:T(1,128)}), f32[128,1,256]{2,1,0:T(1,128)S(1)}, u32[]{:S(2)}, u32[]{:S(2)}) %all-to-all-start) | async-done | bytes 131104 | tf_op jit(solution)/shard_map/all_to_all | solution.py:563
  33.4 1.6 scale.1
  35.0 0.5 collective-permute-start.6
  35.5 1.6 collective-permute-start.8
  37.0 5.4 %project_rest.1 = (bf16[128,3200]{1,0:T(8,128)(2,1)S(1)}, bf16[128,3200]{1,0:T(8,128)(2,1)S(1)}) custom-call(s32[4]{0:T(128)S(1)} %pad_add_fusion.place, f32[128,256]{1,0:T(8,128)S(1)} %bitcast.9, f32[8,3200]{1,0:T(8,128)S(1)} %get-tuple-element.44.gain_row, bf16[1,1152]{1,0:T(2,128)(2,1)S(1)} %broadcast_in_dim.2.gain, ...), custom_call_target="tpu_custom_call" | custom-call | flops 5000000000 | bytes 10000000 | tf_op jit(solution)/shard_map/project_rest/pallas_call | solution.py:254
  42.5 1.3 collective-permute-start.7
  43.8 1.3 collective-permute-start.23
  45.1 1.4 collective-permute-done.6.refs_1_
  46.5 8.6 %collective-permute-done.8.refs_3_ = bf16[128,3200]{1,0:T(8,128)(2,1)S(1)} collective-permute-done((bf16[128,3200]{1,0:T(8,128)(2,1)S(1)}, bf16[128,3200]{1,0:T(8,128)(2,1)S(1)}, u32[]{:S(2)}, u32[]{:S(2)}) %collective-permute-start.8) | collective-permute-done | bytes 819232 | tf_op jit(solution)/shard_map/ppermute | solution.py:37
  55.1 1.8 %collective-permute-done.7.refs_2_ = bf16[128,3200]{1,0:T(8,128)(2,1)S(1)} collective-permute-done((bf16[128,3200]{1,0:T(8,128)(2,1)S(1)}, bf16[128,3200]{1,0:T(8,128)(2,1)S(1)}, u32[]{:S(2)}, u32[]{:S(2)}) %collective-permute-start.7) | collective-permute-done | bytes 819232 | tf_op jit(solution)/shard_map/ppermute | solution.py:37
  56.9 0.4 add_and_cut.1
  57.3 2.7 %collective-permute-start.10 = (bf16[32,3200]{1,0:T(8,128)(2,1)S(1)}, bf16[32,3200]{1,0:T(8,128)(2,1)S(1)}, u32[]{:S(2)}, u32[]{:S(2)}) collective-permute-start(bf16[32,3200]{1,0:T(8,128)(2,1)S(1)} %get-tuple-element.52), channel_id=1, source_target_pairs={{0,16},{1,65},{2,18},{3,67},{4,20},{5,69},{6,22},{7,71},{8,24},{9,... | collective-permute-start | bytes 614408 | tf_op jit(solution)/shard_map/ppermute | solution.py:41
  60.0 0.8 collective-permute-start.11
  61.0 2.5 %collective-permute-done.10.refs_2_ = bf16[32,3200]{1,0:T(8,128)(2,1)S(1)} collective-permute-done((bf16[32,3200]{1,0:T(8,128)(2,1)S(1)}, bf16[32,3200]{1,0:T(8,128)(2,1)S(1)}, u32[]{:S(2)}, u32[]{:S(2)}) %collective-permute-start.10) | collective-permute-done | bytes 204832 | tf_op jit(solution)/shard_map/ppermute | solution.py:41
  63.5 2.6 %collective-permute-done.11.refs_3_ = bf16[32,3200]{1,0:T(8,128)(2,1)S(1)} collective-permute-done((bf16[32,3200]{1,0:T(8,128)(2,1)S(1)}, bf16[32,3200]{1,0:T(8,128)(2,1)S(1)}, u32[]{:S(2)}, u32[]{:S(2)}) %collective-permute-start.11) | collective-permute-done | bytes 204832 | tf_op jit(solution)/shard_map/ppermute | solution.py:41
  66.2 0.7 finish.1
  67.0 1.3 collective-permute-start.13
  68.2 2.6 %collective-permute-start.14 = (bf16[8,3200]{1,0:T(8,128)(2,1)S(1)}, bf16[8,3200]{1,0:T(8,128)(2,1)S(1)}, u32[]{:S(2)}, u32[]{:S(2)}) collective-permute-start(bf16[8,3200]{1,0:T(8,128)(2,1)S(1)} %get-tuple-element.57), channel_id=1, source_target_pairs={{0,6},{1,7},{2,4},{3,5},{4,2},{5,3},{6,0},{7,1},{8,14},{9,15},{10,... | collective-permute-start | bytes 153608 | tf_op jit(solution)/shard_map/ppermute | solution.py:45
  70.8 0.1 multiply_sine_fusion
  70.9 0.8 collective-permute-done.13.refs_2_
  71.7 0.7 collective-permute-done.14.refs_3_
  72.4 7.5 %attend.1 = (bf16[8,3072]{1,0:T(8,128)(2,1)S(1)}, bf16[8,3072]{1,0:T(8,128)(2,1)S(1)}, bf16[8,3072]{1,0:T(8,128)(2,1)S(1)}, bf16[8,3072]{1,0:T(8,128)(2,1)S(1)}) custom-call(s32[4]{0:T(128)S(1)} %copy-done.1, s32[4]{0:T(128)S(1)} %pad_add_fusion.place, bf16[8,3200]{1,0:T(8,128)(2,1)S(1)} %get-tuple-element.54.refs_0_, ...), custom_call_target="tpu_custom_call" | custom-call | flops 6000000000 | bytes 18000000 | tf_op jit(solution)/shard_map/attend/pallas_call | solution.py:414
  79.9 0.6 collective-permute-start.15
  80.5 3.3 %collective-permute-start.16 = (bf16[8,3072]{1,0:T(8,128)(2,1)S(1)}, bf16[8,3072]{1,0:T(8,128)(2,1)S(1)}, u32[]{:S(2)}, u32[]{:S(2)}) collective-permute-start(bf16[8,3072]{1,0:T(8,128)(2,1)S(1)} %get-tuple-element.60), channel_id=1, source_target_pairs={{0,4},{1,5},{2,6},{3,7},{4,0},{5,1},{6,2},{7,3},{8,12},{9,13},{10,... | collective-permute-start | bytes 147464 | tf_op jit(solution)/shard_map/ppermute | solution.py:45
  83.7 0.1 collective-permute-start.17
  83.8 1.9 %collective-permute-done.16.refs_2_ = bf16[8,3072]{1,0:T(8,128)(2,1)S(1)} collective-permute-done((bf16[8,3072]{1,0:T(8,128)(2,1)S(1)}, bf16[8,3072]{1,0:T(8,128)(2,1)S(1)}, u32[]{:S(2)}, u32[]{:S(2)}) %collective-permute-start.16) | collective-permute-done | bytes 49184 | tf_op jit(solution)/shard_map/ppermute | solution.py:45
  85.7 2.1 %collective-permute-done.17.refs_3_ = bf16[8,3072]{1,0:T(8,128)(2,1)S(1)} collective-permute-done((bf16[8,3072]{1,0:T(8,128)(2,1)S(1)}, bf16[8,3072]{1,0:T(8,128)(2,1)S(1)}, u32[]{:S(2)}, u32[]{:S(2)}) %collective-permute-start.17) | collective-permute-done | bytes 49184 | tf_op jit(solution)/shard_map/ppermute | solution.py:45
  87.9 0.6 line_up.1
  88.6 3.0 %collective-permute-start.19 = (bf16[32,3072]{1,0:T(8,128)(2,1)S(1)}, bf16[32,3072]{1,0:T(8,128)(2,1)S(1)}, u32[]{:S(2)}, u32[]{:S(2)}) collective-permute-start(bf16[32,3072]{1,0:T(8,128)(2,1)S(1)} %line_up.1), channel_id=1, source_target_pairs={{0,64},{1,17},{2,66},{3,19},{4,68},{5,21},{6,70},{7,23},{8,72},{9,... | collective-permute-start | bytes 589832 | tf_op jit(solution)/shard_map/ppermute | solution.py:37
  91.6 0.8 collective-permute-start.20
  92.4 0.7 collective-permute-done.18
  93.1 3.8 %collective-permute-done.19 = bf16[32,3072]{1,0:T(8,128)(2,1)S(1)} collective-permute-done((bf16[32,3072]{1,0:T(8,128)(2,1)S(1)}, bf16[32,3072]{1,0:T(8,128)(2,1)S(1)}, u32[]{:S(2)}, u32[]{:S(2)}) %collective-permute-start.19) | collective-permute-done | bytes 196640 | tf_op jit(solution)/shard_map/ppermute | solution.py:37
  96.9 2.0 %collective-permute-done.20 = bf16[32,3072]{1,0:T(8,128)(2,1)S(1)} collective-permute-done((bf16[32,3072]{1,0:T(8,128)(2,1)S(1)}, bf16[32,3072]{1,0:T(8,128)(2,1)S(1)}, u32[]{:S(2)}, u32[]{:S(2)}) %collective-permute-start.20) | collective-permute-done | bytes 196640 | tf_op jit(solution)/shard_map/ppermute | solution.py:37
  98.9 1.0 collective-permute-start.21
  99.9 1.6 collective-permute-start.22
  101.5 10.3 %collective-permute-done.21.refs_1_ = bf16[128,3072]{1,0:T(8,128)(2,1)S(1)} collective-permute-done((bf16[128,3072]{1,0:T(8,128)(2,1)S(1)}, bf16[128,3072]{1,0:T(8,128)(2,1)S(1)}, u32[]{:S(2)}, u32[]{:S(2)}) %collective-permute-start.21) | collective-permute-done | bytes 786464 | tf_op jit(solution)/shard_map/ppermute | solution.py:41
  111.7 3.7 %collective-permute-done.22.refs_2_ = bf16[128,3072]{1,0:T(8,128)(2,1)S(1)} collective-permute-done((bf16[128,3072]{1,0:T(8,128)(2,1)S(1)}, bf16[128,3072]{1,0:T(8,128)(2,1)S(1)}, u32[]{:S(2)}, u32[]{:S(2)}) %collective-permute-start.22) | collective-permute-done | bytes 786464 | tf_op jit(solution)/shard_map/ppermute | solution.py:41
  115.5 6.8 %mix.1.done = bf16[384,1152]{1,0:T(8,128)(2,1)S(1)} custom-call(bf16[128,3072]{1,0:T(8,128)(2,1)S(1)} %pad_maximum_fusion.refs_0_, bf16[128,3072]{1,0:T(8,128)(2,1)S(1)} %collective-permute-done.21.refs_1_, bf16[128,3072]{1,0:T(8,128)(2,1)S(1)} %collective-permute-done.22.refs_2_, bf16[1536,1152]{1,0:T(8,128)(2,1)} %refs_0_.1, ...), custom_call_target="tpu_custom_call" | custom-call | flops 4000000000 | bytes 8000000 | tf_op jit(solution)/shard_map/mix/pallas_call | solution.py:489
  122.3 5.6 %collective-permute-done.24.last = bf16[128,3072]{1,0:T(8,128)(2,1)S(1)} collective-permute-done((bf16[128,3072]{1,0:T(8,128)(2,1)S(1)}, bf16[128,3072]{1,0:T(8,128)(2,1)S(1)}, u32[]{:S(2)}, u32[]{:S(2)}) %collective-permute-start.24) | collective-permute-done | bytes 786464 | tf_op jit(solution)/shard_map/ppermute | solution.py:41
  127.8 5.1 %mix_rest.1 = (bf16[128,1152]{1,0:T(8,128)(2,1)S(1)}, bf16[128,1152]{1,0:T(8,128)(2,1)S(1)}, bf16[128,1152]{1,0:T(8,128)(2,1)S(1)}, bf16[128,1152]{1,0:T(8,128)(2,1)S(1)}) custom-call(s32[4]{0:T(128)S(1)} %pad_add_fusion.place, bf16[384,1152]{1,0:T(8,128)(2,1)S(1)} %mix.1.done, bf16[128,3072]{1,0:T(8,128)(2,1)S(1)} %collective-permute-done.24.last, ...), custom_call_target="tpu_custom_call" | custom-call | flops 4000000000 | bytes 8000000 | tf_op jit(solution)/shard_map/mix_rest/pallas_call | solution.py:503
  133.0 1.4 collective-permute-start.26
  134.4 2.5 %collective-permute-start.27 = (bf16[128,1152]{1,0:T(8,128)(2,1)S(1)}, bf16[128,1152]{1,0:T(8,128)(2,1)S(1)}, u32[]{:S(2)}, u32[]{:S(2)}) collective-permute-start(bf16[128,1152]{1,0:T(8,128)(2,1)S(1)} %get-tuple-element.68), channel_id=1, source_target_pairs={{0,6},{1,7},{2,4},{3,5},{4,2},{5,3},{6,0},{7,1},{8,14},{9,15},{10,... | collective-permute-start | bytes 884744 | tf_op jit(solution)/shard_map/ppermute | solution.py:45
  136.9 1.7 %collective-permute-done.25.refs_1_ = bf16[128,1152]{1,0:T(8,128)(2,1)S(1)} collective-permute-done((bf16[128,1152]{1,0:T(8,128)(2,1)S(1)}, bf16[128,1152]{1,0:T(8,128)(2,1)S(1)}, u32[]{:S(2)}, u32[]{:S(2)}) %collective-permute-start.25) | collective-permute-done | bytes 294944 | tf_op jit(solution)/shard_map/ppermute | solution.py:45
  138.6 3.2 %collective-permute-done.26.refs_2_ = bf16[128,1152]{1,0:T(8,128)(2,1)S(1)} collective-permute-done((bf16[128,1152]{1,0:T(8,128)(2,1)S(1)}, bf16[128,1152]{1,0:T(8,128)(2,1)S(1)}, u32[]{:S(2)}, u32[]{:S(2)}) %collective-permute-start.26) | collective-permute-done | bytes 294944 | tf_op jit(solution)/shard_map/ppermute | solution.py:45
  141.8 2.6 %collective-permute-done.27.refs_3_ = bf16[128,1152]{1,0:T(8,128)(2,1)S(1)} collective-permute-done((bf16[128,1152]{1,0:T(8,128)(2,1)S(1)}, bf16[128,1152]{1,0:T(8,128)(2,1)S(1)}, u32[]{:S(2)}, u32[]{:S(2)}) %collective-permute-start.27) | collective-permute-done | bytes 294944 | tf_op jit(solution)/shard_map/ppermute | solution.py:45
  144.4 0.1 last_sum.1
  144.5 12.8 %collective-permute-start.28 = (bf16[64,1152]{1,0:T(8,128)(2,1)S(1)}, bf16[64,1152]{1,0:T(8,128)(2,1)S(1)}, u32[]{:S(2)}, u32[]{:S(2)}) collective-permute-start(bf16[64,1152]{1,0:T(8,128)(2,1)S(1)} %get-tuple-element.70), channel_id=1, source_target_pairs={{0,1},{1,0},{2,3},{3,2},{4,5},{5,4},{6,7},{7,6},{8,9},{9,8},{10,11... | collective-permute-start | bytes 442376 | tf_op jit(solution)/shard_map/ppermute | solution.py:49
  157.3 1.0 collective-permute-done.28.theirs
  158.3 1.3 interleave.1
  (22 shorter events, 0.6 us)
Async XLA Ops:
  0.0 2.8 %collective-permute-start = (bf16[128,1152]{1,0:T(8,128)(2,1)}, bf16[128,1152]{1,0:T(8,128)(2,1)S(1)}, u32[]{:S(2)}, u32[]{:S(2)}) collective-permute-start(bf16[128,1152]{1,0:T(8,128)(2,1)} %tokens.1), channel_id=1, source_target_pairs={{0,1},{1,0},{2,3},{3,2},{4,5},{5,4},{6,7},{7,6},{8,9},{9,8},{10,11... | collective-permute-start | bytes 884744 | tf_op jit(solution)/shard_map/ppermute | solution.py:49
  2.8 1.0 copy-start
  5.4 19.6 %collective-permute-start.4 = (bf16[1152,1536]{1,0:T(8,128)(2,1)}, bf16[1152,1536]{1,0:T(8,128)(2,1)}, u32[]{:S(2)}, u32[]{:S(2)}) collective-permute-start(bf16[1152,1536]{1,0:T(8,128)(2,1)} %refs_4_.1), channel_id=1, source_target_pairs={{0,1},{1,0},{2,3},{3,2},{4,5},{5,4},{6,7},{7,6},{8,9},{9,8},{10,11... | collective-permute-start | bytes 10616840 | tf_op jit(solution)/shard_map/ppermute | solution.py:49
  5.7 15.5 %collective-permute-start.1 = (bf16[128,1152]{1,0:T(8,128)(2,1)S(1)}, bf16[128,1152]{1,0:T(8,128)(2,1)S(1)}, u32[]{:S(2)}, u32[]{:S(2)}) collective-permute-start(bf16[128,1152]{1,0:T(8,128)(2,1)S(1)} %get-tuple-element.38.refs_0_), channel_id=1, source_target_pairs={{0,2},{1,3},{2,0},{3,1},{4,6},{5,7},{6,4},{7,5},{8,10},{9,11},{10,... | collective-permute-start | bytes 884744 | tf_op jit(solution)/shard_map/ppermute | solution.py:45
  7.0 15.8 %collective-permute-start.2 = (bf16[128,1152]{1,0:T(8,128)(2,1)S(1)}, bf16[128,1152]{1,0:T(8,128)(2,1)S(1)}, u32[]{:S(2)}, u32[]{:S(2)}) collective-permute-start(bf16[128,1152]{1,0:T(8,128)(2,1)S(1)} %get-tuple-element.38.refs_0_), channel_id=1, source_target_pairs={{0,4},{1,5},{2,6},{3,7},{4,0},{5,1},{6,2},{7,3},{8,12},{9,13},{10,... | collective-permute-start | bytes 884744 | tf_op jit(solution)/shard_map/ppermute | solution.py:45
  9.5 15.5 %collective-permute-start.3 = (bf16[128,1152]{1,0:T(8,128)(2,1)S(1)}, bf16[128,1152]{1,0:T(8,128)(2,1)S(1)}, u32[]{:S(2)}, u32[]{:S(2)}) collective-permute-start(bf16[128,1152]{1,0:T(8,128)(2,1)S(1)} %get-tuple-element.38.refs_0_), channel_id=1, source_target_pairs={{0,6},{1,7},{2,4},{3,5},{4,2},{5,3},{6,0},{7,1},{8,14},{9,15},{10,... | collective-permute-start | bytes 884744 | tf_op jit(solution)/shard_map/ppermute | solution.py:45
  9.6 11.6 %collective-permute-start.5 = (bf16[64,1152]{1,0:T(8,128)(2,1)}, bf16[64,1152]{1,0:T(8,128)(2,1)S(1)}, u32[]{:S(2)}, u32[]{:S(2)}) collective-permute-start(bf16[64,1152]{1,0:T(8,128)(2,1)} %bitcast.10), channel_id=1, source_target_pairs={{0,1},{1,0},{2,3},{3,2},{4,5},{5,4},{6,7},{7,6},{8,9},{9,8},{10,11... | collective-permute-start | bytes 442376 | tf_op jit(solution)/shard_map/ppermute | solution.py:49
  11.3 22.1 %all-to-all-start = ((f32[128,1,256]{2,1,0:T(1,128)}), f32[128,1,256]{2,1,0:T(1,128)S(1)}, u32[]{:S(2)}, u32[]{:S(2)}) async-start(f32[128,1,256]{2,1,0:T(1,128)} %get-tuple-element.42), calls=%async_computation | async-start | bytes 262144 | tf_op jit(solution)/shard_map/all_to_all | solution.py:563
  25.0 0.9 copy-start.2
  35.0 11.6 %collective-permute-start.6 = (bf16[128,3200]{1,0:T(8,128)(2,1)S(1)}, bf16[128,3200]{1,0:T(8,128)(2,1)S(1)}, u32[]{:S(2)}, u32[]{:S(2)}) collective-permute-start(bf16[128,3200]{1,0:T(8,128)(2,1)S(1)} %get-tuple-element.47), channel_id=1, source_target_pairs={{0,32},{1,9},{2,34},{3,11},{4,36},{5,13},{6,38},{7,15},{8,40},{9,1... | collective-permute-start | bytes 2457608 | tf_op jit(solution)/shard_map/ppermute | solution.py:37
  35.5 19.6 %collective-permute-start.8 = (bf16[128,3200]{1,0:T(8,128)(2,1)S(1)}, bf16[128,3200]{1,0:T(8,128)(2,1)S(1)}, u32[]{:S(2)}, u32[]{:S(2)}) collective-permute-start(bf16[128,3200]{1,0:T(8,128)(2,1)S(1)} %get-tuple-element.49), channel_id=1, source_target_pairs={{0,96},{1,25},{2,98},{3,27},{4,100},{5,29},{6,102},{7,31},{8,104},... | collective-permute-start | bytes 2457608 | tf_op jit(solution)/shard_map/ppermute | solution.py:37
  42.5 14.5 %collective-permute-start.7 = (bf16[128,3200]{1,0:T(8,128)(2,1)S(1)}, bf16[128,3200]{1,0:T(8,128)(2,1)S(1)}, u32[]{:S(2)}, u32[]{:S(2)}) collective-permute-start(bf16[128,3200]{1,0:T(8,128)(2,1)S(1)} %get-tuple-element.48), channel_id=1, source_target_pairs={{0,64},{1,17},{2,66},{3,19},{4,68},{5,21},{6,70},{7,23},{8,72},{9,... | collective-permute-start | bytes 2457608 | tf_op jit(solution)/shard_map/ppermute | solution.py:37
  43.8 71.7 %collective-permute-start.23 = (bf16[1536,1152]{1,0:T(8,128)(2,1)}, bf16[1536,1152]{1,0:T(8,128)(2,1)}, u32[]{:S(2)}, u32[]{:S(2)}) collective-permute-start(bf16[1536,1152]{1,0:T(8,128)(2,1)} %refs_0_.1), channel_id=1, source_target_pairs={{0,1},{1,0},{2,3},{3,2},{4,5},{5,4},{6,7},{7,6},{8,9},{9,8},{10,11... | collective-permute-start | bytes 10616840 | tf_op jit(solution)/shard_map/ppermute | solution.py:49
  56.9 3.9 %copy-start.1 = (s32[4]{0:T(128)S(1)}, s32[4]{0:T(128)}, u32[]{:S(2)}) copy-start(s32[4]{0:T(128)} %lengths.1) | copy-start | bytes 52
  57.3 6.2 %collective-permute-start.10 = (bf16[32,3200]{1,0:T(8,128)(2,1)S(1)}, bf16[32,3200]{1,0:T(8,128)(2,1)S(1)}, u32[]{:S(2)}, u32[]{:S(2)}) collective-permute-start(bf16[32,3200]{1,0:T(8,128)(2,1)S(1)} %get-tuple-element.52), channel_id=1, source_target_pairs={{0,16},{1,65},{2,18},{3,67},{4,20},{5,69},{6,22},{7,71},{8,24},{9,... | collective-permute-start | bytes 614408 | tf_op jit(solution)/shard_map/ppermute | solution.py:41
  60.0 6.1 %collective-permute-start.11 = (bf16[32,3200]{1,0:T(8,128)(2,1)S(1)}, bf16[32,3200]{1,0:T(8,128)(2,1)S(1)}, u32[]{:S(2)}, u32[]{:S(2)}) collective-permute-start(bf16[32,3200]{1,0:T(8,128)(2,1)S(1)} %get-tuple-element.53), channel_id=1, source_target_pairs={{0,24},{1,97},{2,26},{3,99},{4,28},{5,101},{6,30},{7,103},{8,16},{... | collective-permute-start | bytes 614408 | tf_op jit(solution)/shard_map/ppermute | solution.py:41
  60.8 5.3 %collective-permute-start.9 = (bf16[32,3200]{1,0:T(8,128)(2,1)S(1)}, bf16[32,3200]{1,0:T(8,128)(2,1)S(1)}, u32[]{:S(2)}, u32[]{:S(2)}) collective-permute-start(bf16[32,3200]{1,0:T(8,128)(2,1)S(1)} %get-tuple-element.51), channel_id=1, source_target_pairs={{0,8},{1,33},{2,10},{3,35},{4,12},{5,37},{6,14},{7,39},{8,0},{9,41... | collective-permute-start | bytes 614408 | tf_op jit(solution)/shard_map/ppermute | solution.py:41
  66.9 4.1 %collective-permute-start.12 = (bf16[8,3200]{1,0:T(8,128)(2,1)S(1)}, bf16[8,3200]{1,0:T(8,128)(2,1)S(1)}, u32[]{:S(2)}, u32[]{:S(2)}) collective-permute-start(bf16[8,3200]{1,0:T(8,128)(2,1)S(1)} %get-tuple-element.55), channel_id=1, source_target_pairs={{0,2},{1,3},{2,0},{3,1},{4,6},{5,7},{6,4},{7,5},{8,10},{9,11},{10,... | collective-permute-start | bytes 153608 | tf_op jit(solution)/shard_map/ppermute | solution.py:45
  67.0 4.7 %collective-permute-start.13 = (bf16[8,3200]{1,0:T(8,128)(2,1)S(1)}, bf16[8,3200]{1,0:T(8,128)(2,1)S(1)}, u32[]{:S(2)}, u32[]{:S(2)}) collective-permute-start(bf16[8,3200]{1,0:T(8,128)(2,1)S(1)} %get-tuple-element.56), channel_id=1, source_target_pairs={{0,4},{1,5},{2,6},{3,7},{4,0},{5,1},{6,2},{7,3},{8,12},{9,13},{10,... | collective-permute-start | bytes 153608 | tf_op jit(solution)/shard_map/ppermute | solution.py:45
  68.2 4.2 %collective-permute-start.14 = (bf16[8,3200]{1,0:T(8,128)(2,1)S(1)}, bf16[8,3200]{1,0:T(8,128)(2,1)S(1)}, u32[]{:S(2)}, u32[]{:S(2)}) collective-permute-start(bf16[8,3200]{1,0:T(8,128)(2,1)S(1)} %get-tuple-element.57), channel_id=1, source_target_pairs={{0,6},{1,7},{2,4},{3,5},{4,2},{5,3},{6,0},{7,1},{8,14},{9,15},{10,... | collective-permute-start | bytes 153608 | tf_op jit(solution)/shard_map/ppermute | solution.py:45
  79.9 3.9 %collective-permute-start.15 = (bf16[8,3072]{1,0:T(8,128)(2,1)S(1)}, bf16[8,3072]{1,0:T(8,128)(2,1)S(1)}, u32[]{:S(2)}, u32[]{:S(2)}) collective-permute-start(bf16[8,3072]{1,0:T(8,128)(2,1)S(1)} %get-tuple-element.59), channel_id=1, source_target_pairs={{0,2},{1,3},{2,0},{3,1},{4,6},{5,7},{6,4},{7,5},{8,10},{9,11},{10,... | collective-permute-start | bytes 147464 | tf_op jit(solution)/shard_map/ppermute | solution.py:45
  80.5 5.3 %collective-permute-start.16 = (bf16[8,3072]{1,0:T(8,128)(2,1)S(1)}, bf16[8,3072]{1,0:T(8,128)(2,1)S(1)}, u32[]{:S(2)}, u32[]{:S(2)}) collective-permute-start(bf16[8,3072]{1,0:T(8,128)(2,1)S(1)} %get-tuple-element.60), channel_id=1, source_target_pairs={{0,4},{1,5},{2,6},{3,7},{4,0},{5,1},{6,2},{7,3},{8,12},{9,13},{10,... | collective-permute-start | bytes 147464 | tf_op jit(solution)/shard_map/ppermute | solution.py:45
  83.7 4.2 %collective-permute-start.17 = (bf16[8,3072]{1,0:T(8,128)(2,1)S(1)}, bf16[8,3072]{1,0:T(8,128)(2,1)S(1)}, u32[]{:S(2)}, u32[]{:S(2)}) collective-permute-start(bf16[8,3072]{1,0:T(8,128)(2,1)S(1)} %get-tuple-element.61), channel_id=1, source_target_pairs={{0,6},{1,7},{2,4},{3,5},{4,2},{5,3},{6,0},{7,1},{8,14},{9,15},{10,... | collective-permute-start | bytes 147464 | tf_op jit(solution)/shard_map/ppermute | solution.py:45
  88.5 4.6 %collective-permute-start.18 = (bf16[32,3072]{1,0:T(8,128)(2,1)S(1)}, bf16[32,3072]{1,0:T(8,128)(2,1)S(1)}, u32[]{:S(2)}, u32[]{:S(2)}) collective-permute-start(bf16[32,3072]{1,0:T(8,128)(2,1)S(1)} %line_up.1), channel_id=1, source_target_pairs={{0,32},{1,9},{2,34},{3,11},{4,36},{5,13},{6,38},{7,15},{8,40},{9,1... | collective-permute-start | bytes 589832 | tf_op jit(solution)/shard_map/ppermute | solution.py:37
  88.6 8.3 %collective-permute-start.19 = (bf16[32,3072]{1,0:T(8,128)(2,1)S(1)}, bf16[32,3072]{1,0:T(8,128)(2,1)S(1)}, u32[]{:S(2)}, u32[]{:S(2)}) collective-permute-start(bf16[32,3072]{1,0:T(8,128)(2,1)S(1)} %line_up.1), channel_id=1, source_target_pairs={{0,64},{1,17},{2,66},{3,19},{4,68},{5,21},{6,70},{7,23},{8,72},{9,... | collective-permute-start | bytes 589832 | tf_op jit(solution)/shard_map/ppermute | solution.py:37
  91.6 7.3 %collective-permute-start.20 = (bf16[32,3072]{1,0:T(8,128)(2,1)S(1)}, bf16[32,3072]{1,0:T(8,128)(2,1)S(1)}, u32[]{:S(2)}, u32[]{:S(2)}) collective-permute-start(bf16[32,3072]{1,0:T(8,128)(2,1)S(1)} %line_up.1), channel_id=1, source_target_pairs={{0,96},{1,25},{2,98},{3,27},{4,100},{5,29},{6,102},{7,31},{8,104},... | collective-permute-start | bytes 589832 | tf_op jit(solution)/shard_map/ppermute | solution.py:37
  98.9 12.8 %collective-permute-start.21 = (bf16[128,3072]{1,0:T(8,128)(2,1)S(1)}, bf16[128,3072]{1,0:T(8,128)(2,1)S(1)}, u32[]{:S(2)}, u32[]{:S(2)}) collective-permute-start(bf16[128,3072]{1,0:T(8,128)(2,1)S(1)} %pad_maximum_fusion.refs_0_), channel_id=1, source_target_pairs={{0,8},{1,33},{2,10},{3,35},{4,12},{5,37},{6,14},{7,39},{8,0},{9,41... | collective-permute-start | bytes 2359304 | tf_op jit(solution)/shard_map/ppermute | solution.py:41
  99.9 15.6 %collective-permute-start.22 = (bf16[128,3072]{1,0:T(8,128)(2,1)S(1)}, bf16[128,3072]{1,0:T(8,128)(2,1)S(1)}, u32[]{:S(2)}, u32[]{:S(2)}) collective-permute-start(bf16[128,3072]{1,0:T(8,128)(2,1)S(1)} %pad_maximum_fusion.refs_0_), channel_id=1, source_target_pairs={{0,24},{1,97},{2,26},{3,99},{4,28},{5,101},{6,30},{7,103},{8,16},{... | collective-permute-start | bytes 2359304 | tf_op jit(solution)/shard_map/ppermute | solution.py:41
  115.5 12.3 %collective-permute-start.24 = (bf16[128,3072]{1,0:T(8,128)(2,1)S(1)}, bf16[128,3072]{1,0:T(8,128)(2,1)S(1)}, u32[]{:S(2)}, u32[]{:S(2)}) collective-permute-start(bf16[128,3072]{1,0:T(8,128)(2,1)S(1)} %pad_maximum_fusion.refs_0_), channel_id=1, source_target_pairs={{0,16},{1,65},{2,18},{3,67},{4,20},{5,69},{6,22},{7,71},{8,24},{9,... | collective-permute-start | bytes 2359304 | tf_op jit(solution)/shard_map/ppermute | solution.py:41
  132.9 5.7 %collective-permute-start.25 = (bf16[128,1152]{1,0:T(8,128)(2,1)S(1)}, bf16[128,1152]{1,0:T(8,128)(2,1)S(1)}, u32[]{:S(2)}, u32[]{:S(2)}) collective-permute-start(bf16[128,1152]{1,0:T(8,128)(2,1)S(1)} %get-tuple-element.66), channel_id=1, source_target_pairs={{0,2},{1,3},{2,0},{3,1},{4,6},{5,7},{6,4},{7,5},{8,10},{9,11},{10,... | collective-permute-start | bytes 884744 | tf_op jit(solution)/shard_map/ppermute | solution.py:45
  133.0 8.7 %collective-permute-start.26 = (bf16[128,1152]{1,0:T(8,128)(2,1)S(1)}, bf16[128,1152]{1,0:T(8,128)(2,1)S(1)}, u32[]{:S(2)}, u32[]{:S(2)}) collective-permute-start(bf16[128,1152]{1,0:T(8,128)(2,1)S(1)} %get-tuple-element.67), channel_id=1, source_target_pairs={{0,4},{1,5},{2,6},{3,7},{4,0},{5,1},{6,2},{7,3},{8,12},{9,13},{10,... | collective-permute-start | bytes 884744 | tf_op jit(solution)/shard_map/ppermute | solution.py:45
  134.4 9.9 %collective-permute-start.27 = (bf16[128,1152]{1,0:T(8,128)(2,1)S(1)}, bf16[128,1152]{1,0:T(8,128)(2,1)S(1)}, u32[]{:S(2)}, u32[]{:S(2)}) collective-permute-start(bf16[128,1152]{1,0:T(8,128)(2,1)S(1)} %get-tuple-element.68), channel_id=1, source_target_pairs={{0,6},{1,7},{2,4},{3,5},{4,2},{5,3},{6,0},{7,1},{8,14},{9,15},{10,... | collective-permute-start | bytes 884744 | tf_op jit(solution)/shard_map/ppermute | solution.py:45
  144.5 13.8 %collective-permute-start.28 = (bf16[64,1152]{1,0:T(8,128)(2,1)S(1)}, bf16[64,1152]{1,0:T(8,128)(2,1)S(1)}, u32[]{:S(2)}, u32[]{:S(2)}) collective-permute-start(bf16[64,1152]{1,0:T(8,128)(2,1)S(1)} %get-tuple-element.70), channel_id=1, source_target_pairs={{0,1},{1,0},{2,3},{3,2},{4,5},{5,4},{6,7},{7,6},{8,9},{9,8},{10,11... | collective-permute-start | bytes 442376 | tf_op jit(solution)/shard_map/ppermute | solution.py:49

commit v6 on v5

--- a/solution.py
+++ b/solution.py
@@ -9,6 +9,7 @@
 
 D = 18432
 HD = 256
+GROUP = 2
 STEPS = 2
 VMEM = pl.BlockSpec(memory_space=pltpu.VMEM)
 SMEM = pl.BlockSpec(memory_space=pltpu.SMEM)
@@ -49,8 +50,11 @@
     return lax.ppermute(value, "gy", [(g, g ^ 1) for g in range(8)])
 
 
-def exchanged(along, parts):
-    return [parts[0]] + [along(parts[m], m) for m in range(1, 4)]
+ORDER = (0, 2, 1, 3)
+
+
+def exchanged(along, parts, order=ORDER):
+    return [along(parts[m], m) if m else parts[0] for m in order]
 
 
 def groups_of(rows, first):
@@ -106,7 +110,7 @@
     y, z, x, c = place[0], place[1], place[2], place[3]
     gains = gain[...].astype(F32)
     along_y = c == 0
-    for m in range(4):
+    for m, piece in zip(ORDER, pieces):
         to_y = x ^ m ^ y
         for j in range(2):
             for b in range(2):
@@ -117,7 +121,7 @@
                 @pl.when((first == blocks[0]) | (first == blocks[1]))
                 def _():
                     at = j * 64 + b * 32
-                    rows = pieces[m][at : at + 32, :].astype(F32)
+                    rows = piece[at : at + 32, :].astype(F32)
                     rows = rows - jnp.sum(rows, axis=1, keepdims=True) / rows.shape[1]
                     slot = jnp.where(first == blocks[0], 0, 4) + second
                     left[pl.ds(pl.multiple_of(slot * 32, 32), 32)] = (rows * gains).astype(BF16)
@@ -319,8 +323,8 @@
 
 def line_up_kernel(place, *refs):
     ins, out, blocks = refs[:4], refs[4], refs[5]
-    for m in range(4):
-        blocks[place[2] ^ m] = ins[m][...].astype(F32)
+    for m, rows in zip(ORDER, ins):
+        blocks[place[2] ^ m] = rows[...].astype(F32)
     out[...] = blocks[...].reshape(out.shape).astype(BF16)
 
 
@@ -338,6 +342,32 @@
     )(place, *values)
 
 
+def attend_one(request, lengths, keys, values, count, query_rows, new_kv, result):
+    per = STEPS * count
+    start = pl.multiple_of(request * per, per)
+    query = jnp.concatenate([query_rows[i, pl.ds(start, per), :] for i in range(2)], axis=-1)
+    query = (query.astype(BF16).astype(F32) * HD ** (-0.5)).astype(BF16)
+    dims = (((1,), (1,)), ((), ()))
+    cached = lax.dot_general(query, keys[...], dims, preferred_element_type=F32)
+    slots = lax.broadcasted_iota(jnp.int32, cached.shape, 1)
+    cached = jnp.where(slots < lengths[request], cached, -jnp.inf)
+    fresh = lax.dot_general(query, new_kv[0], dims, preferred_element_type=F32)
+    row_step = lax.broadcasted_iota(jnp.int32, fresh.shape, 0) // count
+    key_step = lax.broadcasted_iota(jnp.int32, fresh.shape, 1) - request * STEPS
+    fresh = jnp.where((key_step >= 0) & (key_step <= row_step), fresh, -jnp.inf)
+    top = jnp.maximum(
+        jnp.max(cached, axis=-1, keepdims=True), jnp.max(fresh, axis=-1, keepdims=True)
+    )
+    cached = jnp.exp(cached - top)
+    fresh = jnp.exp(fresh - top)
+    denom = jnp.sum(cached, axis=-1, keepdims=True) + jnp.sum(fresh, axis=-1, keepdims=True)
+    mixed = jnp.dot(cached.astype(BF16), values[...], preferred_element_type=F32)
+    mixed = mixed + jnp.dot(fresh.astype(BF16), new_kv[1], preferred_element_type=F32)
+    mixed = mixed / denom
+    for i in range(2):
+        result[i, pl.ds(start, per), :] = mixed[:, i * 128 : i * 128 + 128]
+
+
 def attend_kernel(lengths, place, *refs):
     packed, (cosine, sine, keys, values), outs = refs[:4], refs[4:8], refs[8:12]
     query_rows, new_pieces, new_kv, result = refs[12:]
@@ -354,8 +384,8 @@
         def rotated(first, second):
             return first * cos - second * sin, second * cos + first * sin
 
-        for m in range(4):
-            rows = packed[m][...].astype(F32)
+        for m, rows in zip(ORDER, packed):
+            rows = rows[...].astype(F32)
             for h in range(heads):
                 head = rows[:, h * HD : h * HD + HD]
                 for i, half in enumerate(rotated(head[:, :128], head[:, 128:])):
@@ -370,29 +400,8 @@
         new_kv[0] = jnp.concatenate(rotated(halves[0], halves[1]), axis=-1).astype(BF16)
         new_kv[1] = jnp.concatenate(halves[2:], axis=-1).astype(BF16)
 
-    per = STEPS * count
-    start = pl.multiple_of(request * per, per)
-    query = jnp.concatenate([query_rows[i, pl.ds(start, per), :] for i in range(2)], axis=-1)
-    query = (query.astype(BF16).astype(F32) * HD ** (-0.5)).astype(BF16)
-    dims = (((1,), (1,)), ((), ()))
-    cached = lax.dot_general(query, keys[0], dims, preferred_element_type=F32)
-    slots = lax.broadcasted_iota(jnp.int32, cached.shape, 1)
-    cached = jnp.where(slots < lengths[request], cached, -jnp.inf)
-    fresh = lax.dot_general(query, new_kv[0], dims, preferred_element_type=F32)
-    row_step = lax.broadcasted_iota(jnp.int32, fresh.shape, 0) // count
-    key_step = lax.broadcasted_iota(jnp.int32, fresh.shape, 1) - request * STEPS
-    fresh = jnp.where((key_step >= 0) & (key_step <= row_step), fresh, -jnp.inf)
-    top = jnp.maximum(
-        jnp.max(cached, axis=-1, keepdims=True), jnp.max(fresh, axis=-1, keepdims=True)
-    )
-    cached = jnp.exp(cached - top)
-    fresh = jnp.exp(fresh - top)
-    denom = jnp.sum(cached, axis=-1, keepdims=True) + jnp.sum(fresh, axis=-1, keepdims=True)
-    mixed = jnp.dot(cached.astype(BF16), values[0], preferred_element_type=F32)
-    mixed = mixed + jnp.dot(fresh.astype(BF16), new_kv[1], preferred_element_type=F32)
-    mixed = mixed / denom
-    for i in range(2):
-        result[i, pl.ds(start, per), :] = mixed[:, i * 128 : i * 128 + 128]
+    for i in range(keys.shape[0]):
+        attend_one(request * keys.shape[0] + i, lengths, keys.at[i], values.at[i], count, query_rows, new_kv, result)
 
     @pl.when(request == pl.num_programs(0) - 1)
     def _():
@@ -410,13 +419,13 @@
     total = packed[0].shape[1]
     count = 4 * (width // HD)
     whole = lambda *shape: pl.BlockSpec(shape, lambda r, *_: (0,) * len(shape))
-    cache = pl.BlockSpec((1, slots, HD), lambda r, *_: (r, 0, 0))
+    cache = pl.BlockSpec((GROUP, slots, HD), lambda r, *_: (r, 0, 0))
     return pl.pallas_call(
         attend_kernel,
         out_shape=[jax.ShapeDtypeStruct((8, width), BF16)] * 4,
         grid_spec=pltpu.PrefetchScalarGridSpec(
             num_scalar_prefetch=2,
-            grid=(requests,),
+            grid=(requests // GROUP,),
             in_specs=[whole(8, total)] * 4 + [whole(8, 128)] * 2 + [cache] * 2,
             out_specs=[whole(8, width)] * 4,
             scratch_shapes=[
@@ -468,11 +477,11 @@
         return to_x, (token_z // 2 ^ c) * 2 + token_z % 2
 
     for k in range(12):
-        result[slots((0, 1, 3)[k // 4], k % 4)] = done[k * 32 : k * 32 + 32, :]
+        result[slots((0, 1, 3)[k // 4], ORDER[k % 4])] = done[k * 32 : k * 32 + 32, :]
 
     def put(part, at, size):
         for k in range(4):
-            to_x, slot = slots(2, k)
+            to_x, slot = slots(2, ORDER[k])
             result[to_x, slot, :, at : at + size] = part[k * 32 : k * 32 + 32]
 
     multiply_rows([last], tiles, loads, put)
@@ -573,7 +582,7 @@
     parts = [kept[1], sent[0], kept[0], sent[1]]
 
     parts = add_and_cut(exchanged(along_first, parts))
-    parts = finish(place, exchanged(along_second, parts))
+    parts = finish(place, exchanged(along_second, parts, range(4)))
     packed = exchanged(along_x, parts)
 
     half_dim = HD // 2

time: 160 us -> 151 us (0.944)
  waiting for transfers between devices: 64.5 us -> 58.1 us
  starting transfers between devices: 55.8 us -> 53.9 us
    ppermute x12, waiting for transfers between devices: 16.7 us -> 14.2 us  [along_x(): return lax.ppermute(value, 'gy', [(g, g ^ 2 * m) for g in range(8)])]
    ppermute x6, waiting for transfers between devices: 24.7 us -> 22.2 us  [along_second(): return lax.ppermute(value, ('gx', 'gy'), exchange_pairs(1, m))]
    ppermute x12, starting transfers between devices: 15.7 us -> 13.8 us  [along_x(): return lax.ppermute(value, 'gy', [(g, g ^ 2 * m) for g in range(8)])]
  transfers between devices with their start and end apart: 30 -> 30, of which waited for: 23 -> 22; matrix products, arithmetic and copies ran while one was open for 1% -> 1% of each run, Pallas kernels for 17% -> 17%
where the time goes in v6:
time: 151 us
  waiting for transfers between devices  58.1 us (38%)
  starting transfers between devices  53.9 us (36%)
  Pallas kernels  35.5 us (24%)
  local copies, waits for them, and re-layouts  2.66 us (2%)
    ppermute x6, waiting for transfers between devices, along_second(): return lax.ppermute(value, ('gx', 'gy'), exchange_pairs(1, m))  22.2 us
    ppermute x6, waiting for transfers between devices, along_first(): return lax.ppermute(value, ('gx', 'gy'), exchange_pairs(0, m))  16.9 us
    ppermute x5, starting transfers between devices, other_core(): return lax.ppermute(value, 'gy', [(g, g ^ 1) for g in range(8)])  16.3 us
    ppermute x12, waiting for transfers between devices, along_x(): return lax.ppermute(value, 'gy', [(g, g ^ 2 * m) for g in range(8)])  14.2 us
    ppermute x12, starting transfers between devices, along_x(): return lax.ppermute(value, 'gy', [(g, g ^ 2 * m) for g in range(8)])  13.8 us
    all_to_all x1, starting transfers between devices, per_device(): stats = lax.all_to_all(stats, ('gx', 'gy'), 0, 0, tiled=True)  10 us
    ppermute x6, starting transfers between devices, along_second(): return lax.ppermute(value, ('gx', 'gy'), exchange_pairs(1, m))  7.1 us
    pallas_call x1, Pallas kernels, attend(): pl.pallas_call(attend_kernel, out_shape=[jax.ShapeDtypeStruct((8, width),...  6.84 us
  transfers between devices with their start and end apart: 30, of which 22 were waited for; matrix products, arithmetic and copies ran while one was open for 1% of the time, Pallas kernels for 17%

profile of v6, /device:TPU:1, one launch (start us, length us, event | category | flops | bytes accessed | tf_op | source)
XLA Modules:
  0.0 150.6 jit_solution(4643569826001177187)
XLA Ops:
  0.0 1.4 collective-permute-start
  1.5 1.3 collective-permute-done.theirs
  2.8 1.0 copy-done
  3.8 1.6 %prepare.1 = (f32[128,1,256]{2,1,0:T(1,128)}, bf16[128,1152]{1,0:T(8,128)(2,1)S(1)}) custom-call(s32[4]{0:T(128)S(1)} %pad_add_fusion.place, bf16[128,1152]{1,0:T(8,128)(2,1)S(1)} %copy-done, bf16[128,1152]{1,0:T(8,128)(2,1)S(1)} %collective-permute-done.theirs), custom_call_target="tpu_custom_call" | custom-call | flops 100000000 | bytes 1000000 | tf_op jit(solution)/shard_map/prepare/pallas_call | solution.py:83
  5.4 0.4 collective-permute-start.4
  5.7 2.8 %collective-permute-start.1 = (bf16[128,1152]{1,0:T(8,128)(2,1)S(1)}, bf16[128,1152]{1,0:T(8,128)(2,1)S(1)}, u32[]{:S(2)}, u32[]{:S(2)}) collective-permute-start(bf16[128,1152]{1,0:T(8,128)(2,1)S(1)} %get-tuple-element.38.refs_0_), channel_id=1, source_target_pairs={{0,4},{1,5},{2,6},{3,7},{4,0},{5,1},{6,2},{7,3},{8,12},{9,13},{10,... | collective-permute-start | bytes 884744 | tf_op jit(solution)/shard_map/ppermute | solution.py:46
  8.6 0.3 collective-permute-start.2
  8.9 0.6 collective-permute-start.3
  9.4 0.7 collective-permute-start.5
  10.1 0.7 broadcast_in_dim.2.gain
  10.8 10.0 %all-to-all-start = ((f32[128,1,256]{2,1,0:T(1,128)}), f32[128,1,256]{2,1,0:T(1,128)S(1)}, u32[]{:S(2)}, u32[]{:S(2)}) async-start(f32[128,1,256]{2,1,0:T(1,128)} %get-tuple-element.42), calls=%async_computation | async-start | bytes 262144 | tf_op jit(solution)/shard_map/all_to_all | solution.py:572
  20.9 1.3 collective-permute-done.2.refs_2_
  22.5 0.9 copy-done.2
  23.4 5.0 %project.1 = (bf16[256,3200]{1,0:T(8,128)(2,1)S(1)}, f32[8,3200]{1,0:T(8,128)S(1)}) custom-call(s32[4]{0:T(128)S(1)} %pad_add_fusion.place, bf16[1,1152]{1,0:T(2,128)(2,1)S(1)} %broadcast_in_dim.2.gain, bf16[128,1152]{1,0:T(8,128)(2,1)S(1)} %get-tuple-element.38.refs_0_, bf16[128,1152]{1,0:T(8,128)(2,1)S(1)} %collective-permute-done.1.refs_1_, ...), custom_call_target="tpu_custom_call" | custom-call | flops 4000000000 | bytes 10000000 | tf_op jit(solution)/shard_map/project/pallas_call | solution.py:172
  28.4 2.4 %all-to-all-done = f32[128,1,256]{2,1,0:T(1,128)S(1)} async-done(((f32[128,1,256]{2,1,0:T(1,128)}), f32[128,1,256]{2,1,0:T(1,128)S(1)}, u32[]{:S(2)}, u32[]{:S(2)}) %all-to-all-start) | async-done | bytes 131104 | tf_op jit(solution)/shard_map/all_to_all | solution.py:572
  30.9 1.6 %scale.1 = (bf16[128,3200]{1,0:T(8,128)(2,1)S(1)}, bf16[128,3200]{1,0:T(8,128)(2,1)S(1)}) custom-call(s32[4]{0:T(128)S(1)} %pad_add_fusion.place, f32[128,256]{1,0:T(8,128)S(1)} %bitcast.8, f32[8,3200]{1,0:T(8,128)S(1)} %get-tuple-element.44.gain_row, bf16[256,3200]{1,0:T(8,128)(2,1)S(1)} %get-tuple-element.47.parts), custom_call_target="tpu_custom_call" | custom-call | flops 1000000000 | bytes 2000000 | tf_op jit(solution)/shard_map/scale/pallas_call | solution.py:224
  32.5 0.5 collective-permute-start.7
  32.9 1.2 collective-permute-start.8
  34.2 5.4 %project_rest.1 = (bf16[128,3200]{1,0:T(8,128)(2,1)S(1)}, bf16[128,3200]{1,0:T(8,128)(2,1)S(1)}) custom-call(s32[4]{0:T(128)S(1)} %pad_add_fusion.place, f32[128,256]{1,0:T(8,128)S(1)} %bitcast.9, f32[8,3200]{1,0:T(8,128)S(1)} %get-tuple-element.44.gain_row, bf16[1,1152]{1,0:T(2,128)(2,1)S(1)} %broadcast_in_dim.2.gain, ...), custom_call_target="tpu_custom_call" | custom-call | flops 5000000000 | bytes 10000000 | tf_op jit(solution)/shard_map/project_rest/pallas_call | solution.py:258
  39.6 1.7 %collective-permute-start.6 = (bf16[128,3200]{1,0:T(8,128)(2,1)S(1)}, bf16[128,3200]{1,0:T(8,128)(2,1)S(1)}, u32[]{:S(2)}, u32[]{:S(2)}) collective-permute-start(bf16[128,3200]{1,0:T(8,128)(2,1)S(1)} %get-tuple-element.46), channel_id=1, source_target_pairs={{0,64},{1,17},{2,66},{3,19},{4,68},{5,21},{6,70},{7,23},{8,72},{9,... | collective-permute-start | bytes 2457608 | tf_op jit(solution)/shard_map/ppermute | solution.py:38
  41.3 1.3 collective-permute-start.23
  42.6 1.4 collective-permute-done.7.refs_2_
  44.0 10.4 %collective-permute-done.8.refs_3_ = bf16[128,3200]{1,0:T(8,128)(2,1)S(1)} collective-permute-done((bf16[128,3200]{1,0:T(8,128)(2,1)S(1)}, bf16[128,3200]{1,0:T(8,128)(2,1)S(1)}, u32[]{:S(2)}, u32[]{:S(2)}) %collective-permute-start.8) | collective-permute-done | bytes 819232 | tf_op jit(solution)/shard_map/ppermute | solution.py:38
  54.4 0.4 add_and_cut.1
  54.8 2.2 %collective-permute-start.10 = (bf16[32,3200]{1,0:T(8,128)(2,1)S(1)}, bf16[32,3200]{1,0:T(8,128)(2,1)S(1)}, u32[]{:S(2)}, u32[]{:S(2)}) collective-permute-start(bf16[32,3200]{1,0:T(8,128)(2,1)S(1)} %get-tuple-element.52), channel_id=1, source_target_pairs={{0,16},{1,65},{2,18},{3,67},{4,20},{5,69},{6,22},{7,71},{8,24},{9,... | collective-permute-start | bytes 614408 | tf_op jit(solution)/shard_map/ppermute | solution.py:42
  57.1 0.8 collective-permute-start.11
  58.0 3.3 %collective-permute-done.10.refs_2_ = bf16[32,3200]{1,0:T(8,128)(2,1)S(1)} collective-permute-done((bf16[32,3200]{1,0:T(8,128)(2,1)S(1)}, bf16[32,3200]{1,0:T(8,128)(2,1)S(1)}, u32[]{:S(2)}, u32[]{:S(2)}) %collective-permute-start.10) | collective-permute-done | bytes 204832 | tf_op jit(solution)/shard_map/ppermute | solution.py:42
  61.3 1.9 %collective-permute-done.11.refs_3_ = bf16[32,3200]{1,0:T(8,128)(2,1)S(1)} collective-permute-done((bf16[32,3200]{1,0:T(8,128)(2,1)S(1)}, bf16[32,3200]{1,0:T(8,128)(2,1)S(1)}, u32[]{:S(2)}, u32[]{:S(2)}) %collective-permute-start.11) | collective-permute-done | bytes 204832 | tf_op jit(solution)/shard_map/ppermute | solution.py:42
  63.2 0.7 finish.1
  64.0 2.6 %collective-permute-start.12 = (bf16[8,3200]{1,0:T(8,128)(2,1)S(1)}, bf16[8,3200]{1,0:T(8,128)(2,1)S(1)}, u32[]{:S(2)}, u32[]{:S(2)}) collective-permute-start(bf16[8,3200]{1,0:T(8,128)(2,1)S(1)} %get-tuple-element.55), channel_id=1, source_target_pairs={{0,4},{1,5},{2,6},{3,7},{4,0},{5,1},{6,2},{7,3},{8,12},{9,13},{10,... | collective-permute-start | bytes 153608 | tf_op jit(solution)/shard_map/ppermute | solution.py:46
  66.5 0.3 collective-permute-start.13
  66.9 0.5 collective-permute-start.14
  67.5 1.0 collective-permute-done.12.refs_1_
  68.5 1.0 collective-permute-done.13.refs_2_
  69.5 1.5 %collective-permute-done.14.refs_3_ = bf16[8,3200]{1,0:T(8,128)(2,1)S(1)} collective-permute-done((bf16[8,3200]{1,0:T(8,128)(2,1)S(1)}, bf16[8,3200]{1,0:T(8,128)(2,1)S(1)}, u32[]{:S(2)}, u32[]{:S(2)}) %collective-permute-start.14) | collective-permute-done | bytes 51232 | tf_op jit(solution)/shard_map/ppermute | solution.py:46
  71.1 6.8 %attend.1 = (bf16[8,3072]{1,0:T(8,128)(2,1)S(1)}, bf16[8,3072]{1,0:T(8,128)(2,1)S(1)}, bf16[8,3072]{1,0:T(8,128)(2,1)S(1)}, bf16[8,3072]{1,0:T(8,128)(2,1)S(1)}) custom-call(s32[4]{0:T(128)S(1)} %copy-done.1, s32[4]{0:T(128)S(1)} %pad_add_fusion.place, bf16[8,3200]{1,0:T(8,128)(2,1)S(1)} %get-tuple-element.54.refs_0_, ...), custom_call_target="tpu_custom_call" | custom-call | flops 6000000000 | bytes 18000000 | tf_op jit(solution)/shard_map/attend/pallas_call | solution.py:423
  77.9 0.6 collective-permute-start.15
  78.5 0.6 collective-permute-start.16
  79.0 2.2 %collective-permute-start.17 = (bf16[8,3072]{1,0:T(8,128)(2,1)S(1)}, bf16[8,3072]{1,0:T(8,128)(2,1)S(1)}, u32[]{:S(2)}, u32[]{:S(2)}) collective-permute-start(bf16[8,3072]{1,0:T(8,128)(2,1)S(1)} %get-tuple-element.61), channel_id=1, source_target_pairs={{0,6},{1,7},{2,4},{3,5},{4,2},{5,3},{6,0},{7,1},{8,14},{9,15},{10,... | collective-permute-start | bytes 147464 | tf_op jit(solution)/shard_map/ppermute | solution.py:46
  81.2 1.2 collective-permute-done.15.refs_1_
  82.4 0.8 collective-permute-done.17.refs_3_
  83.2 0.6 line_up.1
  83.8 2.0 %collective-permute-start.18 = (bf16[32,3072]{1,0:T(8,128)(2,1)S(1)}, bf16[32,3072]{1,0:T(8,128)(2,1)S(1)}, u32[]{:S(2)}, u32[]{:S(2)}) collective-permute-start(bf16[32,3072]{1,0:T(8,128)(2,1)S(1)} %line_up.1), channel_id=1, source_target_pairs={{0,64},{1,17},{2,66},{3,19},{4,68},{5,21},{6,70},{7,23},{8,72},{9,... | collective-permute-start | bytes 589832 | tf_op jit(solution)/shard_map/ppermute | solution.py:38
  85.8 0.8 collective-permute-start.19
  86.5 0.6 collective-permute-start.20
  87.1 2.8 %collective-permute-done.18 = bf16[32,3072]{1,0:T(8,128)(2,1)S(1)} collective-permute-done((bf16[32,3072]{1,0:T(8,128)(2,1)S(1)}, bf16[32,3072]{1,0:T(8,128)(2,1)S(1)}, u32[]{:S(2)}, u32[]{:S(2)}) %collective-permute-start.18) | collective-permute-done | bytes 196640 | tf_op jit(solution)/shard_map/ppermute | solution.py:38
  89.9 1.8 %collective-permute-done.19 = bf16[32,3072]{1,0:T(8,128)(2,1)S(1)} collective-permute-done((bf16[32,3072]{1,0:T(8,128)(2,1)S(1)}, bf16[32,3072]{1,0:T(8,128)(2,1)S(1)}, u32[]{:S(2)}, u32[]{:S(2)}) %collective-permute-start.19) | collective-permute-done | bytes 196640 | tf_op jit(solution)/shard_map/ppermute | solution.py:38
  91.7 0.6 collective-permute-done.20
  92.3 1.4 collective-permute-start.21
  93.7 1.2 collective-permute-start.22
  94.9 12.6 %collective-permute-done.21.refs_1_ = bf16[128,3072]{1,0:T(8,128)(2,1)S(1)} collective-permute-done((bf16[128,3072]{1,0:T(8,128)(2,1)S(1)}, bf16[128,3072]{1,0:T(8,128)(2,1)S(1)}, u32[]{:S(2)}, u32[]{:S(2)}) %collective-permute-start.21) | collective-permute-done | bytes 786464 | tf_op jit(solution)/shard_map/ppermute | solution.py:42
  107.5 0.4 collective-permute-done.22.refs_2_
  107.8 1.5 %collective-permute-start.24 = (bf16[128,3072]{1,0:T(8,128)(2,1)S(1)}, bf16[128,3072]{1,0:T(8,128)(2,1)S(1)}, u32[]{:S(2)}, u32[]{:S(2)}) collective-permute-start(bf16[128,3072]{1,0:T(8,128)(2,1)S(1)} %pad_maximum_fusion.refs_0_), channel_id=1, source_target_pairs={{0,16},{1,65},{2,18},{3,67},{4,20},{5,69},{6,22},{7,71},{8,24},{9,... | collective-permute-start | bytes 2359304 | tf_op jit(solution)/shard_map/ppermute | solution.py:42
  109.4 6.8 %mix.1.done = bf16[384,1152]{1,0:T(8,128)(2,1)S(1)} custom-call(bf16[128,3072]{1,0:T(8,128)(2,1)S(1)} %pad_maximum_fusion.refs_0_, bf16[128,3072]{1,0:T(8,128)(2,1)S(1)} %collective-permute-done.21.refs_1_, bf16[128,3072]{1,0:T(8,128)(2,1)S(1)} %collective-permute-done.22.refs_2_, bf16[1536,1152]{1,0:T(8,128)(2,1)} %refs_0_.1, ...), custom_call_target="tpu_custom_call" | custom-call | flops 4000000000 | bytes 8000000 | tf_op jit(solution)/shard_map/mix/pallas_call | solution.py:498
  116.2 4.0 %collective-permute-done.24.last = bf16[128,3072]{1,0:T(8,128)(2,1)S(1)} collective-permute-done((bf16[128,3072]{1,0:T(8,128)(2,1)S(1)}, bf16[128,3072]{1,0:T(8,128)(2,1)S(1)}, u32[]{:S(2)}, u32[]{:S(2)}) %collective-permute-start.24) | collective-permute-done | bytes 786464 | tf_op jit(solution)/shard_map/ppermute | solution.py:42
  120.2 5.1 %mix_rest.1 = (bf16[128,1152]{1,0:T(8,128)(2,1)S(1)}, bf16[128,1152]{1,0:T(8,128)(2,1)S(1)}, bf16[128,1152]{1,0:T(8,128)(2,1)S(1)}, bf16[128,1152]{1,0:T(8,128)(2,1)S(1)}) custom-call(s32[4]{0:T(128)S(1)} %pad_add_fusion.place, bf16[384,1152]{1,0:T(8,128)(2,1)S(1)} %mix.1.done, bf16[128,3072]{1,0:T(8,128)(2,1)S(1)} %collective-permute-done.24.last, ...), custom_call_target="tpu_custom_call" | custom-call | flops 4000000000 | bytes 8000000 | tf_op jit(solution)/shard_map/mix_rest/pallas_call | solution.py:512
  125.3 1.1 collective-permute-start.25
  126.4 2.0 %collective-permute-start.26 = (bf16[128,1152]{1,0:T(8,128)(2,1)S(1)}, bf16[128,1152]{1,0:T(8,128)(2,1)S(1)}, u32[]{:S(2)}, u32[]{:S(2)}) collective-permute-start(bf16[128,1152]{1,0:T(8,128)(2,1)S(1)} %get-tuple-element.67), channel_id=1, source_target_pairs={{0,2},{1,3},{2,0},{3,1},{4,6},{5,7},{6,4},{7,5},{8,10},{9,11},{10,... | collective-permute-start | bytes 884744 | tf_op jit(solution)/shard_map/ppermute | solution.py:46
  128.4 0.3 collective-permute-start.27
  128.6 3.9 %collective-permute-done.25.refs_1_ = bf16[128,1152]{1,0:T(8,128)(2,1)S(1)} collective-permute-done((bf16[128,1152]{1,0:T(8,128)(2,1)S(1)}, bf16[128,1152]{1,0:T(8,128)(2,1)S(1)}, u32[]{:S(2)}, u32[]{:S(2)}) %collective-permute-start.25) | collective-permute-done | bytes 294944 | tf_op jit(solution)/shard_map/ppermute | solution.py:46
  132.5 3.2 %collective-permute-done.26.refs_2_ = bf16[128,1152]{1,0:T(8,128)(2,1)S(1)} collective-permute-done((bf16[128,1152]{1,0:T(8,128)(2,1)S(1)}, bf16[128,1152]{1,0:T(8,128)(2,1)S(1)}, u32[]{:S(2)}, u32[]{:S(2)}) %collective-permute-start.26) | collective-permute-done | bytes 294944 | tf_op jit(solution)/shard_map/ppermute | solution.py:46
  135.9 12.5 %collective-permute-start.28 = (bf16[64,1152]{1,0:T(8,128)(2,1)S(1)}, bf16[64,1152]{1,0:T(8,128)(2,1)S(1)}, u32[]{:S(2)}, u32[]{:S(2)}) collective-permute-start(bf16[64,1152]{1,0:T(8,128)(2,1)S(1)} %get-tuple-element.70), channel_id=1, source_target_pairs={{0,1},{1,0},{2,3},{3,2},{4,5},{5,4},{6,7},{7,6},{8,9},{9,8},{10,11... | collective-permute-start | bytes 442376 | tf_op jit(solution)/shard_map/ppermute | solution.py:50
  148.3 1.0 collective-permute-done.28.theirs
  149.3 1.3 interleave.1
  (22 shorter events, 0.8 us)
Async XLA Ops:
  0.0 2.8 %collective-permute-start = (bf16[128,1152]{1,0:T(8,128)(2,1)}, bf16[128,1152]{1,0:T(8,128)(2,1)S(1)}, u32[]{:S(2)}, u32[]{:S(2)}) collective-permute-start(bf16[128,1152]{1,0:T(8,128)(2,1)} %tokens.1), channel_id=1, source_target_pairs={{0,1},{1,0},{2,3},{3,2},{4,5},{5,4},{6,7},{7,6},{8,9},{9,8},{10,11... | collective-permute-start | bytes 884744 | tf_op jit(solution)/shard_map/ppermute | solution.py:50
  2.8 1.0 copy-start
  5.4 17.1 %collective-permute-start.4 = (bf16[1152,1536]{1,0:T(8,128)(2,1)}, bf16[1152,1536]{1,0:T(8,128)(2,1)}, u32[]{:S(2)}, u32[]{:S(2)}) collective-permute-start(bf16[1152,1536]{1,0:T(8,128)(2,1)} %refs_4_.1), channel_id=1, source_target_pairs={{0,1},{1,0},{2,3},{3,2},{4,5},{5,4},{6,7},{7,6},{8,9},{9,8},{10,11... | collective-permute-start | bytes 10616840 | tf_op jit(solution)/shard_map/ppermute | solution.py:50
  5.7 15.1 %collective-permute-start.1 = (bf16[128,1152]{1,0:T(8,128)(2,1)S(1)}, bf16[128,1152]{1,0:T(8,128)(2,1)S(1)}, u32[]{:S(2)}, u32[]{:S(2)}) collective-permute-start(bf16[128,1152]{1,0:T(8,128)(2,1)S(1)} %get-tuple-element.38.refs_0_), channel_id=1, source_target_pairs={{0,4},{1,5},{2,6},{3,7},{4,0},{5,1},{6,2},{7,3},{8,12},{9,13},{10,... | collective-permute-start | bytes 884744 | tf_op jit(solution)/shard_map/ppermute | solution.py:46
  8.6 13.7 %collective-permute-start.2 = (bf16[128,1152]{1,0:T(8,128)(2,1)S(1)}, bf16[128,1152]{1,0:T(8,128)(2,1)S(1)}, u32[]{:S(2)}, u32[]{:S(2)}) collective-permute-start(bf16[128,1152]{1,0:T(8,128)(2,1)S(1)} %get-tuple-element.38.refs_0_), channel_id=1, source_target_pairs={{0,2},{1,3},{2,0},{3,1},{4,6},{5,7},{6,4},{7,5},{8,10},{9,11},{10,... | collective-permute-start | bytes 884744 | tf_op jit(solution)/shard_map/ppermute | solution.py:46
  8.9 13.6 %collective-permute-start.3 = (bf16[128,1152]{1,0:T(8,128)(2,1)S(1)}, bf16[128,1152]{1,0:T(8,128)(2,1)S(1)}, u32[]{:S(2)}, u32[]{:S(2)}) collective-permute-start(bf16[128,1152]{1,0:T(8,128)(2,1)S(1)} %get-tuple-element.38.refs_0_), channel_id=1, source_target_pairs={{0,6},{1,7},{2,4},{3,5},{4,2},{5,3},{6,0},{7,1},{8,14},{9,15},{10,... | collective-permute-start | bytes 884744 | tf_op jit(solution)/shard_map/ppermute | solution.py:46
  9.4 11.4 %collective-permute-start.5 = (bf16[64,1152]{1,0:T(8,128)(2,1)}, bf16[64,1152]{1,0:T(8,128)(2,1)S(1)}, u32[]{:S(2)}, u32[]{:S(2)}) collective-permute-start(bf16[64,1152]{1,0:T(8,128)(2,1)} %bitcast.10), channel_id=1, source_target_pairs={{0,1},{1,0},{2,3},{3,2},{4,5},{5,4},{6,7},{7,6},{8,9},{9,8},{10,11... | collective-permute-start | bytes 442376 | tf_op jit(solution)/shard_map/ppermute | solution.py:50
  10.8 20.0 %all-to-all-start = ((f32[128,1,256]{2,1,0:T(1,128)}), f32[128,1,256]{2,1,0:T(1,128)S(1)}, u32[]{:S(2)}, u32[]{:S(2)}) async-start(f32[128,1,256]{2,1,0:T(1,128)} %get-tuple-element.42), calls=%async_computation | async-start | bytes 262144 | tf_op jit(solution)/shard_map/all_to_all | solution.py:572
  22.5 0.9 copy-start.2
  32.5 11.6 %collective-permute-start.7 = (bf16[128,3200]{1,0:T(8,128)(2,1)S(1)}, bf16[128,3200]{1,0:T(8,128)(2,1)S(1)}, u32[]{:S(2)}, u32[]{:S(2)}) collective-permute-start(bf16[128,3200]{1,0:T(8,128)(2,1)S(1)} %get-tuple-element.48), channel_id=1, source_target_pairs={{0,32},{1,9},{2,34},{3,11},{4,36},{5,13},{6,38},{7,15},{8,40},{9,1... | collective-permute-start | bytes 2457608 | tf_op jit(solution)/shard_map/ppermute | solution.py:38
  32.9 21.5 %collective-permute-start.8 = (bf16[128,3200]{1,0:T(8,128)(2,1)S(1)}, bf16[128,3200]{1,0:T(8,128)(2,1)S(1)}, u32[]{:S(2)}, u32[]{:S(2)}) collective-permute-start(bf16[128,3200]{1,0:T(8,128)(2,1)S(1)} %get-tuple-element.49), channel_id=1, source_target_pairs={{0,96},{1,25},{2,98},{3,27},{4,100},{5,29},{6,102},{7,31},{8,104},... | collective-permute-start | bytes 2457608 | tf_op jit(solution)/shard_map/ppermute | solution.py:38
  39.6 14.8 %collective-permute-start.6 = (bf16[128,3200]{1,0:T(8,128)(2,1)S(1)}, bf16[128,3200]{1,0:T(8,128)(2,1)S(1)}, u32[]{:S(2)}, u32[]{:S(2)}) collective-permute-start(bf16[128,3200]{1,0:T(8,128)(2,1)S(1)} %get-tuple-element.46), channel_id=1, source_target_pairs={{0,64},{1,17},{2,66},{3,19},{4,68},{5,21},{6,70},{7,23},{8,72},{9,... | collective-permute-start | bytes 2457608 | tf_op jit(solution)/shard_map/ppermute | solution.py:38
  41.3 68.1 %collective-permute-start.23 = (bf16[1536,1152]{1,0:T(8,128)(2,1)}, bf16[1536,1152]{1,0:T(8,128)(2,1)}, u32[]{:S(2)}, u32[]{:S(2)}) collective-permute-start(bf16[1536,1152]{1,0:T(8,128)(2,1)} %refs_0_.1), channel_id=1, source_target_pairs={{0,1},{1,0},{2,3},{3,2},{4,5},{5,4},{6,7},{7,6},{8,9},{9,8},{10,11... | collective-permute-start | bytes 10616840 | tf_op jit(solution)/shard_map/ppermute | solution.py:50
  54.4 3.4 %copy-start.1 = (s32[4]{0:T(128)S(1)}, s32[4]{0:T(128)}, u32[]{:S(2)}) copy-start(s32[4]{0:T(128)} %lengths.1) | copy-start | bytes 52
  54.8 6.5 %collective-permute-start.10 = (bf16[32,3200]{1,0:T(8,128)(2,1)S(1)}, bf16[32,3200]{1,0:T(8,128)(2,1)S(1)}, u32[]{:S(2)}, u32[]{:S(2)}) collective-permute-start(bf16[32,3200]{1,0:T(8,128)(2,1)S(1)} %get-tuple-element.52), channel_id=1, source_target_pairs={{0,16},{1,65},{2,18},{3,67},{4,20},{5,69},{6,22},{7,71},{8,24},{9,... | collective-permute-start | bytes 614408 | tf_op jit(solution)/shard_map/ppermute | solution.py:42
  57.1 6.2 %collective-permute-start.11 = (bf16[32,3200]{1,0:T(8,128)(2,1)S(1)}, bf16[32,3200]{1,0:T(8,128)(2,1)S(1)}, u32[]{:S(2)}, u32[]{:S(2)}) collective-permute-start(bf16[32,3200]{1,0:T(8,128)(2,1)S(1)} %get-tuple-element.53), channel_id=1, source_target_pairs={{0,24},{1,97},{2,26},{3,99},{4,28},{5,101},{6,30},{7,103},{8,16},{... | collective-permute-start | bytes 614408 | tf_op jit(solution)/shard_map/ppermute | solution.py:42
  57.8 5.4 %collective-permute-start.9 = (bf16[32,3200]{1,0:T(8,128)(2,1)S(1)}, bf16[32,3200]{1,0:T(8,128)(2,1)S(1)}, u32[]{:S(2)}, u32[]{:S(2)}) collective-permute-start(bf16[32,3200]{1,0:T(8,128)(2,1)S(1)} %get-tuple-element.51), channel_id=1, source_target_pairs={{0,8},{1,33},{2,10},{3,35},{4,12},{5,37},{6,14},{7,39},{8,0},{9,41... | collective-permute-start | bytes 614408 | tf_op jit(solution)/shard_map/ppermute | solution.py:42
  64.0 4.5 %collective-permute-start.12 = (bf16[8,3200]{1,0:T(8,128)(2,1)S(1)}, bf16[8,3200]{1,0:T(8,128)(2,1)S(1)}, u32[]{:S(2)}, u32[]{:S(2)}) collective-permute-start(bf16[8,3200]{1,0:T(8,128)(2,1)S(1)} %get-tuple-element.55), channel_id=1, source_target_pairs={{0,4},{1,5},{2,6},{3,7},{4,0},{5,1},{6,2},{7,3},{8,12},{9,13},{10,... | collective-permute-start | bytes 153608 | tf_op jit(solution)/shard_map/ppermute | solution.py:46
  66.5 3.0 %collective-permute-start.13 = (bf16[8,3200]{1,0:T(8,128)(2,1)S(1)}, bf16[8,3200]{1,0:T(8,128)(2,1)S(1)}, u32[]{:S(2)}, u32[]{:S(2)}) collective-permute-start(bf16[8,3200]{1,0:T(8,128)(2,1)S(1)} %get-tuple-element.56), channel_id=1, source_target_pairs={{0,2},{1,3},{2,0},{3,1},{4,6},{5,7},{6,4},{7,5},{8,10},{9,11},{10,... | collective-permute-start | bytes 153608 | tf_op jit(solution)/shard_map/ppermute | solution.py:46
  66.9 4.2 %collective-permute-start.14 = (bf16[8,3200]{1,0:T(8,128)(2,1)S(1)}, bf16[8,3200]{1,0:T(8,128)(2,1)S(1)}, u32[]{:S(2)}, u32[]{:S(2)}) collective-permute-start(bf16[8,3200]{1,0:T(8,128)(2,1)S(1)} %get-tuple-element.57), channel_id=1, source_target_pairs={{0,6},{1,7},{2,4},{3,5},{4,2},{5,3},{6,0},{7,1},{8,14},{9,15},{10,... | collective-permute-start | bytes 153608 | tf_op jit(solution)/shard_map/ppermute | solution.py:46
  77.9 4.5 %collective-permute-start.15 = (bf16[8,3072]{1,0:T(8,128)(2,1)S(1)}, bf16[8,3072]{1,0:T(8,128)(2,1)S(1)}, u32[]{:S(2)}, u32[]{:S(2)}) collective-permute-start(bf16[8,3072]{1,0:T(8,128)(2,1)S(1)} %get-tuple-element.59), channel_id=1, source_target_pairs={{0,4},{1,5},{2,6},{3,7},{4,0},{5,1},{6,2},{7,3},{8,12},{9,13},{10,... | collective-permute-start | bytes 147464 | tf_op jit(solution)/shard_map/ppermute | solution.py:46
  78.5 3.9 %collective-permute-start.16 = (bf16[8,3072]{1,0:T(8,128)(2,1)S(1)}, bf16[8,3072]{1,0:T(8,128)(2,1)S(1)}, u32[]{:S(2)}, u32[]{:S(2)}) collective-permute-start(bf16[8,3072]{1,0:T(8,128)(2,1)S(1)} %get-tuple-element.60), channel_id=1, source_target_pairs={{0,2},{1,3},{2,0},{3,1},{4,6},{5,7},{6,4},{7,5},{8,10},{9,11},{10,... | collective-permute-start | bytes 147464 | tf_op jit(solution)/shard_map/ppermute | solution.py:46
  79.0 4.2 %collective-permute-start.17 = (bf16[8,3072]{1,0:T(8,128)(2,1)S(1)}, bf16[8,3072]{1,0:T(8,128)(2,1)S(1)}, u32[]{:S(2)}, u32[]{:S(2)}) collective-permute-start(bf16[8,3072]{1,0:T(8,128)(2,1)S(1)} %get-tuple-element.61), channel_id=1, source_target_pairs={{0,6},{1,7},{2,4},{3,5},{4,2},{5,3},{6,0},{7,1},{8,14},{9,15},{10,... | collective-permute-start | bytes 147464 | tf_op jit(solution)/shard_map/ppermute | solution.py:46
  83.8 6.1 %collective-permute-start.18 = (bf16[32,3072]{1,0:T(8,128)(2,1)S(1)}, bf16[32,3072]{1,0:T(8,128)(2,1)S(1)}, u32[]{:S(2)}, u32[]{:S(2)}) collective-permute-start(bf16[32,3072]{1,0:T(8,128)(2,1)S(1)} %line_up.1), channel_id=1, source_target_pairs={{0,64},{1,17},{2,66},{3,19},{4,68},{5,21},{6,70},{7,23},{8,72},{9,... | collective-permute-start | bytes 589832 | tf_op jit(solution)/shard_map/ppermute | solution.py:38
  85.8 5.9 %collective-permute-start.19 = (bf16[32,3072]{1,0:T(8,128)(2,1)S(1)}, bf16[32,3072]{1,0:T(8,128)(2,1)S(1)}, u32[]{:S(2)}, u32[]{:S(2)}) collective-permute-start(bf16[32,3072]{1,0:T(8,128)(2,1)S(1)} %line_up.1), channel_id=1, source_target_pairs={{0,32},{1,9},{2,34},{3,11},{4,36},{5,13},{6,38},{7,15},{8,40},{9,1... | collective-permute-start | bytes 589832 | tf_op jit(solution)/shard_map/ppermute | solution.py:38
  86.5 5.7 %collective-permute-start.20 = (bf16[32,3072]{1,0:T(8,128)(2,1)S(1)}, bf16[32,3072]{1,0:T(8,128)(2,1)S(1)}, u32[]{:S(2)}, u32[]{:S(2)}) collective-permute-start(bf16[32,3072]{1,0:T(8,128)(2,1)S(1)} %line_up.1), channel_id=1, source_target_pairs={{0,96},{1,25},{2,98},{3,27},{4,100},{5,29},{6,102},{7,31},{8,104},... | collective-permute-start | bytes 589832 | tf_op jit(solution)/shard_map/ppermute | solution.py:38
  92.3 15.2 %collective-permute-start.21 = (bf16[128,3072]{1,0:T(8,128)(2,1)S(1)}, bf16[128,3072]{1,0:T(8,128)(2,1)S(1)}, u32[]{:S(2)}, u32[]{:S(2)}) collective-permute-start(bf16[128,3072]{1,0:T(8,128)(2,1)S(1)} %pad_maximum_fusion.refs_0_), channel_id=1, source_target_pairs={{0,8},{1,33},{2,10},{3,35},{4,12},{5,37},{6,14},{7,39},{8,0},{9,41... | collective-permute-start | bytes 2359304 | tf_op jit(solution)/shard_map/ppermute | solution.py:42
  93.7 14.2 %collective-permute-start.22 = (bf16[128,3072]{1,0:T(8,128)(2,1)S(1)}, bf16[128,3072]{1,0:T(8,128)(2,1)S(1)}, u32[]{:S(2)}, u32[]{:S(2)}) collective-permute-start(bf16[128,3072]{1,0:T(8,128)(2,1)S(1)} %pad_maximum_fusion.refs_0_), channel_id=1, source_target_pairs={{0,24},{1,97},{2,26},{3,99},{4,28},{5,101},{6,30},{7,103},{8,16},{... | collective-permute-start | bytes 2359304 | tf_op jit(solution)/shard_map/ppermute | solution.py:42
  107.8 12.3 %collective-permute-start.24 = (bf16[128,3072]{1,0:T(8,128)(2,1)S(1)}, bf16[128,3072]{1,0:T(8,128)(2,1)S(1)}, u32[]{:S(2)}, u32[]{:S(2)}) collective-permute-start(bf16[128,3072]{1,0:T(8,128)(2,1)S(1)} %pad_maximum_fusion.refs_0_), channel_id=1, source_target_pairs={{0,16},{1,65},{2,18},{3,67},{4,20},{5,69},{6,22},{7,71},{8,24},{9,... | collective-permute-start | bytes 2359304 | tf_op jit(solution)/shard_map/ppermute | solution.py:42
  125.3 7.2 %collective-permute-start.25 = (bf16[128,1152]{1,0:T(8,128)(2,1)S(1)}, bf16[128,1152]{1,0:T(8,128)(2,1)S(1)}, u32[]{:S(2)}, u32[]{:S(2)}) collective-permute-start(bf16[128,1152]{1,0:T(8,128)(2,1)S(1)} %get-tuple-element.66), channel_id=1, source_target_pairs={{0,4},{1,5},{2,6},{3,7},{4,0},{5,1},{6,2},{7,3},{8,12},{9,13},{10,... | collective-permute-start | bytes 884744 | tf_op jit(solution)/shard_map/ppermute | solution.py:46
  126.4 9.3 %collective-permute-start.26 = (bf16[128,1152]{1,0:T(8,128)(2,1)S(1)}, bf16[128,1152]{1,0:T(8,128)(2,1)S(1)}, u32[]{:S(2)}, u32[]{:S(2)}) collective-permute-start(bf16[128,1152]{1,0:T(8,128)(2,1)S(1)} %get-tuple-element.67), channel_id=1, source_target_pairs={{0,2},{1,3},{2,0},{3,1},{4,6},{5,7},{6,4},{7,5},{8,10},{9,11},{10,... | collective-permute-start | bytes 884744 | tf_op jit(solution)/shard_map/ppermute | solution.py:46
  128.4 7.3 %collective-permute-start.27 = (bf16[128,1152]{1,0:T(8,128)(2,1)S(1)}, bf16[128,1152]{1,0:T(8,128)(2,1)S(1)}, u32[]{:S(2)}, u32[]{:S(2)}) collective-permute-start(bf16[128,1152]{1,0:T(8,128)(2,1)S(1)} %get-tuple-element.68), channel_id=1, source_target_pairs={{0,6},{1,7},{2,4},{3,5},{4,2},{5,3},{6,0},{7,1},{8,14},{9,15},{10,... | collective-permute-start | bytes 884744 | tf_op jit(solution)/shard_map/ppermute | solution.py:46
  135.9 13.5 %collective-permute-start.28 = (bf16[64,1152]{1,0:T(8,128)(2,1)S(1)}, bf16[64,1152]{1,0:T(8,128)(2,1)S(1)}, u32[]{:S(2)}, u32[]{:S(2)}) collective-permute-start(bf16[64,1152]{1,0:T(8,128)(2,1)S(1)} %get-tuple-element.70), channel_id=1, source_target_pairs={{0,1},{1,0},{2,3},{3,2},{4,5},{5,4},{6,7},{7,6},{8,9},{9,8},{10,11... | collective-permute-start | bytes 442376 | tf_op jit(solution)/shard_map/ppermute | solution.py:50

commit v7 on v6

--- a/solution.py
+++ b/solution.py
@@ -62,12 +62,10 @@
     return jnp.concatenate(groups, axis=0)
 
 
-def prepare_kernel(place, tokens, theirs, stats, piece):
-    rows, others = tokens[...].astype(F32), theirs[...].astype(F32)
+def prepare_kernel(tokens, stats, copy):
+    copy[...] = tokens[...]
+    rows = tokens[...].astype(F32)
     by_core = [groups_of(rows, 0), groups_of(rows, 8)]
-    swap = place[3] == 1
-    piece[:64] = jnp.where(swap, by_core[1], by_core[0]).astype(BF16)
-    piece[64:] = jnp.where(swap, groups_of(others, 8), groups_of(others, 0)).astype(BF16)
     lines = []
     for power in range(2):
         sums = [
@@ -79,19 +77,19 @@
     stats[...] = jnp.broadcast_to(line[:, None, :], stats.shape)
 
 
-def prepare(place, tokens, theirs):
+def prepare(tokens):
     return pl.pallas_call(
         prepare_kernel,
         out_shape=[
             jax.ShapeDtypeStruct((128, 1, 256), F32),
-            jax.ShapeDtypeStruct(tokens.shape, BF16),
+            jax.ShapeDtypeStruct(tokens.shape, tokens.dtype),
         ],
-        in_specs=[SMEM, VMEM, VMEM],
+        in_specs=[VMEM],
         out_specs=[VMEM] * 2,
         compiler_params=params(8),
         cost_estimate=cost(1e8, 1e6),
         name="prepare",
-    )(place, tokens, theirs)
+    )(tokens)
 
 
 def load_tiles(source, tiles, sems, at):
@@ -106,36 +104,36 @@
     return loads
 
 
-def fill_left(blocks, place, gain, pieces, left):
+def fill_left(place, gain, pieces, left):
     y, z, x, c = place[0], place[1], place[2], place[3]
     gains = gain[...].astype(F32)
+    left[256:272] = jnp.broadcast_to(gain[...], (16, gain.shape[1]))
     along_y = c == 0
-    for m, piece in zip(ORDER, pieces):
+    for i, m in enumerate(ORDER):
         to_y = x ^ m ^ y
         for j in range(2):
+            rows = pieces[j * 4 + i][...].astype(F32)
+            rows = jnp.where(along_y, groups_of(rows, 0), groups_of(rows, 8))
+            rows = rows - jnp.sum(rows, axis=1, keepdims=True) / rows.shape[1]
+            rows = (rows * gains).astype(BF16)
             for b in range(2):
                 to_z = ((c ^ j) * 2 + b) ^ z
                 first = jnp.where(along_y, to_y, to_z)
                 second = jnp.where(along_y, to_z, to_y)
-
-                @pl.when((first == blocks[0]) | (first == blocks[1]))
-                def _():
-                    at = j * 64 + b * 32
-                    rows = piece[at : at + 32, :].astype(F32)
-                    rows = rows - jnp.sum(rows, axis=1, keepdims=True) / rows.shape[1]
-                    slot = jnp.where(first == blocks[0], 0, 4) + second
-                    left[pl.ds(pl.multiple_of(slot * 32, 32), 32)] = (rows * gains).astype(BF16)
+                at = jnp.where(first % 2 == 1, first // 2 * 128, 400 - first // 2 * 128)
+                at = pl.multiple_of(at + second * 32, 16)
+                left[pl.ds(at, 32)] = rows[b * 32 : b * 32 + 32]
 
 
 def multiply(left, tiles, loads, pairs, put):
     wide = tiles.shape[2]
     width = tiles.shape[0] * wide
-    pair = jnp.concatenate([pairs[0][...], pairs[1][...]], axis=0)
     dims = (((1,), (1,)), ((), ()))
-    put(lax.dot_general(left[...], pair, dims, preferred_element_type=F32), width, pair.shape[0])
+    part = lax.dot_general(left, pairs[...], dims, preferred_element_type=F32)
+    put(part, width, pairs.shape[0])
     for t, load in enumerate(loads):
         load.wait()
-        put(jnp.dot(left[...], tiles[t], preferred_element_type=F32), t * wide, wide)
+        put(jnp.dot(left, tiles[t], preferred_element_type=F32), t * wide, wide)
 
 
 def load_both(weights, tiles, sems):
@@ -143,45 +141,46 @@
     return load_tiles(weights[0], tiles, sems, 0) + load_tiles(weights[1], tiles, sems, count)
 
 
-def project_kernel(blocks, place, gain, *refs):
-    pieces, weights, pairs = refs[:4], refs[4:6], refs[6:8]
-    out, gain_row, left, tiles, sems = refs[8:]
+def project_kernel(place, gain, *refs):
+    pieces, weights, pairs = refs[:8], refs[8:10], refs[10]
+    out, gain_row, rest, left, tiles, sems = refs[11:]
     loads = load_both(weights, tiles, sems)
-    left[256:] = jnp.broadcast_to(gain[...], (16, gain.shape[1]))
-    fill_left(blocks, place, gain, pieces, left)
+    fill_left(place, gain, pieces, left)
+    rest[...] = left[272:]
 
     def put(part, at, size):
         out[:, at : at + size] = part[:256].astype(BF16)
         gain_row[:, at : at + size] = part[256:264]
 
-    multiply(left, tiles, loads, pairs, put)
-
-
-def project_scratch(rows, weights):
+    multiply(left[:272], tiles, loads, pairs, put)
+
+
+def project_scratch(weights):
     depth, width = weights[0].shape
     count = 2 * width // 512
     return [
-        pltpu.VMEM((rows, depth), BF16),
         pltpu.VMEM((count, depth, 512), BF16),
         pltpu.SemaphoreType.DMA((count,)),
     ]
 
 
-def project(blocks, place, gain, pieces, weights, pairs):
-    total = 2 * (weights[0].shape[1] + pairs[0].shape[0])
-    return pl.pallas_call(
-        functools.partial(project_kernel, blocks),
+def project(place, gain, pieces, weights, pairs):
+    depth = weights[0].shape[0]
+    total = 2 * weights[0].shape[1] + pairs.shape[0]
+    return pl.pallas_call(
+        project_kernel,
         out_shape=[
             jax.ShapeDtypeStruct((256, total), BF16),
             jax.ShapeDtypeStruct((8, total), F32),
+            jax.ShapeDtypeStruct((256, depth), BF16),
         ],
-        in_specs=[SMEM] + [VMEM] * 5 + [ANY] * 2 + [VMEM] * 2,
-        out_specs=[VMEM] * 2,
-        scratch_shapes=project_scratch(272, weights),
+        in_specs=[SMEM] + [VMEM] * 9 + [ANY] * 2 + [VMEM],
+        out_specs=[VMEM] * 3,
+        scratch_shapes=[pltpu.VMEM((528, depth), BF16)] + project_scratch(weights),
         compiler_params=params(48),
         cost_estimate=cost(4e9, 1e7),
         name="project",
-    )(place, gain, *pieces, *weights, *pairs)
+    )(place, gain, *pieces, *weights, pairs)
 
 
 def fill_columns(place, stats, shift_of, scale_of):
@@ -233,16 +232,15 @@
     )(place, stats, gain_row, parts)
 
 
-def project_rest_kernel(blocks, place, stats, gain_row, gain, *refs):
-    pieces, weights, pairs = refs[:4], refs[4:6], refs[6:8]
-    outs, (left, tiles, sems, shift_of, scale_of, shift, factor) = refs[8:10], refs[10:]
+def project_rest_kernel(blocks, place, stats, gain_row, left, *refs):
+    weights, pairs, outs = refs[:2], refs[2], refs[3:5]
+    tiles, sems, shift_of, scale_of, shift, factor = refs[5:]
     loads = load_both(weights, tiles, sems)
     fill_columns(place, stats, shift_of, scale_of)
     for k in range(8):
         s, at = columns_of(place, blocks[k // 4], k % 4)
         shift[k * 32 : k * 32 + 32] = shift_of[s, at]
         factor[k * 32 : k * 32 + 32] = scale_of[s, at]
-    fill_left(blocks, place, gain, pieces, left)
 
     def put(part, at, size):
         line = gain_row[0:1, at : at + size]
@@ -250,23 +248,23 @@
         for i, out in enumerate(outs):
             out[:, at : at + size] = part[i * 128 : i * 128 + 128]
 
-    multiply(left, tiles, loads, pairs, put)
-
-
-def project_rest(blocks, place, stats, gain_row, gain, pieces, weights, pairs):
+    multiply(left[...], tiles, loads, pairs, put)
+
+
+def project_rest(blocks, place, stats, gain_row, left, weights, pairs):
     out = jax.ShapeDtypeStruct((128, gain_row.shape[1]), BF16)
     return pl.pallas_call(
         functools.partial(project_rest_kernel, blocks),
         out_shape=[out] * 2,
-        in_specs=[SMEM] + [VMEM] * 7 + [ANY] * 2 + [VMEM] * 2,
+        in_specs=[SMEM] + [VMEM] * 3 + [ANY] * 2 + [VMEM],
         out_specs=[VMEM] * 2,
-        scratch_shapes=project_scratch(256, weights)
+        scratch_shapes=project_scratch(weights)
         + [pltpu.VMEM((8, 128, 1), F32)] * 2
         + [pltpu.VMEM((256, 1), F32)] * 2,
         compiler_params=params(48),
         cost_estimate=cost(5e9, 1e7),
         name="project_rest",
-    )(place, stats, gain_row, gain, *pieces, *weights, *pairs)
+    )(place, stats, gain_row, left, *weights, pairs)
 
 
 def sum_of(refs):
@@ -441,33 +439,33 @@
     )(lengths, place, *packed, cosine, sine, cache_keys, cache_values)
 
 
-def multiply_rows(lefts, tiles, loads, put):
+def multiply_rows(lefts, tiles, put, loads=None):
     left = jnp.concatenate([ref[...] for ref in lefts], axis=0)
     depth = left.shape[1] // 2
     count = tiles.shape[0] // 2
     wide = tiles.shape[2]
     for t in range(count):
-        loads[t].wait()
+        if loads:
+            loads[t].wait()
         part = jnp.dot(left[:, :depth], tiles[t], preferred_element_type=F32)
-        loads[count + t].wait()
+        if loads:
+            loads[count + t].wait()
         part = part + jnp.dot(left[:, depth:], tiles[count + t], preferred_element_type=F32)
         put(part.astype(BF16), t * wide, wide)
 
 
 def mix_kernel(*refs):
-    lefts, weights, out, tiles, sems = refs[:3], refs[3:5], refs[5], refs[6], refs[7]
+    lefts, weights, (out, tiles, sems) = refs[:3], refs[3:5], refs[5:]
     loads = load_tiles(weights[0], tiles, sems, 0) + load_tiles(weights[1], tiles, sems, 3)
 
     def put(part, at, size):
         out[:, at : at + size] = part
 
-    multiply_rows(lefts, tiles, loads, put)
-
-
-def mix_rest_kernel(place, done, last, *refs):
-    weights, outs = refs[:2], refs[2:6]
-    result, tiles, sems = refs[6:]
-    loads = load_tiles(weights[0], tiles, sems, 0) + load_tiles(weights[1], tiles, sems, 3)
+    multiply_rows(lefts, tiles, put, loads)
+
+
+def mix_rest_kernel(place, done, last, tiles, *refs):
+    outs, result = refs[:4], refs[4]
     y, z, x, c = place[0], place[1], place[2], place[3]
     along_y = c == 0
 
@@ -484,41 +482,40 @@
             to_x, slot = slots(2, ORDER[k])
             result[to_x, slot, :, at : at + size] = part[k * 32 : k * 32 + 32]
 
-    multiply_rows([last], tiles, loads, put)
+    multiply_rows([last], tiles, put)
     for k, out in enumerate(outs):
         out[...] = result[k].reshape(out.shape)
 
 
-def mix_scratch(depth, width):
-    return [pltpu.VMEM((6, depth, width // 3), BF16), pltpu.SemaphoreType.DMA((6,))]
-
-
 def mix(lefts, weights):
     depth, width = weights[0].shape
     return pl.pallas_call(
         mix_kernel,
-        out_shape=jax.ShapeDtypeStruct((384, width), BF16),
+        out_shape=[
+            jax.ShapeDtypeStruct((384, width), BF16),
+            jax.ShapeDtypeStruct((6, depth, width // 3), BF16),
+        ],
         in_specs=[VMEM] * 3 + [ANY] * 2,
-        out_specs=VMEM,
-        scratch_shapes=mix_scratch(depth, width),
+        out_specs=[VMEM] * 2,
+        scratch_shapes=[pltpu.SemaphoreType.DMA((6,))],
         compiler_params=params(24),
         cost_estimate=cost(4e9, 8e6),
         name="mix",
     )(*lefts, *weights)
 
 
-def mix_rest(place, done, last, weights):
-    depth, width = weights[0].shape
+def mix_rest(place, done, last, tiles):
+    width = done.shape[1]
     return pl.pallas_call(
         mix_rest_kernel,
         out_shape=[jax.ShapeDtypeStruct((128, width), BF16)] * 4,
-        in_specs=[SMEM] + [VMEM] * 2 + [ANY] * 2,
+        in_specs=[SMEM] + [VMEM] * 3,
         out_specs=[VMEM] * 4,
-        scratch_shapes=[pltpu.VMEM((4, 4, 32, width), BF16)] + mix_scratch(depth, width),
+        scratch_shapes=[pltpu.VMEM((4, 4, 32, width), BF16)],
         compiler_params=params(24),
         cost_estimate=cost(4e9, 8e6),
         name="mix_rest",
-    )(place, done, last, *weights)
+    )(place, done, last, tiles)
 
 
 def last_sum_kernel(*refs):
@@ -567,22 +564,23 @@
     gx, gy = lax.axis_index("gx"), lax.axis_index("gy")
     place = jnp.stack([gx // 4, gx % 4, gy // 2, gy % 2]).astype(jnp.int32)
 
-    stats, piece = prepare(place, tokens, other_core(tokens))
-    pieces = exchanged(along_x, [piece] * 4)
+    stats, held = prepare(tokens)
+    pieces = exchanged(along_x, [held] + [tokens] * 3)
+    pieces += [other_core(piece) for piece in pieces]
     stats = lax.all_to_all(stats, ("gx", "gy"), 0, 0, tiled=True)
     w_pair = w_keyvalue.T
-    w_query, w_pair, piece = lax.optimization_barrier((w_query, w_pair, piece))
-    weights, pairs = [w_query, other_core(w_query)], [w_pair, other_core(w_pair)]
+    weights = [w_query, other_core(w_query)]
+    pairs = jnp.concatenate([w_pair, other_core(w_pair)], axis=0)
     gain = norm_gain[None]
-    parts, gain_row = project((1, 3), place, gain, pieces, weights, pairs)
-    parts, stats = lax.optimization_barrier((parts, stats))
+    parts, gain_row, rest = project(place, gain, pieces, weights, pairs)
+    gain_row, stats = lax.optimization_barrier((gain_row, stats))
     stats = stats.reshape(128, 256)
     sent = scale((1, 3), place, stats, gain_row, parts)
-    kept = project_rest((2, 0), place, stats, gain_row, gain, pieces, weights, pairs)
+    kept = project_rest((2, 0), place, stats, gain_row, rest, weights, pairs)
     parts = [kept[1], sent[0], kept[0], sent[1]]
 
     parts = add_and_cut(exchanged(along_first, parts))
-    parts = finish(place, exchanged(along_second, parts, range(4)))
+    parts = finish(place, exchanged(along_second, parts))
     packed = exchanged(along_x, parts)
 
     half_dim = HD // 2
@@ -606,8 +604,8 @@
     late, *near = lax.optimization_barrier((rows, *near))
     blocks = [rows, near[0], along_second(late, 2), near[1]]
     weights = [w_out, other_core(w_out)]
-    done = mix([blocks[0], blocks[1], blocks[3]], weights)
-    parts = mix_rest(place, done, blocks[2], weights)
+    done, tiles = mix([blocks[0], blocks[1], blocks[3]], weights)
+    parts = mix_rest(place, done, blocks[2], tiles)
     mine, theirs = last_sum(exchanged(along_x, parts))
     return interleave(place, mine, other_core(theirs))
 

time: 151 us -> 146 us (0.967)
  waiting for transfers between devices: 58.1 us -> 54.6 us
  Pallas kernels: 35.5 us -> 32.4 us
    pallas_call x1, Pallas kernels: 5.12 us -> 2.02 us  [mix_rest(): pl.pallas_call(mix_rest_kernel, out_shape=[jax.ShapeDtypeStruct((128, wid...]
    all_to_all x1, waiting for transfers between devices: 2.41 us -> 0.01 us  [per_device(): stats = lax.all_to_all(stats, ('gx', 'gy'), 0, 0, tiled=True)]
    ppermute x12, waiting for transfers between devices: 14.2 us -> 12.5 us  [along_x(): return lax.ppermute(value, 'gy', [(g, g ^ 2 * m) for g in range(8)])]
    ppermute x5 -> x8, starting transfers between devices: 16.3 us -> 15.4 us  [other_core(): return lax.ppermute(value, 'gy', [(g, g ^ 1) for g in range(8)])]
  transfers between devices with their start and end apart: 30 -> 33, of which waited for: 22 -> 23; matrix products, arithmetic and copies ran while one was open for 1% -> 1% of each run, Pallas kernels for 17% -> 19%
where the time goes in v7:
time: 146 us; the launch traced here: 145 us
  waiting for transfers between devices  54.6 us (37%)
  starting transfers between devices  54.4 us (37%)
  Pallas kernels  32.4 us (22%)
  local copies, waits for them, and re-layouts  2.56 us (2%)
    ppermute x6, waiting for transfers between devices, along_second(): return lax.ppermute(value, ('gx', 'gy'), exchange_pairs(1, m))  22.3 us
    ppermute x6, waiting for transfers between devices, along_first(): return lax.ppermute(value, ('gx', 'gy'), exchange_pairs(0, m))  17.9 us
    ppermute x8, starting transfers between devices, other_core(): return lax.ppermute(value, 'gy', [(g, g ^ 1) for g in range(8)])  15.4 us
    ppermute x12, starting transfers between devices, along_x(): return lax.ppermute(value, 'gy', [(g, g ^ 2 * m) for g in range(8)])  14.4 us
    ppermute x12, waiting for transfers between devices, along_x(): return lax.ppermute(value, 'gy', [(g, g ^ 2 * m) for g in range(8)])  12.5 us
    all_to_all x1, starting transfers between devices, per_device(): stats = lax.all_to_all(stats, ('gx', 'gy'), 0, 0, tiled=True)  10 us
    ppermute x6, starting transfers between devices, along_second(): return lax.ppermute(value, ('gx', 'gy'), exchange_pairs(1, m))  7.31 us
    ppermute x6, starting transfers between devices, along_first(): return lax.ppermute(value, ('gx', 'gy'), exchange_pairs(0, m))  7.24 us
  transfers between devices with their start and end apart: 33, of which 23 were waited for; matrix products, arithmetic and copies ran while one was open for 1% of the time, Pallas kernels for 19%

profile of v7, /device:TPU:1, one launch (start us, length us, event | category | flops | bytes accessed | tf_op | source)
XLA Modules:
  0.0 145.3 jit_solution(8515512818984971313)
XLA Ops:
  0.0 1.4 collective-permute-start.7
  1.4 2.8 %collective-permute-start = (bf16[128,1152]{1,0:T(8,128)(2,1)}, bf16[128,1152]{1,0:T(8,128)(2,1)S(1)}, u32[]{:S(2)}, u32[]{:S(2)}) collective-permute-start(bf16[128,1152]{1,0:T(8,128)(2,1)} %tokens.1), channel_id=1, source_target_pairs={{0,4},{1,5},{2,6},{3,7},{4,0},{5,1},{6,2},{7,3},{8,12},{9,13},{10,... | collective-permute-start | bytes 884744 | tf_op jit(solution)/shard_map/ppermute | solution.py:46
  4.6 0.6 collective-permute-start.2
  5.1 0.6 collective-permute-start.8
  5.7 1.0 copy-done.1
  6.6 1.0 prepare.1
  7.6 10.0 %all-to-all-start = ((f32[128,1,256]{2,1,0:T(1,128)}), f32[128,1,256]{2,1,0:T(1,128)S(1)}, u32[]{:S(2)}, u32[]{:S(2)}) async-start(f32[128,1,256]{2,1,0:T(1,128)} %get-tuple-element.41), calls=%async_computation | async-start | bytes 262144 | tf_op jit(solution)/shard_map/all_to_all | solution.py:570
  17.7 0.7 broadcast_in_dim.2.gain
  18.4 1.1 collective-permute-start.3
  19.6 0.4 collective-permute-start.5
  20.2 0.9 pad_maximum_fusion.1.refs_10_.refs_2_
  21.1 0.4 collective-permute-done.5.refs_6_
  21.5 0.4 collective-permute-done.6.refs_7_
  21.9 5.6 %project.1 = (bf16[256,3200]{1,0:T(8,128)(2,1)S(1)}, f32[8,3200]{1,0:T(8,128)S(1)}, bf16[256,1152]{1,0:T(8,128)(2,1)S(1)}) custom-call(s32[4]{0:T(128)S(1)} %pad_add_fusion.place, bf16[1,1152]{1,0:T(2,128)(2,1)S(1)} %broadcast_in_dim.2.gain, bf16[128,1152]{1,0:T(8,128)(2,1)S(1)} %get-tuple-element.39.refs_0_, ...), custom_call_target="tpu_custom_call" | custom-call | flops 4000000000 | bytes 10000000 | tf_op jit(solution)/shard_map/project/pallas_call | solution.py:170
  27.5 0.8 copy-done.2
  28.4 1.6 %scale.1 = (bf16[128,3200]{1,0:T(8,128)(2,1)S(1)}, bf16[128,3200]{1,0:T(8,128)(2,1)S(1)}) custom-call(s32[4]{0:T(128)S(1)} %pad_add_fusion.place, f32[128,256]{1,0:T(8,128)S(1)} %bitcast.8, f32[8,3200]{1,0:T(8,128)S(1)} %get-tuple-element.43.gain_row, bf16[256,3200]{1,0:T(8,128)(2,1)S(1)} %get-tuple-element.47.parts), custom_call_target="tpu_custom_call" | custom-call | flops 1000000000 | bytes 2000000 | tf_op jit(solution)/shard_map/scale/pallas_call | solution.py:223
  30.0 0.9 collective-permute-start.10
  30.9 2.1 %collective-permute-start.11 = (bf16[128,3200]{1,0:T(8,128)(2,1)S(1)}, bf16[128,3200]{1,0:T(8,128)(2,1)S(1)}, u32[]{:S(2)}, u32[]{:S(2)}) collective-permute-start(bf16[128,3200]{1,0:T(8,128)(2,1)S(1)} %get-tuple-element.49), channel_id=1, source_target_pairs={{0,96},{1,25},{2,98},{3,27},{4,100},{5,29},{6,102},{7,31},{8,104},... | collective-permute-start | bytes 2457608 | tf_op jit(solution)/shard_map/ppermute | solution.py:38
  32.9 5.4 %project_rest.1 = (bf16[128,3200]{1,0:T(8,128)(2,1)S(1)}, bf16[128,3200]{1,0:T(8,128)(2,1)S(1)}) custom-call(s32[4]{0:T(128)S(1)} %pad_add_fusion.place, f32[128,256]{1,0:T(8,128)S(1)} %bitcast.9, f32[8,3200]{1,0:T(8,128)S(1)} %get-tuple-element.43.gain_row, bf16[256,1152]{1,0:T(8,128)(2,1)S(1)} %copy-done.3, bf16[1152,1536]{1,0:T(8,128)(2,1)} %refs_0_.1, ...), custom_call_target="tpu_custom_call" | custom-call | flops 5000000000 | bytes 10000000 | tf_op jit(solution)/shard_map/project_rest/pallas_call | solution.py:256
  38.4 1.0 collective-permute-start.9
  39.3 0.7 collective-permute-start.26
  40.0 1.5 %collective-permute-done.10.refs_2_ = bf16[128,3200]{1,0:T(8,128)(2,1)S(1)} collective-permute-done((bf16[128,3200]{1,0:T(8,128)(2,1)S(1)}, bf16[128,3200]{1,0:T(8,128)(2,1)S(1)}, u32[]{:S(2)}, u32[]{:S(2)}) %collective-permute-start.10) | collective-permute-done | bytes 819232 | tf_op jit(solution)/shard_map/ppermute | solution.py:38
  41.5 9.5 %collective-permute-done.11.refs_3_ = bf16[128,3200]{1,0:T(8,128)(2,1)S(1)} collective-permute-done((bf16[128,3200]{1,0:T(8,128)(2,1)S(1)}, bf16[128,3200]{1,0:T(8,128)(2,1)S(1)}, u32[]{:S(2)}, u32[]{:S(2)}) %collective-permute-start.11) | collective-permute-done | bytes 819232 | tf_op jit(solution)/shard_map/ppermute | solution.py:38
  51.0 1.6 %collective-permute-done.9.refs_1_ = bf16[128,3200]{1,0:T(8,128)(2,1)S(1)} collective-permute-done((bf16[128,3200]{1,0:T(8,128)(2,1)S(1)}, bf16[128,3200]{1,0:T(8,128)(2,1)S(1)}, u32[]{:S(2)}, u32[]{:S(2)}) %collective-permute-start.9) | collective-permute-done | bytes 819232 | tf_op jit(solution)/shard_map/ppermute | solution.py:38
  52.6 0.4 add_and_cut.1
  53.0 2.7 %collective-permute-start.12 = (bf16[32,3200]{1,0:T(8,128)(2,1)S(1)}, bf16[32,3200]{1,0:T(8,128)(2,1)S(1)}, u32[]{:S(2)}, u32[]{:S(2)}) collective-permute-start(bf16[32,3200]{1,0:T(8,128)(2,1)S(1)} %get-tuple-element.51), channel_id=1, source_target_pairs={{0,16},{1,65},{2,18},{3,67},{4,20},{5,69},{6,22},{7,71},{8,24},{9,... | collective-permute-start | bytes 614408 | tf_op jit(solution)/shard_map/ppermute | solution.py:42
  56.6 2.9 %collective-permute-done.12.refs_1_ = bf16[32,3200]{1,0:T(8,128)(2,1)S(1)} collective-permute-done((bf16[32,3200]{1,0:T(8,128)(2,1)S(1)}, bf16[32,3200]{1,0:T(8,128)(2,1)S(1)}, u32[]{:S(2)}, u32[]{:S(2)}) %collective-permute-start.12) | collective-permute-done | bytes 204832 | tf_op jit(solution)/shard_map/ppermute | solution.py:42
  59.5 1.9 %collective-permute-done.13.refs_2_ = bf16[32,3200]{1,0:T(8,128)(2,1)S(1)} collective-permute-done((bf16[32,3200]{1,0:T(8,128)(2,1)S(1)}, bf16[32,3200]{1,0:T(8,128)(2,1)S(1)}, u32[]{:S(2)}, u32[]{:S(2)}) %collective-permute-start.13) | collective-permute-done | bytes 204832 | tf_op jit(solution)/shard_map/ppermute | solution.py:42
  61.4 0.5 collective-permute-done.14.refs_3_
  61.9 0.7 finish.1
  62.6 2.7 %collective-permute-start.15 = (bf16[8,3200]{1,0:T(8,128)(2,1)S(1)}, bf16[8,3200]{1,0:T(8,128)(2,1)S(1)}, u32[]{:S(2)}, u32[]{:S(2)}) collective-permute-start(bf16[8,3200]{1,0:T(8,128)(2,1)S(1)} %get-tuple-element.55), channel_id=1, source_target_pairs={{0,4},{1,5},{2,6},{3,7},{4,0},{5,1},{6,2},{7,3},{8,12},{9,13},{10,... | collective-permute-start | bytes 153608 | tf_op jit(solution)/shard_map/ppermute | solution.py:46
  65.6 1.0 collective-permute-start.17
  66.7 0.4 collective-permute-done.15.refs_1_
  67.1 1.1 collective-permute-done.16.refs_2_
  68.2 1.5 %collective-permute-done.17.refs_3_ = bf16[8,3200]{1,0:T(8,128)(2,1)S(1)} collective-permute-done((bf16[8,3200]{1,0:T(8,128)(2,1)S(1)}, bf16[8,3200]{1,0:T(8,128)(2,1)S(1)}, u32[]{:S(2)}, u32[]{:S(2)}) %collective-permute-start.17) | collective-permute-done | bytes 51232 | tf_op jit(solution)/shard_map/ppermute | solution.py:46
  69.8 6.8 %attend.1 = (bf16[8,3072]{1,0:T(8,128)(2,1)S(1)}, bf16[8,3072]{1,0:T(8,128)(2,1)S(1)}, bf16[8,3072]{1,0:T(8,128)(2,1)S(1)}, bf16[8,3072]{1,0:T(8,128)(2,1)S(1)}) custom-call(s32[4]{0:T(128)S(1)} %copy-done, s32[4]{0:T(128)S(1)} %pad_add_fusion.place, bf16[8,3200]{1,0:T(8,128)(2,1)S(1)} %get-tuple-element.54.refs_0_, ...), custom_call_target="tpu_custom_call" | custom-call | flops 6000000000 | bytes 18000000 | tf_op jit(solution)/shard_map/attend/pallas_call | solution.py:421
  76.6 1.1 collective-permute-start.18
  77.7 0.6 collective-permute-start.19
  78.3 1.7 %collective-permute-start.20 = (bf16[8,3072]{1,0:T(8,128)(2,1)S(1)}, bf16[8,3072]{1,0:T(8,128)(2,1)S(1)}, u32[]{:S(2)}, u32[]{:S(2)}) collective-permute-start(bf16[8,3072]{1,0:T(8,128)(2,1)S(1)} %get-tuple-element.61), channel_id=1, source_target_pairs={{0,6},{1,7},{2,4},{3,5},{4,2},{5,3},{6,0},{7,1},{8,14},{9,15},{10,... | collective-permute-start | bytes 147464 | tf_op jit(solution)/shard_map/ppermute | solution.py:46
  79.9 1.2 collective-permute-done.18.refs_1_
  81.1 1.3 collective-permute-done.20.refs_3_
  82.4 0.6 line_up.1
  83.0 2.0 %collective-permute-start.21 = (bf16[32,3072]{1,0:T(8,128)(2,1)S(1)}, bf16[32,3072]{1,0:T(8,128)(2,1)S(1)}, u32[]{:S(2)}, u32[]{:S(2)}) collective-permute-start(bf16[32,3072]{1,0:T(8,128)(2,1)S(1)} %line_up.1), channel_id=1, source_target_pairs={{0,64},{1,17},{2,66},{3,19},{4,68},{5,21},{6,70},{7,23},{8,72},{9,... | collective-permute-start | bytes 589832 | tf_op jit(solution)/shard_map/ppermute | solution.py:38
  85.0 0.9 collective-permute-start.22
  86.0 0.4 collective-permute-start.23
  86.4 2.8 %collective-permute-done.21 = bf16[32,3072]{1,0:T(8,128)(2,1)S(1)} collective-permute-done((bf16[32,3072]{1,0:T(8,128)(2,1)S(1)}, bf16[32,3072]{1,0:T(8,128)(2,1)S(1)}, u32[]{:S(2)}, u32[]{:S(2)}) %collective-permute-start.21) | collective-permute-done | bytes 196640 | tf_op jit(solution)/shard_map/ppermute | solution.py:38
  89.1 2.0 %collective-permute-done.22 = bf16[32,3072]{1,0:T(8,128)(2,1)S(1)} collective-permute-done((bf16[32,3072]{1,0:T(8,128)(2,1)S(1)}, bf16[32,3072]{1,0:T(8,128)(2,1)S(1)}, u32[]{:S(2)}, u32[]{:S(2)}) %collective-permute-start.22) | collective-permute-done | bytes 196640 | tf_op jit(solution)/shard_map/ppermute | solution.py:38
  91.1 0.6 collective-permute-done.23
  91.8 0.5 collective-permute-start.24
  92.3 1.8 %collective-permute-start.25 = (bf16[128,3072]{1,0:T(8,128)(2,1)S(1)}, bf16[128,3072]{1,0:T(8,128)(2,1)S(1)}, u32[]{:S(2)}, u32[]{:S(2)}) collective-permute-start(bf16[128,3072]{1,0:T(8,128)(2,1)S(1)} %pad_maximum_fusion.refs_0_), channel_id=1, source_target_pairs={{0,24},{1,97},{2,26},{3,99},{4,28},{5,101},{6,30},{7,103},{8,16},{... | collective-permute-start | bytes 2359304 | tf_op jit(solution)/shard_map/ppermute | solution.py:42
  94.1 12.6 %collective-permute-done.24.refs_1_ = bf16[128,3072]{1,0:T(8,128)(2,1)S(1)} collective-permute-done((bf16[128,3072]{1,0:T(8,128)(2,1)S(1)}, bf16[128,3072]{1,0:T(8,128)(2,1)S(1)}, u32[]{:S(2)}, u32[]{:S(2)}) %collective-permute-start.24) | collective-permute-done | bytes 786464 | tf_op jit(solution)/shard_map/ppermute | solution.py:42
  106.6 0.5 collective-permute-done.25.refs_2_
  107.1 1.6 %collective-permute-start.27 = (bf16[128,3072]{1,0:T(8,128)(2,1)S(1)}, bf16[128,3072]{1,0:T(8,128)(2,1)S(1)}, u32[]{:S(2)}, u32[]{:S(2)}) collective-permute-start(bf16[128,3072]{1,0:T(8,128)(2,1)S(1)} %pad_maximum_fusion.refs_0_), channel_id=1, source_target_pairs={{0,16},{1,65},{2,18},{3,67},{4,20},{5,69},{6,22},{7,71},{8,24},{9,... | collective-permute-start | bytes 2359304 | tf_op jit(solution)/shard_map/ppermute | solution.py:42
  108.7 6.8 %mix.1 = (bf16[384,1152]{1,0:T(8,128)(2,1)S(1)}, bf16[6,1536,384]{2,1,0:T(8,128)(2,1)S(1)}) custom-call(bf16[128,3072]{1,0:T(8,128)(2,1)S(1)} %pad_maximum_fusion.refs_0_, bf16[128,3072]{1,0:T(8,128)(2,1)S(1)} %collective-permute-done.24.refs_1_, bf16[128,3072]{1,0:T(8,128)(2,1)S(1)} %collective-permute-done.25.refs_2_, bf16[1536,1152]{1,0:T(8,128)(2,1)} %refs_3_.1, ...), custom_call_target="tpu_custom_call" | custom-call | flops 4000000000 | bytes 8000000 | tf_op jit(solution)/shard_map/mix/pallas_call | solution.py:492
  115.5 4.0 %collective-permute-done.27.last = bf16[128,3072]{1,0:T(8,128)(2,1)S(1)} collective-permute-done((bf16[128,3072]{1,0:T(8,128)(2,1)S(1)}, bf16[128,3072]{1,0:T(8,128)(2,1)S(1)}, u32[]{:S(2)}, u32[]{:S(2)}) %collective-permute-start.27) | collective-permute-done | bytes 786464 | tf_op jit(solution)/shard_map/ppermute | solution.py:42
  119.5 2.0 %mix_rest.1 = (bf16[128,1152]{1,0:T(8,128)(2,1)S(1)}, bf16[128,1152]{1,0:T(8,128)(2,1)S(1)}, bf16[128,1152]{1,0:T(8,128)(2,1)S(1)}, bf16[128,1152]{1,0:T(8,128)(2,1)S(1)}) custom-call(s32[4]{0:T(128)S(1)} %pad_add_fusion.place, bf16[384,1152]{1,0:T(8,128)(2,1)S(1)} %get-tuple-element.64.done, bf16[128,3072]{1,0:T(8,128)(2,1)S(1)} %collective-permute-done.27.last, ...), custom_call_target="tpu_custom_call" | custom-call | flops 4000000000 | bytes 8000000 | tf_op jit(solution)/shard_map/mix_rest/pallas_call | solution.py:509
  121.5 1.2 collective-permute-start.28
  122.7 1.5 %collective-permute-start.29 = (bf16[128,1152]{1,0:T(8,128)(2,1)S(1)}, bf16[128,1152]{1,0:T(8,128)(2,1)S(1)}, u32[]{:S(2)}, u32[]{:S(2)}) collective-permute-start(bf16[128,1152]{1,0:T(8,128)(2,1)S(1)} %get-tuple-element.69), channel_id=1, source_target_pairs={{0,2},{1,3},{2,0},{3,1},{4,6},{5,7},{6,4},{7,5},{8,10},{9,11},{10,... | collective-permute-start | bytes 884744 | tf_op jit(solution)/shard_map/ppermute | solution.py:46
  124.2 0.7 collective-permute-start.30
  124.8 4.0 %collective-permute-done.28.refs_1_ = bf16[128,1152]{1,0:T(8,128)(2,1)S(1)} collective-permute-done((bf16[128,1152]{1,0:T(8,128)(2,1)S(1)}, bf16[128,1152]{1,0:T(8,128)(2,1)S(1)}, u32[]{:S(2)}, u32[]{:S(2)}) %collective-permute-start.28) | collective-permute-done | bytes 294944 | tf_op jit(solution)/shard_map/ppermute | solution.py:46
  128.9 2.6 %collective-permute-done.29.refs_2_ = bf16[128,1152]{1,0:T(8,128)(2,1)S(1)} collective-permute-done((bf16[128,1152]{1,0:T(8,128)(2,1)S(1)}, bf16[128,1152]{1,0:T(8,128)(2,1)S(1)}, u32[]{:S(2)}, u32[]{:S(2)}) %collective-permute-start.29) | collective-permute-done | bytes 294944 | tf_op jit(solution)/shard_map/ppermute | solution.py:46
  132.0 11.0 %collective-permute-start.31 = (bf16[64,1152]{1,0:T(8,128)(2,1)S(1)}, bf16[64,1152]{1,0:T(8,128)(2,1)S(1)}, u32[]{:S(2)}, u32[]{:S(2)}) collective-permute-start(bf16[64,1152]{1,0:T(8,128)(2,1)S(1)} %get-tuple-element.72), channel_id=1, source_target_pairs={{0,1},{1,0},{2,3},{3,2},{4,5},{5,4},{6,7},{7,6},{8,9},{9,8},{10,11... | collective-permute-start | bytes 442376 | tf_op jit(solution)/shard_map/ppermute | solution.py:50
  143.0 1.0 collective-permute-done.31.theirs
  144.0 1.3 interleave.1
  (31 shorter events, 2.5 us)
Async XLA Ops:
  0.0 21.9 %collective-permute-start.7 = (bf16[1152,1536]{1,0:T(8,128)(2,1)}, bf16[1152,1536]{1,0:T(8,128)(2,1)}, u32[]{:S(2)}, u32[]{:S(2)}) collective-permute-start(bf16[1152,1536]{1,0:T(8,128)(2,1)} %refs_0_.1), channel_id=1, source_target_pairs={{0,1},{1,0},{2,3},{3,2},{4,5},{5,4},{6,7},{7,6},{8,9},{9,8},{10,11... | collective-permute-start | bytes 10616840 | tf_op jit(solution)/shard_map/ppermute | solution.py:50
  1.4 18.1 %collective-permute-start = (bf16[128,1152]{1,0:T(8,128)(2,1)}, bf16[128,1152]{1,0:T(8,128)(2,1)S(1)}, u32[]{:S(2)}, u32[]{:S(2)}) collective-permute-start(bf16[128,1152]{1,0:T(8,128)(2,1)} %tokens.1), channel_id=1, source_target_pairs={{0,4},{1,5},{2,6},{3,7},{4,0},{5,1},{6,2},{7,3},{8,12},{9,13},{10,... | collective-permute-start | bytes 884744 | tf_op jit(solution)/shard_map/ppermute | solution.py:46
  4.2 15.3 %collective-permute-start.1 = (bf16[128,1152]{1,0:T(8,128)(2,1)}, bf16[128,1152]{1,0:T(8,128)(2,1)S(1)}, u32[]{:S(2)}, u32[]{:S(2)}) collective-permute-start(bf16[128,1152]{1,0:T(8,128)(2,1)} %tokens.1), channel_id=1, source_target_pairs={{0,2},{1,3},{2,0},{3,1},{4,6},{5,7},{6,4},{7,5},{8,10},{9,11},{10,... | collective-permute-start | bytes 884744 | tf_op jit(solution)/shard_map/ppermute | solution.py:46
  4.6 15.4 %collective-permute-start.2 = (bf16[128,1152]{1,0:T(8,128)(2,1)}, bf16[128,1152]{1,0:T(8,128)(2,1)S(1)}, u32[]{:S(2)}, u32[]{:S(2)}) collective-permute-start(bf16[128,1152]{1,0:T(8,128)(2,1)} %tokens.1), channel_id=1, source_target_pairs={{0,6},{1,7},{2,4},{3,5},{4,2},{5,3},{6,0},{7,1},{8,14},{9,15},{10,... | collective-permute-start | bytes 884744 | tf_op jit(solution)/shard_map/ppermute | solution.py:46
  5.1 13.3 %collective-permute-start.8 = (bf16[64,1152]{1,0:T(8,128)(2,1)}, bf16[64,1152]{1,0:T(8,128)(2,1)S(1)}, u32[]{:S(2)}, u32[]{:S(2)}) collective-permute-start(bf16[64,1152]{1,0:T(8,128)(2,1)} %bitcast.10), channel_id=1, source_target_pairs={{0,1},{1,0},{2,3},{3,2},{4,5},{5,4},{6,7},{7,6},{8,9},{9,8},{10,11... | collective-permute-start | bytes 442376 | tf_op jit(solution)/shard_map/ppermute | solution.py:50
  5.7 1.0 copy-start.1
  7.6 20.7 %all-to-all-start = ((f32[128,1,256]{2,1,0:T(1,128)}), f32[128,1,256]{2,1,0:T(1,128)S(1)}, u32[]{:S(2)}, u32[]{:S(2)}) async-start(f32[128,1,256]{2,1,0:T(1,128)} %get-tuple-element.41), calls=%async_computation | async-start | bytes 262144 | tf_op jit(solution)/shard_map/all_to_all | solution.py:570
  18.4 2.7 %collective-permute-start.3 = (bf16[128,1152]{1,0:T(8,128)(2,1)S(1)}, bf16[128,1152]{1,0:T(8,128)(2,1)S(1)}, u32[]{:S(2)}, u32[]{:S(2)}) collective-permute-start(bf16[128,1152]{1,0:T(8,128)(2,1)S(1)} %get-tuple-element.39.refs_0_), channel_id=1, source_target_pairs={{0,1},{1,0},{2,3},{3,2},{4,5},{5,4},{6,7},{7,6},{8,9},{9,8},{10,11... | collective-permute-start | bytes 884744 | tf_op jit(solution)/shard_map/ppermute | solution.py:50
  19.5 1.6 %collective-permute-start.4 = (bf16[128,1152]{1,0:T(8,128)(2,1)S(1)}, bf16[128,1152]{1,0:T(8,128)(2,1)S(1)}, u32[]{:S(2)}, u32[]{:S(2)}) collective-permute-start(bf16[128,1152]{1,0:T(8,128)(2,1)S(1)} %collective-permute-done.refs_1_), channel_id=1, source_target_pairs={{0,1},{1,0},{2,3},{3,2},{4,5},{5,4},{6,7},{7,6},{8,9},{9,8},{10,11... | collective-permute-start | bytes 884744 | tf_op jit(solution)/shard_map/ppermute | solution.py:50
  19.6 2.0 %collective-permute-start.5 = (bf16[128,1152]{1,0:T(8,128)(2,1)S(1)}, bf16[128,1152]{1,0:T(8,128)(2,1)S(1)}, u32[]{:S(2)}, u32[]{:S(2)}) collective-permute-start(bf16[128,1152]{1,0:T(8,128)(2,1)S(1)} %collective-permute-done.1.refs_2_), channel_id=1, source_target_pairs={{0,1},{1,0},{2,3},{3,2},{4,5},{5,4},{6,7},{7,6},{8,9},{9,8},{10,11... | collective-permute-start | bytes 884744 | tf_op jit(solution)/shard_map/ppermute | solution.py:50
  20.0 2.0 %collective-permute-start.6 = (bf16[128,1152]{1,0:T(8,128)(2,1)S(1)}, bf16[128,1152]{1,0:T(8,128)(2,1)S(1)}, u32[]{:S(2)}, u32[]{:S(2)}) collective-permute-start(bf16[128,1152]{1,0:T(8,128)(2,1)S(1)} %collective-permute-done.2.refs_3_), channel_id=1, source_target_pairs={{0,1},{1,0},{2,3},{3,2},{4,5},{5,4},{6,7},{7,6},{8,9},{9,8},{10,11... | collective-permute-start | bytes 884744 | tf_op jit(solution)/shard_map/ppermute | solution.py:50
  27.5 0.8 copy-start.2
  28.4 4.6 %copy-start.3 = (bf16[256,1152]{1,0:T(8,128)(2,1)S(1)}, bf16[256,1152]{1,0:T(8,128)(2,1)}, u32[]{:S(2)}) copy-start(bf16[256,1152]{1,0:T(8,128)(2,1)} %copy-done.2) | copy-start | bytes 1769476
  30.0 11.6 %collective-permute-start.10 = (bf16[128,3200]{1,0:T(8,128)(2,1)S(1)}, bf16[128,3200]{1,0:T(8,128)(2,1)S(1)}, u32[]{:S(2)}, u32[]{:S(2)}) collective-permute-start(bf16[128,3200]{1,0:T(8,128)(2,1)S(1)} %get-tuple-element.48), channel_id=1, source_target_pairs={{0,32},{1,9},{2,34},{3,11},{4,36},{5,13},{6,38},{7,15},{8,40},{9,1... | collective-permute-start | bytes 2457608 | tf_op jit(solution)/shard_map/ppermute | solution.py:38
  30.9 20.1 %collective-permute-start.11 = (bf16[128,3200]{1,0:T(8,128)(2,1)S(1)}, bf16[128,3200]{1,0:T(8,128)(2,1)S(1)}, u32[]{:S(2)}, u32[]{:S(2)}) collective-permute-start(bf16[128,3200]{1,0:T(8,128)(2,1)S(1)} %get-tuple-element.49), channel_id=1, source_target_pairs={{0,96},{1,25},{2,98},{3,27},{4,100},{5,29},{6,102},{7,31},{8,104},... | collective-permute-start | bytes 2457608 | tf_op jit(solution)/shard_map/ppermute | solution.py:38
  38.4 14.2 %collective-permute-start.9 = (bf16[128,3200]{1,0:T(8,128)(2,1)S(1)}, bf16[128,3200]{1,0:T(8,128)(2,1)S(1)}, u32[]{:S(2)}, u32[]{:S(2)}) collective-permute-start(bf16[128,3200]{1,0:T(8,128)(2,1)S(1)} %get-tuple-element.46), channel_id=1, source_target_pairs={{0,64},{1,17},{2,66},{3,19},{4,68},{5,21},{6,70},{7,23},{8,72},{9,... | collective-permute-start | bytes 2457608 | tf_op jit(solution)/shard_map/ppermute | solution.py:38
  39.3 69.4 %collective-permute-start.26 = (bf16[1536,1152]{1,0:T(8,128)(2,1)}, bf16[1536,1152]{1,0:T(8,128)(2,1)}, u32[]{:S(2)}, u32[]{:S(2)}) collective-permute-start(bf16[1536,1152]{1,0:T(8,128)(2,1)} %refs_3_.1), channel_id=1, source_target_pairs={{0,1},{1,0},{2,3},{3,2},{4,5},{5,4},{6,7},{7,6},{8,9},{9,8},{10,11... | collective-permute-start | bytes 10616840 | tf_op jit(solution)/shard_map/ppermute | solution.py:50
  52.6 3.9 %copy-start = (s32[4]{0:T(128)S(1)}, s32[4]{0:T(128)}, u32[]{:S(2)}) copy-start(s32[4]{0:T(128)} %lengths.1) | copy-start | bytes 52
  53.0 6.5 %collective-permute-start.12 = (bf16[32,3200]{1,0:T(8,128)(2,1)S(1)}, bf16[32,3200]{1,0:T(8,128)(2,1)S(1)}, u32[]{:S(2)}, u32[]{:S(2)}) collective-permute-start(bf16[32,3200]{1,0:T(8,128)(2,1)S(1)} %get-tuple-element.51), channel_id=1, source_target_pairs={{0,16},{1,65},{2,18},{3,67},{4,20},{5,69},{6,22},{7,71},{8,24},{9,... | collective-permute-start | bytes 614408 | tf_op jit(solution)/shard_map/ppermute | solution.py:42
  55.7 5.7 %collective-permute-start.13 = (bf16[32,3200]{1,0:T(8,128)(2,1)S(1)}, bf16[32,3200]{1,0:T(8,128)(2,1)S(1)}, u32[]{:S(2)}, u32[]{:S(2)}) collective-permute-start(bf16[32,3200]{1,0:T(8,128)(2,1)S(1)} %get-tuple-element.52), channel_id=1, source_target_pairs={{0,8},{1,33},{2,10},{3,35},{4,12},{5,37},{6,14},{7,39},{8,0},{9,41... | collective-permute-start | bytes 614408 | tf_op jit(solution)/shard_map/ppermute | solution.py:42
  56.1 5.8 %collective-permute-start.14 = (bf16[32,3200]{1,0:T(8,128)(2,1)S(1)}, bf16[32,3200]{1,0:T(8,128)(2,1)S(1)}, u32[]{:S(2)}, u32[]{:S(2)}) collective-permute-start(bf16[32,3200]{1,0:T(8,128)(2,1)S(1)} %get-tuple-element.53), channel_id=1, source_target_pairs={{0,24},{1,97},{2,26},{3,99},{4,28},{5,101},{6,30},{7,103},{8,16},{... | collective-permute-start | bytes 614408 | tf_op jit(solution)/shard_map/ppermute | solution.py:42
  62.6 4.5 %collective-permute-start.15 = (bf16[8,3200]{1,0:T(8,128)(2,1)S(1)}, bf16[8,3200]{1,0:T(8,128)(2,1)S(1)}, u32[]{:S(2)}, u32[]{:S(2)}) collective-permute-start(bf16[8,3200]{1,0:T(8,128)(2,1)S(1)} %get-tuple-element.55), channel_id=1, source_target_pairs={{0,4},{1,5},{2,6},{3,7},{4,0},{5,1},{6,2},{7,3},{8,12},{9,13},{10,... | collective-permute-start | bytes 153608 | tf_op jit(solution)/shard_map/ppermute | solution.py:46
  65.3 3.0 %collective-permute-start.16 = (bf16[8,3200]{1,0:T(8,128)(2,1)S(1)}, bf16[8,3200]{1,0:T(8,128)(2,1)S(1)}, u32[]{:S(2)}, u32[]{:S(2)}) collective-permute-start(bf16[8,3200]{1,0:T(8,128)(2,1)S(1)} %get-tuple-element.56), channel_id=1, source_target_pairs={{0,2},{1,3},{2,0},{3,1},{4,6},{5,7},{6,4},{7,5},{8,10},{9,11},{10,... | collective-permute-start | bytes 153608 | tf_op jit(solution)/shard_map/ppermute | solution.py:46
  65.6 4.2 %collective-permute-start.17 = (bf16[8,3200]{1,0:T(8,128)(2,1)S(1)}, bf16[8,3200]{1,0:T(8,128)(2,1)S(1)}, u32[]{:S(2)}, u32[]{:S(2)}) collective-permute-start(bf16[8,3200]{1,0:T(8,128)(2,1)S(1)} %get-tuple-element.57), channel_id=1, source_target_pairs={{0,6},{1,7},{2,4},{3,5},{4,2},{5,3},{6,0},{7,1},{8,14},{9,15},{10,... | collective-permute-start | bytes 153608 | tf_op jit(solution)/shard_map/ppermute | solution.py:46
  76.6 4.5 %collective-permute-start.18 = (bf16[8,3072]{1,0:T(8,128)(2,1)S(1)}, bf16[8,3072]{1,0:T(8,128)(2,1)S(1)}, u32[]{:S(2)}, u32[]{:S(2)}) collective-permute-start(bf16[8,3072]{1,0:T(8,128)(2,1)S(1)} %get-tuple-element.59), channel_id=1, source_target_pairs={{0,4},{1,5},{2,6},{3,7},{4,0},{5,1},{6,2},{7,3},{8,12},{9,13},{10,... | collective-permute-start | bytes 147464 | tf_op jit(solution)/shard_map/ppermute | solution.py:46
  77.7 3.5 %collective-permute-start.19 = (bf16[8,3072]{1,0:T(8,128)(2,1)S(1)}, bf16[8,3072]{1,0:T(8,128)(2,1)S(1)}, u32[]{:S(2)}, u32[]{:S(2)}) collective-permute-start(bf16[8,3072]{1,0:T(8,128)(2,1)S(1)} %get-tuple-element.60), channel_id=1, source_target_pairs={{0,2},{1,3},{2,0},{3,1},{4,6},{5,7},{6,4},{7,5},{8,10},{9,11},{10,... | collective-permute-start | bytes 147464 | tf_op jit(solution)/shard_map/ppermute | solution.py:46
  78.3 4.2 %collective-permute-start.20 = (bf16[8,3072]{1,0:T(8,128)(2,1)S(1)}, bf16[8,3072]{1,0:T(8,128)(2,1)S(1)}, u32[]{:S(2)}, u32[]{:S(2)}) collective-permute-start(bf16[8,3072]{1,0:T(8,128)(2,1)S(1)} %get-tuple-element.61), channel_id=1, source_target_pairs={{0,6},{1,7},{2,4},{3,5},{4,2},{5,3},{6,0},{7,1},{8,14},{9,15},{10,... | collective-permute-start | bytes 147464 | tf_op jit(solution)/shard_map/ppermute | solution.py:46
  83.0 6.1 %collective-permute-start.21 = (bf16[32,3072]{1,0:T(8,128)(2,1)S(1)}, bf16[32,3072]{1,0:T(8,128)(2,1)S(1)}, u32[]{:S(2)}, u32[]{:S(2)}) collective-permute-start(bf16[32,3072]{1,0:T(8,128)(2,1)S(1)} %line_up.1), channel_id=1, source_target_pairs={{0,64},{1,17},{2,66},{3,19},{4,68},{5,21},{6,70},{7,23},{8,72},{9,... | collective-permute-start | bytes 589832 | tf_op jit(solution)/shard_map/ppermute | solution.py:38
  85.0 6.1 %collective-permute-start.22 = (bf16[32,3072]{1,0:T(8,128)(2,1)S(1)}, bf16[32,3072]{1,0:T(8,128)(2,1)S(1)}, u32[]{:S(2)}, u32[]{:S(2)}) collective-permute-start(bf16[32,3072]{1,0:T(8,128)(2,1)S(1)} %line_up.1), channel_id=1, source_target_pairs={{0,32},{1,9},{2,34},{3,11},{4,36},{5,13},{6,38},{7,15},{8,40},{9,1... | collective-permute-start | bytes 589832 | tf_op jit(solution)/shard_map/ppermute | solution.py:38
  86.0 5.7 %collective-permute-start.23 = (bf16[32,3072]{1,0:T(8,128)(2,1)S(1)}, bf16[32,3072]{1,0:T(8,128)(2,1)S(1)}, u32[]{:S(2)}, u32[]{:S(2)}) collective-permute-start(bf16[32,3072]{1,0:T(8,128)(2,1)S(1)} %line_up.1), channel_id=1, source_target_pairs={{0,96},{1,25},{2,98},{3,27},{4,100},{5,29},{6,102},{7,31},{8,104},... | collective-permute-start | bytes 589832 | tf_op jit(solution)/shard_map/ppermute | solution.py:38
  91.8 14.9 %collective-permute-start.24 = (bf16[128,3072]{1,0:T(8,128)(2,1)S(1)}, bf16[128,3072]{1,0:T(8,128)(2,1)S(1)}, u32[]{:S(2)}, u32[]{:S(2)}) collective-permute-start(bf16[128,3072]{1,0:T(8,128)(2,1)S(1)} %pad_maximum_fusion.refs_0_), channel_id=1, source_target_pairs={{0,8},{1,33},{2,10},{3,35},{4,12},{5,37},{6,14},{7,39},{8,0},{9,41... | collective-permute-start | bytes 2359304 | tf_op jit(solution)/shard_map/ppermute | solution.py:42
  92.3 14.8 %collective-permute-start.25 = (bf16[128,3072]{1,0:T(8,128)(2,1)S(1)}, bf16[128,3072]{1,0:T(8,128)(2,1)S(1)}, u32[]{:S(2)}, u32[]{:S(2)}) collective-permute-start(bf16[128,3072]{1,0:T(8,128)(2,1)S(1)} %pad_maximum_fusion.refs_0_), channel_id=1, source_target_pairs={{0,24},{1,97},{2,26},{3,99},{4,28},{5,101},{6,30},{7,103},{8,16},{... | collective-permute-start | bytes 2359304 | tf_op jit(solution)/shard_map/ppermute | solution.py:42
  107.1 12.3 %collective-permute-start.27 = (bf16[128,3072]{1,0:T(8,128)(2,1)S(1)}, bf16[128,3072]{1,0:T(8,128)(2,1)S(1)}, u32[]{:S(2)}, u32[]{:S(2)}) collective-permute-start(bf16[128,3072]{1,0:T(8,128)(2,1)S(1)} %pad_maximum_fusion.refs_0_), channel_id=1, source_target_pairs={{0,16},{1,65},{2,18},{3,67},{4,20},{5,69},{6,22},{7,71},{8,24},{9,... | collective-permute-start | bytes 2359304 | tf_op jit(solution)/shard_map/ppermute | solution.py:42
  121.5 7.4 %collective-permute-start.28 = (bf16[128,1152]{1,0:T(8,128)(2,1)S(1)}, bf16[128,1152]{1,0:T(8,128)(2,1)S(1)}, u32[]{:S(2)}, u32[]{:S(2)}) collective-permute-start(bf16[128,1152]{1,0:T(8,128)(2,1)S(1)} %get-tuple-element.68), channel_id=1, source_target_pairs={{0,4},{1,5},{2,6},{3,7},{4,0},{5,1},{6,2},{7,3},{8,12},{9,13},{10,... | collective-permute-start | bytes 884744 | tf_op jit(solution)/shard_map/ppermute | solution.py:46
  122.7 8.8 %collective-permute-start.29 = (bf16[128,1152]{1,0:T(8,128)(2,1)S(1)}, bf16[128,1152]{1,0:T(8,128)(2,1)S(1)}, u32[]{:S(2)}, u32[]{:S(2)}) collective-permute-start(bf16[128,1152]{1,0:T(8,128)(2,1)S(1)} %get-tuple-element.69), channel_id=1, source_target_pairs={{0,2},{1,3},{2,0},{3,1},{4,6},{5,7},{6,4},{7,5},{8,10},{9,11},{10,... | collective-permute-start | bytes 884744 | tf_op jit(solution)/shard_map/ppermute | solution.py:46
  124.2 7.6 %collective-permute-start.30 = (bf16[128,1152]{1,0:T(8,128)(2,1)S(1)}, bf16[128,1152]{1,0:T(8,128)(2,1)S(1)}, u32[]{:S(2)}, u32[]{:S(2)}) collective-permute-start(bf16[128,1152]{1,0:T(8,128)(2,1)S(1)} %get-tuple-element.70), channel_id=1, source_target_pairs={{0,6},{1,7},{2,4},{3,5},{4,2},{5,3},{6,0},{7,1},{8,14},{9,15},{10,... | collective-permute-start | bytes 884744 | tf_op jit(solution)/shard_map/ppermute | solution.py:46
  132.0 12.0 %collective-permute-start.31 = (bf16[64,1152]{1,0:T(8,128)(2,1)S(1)}, bf16[64,1152]{1,0:T(8,128)(2,1)S(1)}, u32[]{:S(2)}, u32[]{:S(2)}) collective-permute-start(bf16[64,1152]{1,0:T(8,128)(2,1)S(1)} %get-tuple-element.72), channel_id=1, source_target_pairs={{0,1},{1,0},{2,3},{3,2},{4,5},{5,4},{6,7},{7,6},{8,9},{9,8},{10,11... | collective-permute-start | bytes 442376 | tf_op jit(solution)/shard_map/ppermute | solution.py:50

commit v8 on v7

--- a/solution.py
+++ b/solution.py
@@ -342,7 +342,7 @@
 
 def attend_one(request, lengths, keys, values, count, query_rows, new_kv, result):
     per = STEPS * count
-    start = pl.multiple_of(request * per, per)
+    start = request * per
     query = jnp.concatenate([query_rows[i, pl.ds(start, per), :] for i in range(2)], axis=-1)
     query = (query.astype(BF16).astype(F32) * HD ** (-0.5)).astype(BF16)
     dims = (((1,), (1,)), ((), ()))
@@ -368,71 +368,74 @@
 
 def attend_kernel(lengths, place, *refs):
     packed, (cosine, sine, keys, values), outs = refs[:4], refs[4:8], refs[8:12]
-    query_rows, new_pieces, new_kv, result = refs[12:]
-    request = pl.program_id(0)
+    query_rows, new_pieces, new_kv, result, key_rows, value_rows, sems = refs[12:]
+    requests = keys.shape[0]
+    loads = []
+    for r in range(requests):
+        loads.append(
+            [
+                pltpu.make_async_copy(source.at[r], target.at[r], sems.at[r, i])
+                for i, (source, target) in enumerate(((keys, key_rows), (values, value_rows)))
+            ]
+        )
+        for load in loads[r]:
+            load.start()
     width = outs[0].shape[1]
     heads = width // HD
     count = 4 * heads
-
-    @pl.when(request == 0)
-    def _():
-        x, c = place[2], place[3]
-        cos, sin = cosine[...], sine[...]
-
-        def rotated(first, second):
-            return first * cos - second * sin, second * cos + first * sin
-
-        for m, rows in zip(ORDER, packed):
-            rows = rows[...].astype(F32)
-            for h in range(heads):
-                head = rows[:, h * HD : h * HD + HD]
-                for i, half in enumerate(rotated(head[:, :128], head[:, 128:])):
-                    query_rows[i, pl.ds(m * heads + h, 8, stride=count), :] = half
-            size = (rows.shape[1] - width) // 2
-            for j in range(2):
-                at = width + j * size
-                new_pieces[(x ^ m) * 2 + (c ^ j)] = rows[:, at : at + size]
+    x, c = place[2], place[3]
+    cos, sin = cosine[...], sine[...]
+
+    def rotated(first, second):
+        return first * cos - second * sin, second * cos + first * sin
+
+    for m, rows in zip(ORDER, packed):
+        rows = rows[...].astype(F32)
+        for h in range(heads):
+            head = rows[:, h * HD : h * HD + HD]
+            for i, half in enumerate(rotated(head[:, :128], head[:, 128:])):
+                query_rows[i, pl.ds(m * heads + h, 8, stride=count), :] = half
+        size = (rows.shape[1] - width) // 2
+        for j in range(2):
+            at = width + j * size
+            new_pieces[(x ^ m) * 2 + (c ^ j)] = rows[:, at : at + size]
+    halves = [jnp.concatenate([new_pieces[i], new_pieces[i + 1]], axis=-1) for i in range(0, 8, 2)]
+    new_kv[0] = jnp.concatenate(rotated(halves[0], halves[1]), axis=-1).astype(BF16)
+    new_kv[1] = jnp.concatenate(halves[2:], axis=-1).astype(BF16)
+    for at in range(0, requests, GROUP):
+        for r in range(at, at + GROUP):
+            for load in loads[r]:
+                load.wait()
+        for r in range(at, at + GROUP):
+            attend_one(
+                r, lengths, key_rows.at[r], value_rows.at[r], count, query_rows, new_kv, result
+            )
+    for m, out in enumerate(outs):
         halves = [
-            jnp.concatenate([new_pieces[i], new_pieces[i + 1]], axis=-1) for i in range(0, 8, 2)
+            result[i, pl.ds(m * heads + h, 8, stride=count), :]
+            for h in range(heads)
+            for i in range(2)
         ]
-        new_kv[0] = jnp.concatenate(rotated(halves[0], halves[1]), axis=-1).astype(BF16)
-        new_kv[1] = jnp.concatenate(halves[2:], axis=-1).astype(BF16)
-
-    for i in range(keys.shape[0]):
-        attend_one(request * keys.shape[0] + i, lengths, keys.at[i], values.at[i], count, query_rows, new_kv, result)
-
-    @pl.when(request == pl.num_programs(0) - 1)
-    def _():
-        for m, out in enumerate(outs):
-            halves = [
-                result[i, pl.ds(m * heads + h, 8, stride=count), :]
-                for h in range(heads)
-                for i in range(2)
-            ]
-            out[...] = jnp.concatenate(halves, axis=-1).astype(BF16)
+        out[...] = jnp.concatenate(halves, axis=-1).astype(BF16)
 
 
 def attend(place, packed, cosine, sine, cache_keys, cache_values, lengths, width):
-    requests, slots, _ = cache_keys.shape
     total = packed[0].shape[1]
     count = 4 * (width // HD)
-    whole = lambda *shape: pl.BlockSpec(shape, lambda r, *_: (0,) * len(shape))
-    cache = pl.BlockSpec((GROUP, slots, HD), lambda r, *_: (r, 0, 0))
     return pl.pallas_call(
         attend_kernel,
         out_shape=[jax.ShapeDtypeStruct((8, width), BF16)] * 4,
-        grid_spec=pltpu.PrefetchScalarGridSpec(
-            num_scalar_prefetch=2,
-            grid=(requests // GROUP,),
-            in_specs=[whole(8, total)] * 4 + [whole(8, 128)] * 2 + [cache] * 2,
-            out_specs=[whole(8, width)] * 4,
-            scratch_shapes=[
-                pltpu.VMEM((2, 8 * count, 128), F32),
-                pltpu.VMEM((8, 8, (total - width) // 2), F32),
-                pltpu.VMEM((2, 8, HD), BF16),
-                pltpu.VMEM((2, 8 * count, 128), F32),
-            ],
-        ),
+        in_specs=[SMEM] * 2 + [VMEM] * 6 + [ANY] * 2,
+        out_specs=[VMEM] * 4,
+        scratch_shapes=[
+            pltpu.VMEM((2, 8 * count, 128), F32),
+            pltpu.VMEM((8, 8, (total - width) // 2), F32),
+            pltpu.VMEM((2, 8, HD), BF16),
+            pltpu.VMEM((2, 8 * count, 128), F32),
+            pltpu.VMEM(cache_keys.shape, BF16),
+            pltpu.VMEM(cache_values.shape, BF16),
+            pltpu.SemaphoreType.DMA((cache_keys.shape[0], 2)),
+        ],
         compiler_params=params(52),
         cost_estimate=cost(6e9, 1.8e7),
         name="attend",
@@ -535,29 +538,6 @@
         cost_estimate=cost(1e8, 1e6),
         name="last_sum",
     )(*values)
-
-
-def interleave_kernel(place, mine, theirs, out):
-    first, second = mine[...].astype(F32), theirs[...].astype(F32)
-    swap = place[3] == 1
-    first, second = jnp.where(swap, second, first), jnp.where(swap, first, second)
-    groups = []
-    for i in range(8):
-        groups += [first[i * 8 : i * 8 + 8], second[i * 8 : i * 8 + 8]]
-    out[...] = jnp.concatenate(groups, axis=0).astype(BF16)
-
-
-def interleave(place, mine, theirs):
-    rows, width = mine.shape
-    return pl.pallas_call(
-        interleave_kernel,
-        out_shape=jax.ShapeDtypeStruct((2 * rows, width), BF16),
-        in_specs=[SMEM] + [VMEM] * 2,
-        out_specs=VMEM,
-        compiler_params=params(8),
-        cost_estimate=cost(1e8, 1e6),
-        name="interleave",
-    )(place, mine, theirs)
 
 
 def per_device(tokens, norm_gain, w_query, w_keyvalue, w_out, cache_keys, cache_values, lengths):
@@ -601,13 +581,16 @@
     rows = line_up(place, exchanged(along_x, attended))
     rows = jnp.concatenate(exchanged(along_first, [rows] * 4), axis=0)
     near = [along_second(rows, 1), along_second(rows, 3)]
-    late, *near = lax.optimization_barrier((rows, *near))
+    late, near[0] = lax.optimization_barrier((rows, near[0]))
     blocks = [rows, near[0], along_second(late, 2), near[1]]
     weights = [w_out, other_core(w_out)]
     done, tiles = mix([blocks[0], blocks[1], blocks[3]], weights)
     parts = mix_rest(place, done, blocks[2], tiles)
     mine, theirs = last_sum(exchanged(along_x, parts))
-    return interleave(place, mine, other_core(theirs))
+    theirs, width = other_core(theirs), mine.shape[1]
+    pair = jnp.stack([mine.reshape(8, 8, width), theirs.reshape(8, 8, width)], axis=1)
+    swapped = jnp.stack([theirs.reshape(8, 8, width), mine.reshape(8, 8, width)], axis=1)
+    return jnp.where(place[3] == 1, swapped, pair).reshape(128, width)
 
 
 def solution(mesh):

time: 146 us -> 144 us (0.986)
  starting transfers between devices: 54.4 us -> 52.4 us
  Pallas kernels: 32.4 us -> 30.8 us
  transfers between devices with their start and end apart: 33 -> 33, of which waited for: 23 -> 22; matrix products, arithmetic and copies ran while one was open for 1% -> 1% of each run, Pallas kernels for 19% -> 19%
where the time goes in v8:
time: 144 us; the launch traced here: 143 us
  waiting for transfers between devices  55.2 us (38%)
  starting transfers between devices  52.4 us (36%)
  Pallas kernels  30.8 us (21%)
  local copies, waits for them, and re-layouts  3.3 us (2%)
    ppermute x6, waiting for transfers between devices, along_second(): return lax.ppermute(value, ('gx', 'gy'), exchange_pairs(1, m))  23 us
    ppermute x6, waiting for transfers between devices, along_first(): return lax.ppermute(value, ('gx', 'gy'), exchange_pairs(0, m))  17.9 us
    ppermute x12, starting transfers between devices, along_x(): return lax.ppermute(value, 'gy', [(g, g ^ 2 * m) for g in range(8)])  14.4 us
    ppermute x8, starting transfers between devices, other_core(): return lax.ppermute(value, 'gy', [(g, g ^ 1) for g in range(8)])  14.3 us
    ppermute x12, waiting for transfers between devices, along_x(): return lax.ppermute(value, 'gy', [(g, g ^ 2 * m) for g in range(8)])  12.5 us
    all_to_all x1, starting transfers between devices, per_device(): stats = lax.all_to_all(stats, ('gx', 'gy'), 0, 0, tiled=True)  10 us
    ppermute x6, starting transfers between devices, along_first(): return lax.ppermute(value, ('gx', 'gy'), exchange_pairs(0, m))  7.24 us
    pallas_call x1, Pallas kernels, mix(): pl.pallas_call(mix_kernel, out_shape=[jax.ShapeDtypeStruct((384, width),...  6.78 us
  transfers between devices with their start and end apart: 33, of which 22 were waited for; matrix products, arithmetic and copies ran while one was open for 1% of the time, Pallas kernels for 19%

profile of v8, /device:TPU:1, one launch (start us, length us, event | category | flops | bytes accessed | tf_op | source)
XLA Modules:
  0.0 143.3 jit_solution(16727637231223005741)
XLA Ops:
  0.0 1.4 collective-permute-start.7
  1.4 2.8 %collective-permute-start = (bf16[128,1152]{1,0:T(8,128)(2,1)}, bf16[128,1152]{1,0:T(8,128)(2,1)S(1)}, u32[]{:S(2)}, u32[]{:S(2)}) collective-permute-start(bf16[128,1152]{1,0:T(8,128)(2,1)} %tokens.1), channel_id=1, source_target_pairs={{0,4},{1,5},{2,6},{3,7},{4,0},{5,1},{6,2},{7,3},{8,12},{9,13},{10,... | collective-permute-start | bytes 884744 | tf_op jit(solution)/shard_map/ppermute | solution.py:46
  4.6 0.6 collective-permute-start.2
  5.1 0.6 collective-permute-start.8
  5.7 1.0 copy-done.1
  6.6 1.0 prepare.1
  7.6 10.0 %all-to-all-start = ((f32[128,1,256]{2,1,0:T(1,128)}), f32[128,1,256]{2,1,0:T(1,128)S(1)}, u32[]{:S(2)}, u32[]{:S(2)}) async-start(f32[128,1,256]{2,1,0:T(1,128)} %get-tuple-element.40), calls=%async_computation | async-start | bytes 262144 | tf_op jit(solution)/shard_map/all_to_all | solution.py:550
  17.7 0.7 broadcast_in_dim.2.gain
  18.4 1.1 collective-permute-start.3
  19.6 0.4 collective-permute-start.5
  20.2 0.9 pad_maximum_fusion.1.refs_10_.refs_2_
  21.1 0.4 collective-permute-done.5.refs_6_
  21.5 0.4 collective-permute-done.6.refs_7_
  21.9 5.6 %project.1 = (bf16[256,3200]{1,0:T(8,128)(2,1)S(1)}, f32[8,3200]{1,0:T(8,128)S(1)}, bf16[256,1152]{1,0:T(8,128)(2,1)S(1)}) custom-call(s32[4]{0:T(128)S(1)} %pad_add_fusion.place, bf16[1,1152]{1,0:T(2,128)(2,1)S(1)} %broadcast_in_dim.2.gain, bf16[128,1152]{1,0:T(8,128)(2,1)S(1)} %get-tuple-element.38.refs_0_, ...), custom_call_target="tpu_custom_call" | custom-call | flops 4000000000 | bytes 10000000 | tf_op jit(solution)/shard_map/project/pallas_call | solution.py:170
  27.5 0.8 copy-done.2
  28.4 1.6 %scale.1 = (bf16[128,3200]{1,0:T(8,128)(2,1)S(1)}, bf16[128,3200]{1,0:T(8,128)(2,1)S(1)}) custom-call(s32[4]{0:T(128)S(1)} %pad_add_fusion.place, f32[128,256]{1,0:T(8,128)S(1)} %bitcast.12, f32[8,3200]{1,0:T(8,128)S(1)} %get-tuple-element.42.gain_row, bf16[256,3200]{1,0:T(8,128)(2,1)S(1)} %get-tuple-element.46.parts), custom_call_target="tpu_custom_call" | custom-call | flops 1000000000 | bytes 2000000 | tf_op jit(solution)/shard_map/scale/pallas_call | solution.py:223
  30.0 0.9 collective-permute-start.10
  30.9 2.1 %collective-permute-start.11 = (bf16[128,3200]{1,0:T(8,128)(2,1)S(1)}, bf16[128,3200]{1,0:T(8,128)(2,1)S(1)}, u32[]{:S(2)}, u32[]{:S(2)}) collective-permute-start(bf16[128,3200]{1,0:T(8,128)(2,1)S(1)} %get-tuple-element.48), channel_id=1, source_target_pairs={{0,96},{1,25},{2,98},{3,27},{4,100},{5,29},{6,102},{7,31},{8,104},... | collective-permute-start | bytes 2457608 | tf_op jit(solution)/shard_map/ppermute | solution.py:38
  32.9 5.4 %project_rest.1 = (bf16[128,3200]{1,0:T(8,128)(2,1)S(1)}, bf16[128,3200]{1,0:T(8,128)(2,1)S(1)}) custom-call(s32[4]{0:T(128)S(1)} %pad_add_fusion.place, f32[128,256]{1,0:T(8,128)S(1)} %bitcast.13, f32[8,3200]{1,0:T(8,128)S(1)} %get-tuple-element.42.gain_row, bf16[256,1152]{1,0:T(8,128)(2,1)S(1)} %copy-done.3, bf16[1152,1536]{1,0:T(8,128)(2,1)} %refs_0_.1, ...), custom_call_target="tpu_custom_call" | custom-call | flops 5000000000 | bytes 10000000 | tf_op jit(solution)/shard_map/project_rest/pallas_call | solution.py:256
  38.4 1.0 collective-permute-start.9
  39.3 0.7 collective-permute-start.26
  40.0 1.5 %collective-permute-done.10.refs_2_ = bf16[128,3200]{1,0:T(8,128)(2,1)S(1)} collective-permute-done((bf16[128,3200]{1,0:T(8,128)(2,1)S(1)}, bf16[128,3200]{1,0:T(8,128)(2,1)S(1)}, u32[]{:S(2)}, u32[]{:S(2)}) %collective-permute-start.10) | collective-permute-done | bytes 819232 | tf_op jit(solution)/shard_map/ppermute | solution.py:38
  41.5 9.4 %collective-permute-done.11.refs_3_ = bf16[128,3200]{1,0:T(8,128)(2,1)S(1)} collective-permute-done((bf16[128,3200]{1,0:T(8,128)(2,1)S(1)}, bf16[128,3200]{1,0:T(8,128)(2,1)S(1)}, u32[]{:S(2)}, u32[]{:S(2)}) %collective-permute-start.11) | collective-permute-done | bytes 819232 | tf_op jit(solution)/shard_map/ppermute | solution.py:38
  51.0 1.6 %collective-permute-done.9.refs_1_ = bf16[128,3200]{1,0:T(8,128)(2,1)S(1)} collective-permute-done((bf16[128,3200]{1,0:T(8,128)(2,1)S(1)}, bf16[128,3200]{1,0:T(8,128)(2,1)S(1)}, u32[]{:S(2)}, u32[]{:S(2)}) %collective-permute-start.9) | collective-permute-done | bytes 819232 | tf_op jit(solution)/shard_map/ppermute | solution.py:38
  52.6 0.4 add_and_cut.1
  53.0 2.7 %collective-permute-start.12 = (bf16[32,3200]{1,0:T(8,128)(2,1)S(1)}, bf16[32,3200]{1,0:T(8,128)(2,1)S(1)}, u32[]{:S(2)}, u32[]{:S(2)}) collective-permute-start(bf16[32,3200]{1,0:T(8,128)(2,1)S(1)} %get-tuple-element.50), channel_id=1, source_target_pairs={{0,16},{1,65},{2,18},{3,67},{4,20},{5,69},{6,22},{7,71},{8,24},{9,... | collective-permute-start | bytes 614408 | tf_op jit(solution)/shard_map/ppermute | solution.py:42
  55.7 0.4 collective-permute-start.13
  56.6 2.9 %collective-permute-done.12.refs_1_ = bf16[32,3200]{1,0:T(8,128)(2,1)S(1)} collective-permute-done((bf16[32,3200]{1,0:T(8,128)(2,1)S(1)}, bf16[32,3200]{1,0:T(8,128)(2,1)S(1)}, u32[]{:S(2)}, u32[]{:S(2)}) %collective-permute-start.12) | collective-permute-done | bytes 204832 | tf_op jit(solution)/shard_map/ppermute | solution.py:42
  59.5 1.9 %collective-permute-done.13.refs_2_ = bf16[32,3200]{1,0:T(8,128)(2,1)S(1)} collective-permute-done((bf16[32,3200]{1,0:T(8,128)(2,1)S(1)}, bf16[32,3200]{1,0:T(8,128)(2,1)S(1)}, u32[]{:S(2)}, u32[]{:S(2)}) %collective-permute-start.13) | collective-permute-done | bytes 204832 | tf_op jit(solution)/shard_map/ppermute | solution.py:42
  61.4 0.5 collective-permute-done.14.refs_3_
  61.9 0.7 finish.1
  62.6 2.7 %collective-permute-start.15 = (bf16[8,3200]{1,0:T(8,128)(2,1)S(1)}, bf16[8,3200]{1,0:T(8,128)(2,1)S(1)}, u32[]{:S(2)}, u32[]{:S(2)}) collective-permute-start(bf16[8,3200]{1,0:T(8,128)(2,1)S(1)} %get-tuple-element.54), channel_id=1, source_target_pairs={{0,4},{1,5},{2,6},{3,7},{4,0},{5,1},{6,2},{7,3},{8,12},{9,13},{10,... | collective-permute-start | bytes 153608 | tf_op jit(solution)/shard_map/ppermute | solution.py:46
  65.6 1.0 collective-permute-start.17
  66.7 0.4 collective-permute-done.15.refs_1_
  67.1 1.1 collective-permute-done.16.refs_2_
  68.2 1.5 %collective-permute-done.17.refs_3_ = bf16[8,3200]{1,0:T(8,128)(2,1)S(1)} collective-permute-done((bf16[8,3200]{1,0:T(8,128)(2,1)S(1)}, bf16[8,3200]{1,0:T(8,128)(2,1)S(1)}, u32[]{:S(2)}, u32[]{:S(2)}) %collective-permute-start.17) | collective-permute-done | bytes 51232 | tf_op jit(solution)/shard_map/ppermute | solution.py:46
  69.8 6.6 %attend.1 = (bf16[8,3072]{1,0:T(8,128)(2,1)S(1)}, bf16[8,3072]{1,0:T(8,128)(2,1)S(1)}, bf16[8,3072]{1,0:T(8,128)(2,1)S(1)}, bf16[8,3072]{1,0:T(8,128)(2,1)S(1)}) custom-call(s32[4]{0:T(128)S(1)} %copy-done, s32[4]{0:T(128)S(1)} %pad_add_fusion.place, bf16[8,3200]{1,0:T(8,128)(2,1)S(1)} %get-tuple-element.53.refs_0_, ...), custom_call_target="tpu_custom_call" | custom-call | flops 6000000000 | bytes 18000000 | tf_op jit(solution)/shard_map/attend/pallas_call | solution.py:425
  76.4 1.1 collective-permute-start.18
  77.5 0.6 collective-permute-start.19
  78.1 1.7 %collective-permute-start.20 = (bf16[8,3072]{1,0:T(8,128)(2,1)S(1)}, bf16[8,3072]{1,0:T(8,128)(2,1)S(1)}, u32[]{:S(2)}, u32[]{:S(2)}) collective-permute-start(bf16[8,3072]{1,0:T(8,128)(2,1)S(1)} %get-tuple-element.60), channel_id=1, source_target_pairs={{0,6},{1,7},{2,4},{3,5},{4,2},{5,3},{6,0},{7,1},{8,14},{9,15},{10,... | collective-permute-start | bytes 147464 | tf_op jit(solution)/shard_map/ppermute | solution.py:46
  79.7 1.2 collective-permute-done.18.refs_1_
  80.9 1.3 collective-permute-done.20.refs_3_
  82.2 0.6 line_up.1
  82.8 2.0 %collective-permute-start.21 = (bf16[32,3072]{1,0:T(8,128)(2,1)S(1)}, bf16[32,3072]{1,0:T(8,128)(2,1)S(1)}, u32[]{:S(2)}, u32[]{:S(2)}) collective-permute-start(bf16[32,3072]{1,0:T(8,128)(2,1)S(1)} %line_up.1), channel_id=1, source_target_pairs={{0,64},{1,17},{2,66},{3,19},{4,68},{5,21},{6,70},{7,23},{8,72},{9,... | collective-permute-start | bytes 589832 | tf_op jit(solution)/shard_map/ppermute | solution.py:38
  84.8 0.9 collective-permute-start.22
  85.7 0.4 collective-permute-start.23
  86.1 2.8 %collective-permute-done.21 = bf16[32,3072]{1,0:T(8,128)(2,1)S(1)} collective-permute-done((bf16[32,3072]{1,0:T(8,128)(2,1)S(1)}, bf16[32,3072]{1,0:T(8,128)(2,1)S(1)}, u32[]{:S(2)}, u32[]{:S(2)}) %collective-permute-start.21) | collective-permute-done | bytes 196640 | tf_op jit(solution)/shard_map/ppermute | solution.py:38
  88.9 2.0 %collective-permute-done.22 = bf16[32,3072]{1,0:T(8,128)(2,1)S(1)} collective-permute-done((bf16[32,3072]{1,0:T(8,128)(2,1)S(1)}, bf16[32,3072]{1,0:T(8,128)(2,1)S(1)}, u32[]{:S(2)}, u32[]{:S(2)}) %collective-permute-start.22) | collective-permute-done | bytes 196640 | tf_op jit(solution)/shard_map/ppermute | solution.py:38
  90.9 0.6 collective-permute-done.23
  91.5 0.5 collective-permute-start.24
  92.1 1.8 %collective-permute-start.25 = (bf16[128,3072]{1,0:T(8,128)(2,1)S(1)}, bf16[128,3072]{1,0:T(8,128)(2,1)S(1)}, u32[]{:S(2)}, u32[]{:S(2)}) collective-permute-start(bf16[128,3072]{1,0:T(8,128)(2,1)S(1)} %pad_maximum_fusion.refs_0_), channel_id=1, source_target_pairs={{0,24},{1,97},{2,26},{3,99},{4,28},{5,101},{6,30},{7,103},{8,16},{... | collective-permute-start | bytes 2359304 | tf_op jit(solution)/shard_map/ppermute | solution.py:42
  93.8 12.6 %collective-permute-done.24.refs_1_ = bf16[128,3072]{1,0:T(8,128)(2,1)S(1)} collective-permute-done((bf16[128,3072]{1,0:T(8,128)(2,1)S(1)}, bf16[128,3072]{1,0:T(8,128)(2,1)S(1)}, u32[]{:S(2)}, u32[]{:S(2)}) %collective-permute-start.24) | collective-permute-done | bytes 786464 | tf_op jit(solution)/shard_map/ppermute | solution.py:42
  106.4 0.7 collective-permute-start.27
  107.1 6.8 %mix.1 = (bf16[384,1152]{1,0:T(8,128)(2,1)S(1)}, bf16[6,1536,384]{2,1,0:T(8,128)(2,1)S(1)}) custom-call(bf16[128,3072]{1,0:T(8,128)(2,1)S(1)} %pad_maximum_fusion.refs_0_, bf16[128,3072]{1,0:T(8,128)(2,1)S(1)} %collective-permute-done.24.refs_1_, bf16[128,3072]{1,0:T(8,128)(2,1)S(1)} %collective-permute-done.25.refs_2_, bf16[1536,1152]{1,0:T(8,128)(2,1)} %refs_3_.1, ...), custom_call_target="tpu_custom_call" | custom-call | flops 4000000000 | bytes 8000000 | tf_op jit(solution)/shard_map/mix/pallas_call | solution.py:495
  113.9 5.1 %collective-permute-done.27.last = bf16[128,3072]{1,0:T(8,128)(2,1)S(1)} collective-permute-done((bf16[128,3072]{1,0:T(8,128)(2,1)S(1)}, bf16[128,3072]{1,0:T(8,128)(2,1)S(1)}, u32[]{:S(2)}, u32[]{:S(2)}) %collective-permute-start.27) | collective-permute-done | bytes 786464 | tf_op jit(solution)/shard_map/ppermute | solution.py:42
  119.1 2.0 %mix_rest.1 = (bf16[128,1152]{1,0:T(8,128)(2,1)S(1)}, bf16[128,1152]{1,0:T(8,128)(2,1)S(1)}, bf16[128,1152]{1,0:T(8,128)(2,1)S(1)}, bf16[128,1152]{1,0:T(8,128)(2,1)S(1)}) custom-call(s32[4]{0:T(128)S(1)} %pad_add_fusion.place, bf16[384,1152]{1,0:T(8,128)(2,1)S(1)} %get-tuple-element.62.done, bf16[128,3072]{1,0:T(8,128)(2,1)S(1)} %collective-permute-done.27.last, ...), custom_call_target="tpu_custom_call" | custom-call | flops 4000000000 | bytes 8000000 | tf_op jit(solution)/shard_map/mix_rest/pallas_call | solution.py:512
  121.1 1.1 collective-permute-start.28
  122.2 1.5 %collective-permute-start.29 = (bf16[128,1152]{1,0:T(8,128)(2,1)S(1)}, bf16[128,1152]{1,0:T(8,128)(2,1)S(1)}, u32[]{:S(2)}, u32[]{:S(2)}) collective-permute-start(bf16[128,1152]{1,0:T(8,128)(2,1)S(1)} %get-tuple-element.67), channel_id=1, source_target_pairs={{0,2},{1,3},{2,0},{3,1},{4,6},{5,7},{6,4},{7,5},{8,10},{9,11},{10,... | collective-permute-start | bytes 884744 | tf_op jit(solution)/shard_map/ppermute | solution.py:46
  123.7 0.7 collective-permute-start.30
  124.4 3.9 %collective-permute-done.28.refs_1_ = bf16[128,1152]{1,0:T(8,128)(2,1)S(1)} collective-permute-done((bf16[128,1152]{1,0:T(8,128)(2,1)S(1)}, bf16[128,1152]{1,0:T(8,128)(2,1)S(1)}, u32[]{:S(2)}, u32[]{:S(2)}) %collective-permute-start.28) | collective-permute-done | bytes 294944 | tf_op jit(solution)/shard_map/ppermute | solution.py:46
  128.3 2.7 %collective-permute-done.29.refs_2_ = bf16[128,1152]{1,0:T(8,128)(2,1)S(1)} collective-permute-done((bf16[128,1152]{1,0:T(8,128)(2,1)S(1)}, bf16[128,1152]{1,0:T(8,128)(2,1)S(1)}, u32[]{:S(2)}, u32[]{:S(2)}) %collective-permute-start.29) | collective-permute-done | bytes 294944 | tf_op jit(solution)/shard_map/ppermute | solution.py:46
  131.6 9.9 %collective-permute-start.31 = (bf16[64,1152]{1,0:T(8,128)(2,1)S(1)}, bf16[64,1152]{1,0:T(8,128)(2,1)S(1)}, u32[]{:S(2)}, u32[]{:S(2)}) collective-permute-start(bf16[64,1152]{1,0:T(8,128)(2,1)S(1)} %get-tuple-element.69), channel_id=1, source_target_pairs={{0,1},{1,0},{2,3},{3,2},{4,5},{5,4},{6,7},{7,6},{8,9},{9,8},{10,11... | collective-permute-start | bytes 442376 | tf_op jit(solution)/shard_map/ppermute | solution.py:50
  141.5 1.0 collective-permute-done.31
  142.5 0.7 copy.13
  (32 shorter events, 2.2 us)
Async XLA Ops:
  0.0 21.9 %collective-permute-start.7 = (bf16[1152,1536]{1,0:T(8,128)(2,1)}, bf16[1152,1536]{1,0:T(8,128)(2,1)}, u32[]{:S(2)}, u32[]{:S(2)}) collective-permute-start(bf16[1152,1536]{1,0:T(8,128)(2,1)} %refs_0_.1), channel_id=1, source_target_pairs={{0,1},{1,0},{2,3},{3,2},{4,5},{5,4},{6,7},{7,6},{8,9},{9,8},{10,11... | collective-permute-start | bytes 10616840 | tf_op jit(solution)/shard_map/ppermute | solution.py:50
  1.4 18.1 %collective-permute-start = (bf16[128,1152]{1,0:T(8,128)(2,1)}, bf16[128,1152]{1,0:T(8,128)(2,1)S(1)}, u32[]{:S(2)}, u32[]{:S(2)}) collective-permute-start(bf16[128,1152]{1,0:T(8,128)(2,1)} %tokens.1), channel_id=1, source_target_pairs={{0,4},{1,5},{2,6},{3,7},{4,0},{5,1},{6,2},{7,3},{8,12},{9,13},{10,... | collective-permute-start | bytes 884744 | tf_op jit(solution)/shard_map/ppermute | solution.py:46
  4.2 15.3 %collective-permute-start.1 = (bf16[128,1152]{1,0:T(8,128)(2,1)}, bf16[128,1152]{1,0:T(8,128)(2,1)S(1)}, u32[]{:S(2)}, u32[]{:S(2)}) collective-permute-start(bf16[128,1152]{1,0:T(8,128)(2,1)} %tokens.1), channel_id=1, source_target_pairs={{0,2},{1,3},{2,0},{3,1},{4,6},{5,7},{6,4},{7,5},{8,10},{9,11},{10,... | collective-permute-start | bytes 884744 | tf_op jit(solution)/shard_map/ppermute | solution.py:46
  4.6 15.4 %collective-permute-start.2 = (bf16[128,1152]{1,0:T(8,128)(2,1)}, bf16[128,1152]{1,0:T(8,128)(2,1)S(1)}, u32[]{:S(2)}, u32[]{:S(2)}) collective-permute-start(bf16[128,1152]{1,0:T(8,128)(2,1)} %tokens.1), channel_id=1, source_target_pairs={{0,6},{1,7},{2,4},{3,5},{4,2},{5,3},{6,0},{7,1},{8,14},{9,15},{10,... | collective-permute-start | bytes 884744 | tf_op jit(solution)/shard_map/ppermute | solution.py:46
  5.1 13.3 %collective-permute-start.8 = (bf16[64,1152]{1,0:T(8,128)(2,1)}, bf16[64,1152]{1,0:T(8,128)(2,1)S(1)}, u32[]{:S(2)}, u32[]{:S(2)}) collective-permute-start(bf16[64,1152]{1,0:T(8,128)(2,1)} %bitcast.14), channel_id=1, source_target_pairs={{0,1},{1,0},{2,3},{3,2},{4,5},{5,4},{6,7},{7,6},{8,9},{9,8},{10,11... | collective-permute-start | bytes 442376 | tf_op jit(solution)/shard_map/ppermute | solution.py:50
  5.7 1.0 copy-start.1
  7.6 20.7 %all-to-all-start = ((f32[128,1,256]{2,1,0:T(1,128)}), f32[128,1,256]{2,1,0:T(1,128)S(1)}, u32[]{:S(2)}, u32[]{:S(2)}) async-start(f32[128,1,256]{2,1,0:T(1,128)} %get-tuple-element.40), calls=%async_computation | async-start | bytes 262144 | tf_op jit(solution)/shard_map/all_to_all | solution.py:550
  18.4 2.7 %collective-permute-start.3 = (bf16[128,1152]{1,0:T(8,128)(2,1)S(1)}, bf16[128,1152]{1,0:T(8,128)(2,1)S(1)}, u32[]{:S(2)}, u32[]{:S(2)}) collective-permute-start(bf16[128,1152]{1,0:T(8,128)(2,1)S(1)} %get-tuple-element.38.refs_0_), channel_id=1, source_target_pairs={{0,1},{1,0},{2,3},{3,2},{4,5},{5,4},{6,7},{7,6},{8,9},{9,8},{10,11... | collective-permute-start | bytes 884744 | tf_op jit(solution)/shard_map/ppermute | solution.py:50
  19.5 1.6 %collective-permute-start.4 = (bf16[128,1152]{1,0:T(8,128)(2,1)S(1)}, bf16[128,1152]{1,0:T(8,128)(2,1)S(1)}, u32[]{:S(2)}, u32[]{:S(2)}) collective-permute-start(bf16[128,1152]{1,0:T(8,128)(2,1)S(1)} %collective-permute-done.refs_1_), channel_id=1, source_target_pairs={{0,1},{1,0},{2,3},{3,2},{4,5},{5,4},{6,7},{7,6},{8,9},{9,8},{10,11... | collective-permute-start | bytes 884744 | tf_op jit(solution)/shard_map/ppermute | solution.py:50
  19.6 2.0 %collective-permute-start.5 = (bf16[128,1152]{1,0:T(8,128)(2,1)S(1)}, bf16[128,1152]{1,0:T(8,128)(2,1)S(1)}, u32[]{:S(2)}, u32[]{:S(2)}) collective-permute-start(bf16[128,1152]{1,0:T(8,128)(2,1)S(1)} %collective-permute-done.1.refs_2_), channel_id=1, source_target_pairs={{0,1},{1,0},{2,3},{3,2},{4,5},{5,4},{6,7},{7,6},{8,9},{9,8},{10,11... | collective-permute-start | bytes 884744 | tf_op jit(solution)/shard_map/ppermute | solution.py:50
  20.0 2.0 %collective-permute-start.6 = (bf16[128,1152]{1,0:T(8,128)(2,1)S(1)}, bf16[128,1152]{1,0:T(8,128)(2,1)S(1)}, u32[]{:S(2)}, u32[]{:S(2)}) collective-permute-start(bf16[128,1152]{1,0:T(8,128)(2,1)S(1)} %collective-permute-done.2.refs_3_), channel_id=1, source_target_pairs={{0,1},{1,0},{2,3},{3,2},{4,5},{5,4},{6,7},{7,6},{8,9},{9,8},{10,11... | collective-permute-start | bytes 884744 | tf_op jit(solution)/shard_map/ppermute | solution.py:50
  27.5 0.8 copy-start.2
  28.4 4.6 %copy-start.3 = (bf16[256,1152]{1,0:T(8,128)(2,1)S(1)}, bf16[256,1152]{1,0:T(8,128)(2,1)}, u32[]{:S(2)}) copy-start(bf16[256,1152]{1,0:T(8,128)(2,1)} %copy-done.2) | copy-start | bytes 1769476
  30.0 11.6 %collective-permute-start.10 = (bf16[128,3200]{1,0:T(8,128)(2,1)S(1)}, bf16[128,3200]{1,0:T(8,128)(2,1)S(1)}, u32[]{:S(2)}, u32[]{:S(2)}) collective-permute-start(bf16[128,3200]{1,0:T(8,128)(2,1)S(1)} %get-tuple-element.47), channel_id=1, source_target_pairs={{0,32},{1,9},{2,34},{3,11},{4,36},{5,13},{6,38},{7,15},{8,40},{9,1... | collective-permute-start | bytes 2457608 | tf_op jit(solution)/shard_map/ppermute | solution.py:38
  30.9 20.1 %collective-permute-start.11 = (bf16[128,3200]{1,0:T(8,128)(2,1)S(1)}, bf16[128,3200]{1,0:T(8,128)(2,1)S(1)}, u32[]{:S(2)}, u32[]{:S(2)}) collective-permute-start(bf16[128,3200]{1,0:T(8,128)(2,1)S(1)} %get-tuple-element.48), channel_id=1, source_target_pairs={{0,96},{1,25},{2,98},{3,27},{4,100},{5,29},{6,102},{7,31},{8,104},... | collective-permute-start | bytes 2457608 | tf_op jit(solution)/shard_map/ppermute | solution.py:38
  38.4 14.2 %collective-permute-start.9 = (bf16[128,3200]{1,0:T(8,128)(2,1)S(1)}, bf16[128,3200]{1,0:T(8,128)(2,1)S(1)}, u32[]{:S(2)}, u32[]{:S(2)}) collective-permute-start(bf16[128,3200]{1,0:T(8,128)(2,1)S(1)} %get-tuple-element.45), channel_id=1, source_target_pairs={{0,64},{1,17},{2,66},{3,19},{4,68},{5,21},{6,70},{7,23},{8,72},{9,... | collective-permute-start | bytes 2457608 | tf_op jit(solution)/shard_map/ppermute | solution.py:38
  39.3 67.8 %collective-permute-start.26 = (bf16[1536,1152]{1,0:T(8,128)(2,1)}, bf16[1536,1152]{1,0:T(8,128)(2,1)}, u32[]{:S(2)}, u32[]{:S(2)}) collective-permute-start(bf16[1536,1152]{1,0:T(8,128)(2,1)} %refs_3_.1), channel_id=1, source_target_pairs={{0,1},{1,0},{2,3},{3,2},{4,5},{5,4},{6,7},{7,6},{8,9},{9,8},{10,11... | collective-permute-start | bytes 10616840 | tf_op jit(solution)/shard_map/ppermute | solution.py:50
  52.6 3.9 %copy-start = (s32[4]{0:T(128)S(1)}, s32[4]{0:T(128)}, u32[]{:S(2)}) copy-start(s32[4]{0:T(128)} %lengths.1) | copy-start | bytes 52
  53.0 6.5 %collective-permute-start.12 = (bf16[32,3200]{1,0:T(8,128)(2,1)S(1)}, bf16[32,3200]{1,0:T(8,128)(2,1)S(1)}, u32[]{:S(2)}, u32[]{:S(2)}) collective-permute-start(bf16[32,3200]{1,0:T(8,128)(2,1)S(1)} %get-tuple-element.50), channel_id=1, source_target_pairs={{0,16},{1,65},{2,18},{3,67},{4,20},{5,69},{6,22},{7,71},{8,24},{9,... | collective-permute-start | bytes 614408 | tf_op jit(solution)/shard_map/ppermute | solution.py:42
  55.7 5.7 %collective-permute-start.13 = (bf16[32,3200]{1,0:T(8,128)(2,1)S(1)}, bf16[32,3200]{1,0:T(8,128)(2,1)S(1)}, u32[]{:S(2)}, u32[]{:S(2)}) collective-permute-start(bf16[32,3200]{1,0:T(8,128)(2,1)S(1)} %get-tuple-element.51), channel_id=1, source_target_pairs={{0,8},{1,33},{2,10},{3,35},{4,12},{5,37},{6,14},{7,39},{8,0},{9,41... | collective-permute-start | bytes 614408 | tf_op jit(solution)/shard_map/ppermute | solution.py:42
  56.1 5.8 %collective-permute-start.14 = (bf16[32,3200]{1,0:T(8,128)(2,1)S(1)}, bf16[32,3200]{1,0:T(8,128)(2,1)S(1)}, u32[]{:S(2)}, u32[]{:S(2)}) collective-permute-start(bf16[32,3200]{1,0:T(8,128)(2,1)S(1)} %get-tuple-element.52), channel_id=1, source_target_pairs={{0,24},{1,97},{2,26},{3,99},{4,28},{5,101},{6,30},{7,103},{8,16},{... | collective-permute-start | bytes 614408 | tf_op jit(solution)/shard_map/ppermute | solution.py:42
  62.6 4.5 %collective-permute-start.15 = (bf16[8,3200]{1,0:T(8,128)(2,1)S(1)}, bf16[8,3200]{1,0:T(8,128)(2,1)S(1)}, u32[]{:S(2)}, u32[]{:S(2)}) collective-permute-start(bf16[8,3200]{1,0:T(8,128)(2,1)S(1)} %get-tuple-element.54), channel_id=1, source_target_pairs={{0,4},{1,5},{2,6},{3,7},{4,0},{5,1},{6,2},{7,3},{8,12},{9,13},{10,... | collective-permute-start | bytes 153608 | tf_op jit(solution)/shard_map/ppermute | solution.py:46
  65.3 3.0 %collective-permute-start.16 = (bf16[8,3200]{1,0:T(8,128)(2,1)S(1)}, bf16[8,3200]{1,0:T(8,128)(2,1)S(1)}, u32[]{:S(2)}, u32[]{:S(2)}) collective-permute-start(bf16[8,3200]{1,0:T(8,128)(2,1)S(1)} %get-tuple-element.55), channel_id=1, source_target_pairs={{0,2},{1,3},{2,0},{3,1},{4,6},{5,7},{6,4},{7,5},{8,10},{9,11},{10,... | collective-permute-start | bytes 153608 | tf_op jit(solution)/shard_map/ppermute | solution.py:46
  65.6 4.2 %collective-permute-start.17 = (bf16[8,3200]{1,0:T(8,128)(2,1)S(1)}, bf16[8,3200]{1,0:T(8,128)(2,1)S(1)}, u32[]{:S(2)}, u32[]{:S(2)}) collective-permute-start(bf16[8,3200]{1,0:T(8,128)(2,1)S(1)} %get-tuple-element.56), channel_id=1, source_target_pairs={{0,6},{1,7},{2,4},{3,5},{4,2},{5,3},{6,0},{7,1},{8,14},{9,15},{10,... | collective-permute-start | bytes 153608 | tf_op jit(solution)/shard_map/ppermute | solution.py:46
  76.4 4.5 %collective-permute-start.18 = (bf16[8,3072]{1,0:T(8,128)(2,1)S(1)}, bf16[8,3072]{1,0:T(8,128)(2,1)S(1)}, u32[]{:S(2)}, u32[]{:S(2)}) collective-permute-start(bf16[8,3072]{1,0:T(8,128)(2,1)S(1)} %get-tuple-element.58), channel_id=1, source_target_pairs={{0,4},{1,5},{2,6},{3,7},{4,0},{5,1},{6,2},{7,3},{8,12},{9,13},{10,... | collective-permute-start | bytes 147464 | tf_op jit(solution)/shard_map/ppermute | solution.py:46
  77.5 3.5 %collective-permute-start.19 = (bf16[8,3072]{1,0:T(8,128)(2,1)S(1)}, bf16[8,3072]{1,0:T(8,128)(2,1)S(1)}, u32[]{:S(2)}, u32[]{:S(2)}) collective-permute-start(bf16[8,3072]{1,0:T(8,128)(2,1)S(1)} %get-tuple-element.59), channel_id=1, source_target_pairs={{0,2},{1,3},{2,0},{3,1},{4,6},{5,7},{6,4},{7,5},{8,10},{9,11},{10,... | collective-permute-start | bytes 147464 | tf_op jit(solution)/shard_map/ppermute | solution.py:46
  78.1 4.2 %collective-permute-start.20 = (bf16[8,3072]{1,0:T(8,128)(2,1)S(1)}, bf16[8,3072]{1,0:T(8,128)(2,1)S(1)}, u32[]{:S(2)}, u32[]{:S(2)}) collective-permute-start(bf16[8,3072]{1,0:T(8,128)(2,1)S(1)} %get-tuple-element.60), channel_id=1, source_target_pairs={{0,6},{1,7},{2,4},{3,5},{4,2},{5,3},{6,0},{7,1},{8,14},{9,15},{10,... | collective-permute-start | bytes 147464 | tf_op jit(solution)/shard_map/ppermute | solution.py:46
  82.8 6.1 %collective-permute-start.21 = (bf16[32,3072]{1,0:T(8,128)(2,1)S(1)}, bf16[32,3072]{1,0:T(8,128)(2,1)S(1)}, u32[]{:S(2)}, u32[]{:S(2)}) collective-permute-start(bf16[32,3072]{1,0:T(8,128)(2,1)S(1)} %line_up.1), channel_id=1, source_target_pairs={{0,64},{1,17},{2,66},{3,19},{4,68},{5,21},{6,70},{7,23},{8,72},{9,... | collective-permute-start | bytes 589832 | tf_op jit(solution)/shard_map/ppermute | solution.py:38
  84.8 6.1 %collective-permute-start.22 = (bf16[32,3072]{1,0:T(8,128)(2,1)S(1)}, bf16[32,3072]{1,0:T(8,128)(2,1)S(1)}, u32[]{:S(2)}, u32[]{:S(2)}) collective-permute-start(bf16[32,3072]{1,0:T(8,128)(2,1)S(1)} %line_up.1), channel_id=1, source_target_pairs={{0,32},{1,9},{2,34},{3,11},{4,36},{5,13},{6,38},{7,15},{8,40},{9,1... | collective-permute-start | bytes 589832 | tf_op jit(solution)/shard_map/ppermute | solution.py:38
  85.7 5.7 %collective-permute-start.23 = (bf16[32,3072]{1,0:T(8,128)(2,1)S(1)}, bf16[32,3072]{1,0:T(8,128)(2,1)S(1)}, u32[]{:S(2)}, u32[]{:S(2)}) collective-permute-start(bf16[32,3072]{1,0:T(8,128)(2,1)S(1)} %line_up.1), channel_id=1, source_target_pairs={{0,96},{1,25},{2,98},{3,27},{4,100},{5,29},{6,102},{7,31},{8,104},... | collective-permute-start | bytes 589832 | tf_op jit(solution)/shard_map/ppermute | solution.py:38
  91.5 14.9 %collective-permute-start.24 = (bf16[128,3072]{1,0:T(8,128)(2,1)S(1)}, bf16[128,3072]{1,0:T(8,128)(2,1)S(1)}, u32[]{:S(2)}, u32[]{:S(2)}) collective-permute-start(bf16[128,3072]{1,0:T(8,128)(2,1)S(1)} %pad_maximum_fusion.refs_0_), channel_id=1, source_target_pairs={{0,8},{1,33},{2,10},{3,35},{4,12},{5,37},{6,14},{7,39},{8,0},{9,41... | collective-permute-start | bytes 2359304 | tf_op jit(solution)/shard_map/ppermute | solution.py:42
  92.1 15.1 %collective-permute-start.25 = (bf16[128,3072]{1,0:T(8,128)(2,1)S(1)}, bf16[128,3072]{1,0:T(8,128)(2,1)S(1)}, u32[]{:S(2)}, u32[]{:S(2)}) collective-permute-start(bf16[128,3072]{1,0:T(8,128)(2,1)S(1)} %pad_maximum_fusion.refs_0_), channel_id=1, source_target_pairs={{0,24},{1,97},{2,26},{3,99},{4,28},{5,101},{6,30},{7,103},{8,16},{... | collective-permute-start | bytes 2359304 | tf_op jit(solution)/shard_map/ppermute | solution.py:42
  106.4 12.6 %collective-permute-start.27 = (bf16[128,3072]{1,0:T(8,128)(2,1)S(1)}, bf16[128,3072]{1,0:T(8,128)(2,1)S(1)}, u32[]{:S(2)}, u32[]{:S(2)}) collective-permute-start(bf16[128,3072]{1,0:T(8,128)(2,1)S(1)} %pad_maximum_fusion.refs_0_), channel_id=1, source_target_pairs={{0,16},{1,65},{2,18},{3,67},{4,20},{5,69},{6,22},{7,71},{8,24},{9,... | collective-permute-start | bytes 2359304 | tf_op jit(solution)/shard_map/ppermute | solution.py:42
  121.1 7.3 %collective-permute-start.28 = (bf16[128,1152]{1,0:T(8,128)(2,1)S(1)}, bf16[128,1152]{1,0:T(8,128)(2,1)S(1)}, u32[]{:S(2)}, u32[]{:S(2)}) collective-permute-start(bf16[128,1152]{1,0:T(8,128)(2,1)S(1)} %get-tuple-element.66), channel_id=1, source_target_pairs={{0,4},{1,5},{2,6},{3,7},{4,0},{5,1},{6,2},{7,3},{8,12},{9,13},{10,... | collective-permute-start | bytes 884744 | tf_op jit(solution)/shard_map/ppermute | solution.py:46
  122.2 8.8 %collective-permute-start.29 = (bf16[128,1152]{1,0:T(8,128)(2,1)S(1)}, bf16[128,1152]{1,0:T(8,128)(2,1)S(1)}, u32[]{:S(2)}, u32[]{:S(2)}) collective-permute-start(bf16[128,1152]{1,0:T(8,128)(2,1)S(1)} %get-tuple-element.67), channel_id=1, source_target_pairs={{0,2},{1,3},{2,0},{3,1},{4,6},{5,7},{6,4},{7,5},{8,10},{9,11},{10,... | collective-permute-start | bytes 884744 | tf_op jit(solution)/shard_map/ppermute | solution.py:46
  123.7 7.7 %collective-permute-start.30 = (bf16[128,1152]{1,0:T(8,128)(2,1)S(1)}, bf16[128,1152]{1,0:T(8,128)(2,1)S(1)}, u32[]{:S(2)}, u32[]{:S(2)}) collective-permute-start(bf16[128,1152]{1,0:T(8,128)(2,1)S(1)} %get-tuple-element.68), channel_id=1, source_target_pairs={{0,6},{1,7},{2,4},{3,5},{4,2},{5,3},{6,0},{7,1},{8,14},{9,15},{10,... | collective-permute-start | bytes 884744 | tf_op jit(solution)/shard_map/ppermute | solution.py:46
  131.6 10.9 %collective-permute-start.31 = (bf16[64,1152]{1,0:T(8,128)(2,1)S(1)}, bf16[64,1152]{1,0:T(8,128)(2,1)S(1)}, u32[]{:S(2)}, u32[]{:S(2)}) collective-permute-start(bf16[64,1152]{1,0:T(8,128)(2,1)S(1)} %get-tuple-element.69), channel_id=1, source_target_pairs={{0,1},{1,0},{2,3},{3,2},{4,5},{5,4},{6,7},{7,6},{8,9},{9,8},{10,11... | collective-permute-start | bytes 442376 | tf_op jit(solution)/shard_map/ppermute | solution.py:50

commit v9 on v8

--- a/solution.py
+++ b/solution.py
@@ -347,8 +347,10 @@
     query = (query.astype(BF16).astype(F32) * HD ** (-0.5)).astype(BF16)
     dims = (((1,), (1,)), ((), ()))
     cached = lax.dot_general(query, keys[...], dims, preferred_element_type=F32)
-    slots = lax.broadcasted_iota(jnp.int32, cached.shape, 1)
-    cached = jnp.where(slots < lengths[request], cached, -jnp.inf)
+    half = cached.shape[1] // 2
+    slots = lax.broadcasted_iota(jnp.int32, (per, half), 1) + half
+    masked = jnp.where(slots < lengths[request], cached[:, half:], -jnp.inf)
+    cached = jnp.concatenate([cached[:, :half], masked], axis=1)
     fresh = lax.dot_general(query, new_kv[0], dims, preferred_element_type=F32)
     row_step = lax.broadcasted_iota(jnp.int32, fresh.shape, 0) // count
     key_step = lax.broadcasted_iota(jnp.int32, fresh.shape, 1) - request * STEPS

time: 144 us -> 143 us (level)
  no operation moved by 1% of the time
where the time goes in v9:
time: 143 us
  waiting for transfers between devices  55.2 us (39%)
  starting transfers between devices  52.4 us (37%)
  Pallas kernels  30.8 us (22%)
  local copies, waits for them, and re-layouts  3.3 us (2%)
    ppermute x6, waiting for transfers between devices, along_second(): return lax.ppermute(value, ('gx', 'gy'), exchange_pairs(1, m))  23 us
    ppermute x6, waiting for transfers between devices, along_first(): return lax.ppermute(value, ('gx', 'gy'), exchange_pairs(0, m))  17.9 us
    ppermute x12, starting transfers between devices, along_x(): return lax.ppermute(value, 'gy', [(g, g ^ 2 * m) for g in range(8)])  14.4 us
    ppermute x8, starting transfers between devices, other_core(): return lax.ppermute(value, 'gy', [(g, g ^ 1) for g in range(8)])  14.3 us
    ppermute x12, waiting for transfers between devices, along_x(): return lax.ppermute(value, 'gy', [(g, g ^ 2 * m) for g in range(8)])  12.5 us
    all_to_all x1, starting transfers between devices, per_device(): stats = lax.all_to_all(stats, ('gx', 'gy'), 0, 0, tiled=True)  10 us
    ppermute x6, starting transfers between devices, along_first(): return lax.ppermute(value, ('gx', 'gy'), exchange_pairs(0, m))  7.24 us
    pallas_call x1, Pallas kernels, mix(): pl.pallas_call(mix_kernel, out_shape=[jax.ShapeDtypeStruct((384, width),...  6.78 us
  transfers between devices with their start and end apart: 33, of which 22 were waited for; matrix products, arithmetic and copies ran while one was open for 1% of the time, Pallas kernels for 19%

profile of v9, /device:TPU:1, one launch (start us, length us, event | category | flops | bytes accessed | tf_op | source)
XLA Modules:
  0.0 143.3 jit_solution(9372034386780510229)
XLA Ops:
  0.0 1.4 collective-permute-start.7
  1.4 2.8 %collective-permute-start = (bf16[128,1152]{1,0:T(8,128)(2,1)}, bf16[128,1152]{1,0:T(8,128)(2,1)S(1)}, u32[]{:S(2)}, u32[]{:S(2)}) collective-permute-start(bf16[128,1152]{1,0:T(8,128)(2,1)} %tokens.1), channel_id=1, source_target_pairs={{0,4},{1,5},{2,6},{3,7},{4,0},{5,1},{6,2},{7,3},{8,12},{9,13},{10,... | collective-permute-start | bytes 884744 | tf_op jit(solution)/shard_map/ppermute | solution.py:46
  4.6 0.6 collective-permute-start.2
  5.1 0.6 collective-permute-start.8
  5.7 1.0 copy-done.1
  6.6 1.0 prepare.1
  7.6 10.0 %all-to-all-start = ((f32[128,1,256]{2,1,0:T(1,128)}), f32[128,1,256]{2,1,0:T(1,128)S(1)}, u32[]{:S(2)}, u32[]{:S(2)}) async-start(f32[128,1,256]{2,1,0:T(1,128)} %get-tuple-element.40), calls=%async_computation | async-start | bytes 262144 | tf_op jit(solution)/shard_map/all_to_all | solution.py:552
  17.7 0.7 broadcast_in_dim.2.gain
  18.4 1.1 collective-permute-start.3
  19.6 0.4 collective-permute-start.5
  20.2 0.9 pad_maximum_fusion.1.refs_10_.refs_2_
  21.1 0.4 collective-permute-done.5.refs_6_
  21.5 0.4 collective-permute-done.6.refs_7_
  21.9 5.6 %project.1 = (bf16[256,3200]{1,0:T(8,128)(2,1)S(1)}, f32[8,3200]{1,0:T(8,128)S(1)}, bf16[256,1152]{1,0:T(8,128)(2,1)S(1)}) custom-call(s32[4]{0:T(128)S(1)} %pad_add_fusion.place, bf16[1,1152]{1,0:T(2,128)(2,1)S(1)} %broadcast_in_dim.2.gain, bf16[128,1152]{1,0:T(8,128)(2,1)S(1)} %get-tuple-element.38.refs_0_, ...), custom_call_target="tpu_custom_call" | custom-call | flops 4000000000 | bytes 10000000 | tf_op jit(solution)/shard_map/project/pallas_call | solution.py:170
  27.5 0.8 copy-done.2
  28.4 1.6 %scale.1 = (bf16[128,3200]{1,0:T(8,128)(2,1)S(1)}, bf16[128,3200]{1,0:T(8,128)(2,1)S(1)}) custom-call(s32[4]{0:T(128)S(1)} %pad_add_fusion.place, f32[128,256]{1,0:T(8,128)S(1)} %bitcast.12, f32[8,3200]{1,0:T(8,128)S(1)} %get-tuple-element.42.gain_row, bf16[256,3200]{1,0:T(8,128)(2,1)S(1)} %get-tuple-element.46.parts), custom_call_target="tpu_custom_call" | custom-call | flops 1000000000 | bytes 2000000 | tf_op jit(solution)/shard_map/scale/pallas_call | solution.py:223
  30.0 0.9 collective-permute-start.10
  30.9 2.1 %collective-permute-start.11 = (bf16[128,3200]{1,0:T(8,128)(2,1)S(1)}, bf16[128,3200]{1,0:T(8,128)(2,1)S(1)}, u32[]{:S(2)}, u32[]{:S(2)}) collective-permute-start(bf16[128,3200]{1,0:T(8,128)(2,1)S(1)} %get-tuple-element.48), channel_id=1, source_target_pairs={{0,96},{1,25},{2,98},{3,27},{4,100},{5,29},{6,102},{7,31},{8,104},... | collective-permute-start | bytes 2457608 | tf_op jit(solution)/shard_map/ppermute | solution.py:38
  32.9 5.4 %project_rest.1 = (bf16[128,3200]{1,0:T(8,128)(2,1)S(1)}, bf16[128,3200]{1,0:T(8,128)(2,1)S(1)}) custom-call(s32[4]{0:T(128)S(1)} %pad_add_fusion.place, f32[128,256]{1,0:T(8,128)S(1)} %bitcast.13, f32[8,3200]{1,0:T(8,128)S(1)} %get-tuple-element.42.gain_row, bf16[256,1152]{1,0:T(8,128)(2,1)S(1)} %copy-done.3, bf16[1152,1536]{1,0:T(8,128)(2,1)} %refs_0_.1, ...), custom_call_target="tpu_custom_call" | custom-call | flops 5000000000 | bytes 10000000 | tf_op jit(solution)/shard_map/project_rest/pallas_call | solution.py:256
  38.4 1.0 collective-permute-start.9
  39.3 0.7 collective-permute-start.26
  40.0 1.5 %collective-permute-done.10.refs_2_ = bf16[128,3200]{1,0:T(8,128)(2,1)S(1)} collective-permute-done((bf16[128,3200]{1,0:T(8,128)(2,1)S(1)}, bf16[128,3200]{1,0:T(8,128)(2,1)S(1)}, u32[]{:S(2)}, u32[]{:S(2)}) %collective-permute-start.10) | collective-permute-done | bytes 819232 | tf_op jit(solution)/shard_map/ppermute | solution.py:38
  41.5 9.4 %collective-permute-done.11.refs_3_ = bf16[128,3200]{1,0:T(8,128)(2,1)S(1)} collective-permute-done((bf16[128,3200]{1,0:T(8,128)(2,1)S(1)}, bf16[128,3200]{1,0:T(8,128)(2,1)S(1)}, u32[]{:S(2)}, u32[]{:S(2)}) %collective-permute-start.11) | collective-permute-done | bytes 819232 | tf_op jit(solution)/shard_map/ppermute | solution.py:38
  51.0 1.6 %collective-permute-done.9.refs_1_ = bf16[128,3200]{1,0:T(8,128)(2,1)S(1)} collective-permute-done((bf16[128,3200]{1,0:T(8,128)(2,1)S(1)}, bf16[128,3200]{1,0:T(8,128)(2,1)S(1)}, u32[]{:S(2)}, u32[]{:S(2)}) %collective-permute-start.9) | collective-permute-done | bytes 819232 | tf_op jit(solution)/shard_map/ppermute | solution.py:38
  52.6 0.4 add_and_cut.1
  53.0 2.7 %collective-permute-start.12 = (bf16[32,3200]{1,0:T(8,128)(2,1)S(1)}, bf16[32,3200]{1,0:T(8,128)(2,1)S(1)}, u32[]{:S(2)}, u32[]{:S(2)}) collective-permute-start(bf16[32,3200]{1,0:T(8,128)(2,1)S(1)} %get-tuple-element.50), channel_id=1, source_target_pairs={{0,16},{1,65},{2,18},{3,67},{4,20},{5,69},{6,22},{7,71},{8,24},{9,... | collective-permute-start | bytes 614408 | tf_op jit(solution)/shard_map/ppermute | solution.py:42
  55.7 0.4 collective-permute-start.13
  56.6 2.9 %collective-permute-done.12.refs_1_ = bf16[32,3200]{1,0:T(8,128)(2,1)S(1)} collective-permute-done((bf16[32,3200]{1,0:T(8,128)(2,1)S(1)}, bf16[32,3200]{1,0:T(8,128)(2,1)S(1)}, u32[]{:S(2)}, u32[]{:S(2)}) %collective-permute-start.12) | collective-permute-done | bytes 204832 | tf_op jit(solution)/shard_map/ppermute | solution.py:42
  59.5 1.9 %collective-permute-done.13.refs_2_ = bf16[32,3200]{1,0:T(8,128)(2,1)S(1)} collective-permute-done((bf16[32,3200]{1,0:T(8,128)(2,1)S(1)}, bf16[32,3200]{1,0:T(8,128)(2,1)S(1)}, u32[]{:S(2)}, u32[]{:S(2)}) %collective-permute-start.13) | collective-permute-done | bytes 204832 | tf_op jit(solution)/shard_map/ppermute | solution.py:42
  61.4 0.5 collective-permute-done.14.refs_3_
  61.9 0.7 finish.1
  62.6 2.7 %collective-permute-start.15 = (bf16[8,3200]{1,0:T(8,128)(2,1)S(1)}, bf16[8,3200]{1,0:T(8,128)(2,1)S(1)}, u32[]{:S(2)}, u32[]{:S(2)}) collective-permute-start(bf16[8,3200]{1,0:T(8,128)(2,1)S(1)} %get-tuple-element.54), channel_id=1, source_target_pairs={{0,4},{1,5},{2,6},{3,7},{4,0},{5,1},{6,2},{7,3},{8,12},{9,13},{10,... | collective-permute-start | bytes 153608 | tf_op jit(solution)/shard_map/ppermute | solution.py:46
  65.6 1.0 collective-permute-start.17
  66.7 0.4 collective-permute-done.15.refs_1_
  67.1 1.1 collective-permute-done.16.refs_2_
  68.2 1.5 %collective-permute-done.17.refs_3_ = bf16[8,3200]{1,0:T(8,128)(2,1)S(1)} collective-permute-done((bf16[8,3200]{1,0:T(8,128)(2,1)S(1)}, bf16[8,3200]{1,0:T(8,128)(2,1)S(1)}, u32[]{:S(2)}, u32[]{:S(2)}) %collective-permute-start.17) | collective-permute-done | bytes 51232 | tf_op jit(solution)/shard_map/ppermute | solution.py:46
  69.8 6.6 %attend.1 = (bf16[8,3072]{1,0:T(8,128)(2,1)S(1)}, bf16[8,3072]{1,0:T(8,128)(2,1)S(1)}, bf16[8,3072]{1,0:T(8,128)(2,1)S(1)}, bf16[8,3072]{1,0:T(8,128)(2,1)S(1)}) custom-call(s32[4]{0:T(128)S(1)} %copy-done, s32[4]{0:T(128)S(1)} %pad_add_fusion.place, bf16[8,3200]{1,0:T(8,128)(2,1)S(1)} %get-tuple-element.53.refs_0_, ...), custom_call_target="tpu_custom_call" | custom-call | flops 6000000000 | bytes 18000000 | tf_op jit(solution)/shard_map/attend/pallas_call | solution.py:427
  76.4 1.1 collective-permute-start.18
  77.4 0.6 collective-permute-start.19
  78.1 1.7 %collective-permute-start.20 = (bf16[8,3072]{1,0:T(8,128)(2,1)S(1)}, bf16[8,3072]{1,0:T(8,128)(2,1)S(1)}, u32[]{:S(2)}, u32[]{:S(2)}) collective-permute-start(bf16[8,3072]{1,0:T(8,128)(2,1)S(1)} %get-tuple-element.60), channel_id=1, source_target_pairs={{0,6},{1,7},{2,4},{3,5},{4,2},{5,3},{6,0},{7,1},{8,14},{9,15},{10,... | collective-permute-start | bytes 147464 | tf_op jit(solution)/shard_map/ppermute | solution.py:46
  79.7 1.2 collective-permute-done.18.refs_1_
  80.9 1.3 collective-permute-done.20.refs_3_
  82.2 0.6 line_up.1
  82.8 2.0 %collective-permute-start.21 = (bf16[32,3072]{1,0:T(8,128)(2,1)S(1)}, bf16[32,3072]{1,0:T(8,128)(2,1)S(1)}, u32[]{:S(2)}, u32[]{:S(2)}) collective-permute-start(bf16[32,3072]{1,0:T(8,128)(2,1)S(1)} %line_up.1), channel_id=1, source_target_pairs={{0,64},{1,17},{2,66},{3,19},{4,68},{5,21},{6,70},{7,23},{8,72},{9,... | collective-permute-start | bytes 589832 | tf_op jit(solution)/shard_map/ppermute | solution.py:38
  84.8 1.0 collective-permute-start.22
  85.7 0.4 collective-permute-start.23
  86.1 2.8 %collective-permute-done.21 = bf16[32,3072]{1,0:T(8,128)(2,1)S(1)} collective-permute-done((bf16[32,3072]{1,0:T(8,128)(2,1)S(1)}, bf16[32,3072]{1,0:T(8,128)(2,1)S(1)}, u32[]{:S(2)}, u32[]{:S(2)}) %collective-permute-start.21) | collective-permute-done | bytes 196640 | tf_op jit(solution)/shard_map/ppermute | solution.py:38
  88.9 2.0 %collective-permute-done.22 = bf16[32,3072]{1,0:T(8,128)(2,1)S(1)} collective-permute-done((bf16[32,3072]{1,0:T(8,128)(2,1)S(1)}, bf16[32,3072]{1,0:T(8,128)(2,1)S(1)}, u32[]{:S(2)}, u32[]{:S(2)}) %collective-permute-start.22) | collective-permute-done | bytes 196640 | tf_op jit(solution)/shard_map/ppermute | solution.py:38
  90.9 0.6 collective-permute-done.23
  91.5 0.5 collective-permute-start.24
  92.1 1.8 %collective-permute-start.25 = (bf16[128,3072]{1,0:T(8,128)(2,1)S(1)}, bf16[128,3072]{1,0:T(8,128)(2,1)S(1)}, u32[]{:S(2)}, u32[]{:S(2)}) collective-permute-start(bf16[128,3072]{1,0:T(8,128)(2,1)S(1)} %pad_maximum_fusion.refs_0_), channel_id=1, source_target_pairs={{0,24},{1,97},{2,26},{3,99},{4,28},{5,101},{6,30},{7,103},{8,16},{... | collective-permute-start | bytes 2359304 | tf_op jit(solution)/shard_map/ppermute | solution.py:42
  93.8 12.6 %collective-permute-done.24.refs_1_ = bf16[128,3072]{1,0:T(8,128)(2,1)S(1)} collective-permute-done((bf16[128,3072]{1,0:T(8,128)(2,1)S(1)}, bf16[128,3072]{1,0:T(8,128)(2,1)S(1)}, u32[]{:S(2)}, u32[]{:S(2)}) %collective-permute-start.24) | collective-permute-done | bytes 786464 | tf_op jit(solution)/shard_map/ppermute | solution.py:42
  106.4 0.7 collective-permute-start.27
  107.1 6.8 %mix.1 = (bf16[384,1152]{1,0:T(8,128)(2,1)S(1)}, bf16[6,1536,384]{2,1,0:T(8,128)(2,1)S(1)}) custom-call(bf16[128,3072]{1,0:T(8,128)(2,1)S(1)} %pad_maximum_fusion.refs_0_, bf16[128,3072]{1,0:T(8,128)(2,1)S(1)} %collective-permute-done.24.refs_1_, bf16[128,3072]{1,0:T(8,128)(2,1)S(1)} %collective-permute-done.25.refs_2_, bf16[1536,1152]{1,0:T(8,128)(2,1)} %refs_3_.1, ...), custom_call_target="tpu_custom_call" | custom-call | flops 4000000000 | bytes 8000000 | tf_op jit(solution)/shard_map/mix/pallas_call | solution.py:497
  113.9 5.1 %collective-permute-done.27.last = bf16[128,3072]{1,0:T(8,128)(2,1)S(1)} collective-permute-done((bf16[128,3072]{1,0:T(8,128)(2,1)S(1)}, bf16[128,3072]{1,0:T(8,128)(2,1)S(1)}, u32[]{:S(2)}, u32[]{:S(2)}) %collective-permute-start.27) | collective-permute-done | bytes 786464 | tf_op jit(solution)/shard_map/ppermute | solution.py:42
  119.1 2.0 %mix_rest.1 = (bf16[128,1152]{1,0:T(8,128)(2,1)S(1)}, bf16[128,1152]{1,0:T(8,128)(2,1)S(1)}, bf16[128,1152]{1,0:T(8,128)(2,1)S(1)}, bf16[128,1152]{1,0:T(8,128)(2,1)S(1)}) custom-call(s32[4]{0:T(128)S(1)} %pad_add_fusion.place, bf16[384,1152]{1,0:T(8,128)(2,1)S(1)} %get-tuple-element.62.done, bf16[128,3072]{1,0:T(8,128)(2,1)S(1)} %collective-permute-done.27.last, ...), custom_call_target="tpu_custom_call" | custom-call | flops 4000000000 | bytes 8000000 | tf_op jit(solution)/shard_map/mix_rest/pallas_call | solution.py:514
  121.1 1.1 collective-permute-start.28
  122.2 1.5 %collective-permute-start.29 = (bf16[128,1152]{1,0:T(8,128)(2,1)S(1)}, bf16[128,1152]{1,0:T(8,128)(2,1)S(1)}, u32[]{:S(2)}, u32[]{:S(2)}) collective-permute-start(bf16[128,1152]{1,0:T(8,128)(2,1)S(1)} %get-tuple-element.67), channel_id=1, source_target_pairs={{0,2},{1,3},{2,0},{3,1},{4,6},{5,7},{6,4},{7,5},{8,10},{9,11},{10,... | collective-permute-start | bytes 884744 | tf_op jit(solution)/shard_map/ppermute | solution.py:46
  123.7 0.7 collective-permute-start.30
  124.4 3.9 %collective-permute-done.28.refs_1_ = bf16[128,1152]{1,0:T(8,128)(2,1)S(1)} collective-permute-done((bf16[128,1152]{1,0:T(8,128)(2,1)S(1)}, bf16[128,1152]{1,0:T(8,128)(2,1)S(1)}, u32[]{:S(2)}, u32[]{:S(2)}) %collective-permute-start.28) | collective-permute-done | bytes 294944 | tf_op jit(solution)/shard_map/ppermute | solution.py:46
  128.3 2.7 %collective-permute-done.29.refs_2_ = bf16[128,1152]{1,0:T(8,128)(2,1)S(1)} collective-permute-done((bf16[128,1152]{1,0:T(8,128)(2,1)S(1)}, bf16[128,1152]{1,0:T(8,128)(2,1)S(1)}, u32[]{:S(2)}, u32[]{:S(2)}) %collective-permute-start.29) | collective-permute-done | bytes 294944 | tf_op jit(solution)/shard_map/ppermute | solution.py:46
  131.6 9.9 %collective-permute-start.31 = (bf16[64,1152]{1,0:T(8,128)(2,1)S(1)}, bf16[64,1152]{1,0:T(8,128)(2,1)S(1)}, u32[]{:S(2)}, u32[]{:S(2)}) collective-permute-start(bf16[64,1152]{1,0:T(8,128)(2,1)S(1)} %get-tuple-element.69), channel_id=1, source_target_pairs={{0,1},{1,0},{2,3},{3,2},{4,5},{5,4},{6,7},{7,6},{8,9},{9,8},{10,11... | collective-permute-start | bytes 442376 | tf_op jit(solution)/shard_map/ppermute | solution.py:50
  141.5 1.0 collective-permute-done.31
  142.5 0.7 copy.13
  (32 shorter events, 2.2 us)
Async XLA Ops:
  0.0 21.9 %collective-permute-start.7 = (bf16[1152,1536]{1,0:T(8,128)(2,1)}, bf16[1152,1536]{1,0:T(8,128)(2,1)}, u32[]{:S(2)}, u32[]{:S(2)}) collective-permute-start(bf16[1152,1536]{1,0:T(8,128)(2,1)} %refs_0_.1), channel_id=1, source_target_pairs={{0,1},{1,0},{2,3},{3,2},{4,5},{5,4},{6,7},{7,6},{8,9},{9,8},{10,11... | collective-permute-start | bytes 10616840 | tf_op jit(solution)/shard_map/ppermute | solution.py:50
  1.4 18.1 %collective-permute-start = (bf16[128,1152]{1,0:T(8,128)(2,1)}, bf16[128,1152]{1,0:T(8,128)(2,1)S(1)}, u32[]{:S(2)}, u32[]{:S(2)}) collective-permute-start(bf16[128,1152]{1,0:T(8,128)(2,1)} %tokens.1), channel_id=1, source_target_pairs={{0,4},{1,5},{2,6},{3,7},{4,0},{5,1},{6,2},{7,3},{8,12},{9,13},{10,... | collective-permute-start | bytes 884744 | tf_op jit(solution)/shard_map/ppermute | solution.py:46
  4.2 15.3 %collective-permute-start.1 = (bf16[128,1152]{1,0:T(8,128)(2,1)}, bf16[128,1152]{1,0:T(8,128)(2,1)S(1)}, u32[]{:S(2)}, u32[]{:S(2)}) collective-permute-start(bf16[128,1152]{1,0:T(8,128)(2,1)} %tokens.1), channel_id=1, source_target_pairs={{0,2},{1,3},{2,0},{3,1},{4,6},{5,7},{6,4},{7,5},{8,10},{9,11},{10,... | collective-permute-start | bytes 884744 | tf_op jit(solution)/shard_map/ppermute | solution.py:46
  4.6 15.4 %collective-permute-start.2 = (bf16[128,1152]{1,0:T(8,128)(2,1)}, bf16[128,1152]{1,0:T(8,128)(2,1)S(1)}, u32[]{:S(2)}, u32[]{:S(2)}) collective-permute-start(bf16[128,1152]{1,0:T(8,128)(2,1)} %tokens.1), channel_id=1, source_target_pairs={{0,6},{1,7},{2,4},{3,5},{4,2},{5,3},{6,0},{7,1},{8,14},{9,15},{10,... | collective-permute-start | bytes 884744 | tf_op jit(solution)/shard_map/ppermute | solution.py:46
  5.1 13.3 %collective-permute-start.8 = (bf16[64,1152]{1,0:T(8,128)(2,1)}, bf16[64,1152]{1,0:T(8,128)(2,1)S(1)}, u32[]{:S(2)}, u32[]{:S(2)}) collective-permute-start(bf16[64,1152]{1,0:T(8,128)(2,1)} %bitcast.14), channel_id=1, source_target_pairs={{0,1},{1,0},{2,3},{3,2},{4,5},{5,4},{6,7},{7,6},{8,9},{9,8},{10,11... | collective-permute-start | bytes 442376 | tf_op jit(solution)/shard_map/ppermute | solution.py:50
  5.7 1.0 copy-start.1
  7.6 20.7 %all-to-all-start = ((f32[128,1,256]{2,1,0:T(1,128)}), f32[128,1,256]{2,1,0:T(1,128)S(1)}, u32[]{:S(2)}, u32[]{:S(2)}) async-start(f32[128,1,256]{2,1,0:T(1,128)} %get-tuple-element.40), calls=%async_computation | async-start | bytes 262144 | tf_op jit(solution)/shard_map/all_to_all | solution.py:552
  18.4 2.7 %collective-permute-start.3 = (bf16[128,1152]{1,0:T(8,128)(2,1)S(1)}, bf16[128,1152]{1,0:T(8,128)(2,1)S(1)}, u32[]{:S(2)}, u32[]{:S(2)}) collective-permute-start(bf16[128,1152]{1,0:T(8,128)(2,1)S(1)} %get-tuple-element.38.refs_0_), channel_id=1, source_target_pairs={{0,1},{1,0},{2,3},{3,2},{4,5},{5,4},{6,7},{7,6},{8,9},{9,8},{10,11... | collective-permute-start | bytes 884744 | tf_op jit(solution)/shard_map/ppermute | solution.py:50
  19.5 1.6 %collective-permute-start.4 = (bf16[128,1152]{1,0:T(8,128)(2,1)S(1)}, bf16[128,1152]{1,0:T(8,128)(2,1)S(1)}, u32[]{:S(2)}, u32[]{:S(2)}) collective-permute-start(bf16[128,1152]{1,0:T(8,128)(2,1)S(1)} %collective-permute-done.refs_1_), channel_id=1, source_target_pairs={{0,1},{1,0},{2,3},{3,2},{4,5},{5,4},{6,7},{7,6},{8,9},{9,8},{10,11... | collective-permute-start | bytes 884744 | tf_op jit(solution)/shard_map/ppermute | solution.py:50
  19.6 2.0 %collective-permute-start.5 = (bf16[128,1152]{1,0:T(8,128)(2,1)S(1)}, bf16[128,1152]{1,0:T(8,128)(2,1)S(1)}, u32[]{:S(2)}, u32[]{:S(2)}) collective-permute-start(bf16[128,1152]{1,0:T(8,128)(2,1)S(1)} %collective-permute-done.1.refs_2_), channel_id=1, source_target_pairs={{0,1},{1,0},{2,3},{3,2},{4,5},{5,4},{6,7},{7,6},{8,9},{9,8},{10,11... | collective-permute-start | bytes 884744 | tf_op jit(solution)/shard_map/ppermute | solution.py:50
  20.0 2.0 %collective-permute-start.6 = (bf16[128,1152]{1,0:T(8,128)(2,1)S(1)}, bf16[128,1152]{1,0:T(8,128)(2,1)S(1)}, u32[]{:S(2)}, u32[]{:S(2)}) collective-permute-start(bf16[128,1152]{1,0:T(8,128)(2,1)S(1)} %collective-permute-done.2.refs_3_), channel_id=1, source_target_pairs={{0,1},{1,0},{2,3},{3,2},{4,5},{5,4},{6,7},{7,6},{8,9},{9,8},{10,11... | collective-permute-start | bytes 884744 | tf_op jit(solution)/shard_map/ppermute | solution.py:50
  27.5 0.8 copy-start.2
  28.4 4.6 %copy-start.3 = (bf16[256,1152]{1,0:T(8,128)(2,1)S(1)}, bf16[256,1152]{1,0:T(8,128)(2,1)}, u32[]{:S(2)}) copy-start(bf16[256,1152]{1,0:T(8,128)(2,1)} %copy-done.2) | copy-start | bytes 1769476
  30.0 11.6 %collective-permute-start.10 = (bf16[128,3200]{1,0:T(8,128)(2,1)S(1)}, bf16[128,3200]{1,0:T(8,128)(2,1)S(1)}, u32[]{:S(2)}, u32[]{:S(2)}) collective-permute-start(bf16[128,3200]{1,0:T(8,128)(2,1)S(1)} %get-tuple-element.47), channel_id=1, source_target_pairs={{0,32},{1,9},{2,34},{3,11},{4,36},{5,13},{6,38},{7,15},{8,40},{9,1... | collective-permute-start | bytes 2457608 | tf_op jit(solution)/shard_map/ppermute | solution.py:38
  30.9 20.1 %collective-permute-start.11 = (bf16[128,3200]{1,0:T(8,128)(2,1)S(1)}, bf16[128,3200]{1,0:T(8,128)(2,1)S(1)}, u32[]{:S(2)}, u32[]{:S(2)}) collective-permute-start(bf16[128,3200]{1,0:T(8,128)(2,1)S(1)} %get-tuple-element.48), channel_id=1, source_target_pairs={{0,96},{1,25},{2,98},{3,27},{4,100},{5,29},{6,102},{7,31},{8,104},... | collective-permute-start | bytes 2457608 | tf_op jit(solution)/shard_map/ppermute | solution.py:38
  38.4 14.2 %collective-permute-start.9 = (bf16[128,3200]{1,0:T(8,128)(2,1)S(1)}, bf16[128,3200]{1,0:T(8,128)(2,1)S(1)}, u32[]{:S(2)}, u32[]{:S(2)}) collective-permute-start(bf16[128,3200]{1,0:T(8,128)(2,1)S(1)} %get-tuple-element.45), channel_id=1, source_target_pairs={{0,64},{1,17},{2,66},{3,19},{4,68},{5,21},{6,70},{7,23},{8,72},{9,... | collective-permute-start | bytes 2457608 | tf_op jit(solution)/shard_map/ppermute | solution.py:38
  39.3 67.8 %collective-permute-start.26 = (bf16[1536,1152]{1,0:T(8,128)(2,1)}, bf16[1536,1152]{1,0:T(8,128)(2,1)}, u32[]{:S(2)}, u32[]{:S(2)}) collective-permute-start(bf16[1536,1152]{1,0:T(8,128)(2,1)} %refs_3_.1), channel_id=1, source_target_pairs={{0,1},{1,0},{2,3},{3,2},{4,5},{5,4},{6,7},{7,6},{8,9},{9,8},{10,11... | collective-permute-start | bytes 10616840 | tf_op jit(solution)/shard_map/ppermute | solution.py:50
  52.6 3.9 %copy-start = (s32[4]{0:T(128)S(1)}, s32[4]{0:T(128)}, u32[]{:S(2)}) copy-start(s32[4]{0:T(128)} %lengths.1) | copy-start | bytes 52
  53.0 6.5 %collective-permute-start.12 = (bf16[32,3200]{1,0:T(8,128)(2,1)S(1)}, bf16[32,3200]{1,0:T(8,128)(2,1)S(1)}, u32[]{:S(2)}, u32[]{:S(2)}) collective-permute-start(bf16[32,3200]{1,0:T(8,128)(2,1)S(1)} %get-tuple-element.50), channel_id=1, source_target_pairs={{0,16},{1,65},{2,18},{3,67},{4,20},{5,69},{6,22},{7,71},{8,24},{9,... | collective-permute-start | bytes 614408 | tf_op jit(solution)/shard_map/ppermute | solution.py:42
  55.7 5.7 %collective-permute-start.13 = (bf16[32,3200]{1,0:T(8,128)(2,1)S(1)}, bf16[32,3200]{1,0:T(8,128)(2,1)S(1)}, u32[]{:S(2)}, u32[]{:S(2)}) collective-permute-start(bf16[32,3200]{1,0:T(8,128)(2,1)S(1)} %get-tuple-element.51), channel_id=1, source_target_pairs={{0,8},{1,33},{2,10},{3,35},{4,12},{5,37},{6,14},{7,39},{8,0},{9,41... | collective-permute-start | bytes 614408 | tf_op jit(solution)/shard_map/ppermute | solution.py:42
  56.1 5.8 %collective-permute-start.14 = (bf16[32,3200]{1,0:T(8,128)(2,1)S(1)}, bf16[32,3200]{1,0:T(8,128)(2,1)S(1)}, u32[]{:S(2)}, u32[]{:S(2)}) collective-permute-start(bf16[32,3200]{1,0:T(8,128)(2,1)S(1)} %get-tuple-element.52), channel_id=1, source_target_pairs={{0,24},{1,97},{2,26},{3,99},{4,28},{5,101},{6,30},{7,103},{8,16},{... | collective-permute-start | bytes 614408 | tf_op jit(solution)/shard_map/ppermute | solution.py:42
  62.6 4.5 %collective-permute-start.15 = (bf16[8,3200]{1,0:T(8,128)(2,1)S(1)}, bf16[8,3200]{1,0:T(8,128)(2,1)S(1)}, u32[]{:S(2)}, u32[]{:S(2)}) collective-permute-start(bf16[8,3200]{1,0:T(8,128)(2,1)S(1)} %get-tuple-element.54), channel_id=1, source_target_pairs={{0,4},{1,5},{2,6},{3,7},{4,0},{5,1},{6,2},{7,3},{8,12},{9,13},{10,... | collective-permute-start | bytes 153608 | tf_op jit(solution)/shard_map/ppermute | solution.py:46
  65.3 3.0 %collective-permute-start.16 = (bf16[8,3200]{1,0:T(8,128)(2,1)S(1)}, bf16[8,3200]{1,0:T(8,128)(2,1)S(1)}, u32[]{:S(2)}, u32[]{:S(2)}) collective-permute-start(bf16[8,3200]{1,0:T(8,128)(2,1)S(1)} %get-tuple-element.55), channel_id=1, source_target_pairs={{0,2},{1,3},{2,0},{3,1},{4,6},{5,7},{6,4},{7,5},{8,10},{9,11},{10,... | collective-permute-start | bytes 153608 | tf_op jit(solution)/shard_map/ppermute | solution.py:46
  65.6 4.2 %collective-permute-start.17 = (bf16[8,3200]{1,0:T(8,128)(2,1)S(1)}, bf16[8,3200]{1,0:T(8,128)(2,1)S(1)}, u32[]{:S(2)}, u32[]{:S(2)}) collective-permute-start(bf16[8,3200]{1,0:T(8,128)(2,1)S(1)} %get-tuple-element.56), channel_id=1, source_target_pairs={{0,6},{1,7},{2,4},{3,5},{4,2},{5,3},{6,0},{7,1},{8,14},{9,15},{10,... | collective-permute-start | bytes 153608 | tf_op jit(solution)/shard_map/ppermute | solution.py:46
  76.4 4.5 %collective-permute-start.18 = (bf16[8,3072]{1,0:T(8,128)(2,1)S(1)}, bf16[8,3072]{1,0:T(8,128)(2,1)S(1)}, u32[]{:S(2)}, u32[]{:S(2)}) collective-permute-start(bf16[8,3072]{1,0:T(8,128)(2,1)S(1)} %get-tuple-element.58), channel_id=1, source_target_pairs={{0,4},{1,5},{2,6},{3,7},{4,0},{5,1},{6,2},{7,3},{8,12},{9,13},{10,... | collective-permute-start | bytes 147464 | tf_op jit(solution)/shard_map/ppermute | solution.py:46
  77.4 3.5 %collective-permute-start.19 = (bf16[8,3072]{1,0:T(8,128)(2,1)S(1)}, bf16[8,3072]{1,0:T(8,128)(2,1)S(1)}, u32[]{:S(2)}, u32[]{:S(2)}) collective-permute-start(bf16[8,3072]{1,0:T(8,128)(2,1)S(1)} %get-tuple-element.59), channel_id=1, source_target_pairs={{0,2},{1,3},{2,0},{3,1},{4,6},{5,7},{6,4},{7,5},{8,10},{9,11},{10,... | collective-permute-start | bytes 147464 | tf_op jit(solution)/shard_map/ppermute | solution.py:46
  78.1 4.2 %collective-permute-start.20 = (bf16[8,3072]{1,0:T(8,128)(2,1)S(1)}, bf16[8,3072]{1,0:T(8,128)(2,1)S(1)}, u32[]{:S(2)}, u32[]{:S(2)}) collective-permute-start(bf16[8,3072]{1,0:T(8,128)(2,1)S(1)} %get-tuple-element.60), channel_id=1, source_target_pairs={{0,6},{1,7},{2,4},{3,5},{4,2},{5,3},{6,0},{7,1},{8,14},{9,15},{10,... | collective-permute-start | bytes 147464 | tf_op jit(solution)/shard_map/ppermute | solution.py:46
  82.8 6.1 %collective-permute-start.21 = (bf16[32,3072]{1,0:T(8,128)(2,1)S(1)}, bf16[32,3072]{1,0:T(8,128)(2,1)S(1)}, u32[]{:S(2)}, u32[]{:S(2)}) collective-permute-start(bf16[32,3072]{1,0:T(8,128)(2,1)S(1)} %line_up.1), channel_id=1, source_target_pairs={{0,64},{1,17},{2,66},{3,19},{4,68},{5,21},{6,70},{7,23},{8,72},{9,... | collective-permute-start | bytes 589832 | tf_op jit(solution)/shard_map/ppermute | solution.py:38
  84.8 6.1 %collective-permute-start.22 = (bf16[32,3072]{1,0:T(8,128)(2,1)S(1)}, bf16[32,3072]{1,0:T(8,128)(2,1)S(1)}, u32[]{:S(2)}, u32[]{:S(2)}) collective-permute-start(bf16[32,3072]{1,0:T(8,128)(2,1)S(1)} %line_up.1), channel_id=1, source_target_pairs={{0,32},{1,9},{2,34},{3,11},{4,36},{5,13},{6,38},{7,15},{8,40},{9,1... | collective-permute-start | bytes 589832 | tf_op jit(solution)/shard_map/ppermute | solution.py:38
  85.7 5.7 %collective-permute-start.23 = (bf16[32,3072]{1,0:T(8,128)(2,1)S(1)}, bf16[32,3072]{1,0:T(8,128)(2,1)S(1)}, u32[]{:S(2)}, u32[]{:S(2)}) collective-permute-start(bf16[32,3072]{1,0:T(8,128)(2,1)S(1)} %line_up.1), channel_id=1, source_target_pairs={{0,96},{1,25},{2,98},{3,27},{4,100},{5,29},{6,102},{7,31},{8,104},... | collective-permute-start | bytes 589832 | tf_op jit(solution)/shard_map/ppermute | solution.py:38
  91.5 14.9 %collective-permute-start.24 = (bf16[128,3072]{1,0:T(8,128)(2,1)S(1)}, bf16[128,3072]{1,0:T(8,128)(2,1)S(1)}, u32[]{:S(2)}, u32[]{:S(2)}) collective-permute-start(bf16[128,3072]{1,0:T(8,128)(2,1)S(1)} %pad_maximum_fusion.refs_0_), channel_id=1, source_target_pairs={{0,8},{1,33},{2,10},{3,35},{4,12},{5,37},{6,14},{7,39},{8,0},{9,41... | collective-permute-start | bytes 2359304 | tf_op jit(solution)/shard_map/ppermute | solution.py:42
  92.1 15.1 %collective-permute-start.25 = (bf16[128,3072]{1,0:T(8,128)(2,1)S(1)}, bf16[128,3072]{1,0:T(8,128)(2,1)S(1)}, u32[]{:S(2)}, u32[]{:S(2)}) collective-permute-start(bf16[128,3072]{1,0:T(8,128)(2,1)S(1)} %pad_maximum_fusion.refs_0_), channel_id=1, source_target_pairs={{0,24},{1,97},{2,26},{3,99},{4,28},{5,101},{6,30},{7,103},{8,16},{... | collective-permute-start | bytes 2359304 | tf_op jit(solution)/shard_map/ppermute | solution.py:42
  106.4 12.6 %collective-permute-start.27 = (bf16[128,3072]{1,0:T(8,128)(2,1)S(1)}, bf16[128,3072]{1,0:T(8,128)(2,1)S(1)}, u32[]{:S(2)}, u32[]{:S(2)}) collective-permute-start(bf16[128,3072]{1,0:T(8,128)(2,1)S(1)} %pad_maximum_fusion.refs_0_), channel_id=1, source_target_pairs={{0,16},{1,65},{2,18},{3,67},{4,20},{5,69},{6,22},{7,71},{8,24},{9,... | collective-permute-start | bytes 2359304 | tf_op jit(solution)/shard_map/ppermute | solution.py:42
  121.1 7.3 %collective-permute-start.28 = (bf16[128,1152]{1,0:T(8,128)(2,1)S(1)}, bf16[128,1152]{1,0:T(8,128)(2,1)S(1)}, u32[]{:S(2)}, u32[]{:S(2)}) collective-permute-start(bf16[128,1152]{1,0:T(8,128)(2,1)S(1)} %get-tuple-element.66), channel_id=1, source_target_pairs={{0,4},{1,5},{2,6},{3,7},{4,0},{5,1},{6,2},{7,3},{8,12},{9,13},{10,... | collective-permute-start | bytes 884744 | tf_op jit(solution)/shard_map/ppermute | solution.py:46
  122.2 8.8 %collective-permute-start.29 = (bf16[128,1152]{1,0:T(8,128)(2,1)S(1)}, bf16[128,1152]{1,0:T(8,128)(2,1)S(1)}, u32[]{:S(2)}, u32[]{:S(2)}) collective-permute-start(bf16[128,1152]{1,0:T(8,128)(2,1)S(1)} %get-tuple-element.67), channel_id=1, source_target_pairs={{0,2},{1,3},{2,0},{3,1},{4,6},{5,7},{6,4},{7,5},{8,10},{9,11},{10,... | collective-permute-start | bytes 884744 | tf_op jit(solution)/shard_map/ppermute | solution.py:46
  123.7 7.7 %collective-permute-start.30 = (bf16[128,1152]{1,0:T(8,128)(2,1)S(1)}, bf16[128,1152]{1,0:T(8,128)(2,1)S(1)}, u32[]{:S(2)}, u32[]{:S(2)}) collective-permute-start(bf16[128,1152]{1,0:T(8,128)(2,1)S(1)} %get-tuple-element.68), channel_id=1, source_target_pairs={{0,6},{1,7},{2,4},{3,5},{4,2},{5,3},{6,0},{7,1},{8,14},{9,15},{10,... | collective-permute-start | bytes 884744 | tf_op jit(solution)/shard_map/ppermute | solution.py:46
  131.6 10.9 %collective-permute-start.31 = (bf16[64,1152]{1,0:T(8,128)(2,1)S(1)}, bf16[64,1152]{1,0:T(8,128)(2,1)S(1)}, u32[]{:S(2)}, u32[]{:S(2)}) collective-permute-start(bf16[64,1152]{1,0:T(8,128)(2,1)S(1)} %get-tuple-element.69), channel_id=1, source_target_pairs={{0,1},{1,0},{2,3},{3,2},{4,5},{5,4},{6,7},{7,6},{8,9},{9,8},{10,11... | collective-permute-start | bytes 442376 | tf_op jit(solution)/shard_map/ppermute | solution.py:50
